TPU v7x, 32 devices: a whole 2x2x4 slice. The times are simulated.
32 devices in a mesh: group: 2 (over x), exp: 16 (over z, y, core).
Axes of the slice: x: 2, y: 2, z: 4, core: 2. Of those that a mesh axis runs over, the one named last changes fastest.
Arguments:
- tokens: bfloat16 [4096, 3584], P(('group', 'exp')), parts along dimension 0
- norm_gain: float32 [3584], replicated, may hold values from 0.25 to 1.75
- expert_ids: int32 [4096, 8], P(('group', 'exp')), parts along dimension 0, may hold values from 0 to 255, as said below
- gate_weights: float32 [4096, 8], P(('group', 'exp')), parts along dimension 0, may hold values from 0.2 to 2.5
- w_gate: bfloat16 [16, 3584, 512], P('exp'), may hold values from -0.09375 to 0.09375
- w_up: bfloat16 [16, 3584, 512], P('exp'), may hold values from -0.09375 to 0.09375
- w_down: bfloat16 [16, 512, 3584], P('exp'), may hold values from -0.1875 to 0.1875
Outputs:
- routed_out: bfloat16 [4096, 3584], P(('group', 'exp')), parts along dimension 0
There are 2 independent parts, one for each index of `group`. A program takes and returns all parts, laid end to end along the dimension named above; an argument that names none is the same for every part. Nothing has to cross between parts.
Inputs may be any that keep to these rules, and one draw needn't show every extreme that they name: `expert_ids`: each row names 8 different experts. Among the rows of one device an expert below 8 is named by at most 7 rows; in every draw one such expert is named by exactly 7 rows of every device.
All inputs are finite; a program needn't handle non-finite values.
Results may differ from a plain program's by a relative error of at most 0.0072.
Values may be sent and summed in bfloat16 or wider, within the bound.
No kernel may reach another device: no remote copies, remote signals or barrier semaphores. Data moves between devices by JAX's collectives and lax.ppermute only.
A program may use at most 128 MiB of HBM per device.

v0:
```python
import jax
import jax.numpy as jnp
from jax import lax
from jax.sharding import PartitionSpec as P

TOP = 8
CAP = 7


def expert_rows(received, gate_m, up_m, down_m):
    sources, slots, width = received.shape
    flat_rows = received.reshape(sources * slots, width)
    gate_v = jnp.dot(flat_rows, gate_m, preferred_element_type=jnp.float32)
    up_v = jnp.dot(flat_rows, up_m, preferred_element_type=jnp.float32)
    hidden = (jax.nn.silu(gate_v) * up_v).astype(jnp.bfloat16)
    projected = jnp.dot(hidden, down_m, preferred_element_type=jnp.float32)
    return projected.astype(jnp.bfloat16).reshape(sources, slots, width)


def per_device(tokens, norm_gain, expert_ids, gate_weights, w_gate, w_up, w_down):
    owners = lax.axis_size("exp")
    flight = owners // 2
    token_count, width = tokens.shape
    wide = tokens.astype(jnp.float32)
    mean_square = jnp.mean(wide * wide, axis=1, keepdims=True)
    normed = (wide * lax.rsqrt(mean_square + 1e-06) * norm_gain[None, :]).astype(jnp.bfloat16)
    flat_ids = expert_ids.reshape(-1)
    assign_count = flat_ids.shape[0]
    in_flight = flat_ids < flight
    places = jnp.arange(assign_count, dtype=jnp.int32)
    same_id = flat_ids[:, None] == flat_ids[None, :]
    earlier = places[:, None] > places[None, :]
    slot_rank = jnp.sum((same_id & earlier).astype(jnp.int32), axis=1)
    buffer_row = flat_ids * CAP + slot_rank
    target = jnp.where(in_flight, buffer_row, flight * CAP)
    repeated = jnp.broadcast_to(normed[:, None, :], (token_count, TOP, width)).reshape(
        assign_count, width
    )
    outgoing = jnp.zeros((flight * CAP, width), jnp.bfloat16).at[target].set(repeated, mode="drop")
    outgoing = jnp.repeat(outgoing.reshape(flight, CAP, width), 2, axis=0)
    gate_m = w_gate[0]
    up_m = w_up[0]
    down_m = w_down[0]
    finished = expert_rows(
        lax.all_to_all(outgoing, "exp", split_axis=0, concat_axis=0, tiled=True),
        gate_m,
        up_m,
        down_m,
    )
    returned = lax.all_to_all(finished, "exp", split_axis=0, concat_axis=0, tiled=True)
    halves = returned.reshape(flight, 2, CAP, width).astype(jnp.float32)
    joined = (halves[:, 0] + halves[:, 1]).reshape(flight * CAP, width)
    safe_row = jnp.where(in_flight, buffer_row, 0)
    picked_rows = joined[safe_row]
    weighting = jnp.where(in_flight, gate_weights.reshape(-1), 0.0)
    scaled = picked_rows * weighting[:, None]
    combined = jnp.sum(scaled.reshape(token_count, TOP, width), axis=1)
    return combined.astype(jnp.bfloat16)


def solution(mesh):
    placed = (
        P(("group", "exp"), None),
        P(),
        P(("group", "exp"), None),
        P(("group", "exp"), None),
        P("exp", None, None),
        P("exp", None, None),
        P("exp", None, None),
    )
    return jax.shard_map(
        per_device, mesh=mesh, in_specs=placed, out_specs=P(("group", "exp"), None), check_vma=False
    )
```

profile of v0, /device:TPU:0, one launch (start us, length us, event | category | flops | bytes accessed | tf_op | source)
XLA Modules:
  0.0 100.9 jit_solution(11163702684760657106)
XLA Ops:
  0.0 0.7 broadcast_multiply_fusion
  0.7 0.8 copy.19
  1.5 1.4 %fusion.10 = f32[128]{0:T(128)S(1)} fusion(bf16[128,3584]{1,0:T(8,128)(2,1)} %param.7), kind=kLoop, calls=%fused_computation.18 | loop fusion | flops 1376128 | bytes 918016 | tf_op jit(solution)/shard_map/reduce_sum | solution.py:25
  2.9 0.7 broadcast_select_fusion
  3.6 0.1 copy.17
  3.8 0.1 lt.45
  3.9 0.1 copy.18
  4.0 0.1 mul.57
  4.1 0.1 eq.15
  4.2 0.5 convert_reduce_fusion
  4.7 1.5 %fusion.12 = bf16[128,3584]{1,0:T(8,128)(2,1)S(1)} fusion(bf16[128,3584]{1,0:T(8,128)(2,1)} %param.7, f32[3584]{0:T(1024)} %param.8, f32[128]{0:T(128)S(1)} %add_rsqrt_fusion), kind=kLoop, calls=%fused_computation.20 | loop fusion | flops 1835008 | bytes 1849856 | tf_op jit(solution)/shard_map/convert_element_type | solution.py:26
  6.2 9.8 %scatter_custom_fusion = bf16[56,3584]{1,0:T(8,128)(2,1)S(1)} fusion(s32[1024]{0:T(1024)S(1)} %bitcast.45, bf16[128,3584]{1,0:T(8,128)(2,1)S(1)} %fusion.12, bf16[]{:T(256)} %constant.9.clone.1), kind=kCustom, calls=%fused_computation.4 | custom fusion | bytes 1318914 | tf_op jit(solution)/shard_map/scatter | solution.py:39
  16.0 0.1 reshape.115
  16.2 0.1 broadcast_in_dim.31
  16.2 29.7 %all_to_all.10 = bf16[16,7,3584]{2,1,0:T(8,128)(2,1)S(1)} all-to-all(bf16[16,7,3584]{2,1,0:T(8,128)(2,1)S(1)} %bitcast.41), channel_id=1, replica_groups=mesh['group'=2,'exp'=16] {'exp'}, dimensions={0} | all-to-all | bytes 1605632 | tf_op jit(solution)/shard_map/all_to_all | solution.py:45
  46.0 0.3 reshape.117
  46.3 2.7 %fusion.7 = f32[112,512]{1,0:T(8,128)S(1)} fusion(bf16[112,3584]{1,0:T(8,128)(2,1)S(1)} %reshape.117, bf16[1,3584,512]{2,1,0:T(8,128)(2,1)} %param.11), kind=kOutput, calls=%fused_computation.13 | convolution fusion | flops 411041792 | bytes 4702208 | tf_op jit(solution)/shard_map/dot_general | solution.py:13
  49.0 4.5 %convolution_convert_fusion = bf16[112,3584]{1,0:T(8,128)(2,1)S(1)} fusion(bf16[1,512,3584]{2,1,0:T(8,128)(2,1)} %param.13, bf16[112,3584]{1,0:T(8,128)(2,1)S(1)} %reshape.117, bf16[1,3584,512]{2,1,0:T(8,128)(2,1)} %param.12, f32[112,512]{1,0:T(8,128)S(1)} %fusion.7), kind=kOutput, calls=%fused_computation.6 | convolution fusion | flops 822829056 | bytes 9175040 | tf_op jit(solution)/shard_map/dot_general | solution.py:16
  53.4 1.2 %reshape.118 = bf16[16,7,3584]{2,1,0:T(8,128)(2,1)} reshape(bf16[112,3584]{1,0:T(8,128)(2,1)S(1)} %convolution_convert_fusion) | data formatting | bytes 1605632 | tf_op jit(solution)/shard_map/reshape | solution.py:17
  54.6 4.5 %all-to-all-start.1 = ((bf16[16,7,3584]{2,1,0:T(8,128)(2,1)}), bf16[16,7,3584]{2,1,0:T(8,128)(2,1)S(1)}, u32[]{:S(2)}, u32[]{:S(2)}) async-start(bf16[16,7,3584]{2,1,0:T(8,128)(2,1)} %reshape.118), calls=%async_computation.1 | async-start | bytes 1835008 | tf_op jit(solution)/shard_map/all_to_all | solution.py:50
  59.1 0.1 copy.22
  59.2 20.7 %all-to-all-done.1 = bf16[16,7,3584]{2,1,0:T(8,128)(2,1)S(1)} async-done(((bf16[16,7,3584]{2,1,0:T(8,128)(2,1)}), bf16[16,7,3584]{2,1,0:T(8,128)(2,1)S(1)}, u32[]{:S(2)}, u32[]{:S(2)}) %all-to-all-start.1) | async-done | bytes 802848 | tf_op jit(solution)/shard_map/all_to_all | solution.py:50
  79.9 0.2 convert.1
  80.1 0.1 fusion.19
  80.2 0.1 add.62
  80.4 8.9 %gather_fusion = f32[1024,3584]{1,0:T(8,128)} fusion(f32[56,3584]{1,0:T(8,128)S(1)} %add.62, s32[1024]{0:T(1024)S(1)} %broadcast_clamp_fusion), kind=kCustom, calls=%fused_computation | custom fusion | bytes 29364224 | tf_op jit(solution)/shard_map/gather | solution.py:54
  89.2 11.7 %fusion = bf16[128,3584]{1,0:T(8,128)(2,1)} fusion(f32[1024,3584]{1,0:T(8,128)} %gather_fusion, f32[128,8]{1,0:T(8,128)S(1)} %copy.22), kind=kLoop, calls=%fused_computation.3 | loop fusion | flops 6881280 | bytes 15601664 | tf_op jit(solution)/shard_map/reduce_sum | solution.py:57
  (3 shorter events, 0.0 us)
Async XLA Ops:
  54.6 25.3 %all-to-all-start.1 = ((bf16[16,7,3584]{2,1,0:T(8,128)(2,1)}), bf16[16,7,3584]{2,1,0:T(8,128)(2,1)S(1)}, u32[]{:S(2)}, u32[]{:S(2)}) async-start(bf16[16,7,3584]{2,1,0:T(8,128)(2,1)} %reshape.118), calls=%async_computation.1 | async-start | bytes 1835008 | tf_op jit(solution)/shard_map/all_to_all | solution.py:50
where the time goes:
time: 102 us; the launch traced here: 101 us
  blocking collectives  29.7 us (29%)
  local copies, waits for them, and re-layouts  21.9 us (21%)
  waiting for transfers between devices  20.7 us (20%)
  other arithmetic  16.9 us (17%)
  matrix products  7.17 us (7%)
  starting transfers between devices  4.48 us (4%)
    all_to_all x1, blocking collectives, per_device(): lax.all_to_all(outgoing, 'exp', split_axis=0, concat_axis=0, tiled=True)  29.7 us
    all_to_all x1, waiting for transfers between devices, per_device(): lax.all_to_all(finished, 'exp', split_axis=0, concat_axis=0, tiled=True)  20.7 us
    reduce_sum x1, other arithmetic, per_device(): combined = jnp.sum(scaled.reshape(token_count, TOP, width), axis=1)  11.7 us
    scatter x1, local copies, waits for them, and re-layouts, per_device(): jnp.zeros((flight * CAP, width), jnp.bfloat16).at[target]  9.82 us
    gather x1, local copies, waits for them, and re-layouts, per_device(): picked_rows = joined[safe_row]  8.87 us
    all_to_all x1, starting transfers between devices, per_device(): lax.all_to_all(finished, 'exp', split_axis=0, concat_axis=0, tiled=True)  4.48 us
    dot_general x1, matrix products, expert_rows(): projected = jnp.dot(hidden, down_m, preferred_element_type=jnp.float32)  4.46 us
    dot_general x1, matrix products, expert_rows(): gate_v = jnp.dot(flat_rows, gate_m, preferred_element_type=jnp.float32)  2.71 us
  transfers between devices with their start and end apart: 1, of which 1 were waited for; matrix products, arithmetic and copies ran while one was open for 0% of the time, Pallas kernels for 0%

commit v1 on v0

v1 whole, which is shorter than its diff:
```python
import functools

import jax
import jax.numpy as jnp
from jax import lax
from jax.experimental import pallas as pl
from jax.experimental.pallas import tpu as pltpu
from jax.sharding import PartitionSpec as P

CAP = 7
SLOTS = 8

VMEM = pl.BlockSpec(memory_space=pltpu.VMEM)
ANY = pl.BlockSpec(memory_space=pl.ANY)


def dispatch_kernel(flight, tok_ref, gain_ref, ids_ref, gw_ref, out_ref, mix_ref):
    count = tok_ref.shape[0]
    wide = tok_ref[...].astype(jnp.float32)
    mean_square = jnp.mean(wide * wide, axis=1, keepdims=True)
    normed = (wide * lax.rsqrt(mean_square + 1e-06) * gain_ref[...]).astype(jnp.bfloat16)

    experts = lax.broadcasted_iota(jnp.int32, (flight, count), 0)
    chosen = jnp.zeros((flight, count), jnp.float32)
    gates = jnp.zeros((flight, count), jnp.float32)
    for k in range(ids_ref.shape[0]):
        hit = ids_ref[k : k + 1, :] == experts
        chosen = jnp.where(hit, 1.0, chosen)
        gates = jnp.where(hit, gw_ref[k : k + 1, :], gates)
    before = (
        lax.broadcasted_iota(jnp.int32, (count, count), 0)
        < lax.broadcasted_iota(jnp.int32, (count, count), 1)
    ).astype(jnp.bfloat16)
    rank = jnp.dot(chosen.astype(jnp.bfloat16), before, preferred_element_type=jnp.float32)
    rank = jnp.where(chosen > 0.0, rank, -1.0)

    slot = lax.broadcasted_iota(jnp.int32, (flight, SLOTS, count), 1).astype(jnp.float32)
    taken = rank[:, None, :] == slot
    pick = jnp.where(taken, 1.0, 0.0).reshape(flight * SLOTS, count).astype(jnp.bfloat16)
    out_ref[...] = jnp.dot(pick, normed, preferred_element_type=jnp.float32).astype(jnp.bfloat16)
    mix = jnp.where(taken, gates[:, None, :], 0.0).reshape(flight * SLOTS, count)
    high = mix.astype(jnp.bfloat16)
    mix_ref[: flight * SLOTS, :] = high
    mix_ref[flight * SLOTS :, :] = (mix - high.astype(jnp.float32)).astype(jnp.bfloat16)


def expert_kernel(own_ref, other_ref, gate_ref, up_ref, down_ref, own_out, other_out):
    rows = own_ref.shape[0]
    x = jnp.concatenate([own_ref[...], other_ref[...]], axis=0)
    gate_v = jnp.dot(x, gate_ref[...], preferred_element_type=jnp.float32)
    up_v = jnp.dot(x, up_ref[...], preferred_element_type=jnp.float32)
    hidden = (gate_v / (1.0 + jnp.exp(-gate_v)) * up_v).astype(jnp.bfloat16)
    part = jnp.dot(hidden, down_ref[...], preferred_element_type=jnp.float32).astype(jnp.bfloat16)
    own_out[...] = part[:rows]
    other_out[...] = part[rows:]


def combine_kernel(mix_ref, rows_ref, out_ref):
    rows = rows_ref[...]
    both = jnp.concatenate([rows, rows], axis=0)
    out_ref[...] = lax.dot_general(
        mix_ref[...], both, (((0,), (0,)), ((), ())), preferred_element_type=jnp.float32
    ).astype(jnp.bfloat16)


def per_device(tokens, norm_gain, expert_ids, gate_weights, w_gate, w_up, w_down):
    owners = lax.axis_size("exp")
    flight = owners // 2
    count, width = tokens.shape
    packed = flight * SLOTS
    same_core = [list(range(core, owners, 2)) for core in range(2)]
    swap = [(i, i ^ 1) for i in range(owners)]
    params = pltpu.CompilerParams(vmem_limit_bytes=24 * 2**20)

    outgoing, mix = pl.pallas_call(
        functools.partial(dispatch_kernel, flight),
        out_shape=(
            jax.ShapeDtypeStruct((packed, width), jnp.bfloat16),
            jax.ShapeDtypeStruct((2 * packed, count), jnp.bfloat16),
        ),
        in_specs=[VMEM] * 4,
        out_specs=(VMEM, VMEM),
        compiler_params=params,
        name="dispatch",
    )(tokens, norm_gain[None, :], expert_ids.T, gate_weights.T)

    own = lax.all_to_all(
        outgoing, "exp", split_axis=0, concat_axis=0, axis_index_groups=same_core, tiled=True
    )
    other = lax.ppermute(own, "exp", swap)
    own_part, other_part = pl.pallas_call(
        expert_kernel,
        out_shape=(jax.ShapeDtypeStruct((packed, width), jnp.bfloat16),) * 2,
        in_specs=[VMEM] * 5,
        out_specs=(VMEM, VMEM),
        compiler_params=params,
        cost_estimate=pl.CostEstimate(
            flops=12 * packed * width * w_gate.shape[2],
            bytes_accessed=6 * width * w_gate.shape[2],
            transcendentals=0,
        ),
        name="experts",
    )(own, other, w_gate[0], w_up[0], w_down[0])
    from_other = lax.ppermute(other_part, "exp", swap)
    joined = (own_part.astype(jnp.float32) + from_other.astype(jnp.float32)).astype(jnp.bfloat16)
    returned = lax.all_to_all(
        joined, "exp", split_axis=0, concat_axis=0, axis_index_groups=same_core, tiled=True
    )
    return pl.pallas_call(
        combine_kernel,
        out_shape=jax.ShapeDtypeStruct((count, width), jnp.bfloat16),
        in_specs=[VMEM] * 2,
        out_specs=VMEM,
        compiler_params=params,
        name="combine",
    )(mix, returned)


def solution(mesh):
    placed = (
        P(("group", "exp"), None),
        P(),
        P(("group", "exp"), None),
        P(("group", "exp"), None),
        P("exp", None, None),
        P("exp", None, None),
        P("exp", None, None),
    )
    return jax.shard_map(
        per_device, mesh=mesh, in_specs=placed, out_specs=P(("group", "exp"), None), check_vma=False
    )
```

time: 102 us -> 54.4 us (0.53)
  waiting for transfers between devices: 20.7 us -> 3.5 us
  other arithmetic: 16.9 us -> 0.11 us
  local copies, waits for them, and re-layouts: 21.9 us -> 9.39 us
  blocking collectives: 29.7 us -> 37.1 us
  matrix products: 7.17 us -> 0 us
  starting transfers between devices: 4.48 us -> 0.2 us
  Pallas kernels: 0 us -> 3.62 us
    all_to_all x1 -> x0, waiting for transfers between devices: 20.7 us -> none  [per_device(): lax.all_to_all(finished, 'exp', split_axis=0, concat_axis=0, tiled=True)]
    reduce_sum x3 -> x0, other arithmetic: 13.7 us -> none  [the longest x1 11.7 us: per_device(): combined = jnp.sum(scaled.reshape(token_count, TOP, width), axis=1)]
    scatter x1 -> x0, local copies, waits for them, and re-layouts: 9.82 us -> none  [per_device(): jnp.zeros((flight * CAP, width), jnp.bfloat16).at[target]]
    gather x1 -> x0, local copies, waits for them, and re-layouts: 8.87 us -> none  [per_device(): picked_rows = joined[safe_row]]
    unnamed x1 -> x12, local copies, waits for them, and re-layouts: 0.79 us -> 8.66 us
    all_to_all x1 -> x2, blocking collectives: 29.7 us -> 37.1 us  [the longest x1 20.3 us: per_device(): lax.all_to_all(outgoing, 'exp', split_axis=0, concat_axis=0, axis_index_g...]
    dot_general x2 -> x0, matrix products: 7.17 us -> none  [the longest x1 4.46 us: expert_rows(): projected = jnp.dot(hidden, down_m, preferred_element_type=jnp.float32)]
    all_to_all x1 -> x0, starting transfers between devices: 4.48 us -> none  [per_device(): lax.all_to_all(finished, 'exp', split_axis=0, concat_axis=0, tiled=True)]
  transfers between devices with their start and end apart: 1 -> 2, of which waited for: 1 -> 2; matrix products, arithmetic and copies ran while one was open for 0% -> 0% of each run, Pallas kernels for 0% -> 0%
where the time goes in v1:
time: 54.4 us; the launch traced here: 54 us
  blocking collectives  37.1 us (68%)
  local copies, waits for them, and re-layouts  9.39 us (17%)
  Pallas kernels  3.62 us (7%)
  waiting for transfers between devices  3.5 us (6%)
    all_to_all x1, blocking collectives, per_device(): lax.all_to_all(outgoing, 'exp', split_axis=0, concat_axis=0, axis_index_g...  20.3 us
    all_to_all x1, blocking collectives, per_device(): lax.all_to_all(joined, 'exp', split_axis=0, concat_axis=0, axis_index_gro...  16.8 us
    unnamed x12, local copies, waits for them, and re-layouts  8.66 us
    ppermute x1, waiting for transfers between devices, per_device(): other = lax.ppermute(own, 'exp', swap)  1.81 us
    pallas_call x1, Pallas kernels, per_device(): pl.pallas_call(expert_kernel, out_shape=(jax.ShapeDtypeStruct((packed, wi...  1.71 us
    ppermute x1, waiting for transfers between devices, per_device(): from_other = lax.ppermute(other_part, 'exp', swap)  1.68 us
    pallas_call x1, Pallas kernels, per_device(): pl.pallas_call(combine_kernel, out_shape=jax.ShapeDtypeStruct((count, wid...  1.35 us
  transfers between devices with their start and end apart: 2, of which 2 were waited for; matrix products, arithmetic and copies ran while one was open for 0% of the time, Pallas kernels for 0%

profile of v1, /device:TPU:0, one launch (start us, length us, event | category | flops | bytes accessed | tf_op | source)
XLA Modules:
  0.0 54.0 jit_solution(15045169213500305288)
XLA Ops:
  0.0 0.7 %broadcast_in_dim.3.gain_ref = f32[1,3584]{1,0:T(1,128)S(1)} reshape(f32[3584]{0:T(1024)} %param.8) | data formatting | bytes 28672 | tf_op jit(solution)/shard_map/broadcast_in_dim | solution.py:85
  0.7 0.0 copy-start.3
  0.7 1.2 %copy-done.3 = bf16[128,3584]{1,0:T(8,128)(2,1)S(1)} copy-done((bf16[128,3584]{1,0:T(8,128)(2,1)S(1)}, bf16[128,3584]{1,0:T(8,128)(2,1)}, u32[]{:S(2)}) %copy-start.3) | copy-done | bytes 917528
  1.9 0.0 copy-start.4
  1.9 0.7 %copy-done.4 = s32[128,8]{0,1:T(8,128)S(1)} copy-done((s32[128,8]{0,1:T(8,128)S(1)}, s32[128,8]{0,1:T(8,128)}, u32[]{:S(2)}) %copy-start.4) | copy-done | bytes 4120
  2.6 0.0 copy-start.5
  2.6 0.7 %copy-done.5 = f32[128,8]{0,1:T(8,128)S(1)} copy-done((f32[128,8]{0,1:T(8,128)S(1)}, f32[128,8]{0,1:T(8,128)}, u32[]{:S(2)}) %copy-start.5) | copy-done | bytes 4120
  3.3 0.6 %dispatch.1 = (bf16[64,3584]{1,0:T(8,128)(2,1)S(1)}, bf16[128,128]{1,0:T(8,128)(2,1)S(1)}) custom-call(bf16[128,3584]{1,0:T(8,128)(2,1)S(1)} %copy-done.3, f32[1,3584]{1,0:T(1,128)S(1)} %broadcast_in_dim.3.gain_ref, s32[8,128]{1,0:T(8,128)S(1)} %bitcast.17, f32[8,128]{1,0:T(8,128)S(1)} %bitcast.18), custom_call_target="tpu_custom_call" | custom-call | tf_op jit(solution)/shard_map/dispatch/pallas_call | solution.py:75
  3.9 20.3 %all_to_all.22 = bf16[8,8,3584]{2,1,0:T(8,128)(2,1)S(1)} all-to-all(bf16[8,8,3584]{2,1,0:T(8,128)(2,1)S(1)} %bitcast.16), channel_id=1, replica_groups={{0,2,4,6,8,10,12,14},{1,3,5,7,9,11,13,15},{16,18,20,22,24,26,28,30},{17..., dimensions={0} | all-to-all | bytes 917504 | tf_op jit(solution)/shard_map/all_to_all | solution.py:87
  24.2 0.0 collective-permute-start
  24.2 1.8 %collective-permute-done.other_ref = bf16[64,3584]{1,0:T(8,128)(2,1)S(1)} collective-permute-done((bf16[64,3584]{1,0:T(8,128)(2,1)S(1)}, bf16[64,3584]{1,0:T(8,128)(2,1)S(1)}, u32[]{:S(2)}, u32[]{:S(2)}) %collective-permute-start) | collective-permute-done | bytes 458784 | tf_op jit(solution)/shard_map/ppermute | solution.py:90
  26.0 0.0 copy-start
  26.0 2.0 %copy-done = bf16[1,3584,512]{2,1,0:T(8,128)(2,1)S(1)} copy-done((bf16[1,3584,512]{2,1,0:T(8,128)(2,1)S(1)}, bf16[1,3584,512]{2,1,0:T(8,128)(2,1)}, u32[]{:S(2)}) %copy-start) | copy-done | bytes 3670040
  28.0 0.0 copy-start.1
  28.0 2.0 %copy-done.1 = bf16[1,3584,512]{2,1,0:T(8,128)(2,1)S(1)} copy-done((bf16[1,3584,512]{2,1,0:T(8,128)(2,1)S(1)}, bf16[1,3584,512]{2,1,0:T(8,128)(2,1)}, u32[]{:S(2)}) %copy-start.1) | copy-done | bytes 3670040
  30.1 0.0 copy-start.2
  30.1 2.0 %copy-done.2 = bf16[1,512,3584]{2,1,0:T(8,128)(2,1)S(1)} copy-done((bf16[1,512,3584]{2,1,0:T(8,128)(2,1)S(1)}, bf16[1,512,3584]{2,1,0:T(8,128)(2,1)}, u32[]{:S(2)}) %copy-start.2) | copy-done | bytes 3670040
  32.1 1.7 %experts.1 = (bf16[64,3584]{1,0:T(8,128)(2,1)S(1)}, bf16[64,3584]{1,0:T(8,128)(2,1)S(1)}) custom-call(bf16[64,3584]{1,0:T(8,128)(2,1)S(1)} %bitcast.15, bf16[64,3584]{1,0:T(8,128)(2,1)S(1)} %collective-permute-done.other_ref, bf16[3584,512]{1,0:T(8,128)(2,1)S(1)} %bitcast.10, bf16[3584,512]{1,0:T(8,128)(2,1)S(1)} %bitcast.11, bf16[512,3584]{1,0:T(8,128)(2,1)S(1)} %bitcast.12), custom_call_target="tpu_custom_call" | custom-call | flops 1409286144 | bytes 11010048 | tf_op jit(solution)/shard_map/experts/pallas_call | solution.py:91
  33.8 0.2 collective-permute-start.1
  34.0 1.7 %collective-permute-done.1 = bf16[64,3584]{1,0:T(8,128)(2,1)S(1)} collective-permute-done((bf16[64,3584]{1,0:T(8,128)(2,1)S(1)}, bf16[64,3584]{1,0:T(8,128)(2,1)S(1)}, u32[]{:S(2)}, u32[]{:S(2)}) %collective-permute-start.1) | collective-permute-done | bytes 458784 | tf_op jit(solution)/shard_map/ppermute | solution.py:104
  35.7 0.1 fusion
  35.8 16.8 %all_to_all.23 = bf16[8,8,3584]{2,1,0:T(8,128)(2,1)S(1)} all-to-all(bf16[8,8,3584]{2,1,0:T(8,128)(2,1)S(1)} %fusion), channel_id=1, replica_groups={{0,2,4,6,8,10,12,14},{1,3,5,7,9,11,13,15},{16,18,20,22,24,26,28,30},{17..., dimensions={0} | all-to-all | bytes 917504 | tf_op jit(solution)/shard_map/all_to_all | solution.py:106
  52.6 1.3 %combine.1 = bf16[128,3584]{1,0:T(8,128)(2,1)} custom-call(bf16[128,128]{1,0:T(8,128)(2,1)S(1)} %get-tuple-element.9.mix_ref, bf16[64,3584]{1,0:T(8,128)(2,1)S(1)} %bitcast.13), custom_call_target="tpu_custom_call" | custom-call | tf_op jit(solution)/shard_map/combine/pallas_call | solution.py:109
Async XLA Ops:
  0.7 1.2 %copy-start.3 = (bf16[128,3584]{1,0:T(8,128)(2,1)S(1)}, bf16[128,3584]{1,0:T(8,128)(2,1)}, u32[]{:S(2)}) copy-start(bf16[128,3584]{1,0:T(8,128)(2,1)} %tok_ref.1) | copy-start | bytes 2752516
  1.9 0.7 %copy-start.4 = (s32[128,8]{0,1:T(8,128)S(1)}, s32[128,8]{0,1:T(8,128)}, u32[]{:S(2)}) copy-start(s32[128,8]{0,1:T(8,128)} %param.9) | copy-start | bytes 12292
  2.6 0.7 %copy-start.5 = (f32[128,8]{0,1:T(8,128)S(1)}, f32[128,8]{0,1:T(8,128)}, u32[]{:S(2)}) copy-start(f32[128,8]{0,1:T(8,128)} %param.10) | copy-start | bytes 12292
  24.2 1.8 %collective-permute-start = (bf16[64,3584]{1,0:T(8,128)(2,1)S(1)}, bf16[64,3584]{1,0:T(8,128)(2,1)S(1)}, u32[]{:S(2)}, u32[]{:S(2)}) collective-permute-start(bf16[64,3584]{1,0:T(8,128)(2,1)S(1)} %bitcast.14), channel_id=1, source_target_pairs={{0,1},{1,0},{2,3},{3,2},{4,5},{5,4},{6,7},{7,6},{8,9},{9,8},{10,11... | collective-permute-start | bytes 1376264 | tf_op jit(solution)/shard_map/ppermute | solution.py:90
  26.0 2.0 %copy-start = (bf16[1,3584,512]{2,1,0:T(8,128)(2,1)S(1)}, bf16[1,3584,512]{2,1,0:T(8,128)(2,1)}, u32[]{:S(2)}) copy-start(bf16[1,3584,512]{2,1,0:T(8,128)(2,1)} %param.11) | copy-start | bytes 11010052
  28.0 2.0 %copy-start.1 = (bf16[1,3584,512]{2,1,0:T(8,128)(2,1)S(1)}, bf16[1,3584,512]{2,1,0:T(8,128)(2,1)}, u32[]{:S(2)}) copy-start(bf16[1,3584,512]{2,1,0:T(8,128)(2,1)} %param.12) | copy-start | bytes 11010052
  30.1 2.0 %copy-start.2 = (bf16[1,512,3584]{2,1,0:T(8,128)(2,1)S(1)}, bf16[1,512,3584]{2,1,0:T(8,128)(2,1)}, u32[]{:S(2)}) copy-start(bf16[1,512,3584]{2,1,0:T(8,128)(2,1)} %param.13) | copy-start | bytes 11010052
  33.8 1.9 %collective-permute-start.1 = (bf16[64,3584]{1,0:T(8,128)(2,1)S(1)}, bf16[64,3584]{1,0:T(8,128)(2,1)S(1)}, u32[]{:S(2)}, u32[]{:S(2)}) collective-permute-start(bf16[64,3584]{1,0:T(8,128)(2,1)S(1)} %get-tuple-element.12), channel_id=1, source_target_pairs={{0,1},{1,0},{2,3},{3,2},{4,5},{5,4},{6,7},{7,6},{8,9},{9,8},{10,11... | collective-permute-start | bytes 1376264 | tf_op jit(solution)/shard_map/ppermute | solution.py:104

commit v2 on v1

v2 whole, which is shorter than its diff:
```python
import functools

import jax
import jax.numpy as jnp
from jax import lax
from jax.experimental import pallas as pl
from jax.experimental.pallas import tpu as pltpu
from jax.sharding import PartitionSpec as P

SLOTS = 8
CHUNKS = 4

VMEM = pl.BlockSpec(memory_space=pltpu.VMEM)
HBM = pl.BlockSpec(memory_space=pltpu.HBM)


def in_hbm(*arrays):
    return [pltpu.with_memory_space_constraint(a, pltpu.HBM) for a in arrays]


def relative(flight):
    return flight <= 8


def dispatch_kernel(flight, tok_hbm, gain_hbm, ids_hbm, gw_hbm, mix_ref, *rest):
    outs = rest[:flight]
    tok, gain, ids, gw, normed, sems = rest[flight:]
    count = tok.shape[0]
    part = count // CHUNKS
    small = [
        pltpu.make_async_copy(ids_hbm, ids, sems.at[0]),
        pltpu.make_async_copy(gw_hbm, gw, sems.at[1]),
        pltpu.make_async_copy(gain_hbm, gain.at[0], sems.at[2]),
    ]
    large = [
        pltpu.make_async_copy(
            tok_hbm.at[pl.ds(i * part, part)], tok.at[pl.ds(i * part, part)], sems.at[3 + i]
        )
        for i in range(CHUNKS)
    ]
    for copy in small + large:
        copy.start()
    small[0].wait()
    small[1].wait()
    chip = lax.axis_index("exp") // 2 if relative(flight) else 0
    experts = lax.broadcasted_iota(jnp.int32, (flight, count), 0) ^ chip
    chosen = jnp.zeros((flight, count), jnp.float32)
    gates = jnp.zeros((flight, count), jnp.float32)
    for k in range(ids.shape[0]):
        hit = ids[k : k + 1, :] == experts
        chosen = jnp.where(hit, 1.0, chosen)
        gates = jnp.where(hit, gw[k : k + 1, :], gates)
    before = (
        lax.broadcasted_iota(jnp.int32, (count, count), 0)
        < lax.broadcasted_iota(jnp.int32, (count, count), 1)
    ).astype(jnp.bfloat16)
    rank = jnp.dot(chosen.astype(jnp.bfloat16), before, preferred_element_type=jnp.float32)
    rank = jnp.where(chosen > 0.0, rank, -1.0)

    slot = lax.broadcasted_iota(jnp.int32, (flight, SLOTS, count), 1).astype(jnp.float32)
    taken = rank[:, None, :] == slot
    pick = jnp.where(taken, 1.0, 0.0).reshape(flight * SLOTS, count).astype(jnp.bfloat16)
    mix = jnp.where(taken, gates[:, None, :], 0.0).reshape(flight * SLOTS, count)
    high = mix.astype(jnp.bfloat16)
    mix_ref[: flight * SLOTS, :] = high
    mix_ref[flight * SLOTS :, :] = (mix - high.astype(jnp.float32)).astype(jnp.bfloat16)

    small[2].wait()
    for i in range(CHUNKS):
        large[i].wait()
        wide = tok[pl.ds(i * part, part), :].astype(jnp.float32)
        mean_square = jnp.mean(wide * wide, axis=1, keepdims=True)
        normed[pl.ds(i * part, part), :] = (
            wide * lax.rsqrt(mean_square + 1e-06) * gain[...]
        ).astype(jnp.bfloat16)
    rows = jnp.dot(pick, normed[...], preferred_element_type=jnp.float32)
    for r in range(flight):
        outs[r][...] = rows[r * SLOTS : (r + 1) * SLOTS].astype(jnp.bfloat16)


def stage_kernel(gate_hbm, up_hbm, down_hbm, gate_ref, up_ref, down_ref, sems):
    copies = [
        pltpu.make_async_copy(source, target, sems.at[i])
        for i, (source, target) in enumerate(
            ((gate_hbm, gate_ref), (up_hbm, up_ref), (down_hbm, down_ref))
        )
    ]
    for copy in copies:
        copy.start()
    for copy in copies:
        copy.wait()


def expert_kernel(flight, *refs):
    blocks = refs[: 2 * flight]
    gate_ref, up_ref, down_ref = refs[2 * flight : 2 * flight + 3]
    outs = refs[2 * flight + 3 :]
    x = jnp.concatenate([b[...].astype(jnp.float32) for b in blocks], axis=0).astype(jnp.bfloat16)
    gate_v = jnp.dot(x, gate_ref[...], preferred_element_type=jnp.float32)
    up_v = jnp.dot(x, up_ref[...], preferred_element_type=jnp.float32)
    hidden = (gate_v / (1.0 + jnp.exp(-gate_v)) * up_v).astype(jnp.bfloat16)
    part = jnp.dot(hidden, down_ref[...], preferred_element_type=jnp.float32)
    for i, out in enumerate(outs):
        out[...] = part[i * SLOTS : (i + 1) * SLOTS].astype(jnp.bfloat16)


def combine_kernel(flight, mix_ref, *refs):
    rows = jnp.concatenate([b[...].astype(jnp.float32) for b in refs[:flight]], axis=0)
    rows = rows.astype(jnp.bfloat16)
    out_ref = refs[flight]
    both = jnp.concatenate([rows, rows], axis=0)
    out_ref[...] = lax.dot_general(
        mix_ref[...], both, (((0,), (0,)), ((), ())), preferred_element_type=jnp.float32
    ).astype(jnp.bfloat16)


def per_device(tokens, norm_gain, expert_ids, gate_weights, w_gate, w_up, w_down):
    owners = lax.axis_size("exp")
    flight = owners // 2
    count, width = tokens.shape
    hidden = w_gate.shape[2]
    packed = flight * SLOTS
    block = jax.ShapeDtypeStruct((SLOTS, width), jnp.bfloat16)

    few = relative(flight)

    def exchange(blocks):
        if few:
            return [blocks[0]] + [
                lax.ppermute(blocks[r], "exp", [(i, i ^ (2 * r)) for i in range(owners)])
                for r in range(1, flight)
            ]
        groups = [list(range(core, owners, 2)) for core in range(2)]
        got = lax.all_to_all(
            jnp.stack(blocks), "exp", split_axis=0, concat_axis=0, axis_index_groups=groups, tiled=True
        )
        return [got[r] for r in range(flight)]

    def swap(blocks):
        pairs = [(i, i ^ 1) for i in range(owners)]
        if few:
            return [lax.ppermute(b, "exp", pairs) for b in blocks]
        got = lax.ppermute(jnp.stack(blocks), "exp", pairs)
        return [got[r] for r in range(flight)]

    mix, *outgoing = pl.pallas_call(
        functools.partial(dispatch_kernel, flight),
        out_shape=(jax.ShapeDtypeStruct((2 * packed, count), jnp.bfloat16),) + (block,) * flight,
        in_specs=[HBM] * 4,
        out_specs=(VMEM,) * (flight + 1),
        scratch_shapes=[
            pltpu.VMEM((count, width), jnp.bfloat16),
            pltpu.VMEM((1, width), jnp.float32),
            pltpu.VMEM(expert_ids.shape[::-1], jnp.int32),
            pltpu.VMEM(gate_weights.shape[::-1], jnp.float32),
            pltpu.VMEM((count, width), jnp.bfloat16),
            pltpu.SemaphoreType.DMA((3 + CHUNKS,)),
        ],
        compiler_params=pltpu.CompilerParams(vmem_limit_bytes=32 * 2**20),
        name="dispatch",
    )(*in_hbm(tokens, norm_gain, expert_ids.T, gate_weights.T))

    staged = pl.pallas_call(
        stage_kernel,
        out_shape=tuple(
            jax.ShapeDtypeStruct(w.shape[1:], w.dtype) for w in (w_gate, w_up, w_down)
        ),
        in_specs=[HBM] * 3,
        out_specs=(VMEM,) * 3,
        scratch_shapes=[pltpu.SemaphoreType.DMA((3,))],
        compiler_params=pltpu.CompilerParams(vmem_limit_bytes=16 * 2**20),
        cost_estimate=pl.CostEstimate(
            flops=0, bytes_accessed=12 * width * hidden, transcendentals=0
        ),
        name="stage",
    )(*in_hbm(w_gate[0], w_up[0], w_down[0]))

    own = exchange(outgoing)
    other = swap(own)
    parts = pl.pallas_call(
        functools.partial(expert_kernel, flight),
        out_shape=(block,) * (2 * flight),
        in_specs=[VMEM] * (2 * flight + 3),
        out_specs=(VMEM,) * (2 * flight),
        compiler_params=pltpu.CompilerParams(vmem_limit_bytes=24 * 2**20),
        cost_estimate=pl.CostEstimate(
            flops=12 * packed * width * hidden,
            bytes_accessed=6 * width * hidden,
            transcendentals=0,
        ),
        name="experts",
    )(*own, *other, *staged)
    from_other = swap(parts[flight:])
    joined = [
        (a.astype(jnp.float32) + b.astype(jnp.float32)).astype(jnp.bfloat16)
        for a, b in zip(parts[:flight], from_other)
    ]
    returned = exchange(joined)
    return pl.pallas_call(
        functools.partial(combine_kernel, flight),
        out_shape=jax.ShapeDtypeStruct((count, width), jnp.bfloat16),
        in_specs=[VMEM] * (flight + 1),
        out_specs=VMEM,
        compiler_params=pltpu.CompilerParams(vmem_limit_bytes=24 * 2**20),
        name="combine",
    )(mix, *returned)


def solution(mesh):
    placed = (
        P(("group", "exp"), None),
        P(),
        P(("group", "exp"), None),
        P(("group", "exp"), None),
        P("exp", None, None),
        P("exp", None, None),
        P("exp", None, None),
    )
    return jax.shard_map(
        per_device, mesh=mesh, in_specs=placed, out_specs=P(("group", "exp"), None), check_vma=False
    )
```

time: 54.4 us -> 47.5 us (0.87)
  blocking collectives: 37.1 us -> 0 us
  starting transfers between devices: 0.2 us -> 28.1 us
  local copies, waits for them, and re-layouts: 9.39 us -> 0 us
  waiting for transfers between devices: 3.5 us -> 9.67 us
  Pallas kernels: 3.62 us -> 9.28 us
    all_to_all x2 -> x0, blocking collectives: 37.1 us -> none  [the longest x1 20.3 us: per_device(): lax.all_to_all(outgoing, 'exp', split_axis=0, concat_axis=0, axis_index_g...]
    ppermute x2 -> x30, starting transfers between devices: 0.2 us -> 28.1 us  [the longest x14 24 us: exchange(): lax.ppermute(blocks[r], 'exp', [(i, i ^ 2 * r) for i in range(owners)])]
    unnamed x12 -> x0, local copies, waits for them, and re-layouts: 8.66 us -> none
    ppermute x2 -> x30, waiting for transfers between devices: 3.5 us -> 9.67 us  [the longest x14 9.29 us: exchange(): lax.ppermute(blocks[r], 'exp', [(i, i ^ 2 * r) for i in range(owners)])]
    pallas_call x2 -> x3, Pallas kernels: 3.06 us -> 7.32 us  [the longest x1 4.23 us: per_device(): pl.pallas_call(stage_kernel, out_shape=tuple((jax.ShapeDtypeStruct(w.shap...]
    pallas_call x1, Pallas kernels: 0.56 us -> 1.96 us  [per_device(): pl.pallas_call(functools.partial(dispatch_kernel, flight), out_shape=(jax...]
    broadcast_in_dim x1 -> x0, local copies, waits for them, and re-layouts: 0.73 us -> none  [per_device(): norm_gain[None, :]]
  transfers between devices with their start and end apart: 2 -> 30, of which waited for: 2 -> 5; matrix products, arithmetic and copies ran while one was open for 0% -> 0% of each run, Pallas kernels for 0% -> 9%
where the time goes in v2:
time: 47.5 us; the launch traced here: 47.3 us
  starting transfers between devices  28.1 us (59%)
  waiting for transfers between devices  9.67 us (20%)
  Pallas kernels  9.28 us (20%)
    ppermute x14, starting transfers between devices, exchange(): lax.ppermute(blocks[r], 'exp', [(i, i ^ 2 * r) for i in range(owners)])  24 us
    ppermute x14, waiting for transfers between devices, exchange(): lax.ppermute(blocks[r], 'exp', [(i, i ^ 2 * r) for i in range(owners)])  9.29 us
    pallas_call x1, Pallas kernels, per_device(): pl.pallas_call(stage_kernel, out_shape=tuple((jax.ShapeDtypeStruct(w.shap...  4.23 us
    ppermute x16, starting transfers between devices, swap(): return [lax.ppermute(b, 'exp', pairs) for b in blocks]  4.12 us
    pallas_call x1, Pallas kernels, per_device(): pl.pallas_call(functools.partial(dispatch_kernel, flight), out_shape=(jax...  1.96 us
    pallas_call x1, Pallas kernels, per_device(): pl.pallas_call(functools.partial(expert_kernel, flight), out_shape=(block...  1.74 us
    pallas_call x1, Pallas kernels, per_device(): pl.pallas_call(functools.partial(combine_kernel, flight), out_shape=jax.S...  1.35 us
  transfers between devices with their start and end apart: 30, of which 5 were waited for; matrix products, arithmetic and copies ran while one was open for 0% of the time, Pallas kernels for 9%

profile of v2, /device:TPU:0, one launch (start us, length us, event | category | flops | bytes accessed | tf_op | source)
XLA Modules:
  0.0 47.3 jit_solution(17385538692123458153)
XLA Ops:
  0.0 2.0 %dispatch.1 = (bf16[128,128]{1,0:T(8,128)(2,1)S(1)}, bf16[8,3584]{1,0:T(8,128)(2,1)S(1)}, bf16[8,3584]{1,0:T(8,128)(2,1)S(1)}, bf16[8,3584]{1,0:T(8,128)(2,1)S(1...) custom-call(bf16[128,3584]{1,0:T(8,128)(2,1)} %tok_hbm.1, ...), custom_call_target="tpu_custom_call" | custom-call | tf_op jit(solution)/shard_map/dispatch/pallas_call | solution.py:146
  2.0 3.0 %collective-permute-start = (bf16[8,3584]{1,0:T(8,128)(2,1)S(1)}, bf16[8,3584]{1,0:T(8,128)(2,1)S(1)}, u32[]{:S(2)}, u32[]{:S(2)}) collective-permute-start(bf16[8,3584]{1,0:T(8,128)(2,1)S(1)} %get-tuple-element.35), channel_id=1, source_target_pairs={{0,2},{1,3},{2,0},{3,1},{4,6},{5,7},{6,4},{7,5},{8,10},{9,11},{10,... | collective-permute-start | bytes 172040 | tf_op jit(solution)/shard_map/ppermute | solution.py:130
  5.0 1.6 %collective-permute-start.1 = (bf16[8,3584]{1,0:T(8,128)(2,1)S(1)}, bf16[8,3584]{1,0:T(8,128)(2,1)S(1)}, u32[]{:S(2)}, u32[]{:S(2)}) collective-permute-start(bf16[8,3584]{1,0:T(8,128)(2,1)S(1)} %get-tuple-element.36), channel_id=1, source_target_pairs={{0,4},{1,5},{2,6},{3,7},{4,0},{5,1},{6,2},{7,3},{8,12},{9,13},{10,... | collective-permute-start | bytes 172040 | tf_op jit(solution)/shard_map/ppermute | solution.py:130
  6.6 3.0 %collective-permute-start.3 = (bf16[8,3584]{1,0:T(8,128)(2,1)S(1)}, bf16[8,3584]{1,0:T(8,128)(2,1)S(1)}, u32[]{:S(2)}, u32[]{:S(2)}) collective-permute-start(bf16[8,3584]{1,0:T(8,128)(2,1)S(1)} %get-tuple-element.38), channel_id=1, source_target_pairs={{0,8},{1,9},{2,10},{3,11},{4,12},{5,13},{6,14},{7,15},{8,0},{9,1},... | collective-permute-start | bytes 172040 | tf_op jit(solution)/shard_map/ppermute | solution.py:130
  9.6 1.3 %collective-permute-start.4 = (bf16[8,3584]{1,0:T(8,128)(2,1)S(1)}, bf16[8,3584]{1,0:T(8,128)(2,1)S(1)}, u32[]{:S(2)}, u32[]{:S(2)}) collective-permute-start(bf16[8,3584]{1,0:T(8,128)(2,1)S(1)} %get-tuple-element.39), channel_id=1, source_target_pairs={{0,10},{1,11},{2,8},{3,9},{4,14},{5,15},{6,12},{7,13},{8,2},{9,3},... | collective-permute-start | bytes 172040 | tf_op jit(solution)/shard_map/ppermute | solution.py:130
  10.9 3.6 %collective-permute-start.5 = (bf16[8,3584]{1,0:T(8,128)(2,1)S(1)}, bf16[8,3584]{1,0:T(8,128)(2,1)S(1)}, u32[]{:S(2)}, u32[]{:S(2)}) collective-permute-start(bf16[8,3584]{1,0:T(8,128)(2,1)S(1)} %get-tuple-element.40), channel_id=1, source_target_pairs={{0,12},{1,13},{2,14},{3,15},{4,8},{5,9},{6,10},{7,11},{8,4},{9,5},... | collective-permute-start | bytes 172040 | tf_op jit(solution)/shard_map/ppermute | solution.py:130
  14.6 0.5 %collective-permute-start.8 = (bf16[8,3584]{1,0:T(8,128)(2,1)S(1)}, bf16[8,3584]{1,0:T(8,128)(2,1)S(1)}, u32[]{:S(2)}, u32[]{:S(2)}) collective-permute-start(bf16[8,3584]{1,0:T(8,128)(2,1)S(1)} %collective-permute-done.refs_1_), channel_id=1, source_target_pairs={{0,1},{1,0},{2,3},{3,2},{4,5},{5,4},{6,7},{7,6},{8,9},{9,8},{10,11... | collective-permute-start | bytes 172040 | tf_op jit(solution)/shard_map/ppermute | solution.py:142
  15.1 3.7 %collective-permute-done.4.refs_5_ = bf16[8,3584]{1,0:T(8,128)(2,1)S(1)} collective-permute-done((bf16[8,3584]{1,0:T(8,128)(2,1)S(1)}, bf16[8,3584]{1,0:T(8,128)(2,1)S(1)}, u32[]{:S(2)}, u32[]{:S(2)}) %collective-permute-start.4) | collective-permute-done | bytes 57376 | tf_op jit(solution)/shard_map/ppermute | solution.py:130
  18.8 0.5 %collective-permute-start.10 = (bf16[8,3584]{1,0:T(8,128)(2,1)S(1)}, bf16[8,3584]{1,0:T(8,128)(2,1)S(1)}, u32[]{:S(2)}, u32[]{:S(2)}) collective-permute-start(bf16[8,3584]{1,0:T(8,128)(2,1)S(1)} %collective-permute-done.2.refs_3_), channel_id=1, source_target_pairs={{0,1},{1,0},{2,3},{3,2},{4,5},{5,4},{6,7},{7,6},{8,9},{9,8},{10,11... | collective-permute-start | bytes 172040 | tf_op jit(solution)/shard_map/ppermute | solution.py:142
  19.3 2.1 %collective-permute-done.6.refs_7_ = bf16[8,3584]{1,0:T(8,128)(2,1)S(1)} collective-permute-done((bf16[8,3584]{1,0:T(8,128)(2,1)S(1)}, bf16[8,3584]{1,0:T(8,128)(2,1)S(1)}, u32[]{:S(2)}, u32[]{:S(2)}) %collective-permute-start.6) | collective-permute-done | bytes 57376 | tf_op jit(solution)/shard_map/ppermute | solution.py:130
  21.3 0.5 %collective-permute-start.12 = (bf16[8,3584]{1,0:T(8,128)(2,1)S(1)}, bf16[8,3584]{1,0:T(8,128)(2,1)S(1)}, u32[]{:S(2)}, u32[]{:S(2)}) collective-permute-start(bf16[8,3584]{1,0:T(8,128)(2,1)S(1)} %collective-permute-done.4.refs_5_), channel_id=1, source_target_pairs={{0,1},{1,0},{2,3},{3,2},{4,5},{5,4},{6,7},{7,6},{8,9},{9,8},{10,11... | collective-permute-start | bytes 172040 | tf_op jit(solution)/shard_map/ppermute | solution.py:142
  21.9 0.4 collective-permute-start.14
  22.4 4.2 %stage.1 = (bf16[3584,512]{1,0:T(8,128)(2,1)S(1)}, bf16[3584,512]{1,0:T(8,128)(2,1)S(1)}, bf16[512,3584]{1,0:T(8,128)(2,1)S(1)}) custom-call(bf16[3584,512]{1,0:T(8,128)(2,1)} %bitcast.5, bf16[3584,512]{1,0:T(8,128)(2,1)} %bitcast.6, bf16[512,3584]{1,0:T(8,128)(2,1)} %bitcast.7), custom_call_target="tpu_custom_call" | custom-call | bytes 22020096 | tf_op jit(solution)/shard_map/stage/pallas_call | solution.py:163
  26.7 1.7 %experts.1 = (bf16[8,3584]{1,0:T(8,128)(2,1)S(1)}, bf16[8,3584]{1,0:T(8,128)(2,1)S(1)}, bf16[8,3584]{1,0:T(8,128)(2,1)S(1)}, bf16[8,3584]{1,0:T(8,128)(2,1)S(1)}...) custom-call(bf16[8,3584]{1,0:T(8,128)(2,1)S(1)} %get-tuple-element.3, ...), custom_call_target="tpu_custom_call" | custom-call | flops 1409286144 | bytes 11010048 | tf_op jit(solution)/shard_map/experts/pallas_call | solution.py:180
  28.4 0.1 collective-permute-start.16
  28.5 0.4 collective-permute-start.15
  29.0 0.1 collective-permute-start.18
  29.1 0.4 collective-permute-start.20
  29.6 0.1 collective-permute-done.16
  29.7 0.3 collective-permute-start.24
  30.0 0.2 collective-permute-done.18
  30.2 0.2 collective-permute-start.26
  30.4 0.4 collective-permute-start.28
  30.9 0.7 %collective-permute-start.17 = (bf16[8,3584]{1,0:T(8,128)(2,1)S(1)}, bf16[8,3584]{1,0:T(8,128)(2,1)S(1)}, u32[]{:S(2)}, u32[]{:S(2)}) collective-permute-start(bf16[8,3584]{1,0:T(8,128)(2,1)S(1)} %add_convert_fusion.6), channel_id=1, source_target_pairs={{0,2},{1,3},{2,0},{3,1},{4,6},{5,7},{6,4},{7,5},{8,10},{9,11},{10,... | collective-permute-start | bytes 172040 | tf_op jit(solution)/shard_map/ppermute | solution.py:130
  31.6 0.9 %collective-permute-start.19 = (bf16[8,3584]{1,0:T(8,128)(2,1)S(1)}, bf16[8,3584]{1,0:T(8,128)(2,1)S(1)}, u32[]{:S(2)}, u32[]{:S(2)}) collective-permute-start(bf16[8,3584]{1,0:T(8,128)(2,1)S(1)} %add_convert_fusion.5), channel_id=1, source_target_pairs={{0,4},{1,5},{2,6},{3,7},{4,0},{5,1},{6,2},{7,3},{8,12},{9,13},{10,... | collective-permute-start | bytes 172040 | tf_op jit(solution)/shard_map/ppermute | solution.py:130
  32.4 2.2 %collective-permute-start.21 = (bf16[8,3584]{1,0:T(8,128)(2,1)S(1)}, bf16[8,3584]{1,0:T(8,128)(2,1)S(1)}, u32[]{:S(2)}, u32[]{:S(2)}) collective-permute-start(bf16[8,3584]{1,0:T(8,128)(2,1)S(1)} %add_convert_fusion.4), channel_id=1, source_target_pairs={{0,6},{1,7},{2,4},{3,5},{4,2},{5,3},{6,0},{7,1},{8,14},{9,15},{10,... | collective-permute-start | bytes 172040 | tf_op jit(solution)/shard_map/ppermute | solution.py:130
  34.6 1.6 %collective-permute-start.23 = (bf16[8,3584]{1,0:T(8,128)(2,1)S(1)}, bf16[8,3584]{1,0:T(8,128)(2,1)S(1)}, u32[]{:S(2)}, u32[]{:S(2)}) collective-permute-start(bf16[8,3584]{1,0:T(8,128)(2,1)S(1)} %add_convert_fusion.3), channel_id=1, source_target_pairs={{0,8},{1,9},{2,10},{3,11},{4,12},{5,13},{6,14},{7,15},{8,0},{9,1},... | collective-permute-start | bytes 172040 | tf_op jit(solution)/shard_map/ppermute | solution.py:130
  36.2 1.5 %collective-permute-start.25 = (bf16[8,3584]{1,0:T(8,128)(2,1)S(1)}, bf16[8,3584]{1,0:T(8,128)(2,1)S(1)}, u32[]{:S(2)}, u32[]{:S(2)}) collective-permute-start(bf16[8,3584]{1,0:T(8,128)(2,1)S(1)} %add_convert_fusion.2), channel_id=1, source_target_pairs={{0,10},{1,11},{2,8},{3,9},{4,14},{5,15},{6,12},{7,13},{8,2},{9,3},... | collective-permute-start | bytes 172040 | tf_op jit(solution)/shard_map/ppermute | solution.py:130
  37.8 0.9 %collective-permute-start.27 = (bf16[8,3584]{1,0:T(8,128)(2,1)S(1)}, bf16[8,3584]{1,0:T(8,128)(2,1)S(1)}, u32[]{:S(2)}, u32[]{:S(2)}) collective-permute-start(bf16[8,3584]{1,0:T(8,128)(2,1)S(1)} %add_convert_fusion.1), channel_id=1, source_target_pairs={{0,12},{1,13},{2,14},{3,15},{4,8},{5,9},{6,10},{7,11},{8,4},{9,5},... | collective-permute-start | bytes 172040 | tf_op jit(solution)/shard_map/ppermute | solution.py:130
  38.7 3.8 %collective-permute-start.29 = (bf16[8,3584]{1,0:T(8,128)(2,1)S(1)}, bf16[8,3584]{1,0:T(8,128)(2,1)S(1)}, u32[]{:S(2)}, u32[]{:S(2)}) collective-permute-start(bf16[8,3584]{1,0:T(8,128)(2,1)S(1)} %add_convert_fusion), channel_id=1, source_target_pairs={{0,14},{1,15},{2,12},{3,13},{4,10},{5,11},{6,8},{7,9},{8,6},{9,7},... | collective-permute-start | bytes 172040 | tf_op jit(solution)/shard_map/ppermute | solution.py:130
  42.5 3.5 %collective-permute-done.25.refs_5_ = bf16[8,3584]{1,0:T(8,128)(2,1)S(1)} collective-permute-done((bf16[8,3584]{1,0:T(8,128)(2,1)S(1)}, bf16[8,3584]{1,0:T(8,128)(2,1)S(1)}, u32[]{:S(2)}, u32[]{:S(2)}) %collective-permute-start.25) | collective-permute-done | bytes 57376 | tf_op jit(solution)/shard_map/ppermute | solution.py:130
  46.0 1.4 %combine.1 = bf16[128,3584]{1,0:T(8,128)(2,1)} custom-call(bf16[128,128]{1,0:T(8,128)(2,1)S(1)} %get-tuple-element.33.mix_ref, bf16[8,3584]{1,0:T(8,128)(2,1)S(1)} %add_convert_fusion.7.refs_0_, bf16[8,3584]{1,0:T(8,128)(2,1)S(1)} %collective-permute-done.17.refs_1_, bf16[8,3584]{1,0:T(8,128)(2,1)S(1)} %collective-permute-done.19.refs_2_, ...), custom_call_target="tpu_custom_call" | custom-call | tf_op jit(solution)/shard_map/combine/pallas_call | solution.py:199
  (40 shorter events, 0.4 us)
Async XLA Ops:
  2.0 8.9 %collective-permute-start = (bf16[8,3584]{1,0:T(8,128)(2,1)S(1)}, bf16[8,3584]{1,0:T(8,128)(2,1)S(1)}, u32[]{:S(2)}, u32[]{:S(2)}) collective-permute-start(bf16[8,3584]{1,0:T(8,128)(2,1)S(1)} %get-tuple-element.35), channel_id=1, source_target_pairs={{0,2},{1,3},{2,0},{3,1},{4,6},{5,7},{6,4},{7,5},{8,10},{9,11},{10,... | collective-permute-start | bytes 172040 | tf_op jit(solution)/shard_map/ppermute | solution.py:130
  5.0 9.5 %collective-permute-start.1 = (bf16[8,3584]{1,0:T(8,128)(2,1)S(1)}, bf16[8,3584]{1,0:T(8,128)(2,1)S(1)}, u32[]{:S(2)}, u32[]{:S(2)}) collective-permute-start(bf16[8,3584]{1,0:T(8,128)(2,1)S(1)} %get-tuple-element.36), channel_id=1, source_target_pairs={{0,4},{1,5},{2,6},{3,7},{4,0},{5,1},{6,2},{7,3},{8,12},{9,13},{10,... | collective-permute-start | bytes 172040 | tf_op jit(solution)/shard_map/ppermute | solution.py:130
  6.6 7.9 %collective-permute-start.2 = (bf16[8,3584]{1,0:T(8,128)(2,1)S(1)}, bf16[8,3584]{1,0:T(8,128)(2,1)S(1)}, u32[]{:S(2)}, u32[]{:S(2)}) collective-permute-start(bf16[8,3584]{1,0:T(8,128)(2,1)S(1)} %get-tuple-element.37), channel_id=1, source_target_pairs={{0,6},{1,7},{2,4},{3,5},{4,2},{5,3},{6,0},{7,1},{8,14},{9,15},{10,... | collective-permute-start | bytes 172040 | tf_op jit(solution)/shard_map/ppermute | solution.py:130
  6.6 8.0 %collective-permute-start.3 = (bf16[8,3584]{1,0:T(8,128)(2,1)S(1)}, bf16[8,3584]{1,0:T(8,128)(2,1)S(1)}, u32[]{:S(2)}, u32[]{:S(2)}) collective-permute-start(bf16[8,3584]{1,0:T(8,128)(2,1)S(1)} %get-tuple-element.38), channel_id=1, source_target_pairs={{0,8},{1,9},{2,10},{3,11},{4,12},{5,13},{6,14},{7,15},{8,0},{9,1},... | collective-permute-start | bytes 172040 | tf_op jit(solution)/shard_map/ppermute | solution.py:130
  9.6 9.2 %collective-permute-start.4 = (bf16[8,3584]{1,0:T(8,128)(2,1)S(1)}, bf16[8,3584]{1,0:T(8,128)(2,1)S(1)}, u32[]{:S(2)}, u32[]{:S(2)}) collective-permute-start(bf16[8,3584]{1,0:T(8,128)(2,1)S(1)} %get-tuple-element.39), channel_id=1, source_target_pairs={{0,10},{1,11},{2,8},{3,9},{4,14},{5,15},{6,12},{7,13},{8,2},{9,3},... | collective-permute-start | bytes 172040 | tf_op jit(solution)/shard_map/ppermute | solution.py:130
  10.9 7.9 %collective-permute-start.5 = (bf16[8,3584]{1,0:T(8,128)(2,1)S(1)}, bf16[8,3584]{1,0:T(8,128)(2,1)S(1)}, u32[]{:S(2)}, u32[]{:S(2)}) collective-permute-start(bf16[8,3584]{1,0:T(8,128)(2,1)S(1)} %get-tuple-element.40), channel_id=1, source_target_pairs={{0,12},{1,13},{2,14},{3,15},{4,8},{5,9},{6,10},{7,11},{8,4},{9,5},... | collective-permute-start | bytes 172040 | tf_op jit(solution)/shard_map/ppermute | solution.py:130
  14.5 6.9 %collective-permute-start.6 = (bf16[8,3584]{1,0:T(8,128)(2,1)S(1)}, bf16[8,3584]{1,0:T(8,128)(2,1)S(1)}, u32[]{:S(2)}, u32[]{:S(2)}) collective-permute-start(bf16[8,3584]{1,0:T(8,128)(2,1)S(1)} %get-tuple-element.41), channel_id=1, source_target_pairs={{0,14},{1,15},{2,12},{3,13},{4,10},{5,11},{6,8},{7,9},{8,6},{9,7},... | collective-permute-start | bytes 172040 | tf_op jit(solution)/shard_map/ppermute | solution.py:130
  14.5 6.9 %collective-permute-start.7 = (bf16[8,3584]{1,0:T(8,128)(2,1)S(1)}, bf16[8,3584]{1,0:T(8,128)(2,1)S(1)}, u32[]{:S(2)}, u32[]{:S(2)}) collective-permute-start(bf16[8,3584]{1,0:T(8,128)(2,1)S(1)} %get-tuple-element.34.refs_0_), channel_id=1, source_target_pairs={{0,1},{1,0},{2,3},{3,2},{4,5},{5,4},{6,7},{7,6},{8,9},{9,8},{10,11... | collective-permute-start | bytes 172040 | tf_op jit(solution)/shard_map/ppermute | solution.py:142
  14.6 7.3 %collective-permute-start.8 = (bf16[8,3584]{1,0:T(8,128)(2,1)S(1)}, bf16[8,3584]{1,0:T(8,128)(2,1)S(1)}, u32[]{:S(2)}, u32[]{:S(2)}) collective-permute-start(bf16[8,3584]{1,0:T(8,128)(2,1)S(1)} %collective-permute-done.refs_1_), channel_id=1, source_target_pairs={{0,1},{1,0},{2,3},{3,2},{4,5},{5,4},{6,7},{7,6},{8,9},{9,8},{10,11... | collective-permute-start | bytes 172040 | tf_op jit(solution)/shard_map/ppermute | solution.py:142
  18.8 3.2 %collective-permute-start.9 = (bf16[8,3584]{1,0:T(8,128)(2,1)S(1)}, bf16[8,3584]{1,0:T(8,128)(2,1)S(1)}, u32[]{:S(2)}, u32[]{:S(2)}) collective-permute-start(bf16[8,3584]{1,0:T(8,128)(2,1)S(1)} %collective-permute-done.1.refs_2_), channel_id=1, source_target_pairs={{0,1},{1,0},{2,3},{3,2},{4,5},{5,4},{6,7},{7,6},{8,9},{9,8},{10,11... | collective-permute-start | bytes 172040 | tf_op jit(solution)/shard_map/ppermute | solution.py:142
  18.8 7.8 %collective-permute-start.10 = (bf16[8,3584]{1,0:T(8,128)(2,1)S(1)}, bf16[8,3584]{1,0:T(8,128)(2,1)S(1)}, u32[]{:S(2)}, u32[]{:S(2)}) collective-permute-start(bf16[8,3584]{1,0:T(8,128)(2,1)S(1)} %collective-permute-done.2.refs_3_), channel_id=1, source_target_pairs={{0,1},{1,0},{2,3},{3,2},{4,5},{5,4},{6,7},{7,6},{8,9},{9,8},{10,11... | collective-permute-start | bytes 172040 | tf_op jit(solution)/shard_map/ppermute | solution.py:142
  21.3 5.3 %collective-permute-start.11 = (bf16[8,3584]{1,0:T(8,128)(2,1)S(1)}, bf16[8,3584]{1,0:T(8,128)(2,1)S(1)}, u32[]{:S(2)}, u32[]{:S(2)}) collective-permute-start(bf16[8,3584]{1,0:T(8,128)(2,1)S(1)} %collective-permute-done.3.refs_4_), channel_id=1, source_target_pairs={{0,1},{1,0},{2,3},{3,2},{4,5},{5,4},{6,7},{7,6},{8,9},{9,8},{10,11... | collective-permute-start | bytes 172040 | tf_op jit(solution)/shard_map/ppermute | solution.py:142
  21.3 5.3 %collective-permute-start.12 = (bf16[8,3584]{1,0:T(8,128)(2,1)S(1)}, bf16[8,3584]{1,0:T(8,128)(2,1)S(1)}, u32[]{:S(2)}, u32[]{:S(2)}) collective-permute-start(bf16[8,3584]{1,0:T(8,128)(2,1)S(1)} %collective-permute-done.4.refs_5_), channel_id=1, source_target_pairs={{0,1},{1,0},{2,3},{3,2},{4,5},{5,4},{6,7},{7,6},{8,9},{9,8},{10,11... | collective-permute-start | bytes 172040 | tf_op jit(solution)/shard_map/ppermute | solution.py:142
  21.9 4.8 %collective-permute-start.13 = (bf16[8,3584]{1,0:T(8,128)(2,1)S(1)}, bf16[8,3584]{1,0:T(8,128)(2,1)S(1)}, u32[]{:S(2)}, u32[]{:S(2)}) collective-permute-start(bf16[8,3584]{1,0:T(8,128)(2,1)S(1)} %collective-permute-done.5.refs_6_), channel_id=1, source_target_pairs={{0,1},{1,0},{2,3},{3,2},{4,5},{5,4},{6,7},{7,6},{8,9},{9,8},{10,11... | collective-permute-start | bytes 172040 | tf_op jit(solution)/shard_map/ppermute | solution.py:142
  21.9 4.7 %collective-permute-start.14 = (bf16[8,3584]{1,0:T(8,128)(2,1)S(1)}, bf16[8,3584]{1,0:T(8,128)(2,1)S(1)}, u32[]{:S(2)}, u32[]{:S(2)}) collective-permute-start(bf16[8,3584]{1,0:T(8,128)(2,1)S(1)} %collective-permute-done.6.refs_7_), channel_id=1, source_target_pairs={{0,1},{1,0},{2,3},{3,2},{4,5},{5,4},{6,7},{7,6},{8,9},{9,8},{10,11... | collective-permute-start | bytes 172040 | tf_op jit(solution)/shard_map/ppermute | solution.py:142
  28.4 1.3 %collective-permute-start.16 = (bf16[8,3584]{1,0:T(8,128)(2,1)S(1)}, bf16[8,3584]{1,0:T(8,128)(2,1)S(1)}, u32[]{:S(2)}, u32[]{:S(2)}) collective-permute-start(bf16[8,3584]{1,0:T(8,128)(2,1)S(1)} %get-tuple-element.48), channel_id=1, source_target_pairs={{0,1},{1,0},{2,3},{3,2},{4,5},{5,4},{6,7},{7,6},{8,9},{9,8},{10,11... | collective-permute-start | bytes 172040 | tf_op jit(solution)/shard_map/ppermute | solution.py:142
  28.5 7.7 %collective-permute-start.15 = (bf16[8,3584]{1,0:T(8,128)(2,1)S(1)}, bf16[8,3584]{1,0:T(8,128)(2,1)S(1)}, u32[]{:S(2)}, u32[]{:S(2)}) collective-permute-start(bf16[8,3584]{1,0:T(8,128)(2,1)S(1)} %get-tuple-element.46), channel_id=1, source_target_pairs={{0,1},{1,0},{2,3},{3,2},{4,5},{5,4},{6,7},{7,6},{8,9},{9,8},{10,11... | collective-permute-start | bytes 172040 | tf_op jit(solution)/shard_map/ppermute | solution.py:142
  29.0 1.2 %collective-permute-start.18 = (bf16[8,3584]{1,0:T(8,128)(2,1)S(1)}, bf16[8,3584]{1,0:T(8,128)(2,1)S(1)}, u32[]{:S(2)}, u32[]{:S(2)}) collective-permute-start(bf16[8,3584]{1,0:T(8,128)(2,1)S(1)} %get-tuple-element.50), channel_id=1, source_target_pairs={{0,1},{1,0},{2,3},{3,2},{4,5},{5,4},{6,7},{7,6},{8,9},{9,8},{10,11... | collective-permute-start | bytes 172040 | tf_op jit(solution)/shard_map/ppermute | solution.py:142
  29.1 1.3 %collective-permute-start.20 = (bf16[8,3584]{1,0:T(8,128)(2,1)S(1)}, bf16[8,3584]{1,0:T(8,128)(2,1)S(1)}, u32[]{:S(2)}, u32[]{:S(2)}) collective-permute-start(bf16[8,3584]{1,0:T(8,128)(2,1)S(1)} %get-tuple-element.52), channel_id=1, source_target_pairs={{0,1},{1,0},{2,3},{3,2},{4,5},{5,4},{6,7},{7,6},{8,9},{9,8},{10,11... | collective-permute-start | bytes 172040 | tf_op jit(solution)/shard_map/ppermute | solution.py:142
  29.5 1.4 %collective-permute-start.22 = (bf16[8,3584]{1,0:T(8,128)(2,1)S(1)}, bf16[8,3584]{1,0:T(8,128)(2,1)S(1)}, u32[]{:S(2)}, u32[]{:S(2)}) collective-permute-start(bf16[8,3584]{1,0:T(8,128)(2,1)S(1)} %get-tuple-element.54), channel_id=1, source_target_pairs={{0,1},{1,0},{2,3},{3,2},{4,5},{5,4},{6,7},{7,6},{8,9},{9,8},{10,11... | collective-permute-start | bytes 172040 | tf_op jit(solution)/shard_map/ppermute | solution.py:142
  29.7 1.8 %collective-permute-start.24 = (bf16[8,3584]{1,0:T(8,128)(2,1)S(1)}, bf16[8,3584]{1,0:T(8,128)(2,1)S(1)}, u32[]{:S(2)}, u32[]{:S(2)}) collective-permute-start(bf16[8,3584]{1,0:T(8,128)(2,1)S(1)} %get-tuple-element.56), channel_id=1, source_target_pairs={{0,1},{1,0},{2,3},{3,2},{4,5},{5,4},{6,7},{7,6},{8,9},{9,8},{10,11... | collective-permute-start | bytes 172040 | tf_op jit(solution)/shard_map/ppermute | solution.py:142
  30.2 2.2 %collective-permute-start.26 = (bf16[8,3584]{1,0:T(8,128)(2,1)S(1)}, bf16[8,3584]{1,0:T(8,128)(2,1)S(1)}, u32[]{:S(2)}, u32[]{:S(2)}) collective-permute-start(bf16[8,3584]{1,0:T(8,128)(2,1)S(1)} %get-tuple-element.58), channel_id=1, source_target_pairs={{0,1},{1,0},{2,3},{3,2},{4,5},{5,4},{6,7},{7,6},{8,9},{9,8},{10,11... | collective-permute-start | bytes 172040 | tf_op jit(solution)/shard_map/ppermute | solution.py:142
  30.4 4.2 %collective-permute-start.28 = (bf16[8,3584]{1,0:T(8,128)(2,1)S(1)}, bf16[8,3584]{1,0:T(8,128)(2,1)S(1)}, u32[]{:S(2)}, u32[]{:S(2)}) collective-permute-start(bf16[8,3584]{1,0:T(8,128)(2,1)S(1)} %get-tuple-element.60), channel_id=1, source_target_pairs={{0,1},{1,0},{2,3},{3,2},{4,5},{5,4},{6,7},{7,6},{8,9},{9,8},{10,11... | collective-permute-start | bytes 172040 | tf_op jit(solution)/shard_map/ppermute | solution.py:142
  30.9 6.9 %collective-permute-start.17 = (bf16[8,3584]{1,0:T(8,128)(2,1)S(1)}, bf16[8,3584]{1,0:T(8,128)(2,1)S(1)}, u32[]{:S(2)}, u32[]{:S(2)}) collective-permute-start(bf16[8,3584]{1,0:T(8,128)(2,1)S(1)} %add_convert_fusion.6), channel_id=1, source_target_pairs={{0,2},{1,3},{2,0},{3,1},{4,6},{5,7},{6,4},{7,5},{8,10},{9,11},{10,... | collective-permute-start | bytes 172040 | tf_op jit(solution)/shard_map/ppermute | solution.py:130
  31.6 7.1 %collective-permute-start.19 = (bf16[8,3584]{1,0:T(8,128)(2,1)S(1)}, bf16[8,3584]{1,0:T(8,128)(2,1)S(1)}, u32[]{:S(2)}, u32[]{:S(2)}) collective-permute-start(bf16[8,3584]{1,0:T(8,128)(2,1)S(1)} %add_convert_fusion.5), channel_id=1, source_target_pairs={{0,4},{1,5},{2,6},{3,7},{4,0},{5,1},{6,2},{7,3},{8,12},{9,13},{10,... | collective-permute-start | bytes 172040 | tf_op jit(solution)/shard_map/ppermute | solution.py:130
  32.4 10.0 %collective-permute-start.21 = (bf16[8,3584]{1,0:T(8,128)(2,1)S(1)}, bf16[8,3584]{1,0:T(8,128)(2,1)S(1)}, u32[]{:S(2)}, u32[]{:S(2)}) collective-permute-start(bf16[8,3584]{1,0:T(8,128)(2,1)S(1)} %add_convert_fusion.4), channel_id=1, source_target_pairs={{0,6},{1,7},{2,4},{3,5},{4,2},{5,3},{6,0},{7,1},{8,14},{9,15},{10,... | collective-permute-start | bytes 172040 | tf_op jit(solution)/shard_map/ppermute | solution.py:130
  34.6 7.8 %collective-permute-start.23 = (bf16[8,3584]{1,0:T(8,128)(2,1)S(1)}, bf16[8,3584]{1,0:T(8,128)(2,1)S(1)}, u32[]{:S(2)}, u32[]{:S(2)}) collective-permute-start(bf16[8,3584]{1,0:T(8,128)(2,1)S(1)} %add_convert_fusion.3), channel_id=1, source_target_pairs={{0,8},{1,9},{2,10},{3,11},{4,12},{5,13},{6,14},{7,15},{8,0},{9,1},... | collective-permute-start | bytes 172040 | tf_op jit(solution)/shard_map/ppermute | solution.py:130
  36.2 9.8 %collective-permute-start.25 = (bf16[8,3584]{1,0:T(8,128)(2,1)S(1)}, bf16[8,3584]{1,0:T(8,128)(2,1)S(1)}, u32[]{:S(2)}, u32[]{:S(2)}) collective-permute-start(bf16[8,3584]{1,0:T(8,128)(2,1)S(1)} %add_convert_fusion.2), channel_id=1, source_target_pairs={{0,10},{1,11},{2,8},{3,9},{4,14},{5,15},{6,12},{7,13},{8,2},{9,3},... | collective-permute-start | bytes 172040 | tf_op jit(solution)/shard_map/ppermute | solution.py:130
  37.8 8.2 %collective-permute-start.27 = (bf16[8,3584]{1,0:T(8,128)(2,1)S(1)}, bf16[8,3584]{1,0:T(8,128)(2,1)S(1)}, u32[]{:S(2)}, u32[]{:S(2)}) collective-permute-start(bf16[8,3584]{1,0:T(8,128)(2,1)S(1)} %add_convert_fusion.1), channel_id=1, source_target_pairs={{0,12},{1,13},{2,14},{3,15},{4,8},{5,9},{6,10},{7,11},{8,4},{9,5},... | collective-permute-start | bytes 172040 | tf_op jit(solution)/shard_map/ppermute | solution.py:130
  38.7 7.3 %collective-permute-start.29 = (bf16[8,3584]{1,0:T(8,128)(2,1)S(1)}, bf16[8,3584]{1,0:T(8,128)(2,1)S(1)}, u32[]{:S(2)}, u32[]{:S(2)}) collective-permute-start(bf16[8,3584]{1,0:T(8,128)(2,1)S(1)} %add_convert_fusion), channel_id=1, source_target_pairs={{0,14},{1,15},{2,12},{3,13},{4,10},{5,11},{6,8},{7,9},{8,6},{9,7},... | collective-permute-start | bytes 172040 | tf_op jit(solution)/shard_map/ppermute | solution.py:130

commit v3 on v2

--- a/solution.py
+++ b/solution.py
@@ -18,13 +18,8 @@
     return [pltpu.with_memory_space_constraint(a, pltpu.HBM) for a in arrays]
 
 
-def relative(flight):
-    return flight <= 8
-
-
 def dispatch_kernel(flight, tok_hbm, gain_hbm, ids_hbm, gw_hbm, mix_ref, *rest):
-    outs = rest[:flight]
-    tok, gain, ids, gw, normed, sems = rest[flight:]
+    out_ref, tok, gain, ids, gw, normed, sems = rest
     count = tok.shape[0]
     part = count // CHUNKS
     small = [
@@ -42,8 +37,7 @@
         copy.start()
     small[0].wait()
     small[1].wait()
-    chip = lax.axis_index("exp") // 2 if relative(flight) else 0
-    experts = lax.broadcasted_iota(jnp.int32, (flight, count), 0) ^ chip
+    experts = lax.broadcasted_iota(jnp.int32, (flight, count), 0)
     chosen = jnp.zeros((flight, count), jnp.float32)
     gates = jnp.zeros((flight, count), jnp.float32)
     for k in range(ids.shape[0]):
@@ -73,9 +67,7 @@
         normed[pl.ds(i * part, part), :] = (
             wide * lax.rsqrt(mean_square + 1e-06) * gain[...]
         ).astype(jnp.bfloat16)
-    rows = jnp.dot(pick, normed[...], preferred_element_type=jnp.float32)
-    for r in range(flight):
-        outs[r][...] = rows[r * SLOTS : (r + 1) * SLOTS].astype(jnp.bfloat16)
+    out_ref[...] = jnp.dot(pick, normed[...], preferred_element_type=jnp.float32).astype(jnp.bfloat16)
 
 
 def stage_kernel(gate_hbm, up_hbm, down_hbm, gate_ref, up_ref, down_ref, sems):
@@ -91,23 +83,19 @@
         copy.wait()
 
 
-def expert_kernel(flight, *refs):
-    blocks = refs[: 2 * flight]
-    gate_ref, up_ref, down_ref = refs[2 * flight : 2 * flight + 3]
-    outs = refs[2 * flight + 3 :]
-    x = jnp.concatenate([b[...].astype(jnp.float32) for b in blocks], axis=0).astype(jnp.bfloat16)
+def expert_kernel(own_ref, other_ref, gate_ref, up_ref, down_ref, own_out, other_out):
+    rows = own_ref.shape[0]
+    x = jnp.concatenate([own_ref[...], other_ref[...]], axis=0)
     gate_v = jnp.dot(x, gate_ref[...], preferred_element_type=jnp.float32)
     up_v = jnp.dot(x, up_ref[...], preferred_element_type=jnp.float32)
     hidden = (gate_v / (1.0 + jnp.exp(-gate_v)) * up_v).astype(jnp.bfloat16)
-    part = jnp.dot(hidden, down_ref[...], preferred_element_type=jnp.float32)
-    for i, out in enumerate(outs):
-        out[...] = part[i * SLOTS : (i + 1) * SLOTS].astype(jnp.bfloat16)
+    part = jnp.dot(hidden, down_ref[...], preferred_element_type=jnp.float32).astype(jnp.bfloat16)
+    own_out[...] = part[:rows]
+    other_out[...] = part[rows:]
 
 
-def combine_kernel(flight, mix_ref, *refs):
-    rows = jnp.concatenate([b[...].astype(jnp.float32) for b in refs[:flight]], axis=0)
-    rows = rows.astype(jnp.bfloat16)
-    out_ref = refs[flight]
+def combine_kernel(mix_ref, rows_ref, out_ref):
+    rows = rows_ref[...]
     both = jnp.concatenate([rows, rows], axis=0)
     out_ref[...] = lax.dot_general(
         mix_ref[...], both, (((0,), (0,)), ((), ())), preferred_element_type=jnp.float32
@@ -120,34 +108,20 @@
     count, width = tokens.shape
     hidden = w_gate.shape[2]
     packed = flight * SLOTS
-    block = jax.ShapeDtypeStruct((SLOTS, width), jnp.bfloat16)
+    block = jax.ShapeDtypeStruct((packed, width), jnp.bfloat16)
+    pairs = [(i, i ^ 1) for i in range(owners)]
+    groups = [list(range(core, owners, 2)) for core in range(2)]
 
-    few = relative(flight)
+    def exchange(rows):
+        return lax.all_to_all(
+            rows, "exp", split_axis=0, concat_axis=0, axis_index_groups=groups, tiled=True
+        )
 
-    def exchange(blocks):
-        if few:
-            return [blocks[0]] + [
-                lax.ppermute(blocks[r], "exp", [(i, i ^ (2 * r)) for i in range(owners)])
-                for r in range(1, flight)
-            ]
-        groups = [list(range(core, owners, 2)) for core in range(2)]
-        got = lax.all_to_all(
-            jnp.stack(blocks), "exp", split_axis=0, concat_axis=0, axis_index_groups=groups, tiled=True
-        )
-        return [got[r] for r in range(flight)]
-
-    def swap(blocks):
-        pairs = [(i, i ^ 1) for i in range(owners)]
-        if few:
-            return [lax.ppermute(b, "exp", pairs) for b in blocks]
-        got = lax.ppermute(jnp.stack(blocks), "exp", pairs)
-        return [got[r] for r in range(flight)]
-
-    mix, *outgoing = pl.pallas_call(
+    mix, outgoing = pl.pallas_call(
         functools.partial(dispatch_kernel, flight),
-        out_shape=(jax.ShapeDtypeStruct((2 * packed, count), jnp.bfloat16),) + (block,) * flight,
+        out_shape=(jax.ShapeDtypeStruct((2 * packed, count), jnp.bfloat16), block),
         in_specs=[HBM] * 4,
-        out_specs=(VMEM,) * (flight + 1),
+        out_specs=(VMEM, VMEM),
         scratch_shapes=[
             pltpu.VMEM((count, width), jnp.bfloat16),
             pltpu.VMEM((1, width), jnp.float32),
@@ -176,12 +150,12 @@
     )(*in_hbm(w_gate[0], w_up[0], w_down[0]))
 
     own = exchange(outgoing)
-    other = swap(own)
-    parts = pl.pallas_call(
-        functools.partial(expert_kernel, flight),
-        out_shape=(block,) * (2 * flight),
-        in_specs=[VMEM] * (2 * flight + 3),
-        out_specs=(VMEM,) * (2 * flight),
+    other = lax.ppermute(own, "exp", pairs)
+    own_part, other_part = pl.pallas_call(
+        expert_kernel,
+        out_shape=(block, block),
+        in_specs=[VMEM] * 5,
+        out_specs=(VMEM, VMEM),
         compiler_params=pltpu.CompilerParams(vmem_limit_bytes=24 * 2**20),
         cost_estimate=pl.CostEstimate(
             flops=12 * packed * width * hidden,
@@ -189,21 +163,17 @@
             transcendentals=0,
         ),
         name="experts",
-    )(*own, *other, *staged)
-    from_other = swap(parts[flight:])
-    joined = [
-        (a.astype(jnp.float32) + b.astype(jnp.float32)).astype(jnp.bfloat16)
-        for a, b in zip(parts[:flight], from_other)
-    ]
-    returned = exchange(joined)
+    )(own, other, *staged)
+    from_other = lax.ppermute(other_part, "exp", pairs)
+    joined = (own_part.astype(jnp.float32) + from_other.astype(jnp.float32)).astype(jnp.bfloat16)
     return pl.pallas_call(
-        functools.partial(combine_kernel, flight),
+        combine_kernel,
         out_shape=jax.ShapeDtypeStruct((count, width), jnp.bfloat16),
-        in_specs=[VMEM] * (flight + 1),
+        in_specs=[VMEM] * 2,
         out_specs=VMEM,
         compiler_params=pltpu.CompilerParams(vmem_limit_bytes=24 * 2**20),
         name="combine",
-    )(mix, *returned)
+    )(mix, exchange(joined))
 
 
 def solution(mesh):

time: 47.5 us -> 49 us (1.032)
  blocking collectives: 0 us -> 37.3 us
  starting transfers between devices: 28.1 us -> 0.58 us
  waiting for transfers between devices: 9.67 us -> 1.45 us
    all_to_all x0 -> x2, blocking collectives: none -> 37.3 us  [exchange(): lax.all_to_all(rows, 'exp', split_axis=0, concat_axis=0, axis_index_group...]
    ppermute x30 -> x2, starting transfers between devices: 28.1 us -> 0.58 us  [the longest x1 0.57 us: per_device(): from_other = lax.ppermute(other_part, 'exp', pairs)]
    ppermute x30 -> x2, waiting for transfers between devices: 9.67 us -> 1.45 us  [the longest x1 1.44 us: per_device(): from_other = lax.ppermute(other_part, 'exp', pairs)]
  transfers between devices with their start and end apart: 30 -> 2, of which waited for: 5 -> 1; matrix products, arithmetic and copies ran while one was open for 0% -> 0% of each run, Pallas kernels for 9% -> 9%
where the time goes in v3:
time: 49 us; the launch traced here: 48.7 us
  blocking collectives  37.3 us (76%)
  Pallas kernels  9.25 us (19%)
  waiting for transfers between devices  1.45 us (3%)
  starting transfers between devices  0.58 us (1%)
    all_to_all x2, blocking collectives, exchange(): lax.all_to_all(rows, 'exp', split_axis=0, concat_axis=0, axis_index_group...  37.3 us
    pallas_call x1, Pallas kernels, per_device(): pl.pallas_call(stage_kernel, out_shape=tuple((jax.ShapeDtypeStruct(w.shap...  4.23 us
    pallas_call x1, Pallas kernels, per_device(): pl.pallas_call(functools.partial(dispatch_kernel, flight), out_shape=(jax...  1.96 us
    pallas_call x1, Pallas kernels, per_device(): pl.pallas_call(expert_kernel, out_shape=(block, block), in_specs=[VMEM] *...  1.71 us
    ppermute x1, waiting for transfers between devices, per_device(): from_other = lax.ppermute(other_part, 'exp', pairs)  1.44 us
    pallas_call x1, Pallas kernels, per_device(): pl.pallas_call(combine_kernel, out_shape=jax.ShapeDtypeStruct((count, wid...  1.35 us
  transfers between devices with their start and end apart: 2, of which 1 were waited for; matrix products, arithmetic and copies ran while one was open for 0% of the time, Pallas kernels for 9%

profile of v3, /device:TPU:0, one launch (start us, length us, event | category | flops | bytes accessed | tf_op | source)
XLA Modules:
  0.0 48.7 jit_solution(11024285501515746894)
XLA Ops:
  0.0 2.0 %dispatch.1 = (bf16[128,128]{1,0:T(8,128)(2,1)S(1)}, bf16[64,3584]{1,0:T(8,128)(2,1)S(1)}) custom-call(bf16[128,3584]{1,0:T(8,128)(2,1)} %tok_hbm.1, f32[3584]{0:T(1024)} %gain_hbm.1, s32[8,128]{1,0:T(8,128)} %bitcast.17, f32[8,128]{1,0:T(8,128)} %bitcast.18), custom_call_target="tpu_custom_call" | custom-call | tf_op jit(solution)/shard_map/dispatch/pallas_call | solution.py:120
  2.0 20.3 %all_to_all.22 = bf16[8,8,3584]{2,1,0:T(8,128)(2,1)S(1)} all-to-all(bf16[8,8,3584]{2,1,0:T(8,128)(2,1)S(1)} %bitcast.13), channel_id=1, replica_groups={{0,2,4,6,8,10,12,14},{1,3,5,7,9,11,13,15},{16,18,20,22,24,26,28,30},{17..., dimensions={0} | all-to-all | bytes 917504 | tf_op jit(solution)/shard_map/all_to_all | solution.py:116
  22.3 0.0 collective-permute-start
  22.3 4.2 %stage.1 = (bf16[3584,512]{1,0:T(8,128)(2,1)S(1)}, bf16[3584,512]{1,0:T(8,128)(2,1)S(1)}, bf16[512,3584]{1,0:T(8,128)(2,1)S(1)}) custom-call(bf16[3584,512]{1,0:T(8,128)(2,1)} %bitcast.14, bf16[3584,512]{1,0:T(8,128)(2,1)} %bitcast.15, bf16[512,3584]{1,0:T(8,128)(2,1)} %bitcast.16), custom_call_target="tpu_custom_call" | custom-call | bytes 22020096 | tf_op jit(solution)/shard_map/stage/pallas_call | solution.py:137
  26.5 0.0 collective-permute-done.other_ref
  26.5 1.7 %experts.1 = (bf16[64,3584]{1,0:T(8,128)(2,1)S(1)}, bf16[64,3584]{1,0:T(8,128)(2,1)S(1)}) custom-call(bf16[64,3584]{1,0:T(8,128)(2,1)S(1)} %bitcast.12, bf16[64,3584]{1,0:T(8,128)(2,1)S(1)} %collective-permute-done.other_ref, bf16[3584,512]{1,0:T(8,128)(2,1)S(1)} %get-tuple-element.14.gate_ref, bf16[3584,512]{1,0:T(8,128)(2,1)S(1)} %get-tuple-element.15.up_ref, ...), custom_call_target="tpu_custom_call" | custom-call | flops 1409286144 | bytes 11010048 | tf_op jit(solution)/shard_map/experts/pallas_call | solution.py:154
  28.3 0.6 %collective-permute-start.1 = (bf16[64,3584]{1,0:T(8,128)(2,1)S(1)}, bf16[64,3584]{1,0:T(8,128)(2,1)S(1)}, u32[]{:S(2)}, u32[]{:S(2)}) collective-permute-start(bf16[64,3584]{1,0:T(8,128)(2,1)S(1)} %get-tuple-element.18), channel_id=1, source_target_pairs={{0,1},{1,0},{2,3},{3,2},{4,5},{5,4},{6,7},{7,6},{8,9},{9,8},{10,11... | collective-permute-start | bytes 1376264 | tf_op jit(solution)/shard_map/ppermute | solution.py:167
  28.8 1.4 %collective-permute-done.1 = bf16[64,3584]{1,0:T(8,128)(2,1)S(1)} collective-permute-done((bf16[64,3584]{1,0:T(8,128)(2,1)S(1)}, bf16[64,3584]{1,0:T(8,128)(2,1)S(1)}, u32[]{:S(2)}, u32[]{:S(2)}) %collective-permute-start.1) | collective-permute-done | bytes 458784 | tf_op jit(solution)/shard_map/ppermute | solution.py:167
  30.3 0.1 fusion
  30.4 17.0 %all_to_all.23 = bf16[8,8,3584]{2,1,0:T(8,128)(2,1)S(1)} all-to-all(bf16[8,8,3584]{2,1,0:T(8,128)(2,1)S(1)} %fusion), channel_id=1, replica_groups={{0,2,4,6,8,10,12,14},{1,3,5,7,9,11,13,15},{16,18,20,22,24,26,28,30},{17..., dimensions={0} | all-to-all | bytes 917504 | tf_op jit(solution)/shard_map/all_to_all | solution.py:116
  47.4 1.3 %combine.1 = bf16[128,3584]{1,0:T(8,128)(2,1)} custom-call(bf16[128,128]{1,0:T(8,128)(2,1)S(1)} %get-tuple-element.12.mix_ref, bf16[64,3584]{1,0:T(8,128)(2,1)S(1)} %bitcast.10), custom_call_target="tpu_custom_call" | custom-call | tf_op jit(solution)/shard_map/combine/pallas_call | solution.py:169
Async XLA Ops:
  22.3 4.2 %collective-permute-start = (bf16[64,3584]{1,0:T(8,128)(2,1)S(1)}, bf16[64,3584]{1,0:T(8,128)(2,1)S(1)}, u32[]{:S(2)}, u32[]{:S(2)}) collective-permute-start(bf16[64,3584]{1,0:T(8,128)(2,1)S(1)} %bitcast.11), channel_id=1, source_target_pairs={{0,1},{1,0},{2,3},{3,2},{4,5},{5,4},{6,7},{7,6},{8,9},{9,8},{10,11... | collective-permute-start | bytes 1376264 | tf_op jit(solution)/shard_map/ppermute | solution.py:153
  28.3 2.0 %collective-permute-start.1 = (bf16[64,3584]{1,0:T(8,128)(2,1)S(1)}, bf16[64,3584]{1,0:T(8,128)(2,1)S(1)}, u32[]{:S(2)}, u32[]{:S(2)}) collective-permute-start(bf16[64,3584]{1,0:T(8,128)(2,1)S(1)} %get-tuple-element.18), channel_id=1, source_target_pairs={{0,1},{1,0},{2,3},{3,2},{4,5},{5,4},{6,7},{7,6},{8,9},{9,8},{10,11... | collective-permute-start | bytes 1376264 | tf_op jit(solution)/shard_map/ppermute | solution.py:167

commit v4 on v3

--- a/solution.py
+++ b/solution.py
@@ -149,7 +149,7 @@
         name="stage",
     )(*in_hbm(w_gate[0], w_up[0], w_down[0]))
 
-    own = exchange(outgoing)
+    own, staged = lax.optimization_barrier((exchange(outgoing), staged))
     other = lax.ppermute(own, "exp", pairs)
     own_part, other_part = pl.pallas_call(
         expert_kernel,

time: 49 us -> 53.4 us (1.090)
  blocking collectives: 37.3 us -> 16.9 us
  local copies, waits for them, and re-layouts: 0 us -> 11.7 us
  starting transfers between devices: 0.58 us -> 7.5 us
  waiting for transfers between devices: 1.45 us -> 6.78 us
  Pallas kernels: 9.25 us -> 10 us
    all_to_all x2 -> x1, blocking collectives: 37.3 us -> 16.9 us  [exchange(): lax.all_to_all(rows, 'exp', split_axis=0, concat_axis=0, axis_index_group...]
    unnamed x0 -> x12, local copies, waits for them, and re-layouts: none -> 11.7 us
    all_to_all x0 -> x1, starting transfers between devices: none -> 7.3 us  [exchange(): lax.all_to_all(rows, 'exp', split_axis=0, concat_axis=0, axis_index_group...]
    all_to_all x0 -> x1, waiting for transfers between devices: none -> 3.29 us  [exchange(): lax.all_to_all(rows, 'exp', split_axis=0, concat_axis=0, axis_index_group...]
    ppermute x1, waiting for transfers between devices: 0.01 us -> 1.81 us  [per_device(): other = lax.ppermute(own, 'exp', pairs)]
    pallas_call x1, Pallas kernels: 1.96 us -> 2.73 us  [per_device(): pl.pallas_call(functools.partial(dispatch_kernel, flight), out_shape=(jax...]
  transfers between devices with their start and end apart: 2 -> 3, of which waited for: 1 -> 3; matrix products, arithmetic and copies ran while one was open for 0% -> 0% of each run, Pallas kernels for 9% -> 8%
where the time goes in v4:
time: 53.4 us; the launch traced here: 53 us
  blocking collectives  16.9 us (32%)
  local copies, waits for them, and re-layouts  11.7 us (22%)
  Pallas kernels  10 us (19%)
  starting transfers between devices  7.5 us (14%)
  waiting for transfers between devices  6.78 us (13%)
    all_to_all x1, blocking collectives, exchange(): lax.all_to_all(rows, 'exp', split_axis=0, concat_axis=0, axis_index_group...  16.9 us
    unnamed x12, local copies, waits for them, and re-layouts  11.7 us
    all_to_all x1, starting transfers between devices, exchange(): lax.all_to_all(rows, 'exp', split_axis=0, concat_axis=0, axis_index_group...  7.3 us
    pallas_call x1, Pallas kernels, per_device(): pl.pallas_call(stage_kernel, out_shape=tuple((jax.ShapeDtypeStruct(w.shap...  4.23 us
    all_to_all x1, waiting for transfers between devices, exchange(): lax.all_to_all(rows, 'exp', split_axis=0, concat_axis=0, axis_index_group...  3.29 us
    pallas_call x1, Pallas kernels, per_device(): pl.pallas_call(functools.partial(dispatch_kernel, flight), out_shape=(jax...  2.73 us
    ppermute x1, waiting for transfers between devices, per_device(): other = lax.ppermute(own, 'exp', pairs)  1.81 us
    pallas_call x1, Pallas kernels, per_device(): pl.pallas_call(expert_kernel, out_shape=(block, block), in_specs=[VMEM] *...  1.71 us
  transfers between devices with their start and end apart: 3, of which 3 were waited for; matrix products, arithmetic and copies ran while one was open for 0% of the time, Pallas kernels for 8%

profile of v4, /device:TPU:0, one launch (start us, length us, event | category | flops | bytes accessed | tf_op | source)
XLA Modules:
  0.0 53.0 jit_solution(1033057002465293174)
XLA Ops:
  0.0 2.7 %dispatch.1 = (bf16[128,128]{1,0:T(8,128)(2,1)S(1)}, bf16[64,3584]{1,0:T(8,128)(2,1)}) custom-call(bf16[128,3584]{1,0:T(8,128)(2,1)} %tok_hbm.1, f32[3584]{0:T(1024)} %gain_hbm.1, s32[8,128]{1,0:T(8,128)} %bitcast.16, f32[8,128]{1,0:T(8,128)} %bitcast.17), custom_call_target="tpu_custom_call" | custom-call | tf_op jit(solution)/shard_map/dispatch/pallas_call | solution.py:120
  2.7 7.3 %all-to-all-start = ((bf16[8,8,3584]{2,1,0:T(8,128)(2,1)}), bf16[8,8,3584]{2,1,0:T(8,128)(2,1)S(1)}, u32[]{:S(2)}, u32[]{:S(2)}) async-start(bf16[8,8,3584]{2,1,0:T(8,128)(2,1)} %bitcast.2), calls=%async_computation | async-start | bytes 917504 | tf_op jit(solution)/shard_map/all_to_all | solution.py:116
  10.0 4.2 %stage.1 = (bf16[3584,512]{1,0:T(8,128)(2,1)S(1)}, bf16[3584,512]{1,0:T(8,128)(2,1)S(1)}, bf16[512,3584]{1,0:T(8,128)(2,1)S(1)}) custom-call(bf16[3584,512]{1,0:T(8,128)(2,1)} %bitcast.13, bf16[3584,512]{1,0:T(8,128)(2,1)} %bitcast.14, bf16[512,3584]{1,0:T(8,128)(2,1)} %bitcast.15), custom_call_target="tpu_custom_call" | custom-call | bytes 22020096 | tf_op jit(solution)/shard_map/stage/pallas_call | solution.py:137
  14.3 0.0 copy-start
  14.3 1.8 %copy-done = bf16[3584,512]{1,0:T(8,128)(2,1)} copy-done((bf16[3584,512]{1,0:T(8,128)(2,1)}, bf16[3584,512]{1,0:T(8,128)(2,1)S(1)}, u32[]{:S(2)}) %copy-start) | copy-done | bytes 3670040
  16.1 0.0 copy-start.2
  16.1 1.8 %copy-done.2 = bf16[3584,512]{1,0:T(8,128)(2,1)} copy-done((bf16[3584,512]{1,0:T(8,128)(2,1)}, bf16[3584,512]{1,0:T(8,128)(2,1)S(1)}, u32[]{:S(2)}) %copy-start.2) | copy-done | bytes 3670040
  17.9 0.0 copy-start.4
  17.9 1.9 %copy-done.4 = bf16[512,3584]{1,0:T(8,128)(2,1)} copy-done((bf16[512,3584]{1,0:T(8,128)(2,1)}, bf16[512,3584]{1,0:T(8,128)(2,1)S(1)}, u32[]{:S(2)}) %copy-start.4) | copy-done | bytes 3670040
  19.8 3.3 %all-to-all-done = bf16[8,8,3584]{2,1,0:T(8,128)(2,1)S(1)} async-done(((bf16[8,8,3584]{2,1,0:T(8,128)(2,1)}), bf16[8,8,3584]{2,1,0:T(8,128)(2,1)S(1)}, u32[]{:S(2)}, u32[]{:S(2)}) %all-to-all-start) | async-done | bytes 458784 | tf_op jit(solution)/shard_map/all_to_all | solution.py:116
  23.1 0.0 collective-permute-start
  23.1 1.8 %collective-permute-done.other_ref = bf16[64,3584]{1,0:T(8,128)(2,1)S(1)} collective-permute-done((bf16[64,3584]{1,0:T(8,128)(2,1)S(1)}, bf16[64,3584]{1,0:T(8,128)(2,1)S(1)}, u32[]{:S(2)}, u32[]{:S(2)}) %collective-permute-start) | collective-permute-done | bytes 458784 | tf_op jit(solution)/shard_map/ppermute | solution.py:153
  24.9 0.0 copy-start.1
  24.9 2.0 %copy-done.1 = bf16[3584,512]{1,0:T(8,128)(2,1)S(1)} copy-done((bf16[3584,512]{1,0:T(8,128)(2,1)S(1)}, bf16[3584,512]{1,0:T(8,128)(2,1)}, u32[]{:S(2)}) %copy-start.1) | copy-done | bytes 3670040
  27.0 0.0 copy-start.3
  27.0 2.0 %copy-done.3 = bf16[3584,512]{1,0:T(8,128)(2,1)S(1)} copy-done((bf16[3584,512]{1,0:T(8,128)(2,1)S(1)}, bf16[3584,512]{1,0:T(8,128)(2,1)}, u32[]{:S(2)}) %copy-start.3) | copy-done | bytes 3670040
  29.0 0.0 copy-start.5
  29.0 2.0 %copy-done.5 = bf16[512,3584]{1,0:T(8,128)(2,1)S(1)} copy-done((bf16[512,3584]{1,0:T(8,128)(2,1)S(1)}, bf16[512,3584]{1,0:T(8,128)(2,1)}, u32[]{:S(2)}) %copy-start.5) | copy-done | bytes 3670040
  31.0 1.7 %experts.1 = (bf16[64,3584]{1,0:T(8,128)(2,1)S(1)}, bf16[64,3584]{1,0:T(8,128)(2,1)S(1)}) custom-call(bf16[64,3584]{1,0:T(8,128)(2,1)S(1)} %bitcast.12, bf16[64,3584]{1,0:T(8,128)(2,1)S(1)} %collective-permute-done.other_ref, bf16[3584,512]{1,0:T(8,128)(2,1)S(1)} %copy-done.1, bf16[3584,512]{1,0:T(8,128)(2,1)S(1)} %copy-done.3, bf16[512,3584]{1,0:T(8,128)(2,1)S(1)} %copy-done.5), custom_call_target="tpu_custom_call" | custom-call | flops 1409286144 | bytes 11010048 | tf_op jit(solution)/shard_map/experts/pallas_call | solution.py:154
  32.8 0.2 collective-permute-start.1
  33.0 1.7 %collective-permute-done.1 = bf16[64,3584]{1,0:T(8,128)(2,1)S(1)} collective-permute-done((bf16[64,3584]{1,0:T(8,128)(2,1)S(1)}, bf16[64,3584]{1,0:T(8,128)(2,1)S(1)}, u32[]{:S(2)}, u32[]{:S(2)}) %collective-permute-start.1) | collective-permute-done | bytes 458784 | tf_op jit(solution)/shard_map/ppermute | solution.py:167
  34.6 0.1 fusion
  34.8 16.9 %all_to_all.23 = bf16[8,8,3584]{2,1,0:T(8,128)(2,1)S(1)} all-to-all(bf16[8,8,3584]{2,1,0:T(8,128)(2,1)S(1)} %fusion), channel_id=1, replica_groups={{0,2,4,6,8,10,12,14},{1,3,5,7,9,11,13,15},{16,18,20,22,24,26,28,30},{17..., dimensions={0} | all-to-all | bytes 917504 | tf_op jit(solution)/shard_map/all_to_all | solution.py:116
  51.7 1.3 %combine.1 = bf16[128,3584]{1,0:T(8,128)(2,1)} custom-call(bf16[128,128]{1,0:T(8,128)(2,1)S(1)} %get-tuple-element.16.mix_ref, bf16[64,3584]{1,0:T(8,128)(2,1)S(1)} %bitcast.10), custom_call_target="tpu_custom_call" | custom-call | tf_op jit(solution)/shard_map/combine/pallas_call | solution.py:169
Async XLA Ops:
  2.7 20.4 %all-to-all-start = ((bf16[8,8,3584]{2,1,0:T(8,128)(2,1)}), bf16[8,8,3584]{2,1,0:T(8,128)(2,1)S(1)}, u32[]{:S(2)}, u32[]{:S(2)}) async-start(bf16[8,8,3584]{2,1,0:T(8,128)(2,1)} %bitcast.2), calls=%async_computation | async-start | bytes 917504 | tf_op jit(solution)/shard_map/all_to_all | solution.py:116
  14.3 1.8 %copy-start = (bf16[3584,512]{1,0:T(8,128)(2,1)}, bf16[3584,512]{1,0:T(8,128)(2,1)S(1)}, u32[]{:S(2)}) copy-start(bf16[3584,512]{1,0:T(8,128)(2,1)S(1)} %get-tuple-element.22.gate_ref) | copy-start | bytes 11010052
  16.1 1.8 %copy-start.2 = (bf16[3584,512]{1,0:T(8,128)(2,1)}, bf16[3584,512]{1,0:T(8,128)(2,1)S(1)}, u32[]{:S(2)}) copy-start(bf16[3584,512]{1,0:T(8,128)(2,1)S(1)} %get-tuple-element.23.up_ref) | copy-start | bytes 11010052
  17.9 1.9 %copy-start.4 = (bf16[512,3584]{1,0:T(8,128)(2,1)}, bf16[512,3584]{1,0:T(8,128)(2,1)S(1)}, u32[]{:S(2)}) copy-start(bf16[512,3584]{1,0:T(8,128)(2,1)S(1)} %get-tuple-element.24.down_ref) | copy-start | bytes 11010052
  23.1 1.8 %collective-permute-start = (bf16[64,3584]{1,0:T(8,128)(2,1)S(1)}, bf16[64,3584]{1,0:T(8,128)(2,1)S(1)}, u32[]{:S(2)}, u32[]{:S(2)}) collective-permute-start(bf16[64,3584]{1,0:T(8,128)(2,1)S(1)} %bitcast.11), channel_id=1, source_target_pairs={{0,1},{1,0},{2,3},{3,2},{4,5},{5,4},{6,7},{7,6},{8,9},{9,8},{10,11... | collective-permute-start | bytes 1376264 | tf_op jit(solution)/shard_map/ppermute | solution.py:153
  24.9 2.0 %copy-start.1 = (bf16[3584,512]{1,0:T(8,128)(2,1)S(1)}, bf16[3584,512]{1,0:T(8,128)(2,1)}, u32[]{:S(2)}) copy-start(bf16[3584,512]{1,0:T(8,128)(2,1)} %copy-done) | copy-start | bytes 11010052
  27.0 2.0 %copy-start.3 = (bf16[3584,512]{1,0:T(8,128)(2,1)S(1)}, bf16[3584,512]{1,0:T(8,128)(2,1)}, u32[]{:S(2)}) copy-start(bf16[3584,512]{1,0:T(8,128)(2,1)} %copy-done.2) | copy-start | bytes 11010052
  29.0 2.0 %copy-start.5 = (bf16[512,3584]{1,0:T(8,128)(2,1)S(1)}, bf16[512,3584]{1,0:T(8,128)(2,1)}, u32[]{:S(2)}) copy-start(bf16[512,3584]{1,0:T(8,128)(2,1)} %copy-done.4) | copy-start | bytes 11010052
  32.8 1.9 %collective-permute-start.1 = (bf16[64,3584]{1,0:T(8,128)(2,1)S(1)}, bf16[64,3584]{1,0:T(8,128)(2,1)S(1)}, u32[]{:S(2)}, u32[]{:S(2)}) collective-permute-start(bf16[64,3584]{1,0:T(8,128)(2,1)S(1)} %get-tuple-element.26), channel_id=1, source_target_pairs={{0,1},{1,0},{2,3},{3,2},{4,5},{5,4},{6,7},{7,6},{8,9},{9,8},{10,11... | collective-permute-start | bytes 1376264 | tf_op jit(solution)/shard_map/ppermute | solution.py:167

commit v5 on v2

v5 whole, which is shorter than its diff:
```python
import functools

import jax
import jax.numpy as jnp
from jax import lax
from jax.experimental import pallas as pl
from jax.experimental.pallas import tpu as pltpu
from jax.sharding import PartitionSpec as P

SLOTS = 8
CHUNKS = 4

VMEM = pl.BlockSpec(memory_space=pltpu.VMEM)
HBM = pl.BlockSpec(memory_space=pltpu.HBM)


def in_hbm(*arrays):
    return [pltpu.with_memory_space_constraint(a, pltpu.HBM) for a in arrays]


def relative(flight):
    return flight <= 8


def block_order(flight):
    far = list(range(flight // 2, flight))
    return far + list(range(1, flight // 2)) + [0]


def dispatch_kernel(
    flight, tok_hbm, gain_hbm, ids_hbm, gw_hbm, gate_hbm, mix_ref, gate_ref, *rest
):
    outs = rest[:flight]
    tok, gain, ids, gw, normed, sems = rest[flight:]
    count = tok.shape[0]
    part = count // CHUNKS
    small = [
        pltpu.make_async_copy(ids_hbm, ids, sems.at[0]),
        pltpu.make_async_copy(gw_hbm, gw, sems.at[1]),
        pltpu.make_async_copy(gain_hbm, gain.at[0], sems.at[2]),
    ]
    large = [
        pltpu.make_async_copy(
            tok_hbm.at[pl.ds(i * part, part)], tok.at[pl.ds(i * part, part)], sems.at[3 + i]
        )
        for i in range(CHUNKS)
    ]
    weights = pltpu.make_async_copy(gate_hbm, gate_ref, sems.at[3 + CHUNKS])
    for copy in small + large + [weights]:
        copy.start()
    small[0].wait()
    small[1].wait()
    chip = lax.axis_index("exp") // 2 if relative(flight) else 0
    where = lax.broadcasted_iota(jnp.int32, (flight, count), 0)
    experts = jnp.zeros((flight, count), jnp.int32)
    for i, r in enumerate(block_order(flight)):
        experts = jnp.where(where == i, r ^ chip, experts)
    chosen = jnp.zeros((flight, count), jnp.float32)
    gates = jnp.zeros((flight, count), jnp.float32)
    for k in range(ids.shape[0]):
        hit = ids[k : k + 1, :] == experts
        chosen = jnp.where(hit, 1.0, chosen)
        gates = jnp.where(hit, gw[k : k + 1, :], gates)
    before = (
        lax.broadcasted_iota(jnp.int32, (count, count), 0)
        < lax.broadcasted_iota(jnp.int32, (count, count), 1)
    ).astype(jnp.bfloat16)
    rank = jnp.dot(chosen.astype(jnp.bfloat16), before, preferred_element_type=jnp.float32)
    rank = jnp.where(chosen > 0.0, rank, -1.0)

    slot = lax.broadcasted_iota(jnp.int32, (flight, SLOTS, count), 1).astype(jnp.float32)
    taken = rank[:, None, :] == slot
    pick = jnp.where(taken, 1.0, 0.0).reshape(flight * SLOTS, count).astype(jnp.bfloat16)
    mix = jnp.where(taken, gates[:, None, :], 0.0).reshape(flight * SLOTS, count)
    high = mix.astype(jnp.bfloat16)
    mix_ref[: flight * SLOTS, :] = high
    mix_ref[flight * SLOTS :, :] = (mix - high.astype(jnp.float32)).astype(jnp.bfloat16)

    small[2].wait()
    for i in range(CHUNKS):
        large[i].wait()
        wide = tok[pl.ds(i * part, part), :].astype(jnp.float32)
        mean_square = jnp.mean(wide * wide, axis=1, keepdims=True)
        normed[pl.ds(i * part, part), :] = (
            wide * lax.rsqrt(mean_square + 1e-06) * gain[...]
        ).astype(jnp.bfloat16)
    rows = jnp.dot(pick, normed[...], preferred_element_type=jnp.float32)
    for i in range(flight):
        outs[i][...] = rows[i * SLOTS : (i + 1) * SLOTS].astype(jnp.bfloat16)
    weights.wait()


def stage_kernel(source, target, sem):
    copy = pltpu.make_async_copy(source, target, sem)
    copy.start()
    copy.wait()


def together(refs):
    return jnp.concatenate([b[...].astype(jnp.float32) for b in refs], axis=0).astype(jnp.bfloat16)


def expert_kernel(flight, *refs):
    blocks = refs[: 2 * flight]
    gate_ref, up_ref, down_hbm = refs[2 * flight : 2 * flight + 3]
    outs = refs[2 * flight + 3 : 2 * flight + 7]
    down, sem = refs[2 * flight + 7 :]
    copy = pltpu.make_async_copy(down_hbm, down, sem)
    copy.start()
    x = together(blocks)
    gate_v = jnp.dot(x, gate_ref[...], preferred_element_type=jnp.float32)
    up_v = jnp.dot(x, up_ref[...], preferred_element_type=jnp.float32)
    hidden = (gate_v / (1.0 + jnp.exp(-gate_v)) * up_v).astype(jnp.bfloat16)
    copy.wait()
    part = jnp.dot(hidden, down[...], preferred_element_type=jnp.float32).astype(jnp.bfloat16)
    rows = outs[0].shape[0]
    for i, out in enumerate(outs):
        out[...] = part[i * rows : (i + 1) * rows]


def join_kernel(mine_ref, got_ref, *outs):
    joined = mine_ref[...].astype(jnp.float32) + got_ref[...].astype(jnp.float32)
    for i, out in enumerate(outs):
        out[...] = joined[i * SLOTS : (i + 1) * SLOTS].astype(jnp.bfloat16)


def combine_kernel(flight, mix_ref, *refs):
    rows = together(refs[:flight])
    both = jnp.concatenate([rows, rows], axis=0)
    refs[flight][...] = lax.dot_general(
        mix_ref[...], both, (((0,), (0,)), ((), ())), preferred_element_type=jnp.float32
    ).astype(jnp.bfloat16)


def per_device(tokens, norm_gain, expert_ids, gate_weights, w_gate, w_up, w_down):
    owners = lax.axis_size("exp")
    flight = owners // 2
    count, width = tokens.shape
    hidden = w_gate.shape[2]
    packed = flight * SLOTS
    order = block_order(flight)
    block = jax.ShapeDtypeStruct((SLOTS, width), jnp.bfloat16)
    half = jax.ShapeDtypeStruct((packed // 2, width), jnp.bfloat16)
    pairs = [(i, i ^ 1) for i in range(owners)]
    few = relative(flight)

    def exchange(blocks):
        if few:
            return [
                lax.ppermute(b, "exp", [(i, i ^ (2 * r)) for i in range(owners)]) if r else b
                for b, r in zip(blocks, order)
            ]
        groups = [list(range(core, owners, 2)) for core in range(2)]
        stacked = jnp.stack([blocks[order.index(r)] for r in range(flight)])
        got = lax.all_to_all(
            stacked, "exp", split_axis=0, concat_axis=0, axis_index_groups=groups, tiled=True
        )
        return [got[r] for r in order]

    def swap(blocks):
        if few:
            return [lax.ppermute(b, "exp", pairs) for b in blocks]
        got = lax.ppermute(jnp.stack(blocks), "exp", pairs)
        return [got[r] for r in range(flight)]

    mix, gate, *outgoing = pl.pallas_call(
        functools.partial(dispatch_kernel, flight),
        out_shape=(
            jax.ShapeDtypeStruct((2 * packed, count), jnp.bfloat16),
            jax.ShapeDtypeStruct(w_gate.shape[1:], w_gate.dtype),
        )
        + (block,) * flight,
        in_specs=[HBM] * 5,
        out_specs=(VMEM,) * (flight + 2),
        scratch_shapes=[
            pltpu.VMEM((count, width), jnp.bfloat16),
            pltpu.VMEM((1, width), jnp.float32),
            pltpu.VMEM(expert_ids.shape[::-1], jnp.int32),
            pltpu.VMEM(gate_weights.shape[::-1], jnp.float32),
            pltpu.VMEM((count, width), jnp.bfloat16),
            pltpu.SemaphoreType.DMA((4 + CHUNKS,)),
        ],
        compiler_params=pltpu.CompilerParams(vmem_limit_bytes=24 * 2**20),
        name="dispatch",
    )(*in_hbm(tokens, norm_gain, expert_ids.T, gate_weights.T, w_gate[0]))

    up = pl.pallas_call(
        stage_kernel,
        out_shape=jax.ShapeDtypeStruct(w_up.shape[1:], w_up.dtype),
        in_specs=[HBM],
        out_specs=VMEM,
        scratch_shapes=[pltpu.SemaphoreType.DMA],
        compiler_params=pltpu.CompilerParams(vmem_limit_bytes=16 * 2**20),
        cost_estimate=pl.CostEstimate(flops=0, bytes_accessed=4 * width * hidden, transcendentals=0),
        name="stage",
    )(*in_hbm(w_up[0]))

    own = exchange(outgoing)
    last = flight // 2 - 1
    own[last], up = lax.optimization_barrier((own[last], up))
    other = swap(own)
    own_far, own_near, other_far, other_near = pl.pallas_call(
        functools.partial(expert_kernel, flight),
        out_shape=(half,) * 4,
        in_specs=[VMEM] * (2 * flight + 2) + [HBM],
        out_specs=(VMEM,) * 4,
        scratch_shapes=[pltpu.VMEM(w_down.shape[1:], w_down.dtype), pltpu.SemaphoreType.DMA],
        compiler_params=pltpu.CompilerParams(vmem_limit_bytes=32 * 2**20),
        cost_estimate=pl.CostEstimate(
            flops=12 * packed * width * hidden,
            bytes_accessed=6 * width * hidden,
            transcendentals=0,
        ),
        name="experts",
    )(*own, *other, gate, up, *in_hbm(w_down[0]))

    def join(mine, theirs):
        return pl.pallas_call(
            join_kernel,
            out_shape=(block,) * (flight // 2),
            in_specs=[VMEM] * 2,
            out_specs=(VMEM,) * (flight // 2),
            compiler_params=pltpu.CompilerParams(vmem_limit_bytes=24 * 2**20),
            name="join",
        )(mine, lax.ppermute(theirs, "exp", pairs))

    returned = exchange([*join(own_far, other_far), *join(own_near, other_near)])
    return pl.pallas_call(
        functools.partial(combine_kernel, flight),
        out_shape=jax.ShapeDtypeStruct((count, width), jnp.bfloat16),
        in_specs=[VMEM] * (flight + 1),
        out_specs=VMEM,
        compiler_params=pltpu.CompilerParams(vmem_limit_bytes=24 * 2**20),
        name="combine",
    )(mix, *returned)


def solution(mesh):
    placed = (
        P(("group", "exp"), None),
        P(),
        P(("group", "exp"), None),
        P(("group", "exp"), None),
        P("exp", None, None),
        P("exp", None, None),
        P("exp", None, None),
    )
    return jax.shard_map(
        per_device, mesh=mesh, in_specs=placed, out_specs=P(("group", "exp"), None), check_vma=False
    )
```

time: 47.5 us -> 47.2 us (level)
  starting transfers between devices: 28.1 us -> 22.9 us
  waiting for transfers between devices: 9.67 us -> 14.3 us
    ppermute x14 -> x16, waiting for transfers between devices: 9.29 us -> 13.1 us  [the longest x14 12.2 us: exchange(): lax.ppermute(b, 'exp', [(i, i ^ 2 * r) for i in range(owners)])]
    ppermute x14 -> x16, starting transfers between devices: 24 us -> 21.2 us  [the longest x14 20.6 us: exchange(): lax.ppermute(b, 'exp', [(i, i ^ 2 * r) for i in range(owners)])]
    ppermute x16 -> x8, starting transfers between devices: 4.12 us -> 1.67 us  [swap(): return [lax.ppermute(b, 'exp', pairs) for b in blocks]]
    ppermute x16 -> x8, waiting for transfers between devices: 0.38 us -> 1.16 us  [swap(): return [lax.ppermute(b, 'exp', pairs) for b in blocks]]
    pallas_call x1, Pallas kernels: 1.96 us -> 2.57 us  [per_device(): pl.pallas_call(functools.partial(dispatch_kernel, flight), out_shape=(jax...]
    pallas_call x2 -> x4, Pallas kernels: 5.96 us -> 5.81 us  [the longest x1 3.66 us: per_device(): pl.pallas_call(functools.partial(expert_kernel, flight), out_shape=(half,...]
  transfers between devices with their start and end apart: 30 -> 24, of which waited for: 5 -> 11; matrix products, arithmetic and copies ran while one was open for 0% -> 0% of each run, Pallas kernels for 9% -> 5%
where the time goes in v5:
time: 47.2 us; the launch traced here: 47 us
  starting transfers between devices  22.9 us (49%)
  waiting for transfers between devices  14.3 us (30%)
  Pallas kernels  9.73 us (21%)
    ppermute x14, starting transfers between devices, exchange(): lax.ppermute(b, 'exp', [(i, i ^ 2 * r) for i in range(owners)])  20.6 us
    ppermute x14, waiting for transfers between devices, exchange(): lax.ppermute(b, 'exp', [(i, i ^ 2 * r) for i in range(owners)])  12.2 us
    pallas_call x1, Pallas kernels, per_device(): pl.pallas_call(functools.partial(expert_kernel, flight), out_shape=(half,...  3.66 us
    pallas_call x1, Pallas kernels, per_device(): pl.pallas_call(functools.partial(dispatch_kernel, flight), out_shape=(jax...  2.57 us
    pallas_call x1, Pallas kernels, per_device(): pl.pallas_call(stage_kernel, out_shape=jax.ShapeDtypeStruct(w_up.shape[1:...  2.05 us
    ppermute x8, starting transfers between devices, swap(): return [lax.ppermute(b, 'exp', pairs) for b in blocks]  1.67 us
    pallas_call x1, Pallas kernels, per_device(): pl.pallas_call(functools.partial(combine_kernel, flight), out_shape=jax.S...  1.35 us
    ppermute x8, waiting for transfers between devices, swap(): return [lax.ppermute(b, 'exp', pairs) for b in blocks]  1.16 us
  transfers between devices with their start and end apart: 24, of which 11 were waited for; matrix products, arithmetic and copies ran while one was open for 0% of the time, Pallas kernels for 5%

profile of v5, /device:TPU:0, one launch (start us, length us, event | category | flops | bytes accessed | tf_op | source)
XLA Modules:
  0.0 47.0 jit_solution(18151179259521269406)
XLA Ops:
  0.0 2.6 %dispatch.1 = (bf16[128,128]{1,0:T(8,128)(2,1)S(1)}, bf16[3584,512]{1,0:T(8,128)(2,1)S(1)}, bf16[8,3584]{1,0:T(8,128)(2,1)S(1)}, bf16[8,3584]{1,0:T(8,128)(2,1)S...) custom-call(bf16[128,3584]{1,0:T(8,128)(2,1)} %tok_hbm.1, ...), custom_call_target="tpu_custom_call" | custom-call | tf_op jit(solution)/shard_map/dispatch/pallas_call | solution.py:166
  2.6 4.1 %collective-permute-start = (bf16[8,3584]{1,0:T(8,128)(2,1)S(1)}, bf16[8,3584]{1,0:T(8,128)(2,1)S(1)}, u32[]{:S(2)}, u32[]{:S(2)}) collective-permute-start(bf16[8,3584]{1,0:T(8,128)(2,1)S(1)} %get-tuple-element.30), channel_id=1, source_target_pairs={{0,8},{1,9},{2,10},{3,11},{4,12},{5,13},{6,14},{7,15},{8,0},{9,1},... | collective-permute-start | bytes 172040 | tf_op jit(solution)/shard_map/ppermute | solution.py:150
  6.7 1.3 %collective-permute-start.1 = (bf16[8,3584]{1,0:T(8,128)(2,1)S(1)}, bf16[8,3584]{1,0:T(8,128)(2,1)S(1)}, u32[]{:S(2)}, u32[]{:S(2)}) collective-permute-start(bf16[8,3584]{1,0:T(8,128)(2,1)S(1)} %get-tuple-element.31), channel_id=1, source_target_pairs={{0,10},{1,11},{2,8},{3,9},{4,14},{5,15},{6,12},{7,13},{8,2},{9,3},... | collective-permute-start | bytes 172040 | tf_op jit(solution)/shard_map/ppermute | solution.py:150
  8.0 3.6 %collective-permute-start.2 = (bf16[8,3584]{1,0:T(8,128)(2,1)S(1)}, bf16[8,3584]{1,0:T(8,128)(2,1)S(1)}, u32[]{:S(2)}, u32[]{:S(2)}) collective-permute-start(bf16[8,3584]{1,0:T(8,128)(2,1)S(1)} %get-tuple-element.32), channel_id=1, source_target_pairs={{0,12},{1,13},{2,14},{3,15},{4,8},{5,9},{6,10},{7,11},{8,4},{9,5},... | collective-permute-start | bytes 172040 | tf_op jit(solution)/shard_map/ppermute | solution.py:150
  11.6 1.7 %collective-permute-start.4 = (bf16[8,3584]{1,0:T(8,128)(2,1)S(1)}, bf16[8,3584]{1,0:T(8,128)(2,1)S(1)}, u32[]{:S(2)}, u32[]{:S(2)}) collective-permute-start(bf16[8,3584]{1,0:T(8,128)(2,1)S(1)} %get-tuple-element.35), channel_id=1, source_target_pairs={{0,2},{1,3},{2,0},{3,1},{4,6},{5,7},{6,4},{7,5},{8,10},{9,11},{10,... | collective-permute-start | bytes 172040 | tf_op jit(solution)/shard_map/ppermute | solution.py:150
  13.3 2.1 %collective-permute-done.1.refs_1_ = bf16[8,3584]{1,0:T(8,128)(2,1)S(1)} collective-permute-done((bf16[8,3584]{1,0:T(8,128)(2,1)S(1)}, bf16[8,3584]{1,0:T(8,128)(2,1)S(1)}, u32[]{:S(2)}, u32[]{:S(2)}) %collective-permute-start.1) | collective-permute-done | bytes 57376 | tf_op jit(solution)/shard_map/ppermute | solution.py:150
  15.4 1.1 %collective-permute-start.6 = (bf16[8,3584]{1,0:T(8,128)(2,1)S(1)}, bf16[8,3584]{1,0:T(8,128)(2,1)S(1)}, u32[]{:S(2)}, u32[]{:S(2)}) collective-permute-start(bf16[8,3584]{1,0:T(8,128)(2,1)S(1)} %get-tuple-element.37), channel_id=1, source_target_pairs={{0,6},{1,7},{2,4},{3,5},{4,2},{5,3},{6,0},{7,1},{8,14},{9,15},{10,... | collective-permute-start | bytes 172040 | tf_op jit(solution)/shard_map/ppermute | solution.py:150
  16.5 2.1 %collective-permute-done.3.refs_3_ = bf16[8,3584]{1,0:T(8,128)(2,1)S(1)} collective-permute-done((bf16[8,3584]{1,0:T(8,128)(2,1)S(1)}, bf16[8,3584]{1,0:T(8,128)(2,1)S(1)}, u32[]{:S(2)}, u32[]{:S(2)}) %collective-permute-start.3) | collective-permute-done | bytes 57376 | tf_op jit(solution)/shard_map/ppermute | solution.py:150
  18.6 0.5 %collective-permute-start.8 = (bf16[8,3584]{1,0:T(8,128)(2,1)S(1)}, bf16[8,3584]{1,0:T(8,128)(2,1)S(1)}, u32[]{:S(2)}, u32[]{:S(2)}) collective-permute-start(bf16[8,3584]{1,0:T(8,128)(2,1)S(1)} %collective-permute-done.1.refs_1_), channel_id=1, source_target_pairs={{0,1},{1,0},{2,3},{3,2},{4,5},{5,4},{6,7},{7,6},{8,9},{9,8},{10,11... | collective-permute-start | bytes 172040 | tf_op jit(solution)/shard_map/ppermute | solution.py:162
  19.1 2.0 %stage.1.refs_17_ = bf16[3584,512]{1,0:T(8,128)(2,1)S(1)} custom-call(bf16[3584,512]{1,0:T(8,128)(2,1)} %bitcast.5), custom_call_target="tpu_custom_call" | custom-call | bytes 7340032 | tf_op jit(solution)/shard_map/stage/pallas_call | solution.py:187
  21.3 0.5 %collective-permute-start.9 = (bf16[8,3584]{1,0:T(8,128)(2,1)S(1)}, bf16[8,3584]{1,0:T(8,128)(2,1)S(1)}, u32[]{:S(2)}, u32[]{:S(2)}) collective-permute-start(bf16[8,3584]{1,0:T(8,128)(2,1)S(1)} %collective-permute-done.2.refs_2_), channel_id=1, source_target_pairs={{0,1},{1,0},{2,3},{3,2},{4,5},{5,4},{6,7},{7,6},{8,9},{9,8},{10,11... | collective-permute-start | bytes 172040 | tf_op jit(solution)/shard_map/ppermute | solution.py:162
  21.8 0.1 collective-permute-start.11
  21.8 0.4 collective-permute-start.12
  22.3 0.1 collective-permute-start.13
  22.4 0.3 collective-permute-done.9.refs_10_
  22.7 0.4 collective-permute-done.11.refs_12_
  23.0 0.2 collective-permute-done.12.refs_13_
  23.2 0.4 collective-permute-done.13.refs_14_
  23.5 3.7 %experts.1 = (bf16[32,3584]{1,0:T(8,128)(2,1)S(1)}, bf16[32,3584]{1,0:T(8,128)(2,1)S(1)}, bf16[32,3584]{1,0:T(8,128)(2,1)S(1)}, bf16[32,3584]{1,0:T(8,128)(2,1)S(1)}) custom-call(bf16[8,3584]{1,0:T(8,128)(2,1)S(1)} %collective-permute-done.refs_0_, bf16[8,3584]{1,0:T(8,128)(2,1)S(1)} %collective-permute-done.1.refs_1_, ...), custom_call_target="tpu_custom_call" | custom-call | flops 1409286144 | bytes 11010048 | tf_op jit(solution)/shard_map/experts/pallas_call | solution.py:202
  27.2 0.2 collective-permute-start.15
  27.4 0.3 collective-permute-start.20
  27.8 1.0 %collective-permute-done.15.got_ref = bf16[32,3584]{1,0:T(8,128)(2,1)S(1)} collective-permute-done((bf16[32,3584]{1,0:T(8,128)(2,1)S(1)}, bf16[32,3584]{1,0:T(8,128)(2,1)S(1)}, u32[]{:S(2)}, u32[]{:S(2)}) %collective-permute-start.15) | collective-permute-done | bytes 229408 | tf_op jit(solution)/shard_map/ppermute | solution.py:225
  28.8 2.6 %collective-permute-start.16 = (bf16[8,3584]{1,0:T(8,128)(2,1)S(1)}, bf16[8,3584]{1,0:T(8,128)(2,1)S(1)}, u32[]{:S(2)}, u32[]{:S(2)}) collective-permute-start(bf16[8,3584]{1,0:T(8,128)(2,1)S(1)} %get-tuple-element.43), channel_id=1, source_target_pairs={{0,8},{1,9},{2,10},{3,11},{4,12},{5,13},{6,14},{7,15},{8,0},{9,1},... | collective-permute-start | bytes 172040 | tf_op jit(solution)/shard_map/ppermute | solution.py:150
  31.4 1.0 %collective-permute-start.17 = (bf16[8,3584]{1,0:T(8,128)(2,1)S(1)}, bf16[8,3584]{1,0:T(8,128)(2,1)S(1)}, u32[]{:S(2)}, u32[]{:S(2)}) collective-permute-start(bf16[8,3584]{1,0:T(8,128)(2,1)S(1)} %get-tuple-element.44), channel_id=1, source_target_pairs={{0,10},{1,11},{2,8},{3,9},{4,14},{5,15},{6,12},{7,13},{8,2},{9,3},... | collective-permute-start | bytes 172040 | tf_op jit(solution)/shard_map/ppermute | solution.py:150
  32.3 2.6 %collective-permute-start.18 = (bf16[8,3584]{1,0:T(8,128)(2,1)S(1)}, bf16[8,3584]{1,0:T(8,128)(2,1)S(1)}, u32[]{:S(2)}, u32[]{:S(2)}) collective-permute-start(bf16[8,3584]{1,0:T(8,128)(2,1)S(1)} %get-tuple-element.45), channel_id=1, source_target_pairs={{0,12},{1,13},{2,14},{3,15},{4,8},{5,9},{6,10},{7,11},{8,4},{9,5},... | collective-permute-start | bytes 172040 | tf_op jit(solution)/shard_map/ppermute | solution.py:150
  34.9 1.6 %collective-permute-start.19 = (bf16[8,3584]{1,0:T(8,128)(2,1)S(1)}, bf16[8,3584]{1,0:T(8,128)(2,1)S(1)}, u32[]{:S(2)}, u32[]{:S(2)}) collective-permute-start(bf16[8,3584]{1,0:T(8,128)(2,1)S(1)} %get-tuple-element.46), channel_id=1, source_target_pairs={{0,14},{1,15},{2,12},{3,13},{4,10},{5,11},{6,8},{7,9},{8,6},{9,7},... | collective-permute-start | bytes 172040 | tf_op jit(solution)/shard_map/ppermute | solution.py:150
  36.6 1.2 %collective-permute-start.21 = (bf16[8,3584]{1,0:T(8,128)(2,1)S(1)}, bf16[8,3584]{1,0:T(8,128)(2,1)S(1)}, u32[]{:S(2)}, u32[]{:S(2)}) collective-permute-start(bf16[8,3584]{1,0:T(8,128)(2,1)S(1)} %get-tuple-element.49), channel_id=1, source_target_pairs={{0,2},{1,3},{2,0},{3,1},{4,6},{5,7},{6,4},{7,5},{8,10},{9,11},{10,... | collective-permute-start | bytes 172040 | tf_op jit(solution)/shard_map/ppermute | solution.py:150
  37.7 2.8 %collective-permute-done.17.refs_1_ = bf16[8,3584]{1,0:T(8,128)(2,1)S(1)} collective-permute-done((bf16[8,3584]{1,0:T(8,128)(2,1)S(1)}, bf16[8,3584]{1,0:T(8,128)(2,1)S(1)}, u32[]{:S(2)}, u32[]{:S(2)}) %collective-permute-start.17) | collective-permute-done | bytes 57376 | tf_op jit(solution)/shard_map/ppermute | solution.py:150
  40.6 1.4 %collective-permute-done.19.refs_3_ = bf16[8,3584]{1,0:T(8,128)(2,1)S(1)} collective-permute-done((bf16[8,3584]{1,0:T(8,128)(2,1)S(1)}, bf16[8,3584]{1,0:T(8,128)(2,1)S(1)}, u32[]{:S(2)}, u32[]{:S(2)}) %collective-permute-start.19) | collective-permute-done | bytes 57376 | tf_op jit(solution)/shard_map/ppermute | solution.py:150
  42.0 0.4 collective-permute-done.22.refs_5_
  42.4 3.3 %collective-permute-done.23.refs_6_ = bf16[8,3584]{1,0:T(8,128)(2,1)S(1)} collective-permute-done((bf16[8,3584]{1,0:T(8,128)(2,1)S(1)}, bf16[8,3584]{1,0:T(8,128)(2,1)S(1)}, u32[]{:S(2)}, u32[]{:S(2)}) %collective-permute-start.23) | collective-permute-done | bytes 57376 | tf_op jit(solution)/shard_map/ppermute | solution.py:150
  45.6 1.3 %combine.1 = bf16[128,3584]{1,0:T(8,128)(2,1)} custom-call(bf16[128,128]{1,0:T(8,128)(2,1)S(1)} %get-tuple-element.29.mix_ref, bf16[8,3584]{1,0:T(8,128)(2,1)S(1)} %collective-permute-done.16.refs_0_, bf16[8,3584]{1,0:T(8,128)(2,1)S(1)} %collective-permute-done.17.refs_1_, bf16[8,3584]{1,0:T(8,128)(2,1)S(1)} %collective-permute-done.18.refs_2_, ...), custom_call_target="tpu_custom_call" | custom-call | tf_op jit(solution)/shard_map/combine/pallas_call | solution.py:228
  (22 shorter events, 0.2 us)
Async XLA Ops:
  2.6 10.7 %collective-permute-start = (bf16[8,3584]{1,0:T(8,128)(2,1)S(1)}, bf16[8,3584]{1,0:T(8,128)(2,1)S(1)}, u32[]{:S(2)}, u32[]{:S(2)}) collective-permute-start(bf16[8,3584]{1,0:T(8,128)(2,1)S(1)} %get-tuple-element.30), channel_id=1, source_target_pairs={{0,8},{1,9},{2,10},{3,11},{4,12},{5,13},{6,14},{7,15},{8,0},{9,1},... | collective-permute-start | bytes 172040 | tf_op jit(solution)/shard_map/ppermute | solution.py:150
  6.7 8.7 %collective-permute-start.1 = (bf16[8,3584]{1,0:T(8,128)(2,1)S(1)}, bf16[8,3584]{1,0:T(8,128)(2,1)S(1)}, u32[]{:S(2)}, u32[]{:S(2)}) collective-permute-start(bf16[8,3584]{1,0:T(8,128)(2,1)S(1)} %get-tuple-element.31), channel_id=1, source_target_pairs={{0,10},{1,11},{2,8},{3,9},{4,14},{5,15},{6,12},{7,13},{8,2},{9,3},... | collective-permute-start | bytes 172040 | tf_op jit(solution)/shard_map/ppermute | solution.py:150
  8.0 8.5 %collective-permute-start.2 = (bf16[8,3584]{1,0:T(8,128)(2,1)S(1)}, bf16[8,3584]{1,0:T(8,128)(2,1)S(1)}, u32[]{:S(2)}, u32[]{:S(2)}) collective-permute-start(bf16[8,3584]{1,0:T(8,128)(2,1)S(1)} %get-tuple-element.32), channel_id=1, source_target_pairs={{0,12},{1,13},{2,14},{3,15},{4,8},{5,9},{6,10},{7,11},{8,4},{9,5},... | collective-permute-start | bytes 172040 | tf_op jit(solution)/shard_map/ppermute | solution.py:150
  11.6 7.0 %collective-permute-start.3 = (bf16[8,3584]{1,0:T(8,128)(2,1)S(1)}, bf16[8,3584]{1,0:T(8,128)(2,1)S(1)}, u32[]{:S(2)}, u32[]{:S(2)}) collective-permute-start(bf16[8,3584]{1,0:T(8,128)(2,1)S(1)} %get-tuple-element.33), channel_id=1, source_target_pairs={{0,14},{1,15},{2,12},{3,13},{4,10},{5,11},{6,8},{7,9},{8,6},{9,7},... | collective-permute-start | bytes 172040 | tf_op jit(solution)/shard_map/ppermute | solution.py:150
  11.6 7.0 %collective-permute-start.4 = (bf16[8,3584]{1,0:T(8,128)(2,1)S(1)}, bf16[8,3584]{1,0:T(8,128)(2,1)S(1)}, u32[]{:S(2)}, u32[]{:S(2)}) collective-permute-start(bf16[8,3584]{1,0:T(8,128)(2,1)S(1)} %get-tuple-element.35), channel_id=1, source_target_pairs={{0,2},{1,3},{2,0},{3,1},{4,6},{5,7},{6,4},{7,5},{8,10},{9,11},{10,... | collective-permute-start | bytes 172040 | tf_op jit(solution)/shard_map/ppermute | solution.py:150
  13.3 7.9 %collective-permute-start.5 = (bf16[8,3584]{1,0:T(8,128)(2,1)S(1)}, bf16[8,3584]{1,0:T(8,128)(2,1)S(1)}, u32[]{:S(2)}, u32[]{:S(2)}) collective-permute-start(bf16[8,3584]{1,0:T(8,128)(2,1)S(1)} %get-tuple-element.36), channel_id=1, source_target_pairs={{0,4},{1,5},{2,6},{3,7},{4,0},{5,1},{6,2},{7,3},{8,12},{9,13},{10,... | collective-permute-start | bytes 172040 | tf_op jit(solution)/shard_map/ppermute | solution.py:150
  15.4 5.9 %collective-permute-start.6 = (bf16[8,3584]{1,0:T(8,128)(2,1)S(1)}, bf16[8,3584]{1,0:T(8,128)(2,1)S(1)}, u32[]{:S(2)}, u32[]{:S(2)}) collective-permute-start(bf16[8,3584]{1,0:T(8,128)(2,1)S(1)} %get-tuple-element.37), channel_id=1, source_target_pairs={{0,6},{1,7},{2,4},{3,5},{4,2},{5,3},{6,0},{7,1},{8,14},{9,15},{10,... | collective-permute-start | bytes 172040 | tf_op jit(solution)/shard_map/ppermute | solution.py:150
  16.5 5.3 %collective-permute-start.14 = (bf16[8,3584]{1,0:T(8,128)(2,1)S(1)}, bf16[8,3584]{1,0:T(8,128)(2,1)S(1)}, u32[]{:S(2)}, u32[]{:S(2)}) collective-permute-start(bf16[8,3584]{1,0:T(8,128)(2,1)S(1)} %get-tuple-element.38.refs_7_), channel_id=1, source_target_pairs={{0,1},{1,0},{2,3},{3,2},{4,5},{5,4},{6,7},{7,6},{8,9},{9,8},{10,11... | collective-permute-start | bytes 172040 | tf_op jit(solution)/shard_map/ppermute | solution.py:162
  18.6 3.3 %collective-permute-start.7 = (bf16[8,3584]{1,0:T(8,128)(2,1)S(1)}, bf16[8,3584]{1,0:T(8,128)(2,1)S(1)}, u32[]{:S(2)}, u32[]{:S(2)}) collective-permute-start(bf16[8,3584]{1,0:T(8,128)(2,1)S(1)} %collective-permute-done.refs_0_), channel_id=1, source_target_pairs={{0,1},{1,0},{2,3},{3,2},{4,5},{5,4},{6,7},{7,6},{8,9},{9,8},{10,11... | collective-permute-start | bytes 172040 | tf_op jit(solution)/shard_map/ppermute | solution.py:162
  18.6 3.7 %collective-permute-start.8 = (bf16[8,3584]{1,0:T(8,128)(2,1)S(1)}, bf16[8,3584]{1,0:T(8,128)(2,1)S(1)}, u32[]{:S(2)}, u32[]{:S(2)}) collective-permute-start(bf16[8,3584]{1,0:T(8,128)(2,1)S(1)} %collective-permute-done.1.refs_1_), channel_id=1, source_target_pairs={{0,1},{1,0},{2,3},{3,2},{4,5},{5,4},{6,7},{7,6},{8,9},{9,8},{10,11... | collective-permute-start | bytes 172040 | tf_op jit(solution)/shard_map/ppermute | solution.py:162
  21.2 1.5 %collective-permute-start.10 = (bf16[8,3584]{1,0:T(8,128)(2,1)S(1)}, bf16[8,3584]{1,0:T(8,128)(2,1)S(1)}, u32[]{:S(2)}, u32[]{:S(2)}) collective-permute-start(bf16[8,3584]{1,0:T(8,128)(2,1)S(1)} %collective-permute-done.3.refs_3_), channel_id=1, source_target_pairs={{0,1},{1,0},{2,3},{3,2},{4,5},{5,4},{6,7},{7,6},{8,9},{9,8},{10,11... | collective-permute-start | bytes 172040 | tf_op jit(solution)/shard_map/ppermute | solution.py:162
  21.3 1.4 %collective-permute-start.9 = (bf16[8,3584]{1,0:T(8,128)(2,1)S(1)}, bf16[8,3584]{1,0:T(8,128)(2,1)S(1)}, u32[]{:S(2)}, u32[]{:S(2)}) collective-permute-start(bf16[8,3584]{1,0:T(8,128)(2,1)S(1)} %collective-permute-done.2.refs_2_), channel_id=1, source_target_pairs={{0,1},{1,0},{2,3},{3,2},{4,5},{5,4},{6,7},{7,6},{8,9},{9,8},{10,11... | collective-permute-start | bytes 172040 | tf_op jit(solution)/shard_map/ppermute | solution.py:162
  21.8 1.2 %collective-permute-start.11 = (bf16[8,3584]{1,0:T(8,128)(2,1)S(1)}, bf16[8,3584]{1,0:T(8,128)(2,1)S(1)}, u32[]{:S(2)}, u32[]{:S(2)}) collective-permute-start(bf16[8,3584]{1,0:T(8,128)(2,1)S(1)} %collective-permute-done.4.refs_4_), channel_id=1, source_target_pairs={{0,1},{1,0},{2,3},{3,2},{4,5},{5,4},{6,7},{7,6},{8,9},{9,8},{10,11... | collective-permute-start | bytes 172040 | tf_op jit(solution)/shard_map/ppermute | solution.py:162
  21.8 1.3 %collective-permute-start.12 = (bf16[8,3584]{1,0:T(8,128)(2,1)S(1)}, bf16[8,3584]{1,0:T(8,128)(2,1)S(1)}, u32[]{:S(2)}, u32[]{:S(2)}) collective-permute-start(bf16[8,3584]{1,0:T(8,128)(2,1)S(1)} %collective-permute-done.5.refs_5_), channel_id=1, source_target_pairs={{0,1},{1,0},{2,3},{3,2},{4,5},{5,4},{6,7},{7,6},{8,9},{9,8},{10,11... | collective-permute-start | bytes 172040 | tf_op jit(solution)/shard_map/ppermute | solution.py:162
  22.3 1.2 %collective-permute-start.13 = (bf16[8,3584]{1,0:T(8,128)(2,1)S(1)}, bf16[8,3584]{1,0:T(8,128)(2,1)S(1)}, u32[]{:S(2)}, u32[]{:S(2)}) collective-permute-start(bf16[8,3584]{1,0:T(8,128)(2,1)S(1)} %collective-permute-done.6.refs_6_), channel_id=1, source_target_pairs={{0,1},{1,0},{2,3},{3,2},{4,5},{5,4},{6,7},{7,6},{8,9},{9,8},{10,11... | collective-permute-start | bytes 172040 | tf_op jit(solution)/shard_map/ppermute | solution.py:162
  27.2 1.6 %collective-permute-start.15 = (bf16[32,3584]{1,0:T(8,128)(2,1)S(1)}, bf16[32,3584]{1,0:T(8,128)(2,1)S(1)}, u32[]{:S(2)}, u32[]{:S(2)}) collective-permute-start(bf16[32,3584]{1,0:T(8,128)(2,1)S(1)} %get-tuple-element.42), channel_id=1, source_target_pairs={{0,1},{1,0},{2,3},{3,2},{4,5},{5,4},{6,7},{7,6},{8,9},{9,8},{10,11... | collective-permute-start | bytes 688136 | tf_op jit(solution)/shard_map/ppermute | solution.py:225
  27.4 9.1 %collective-permute-start.20 = (bf16[32,3584]{1,0:T(8,128)(2,1)S(1)}, bf16[32,3584]{1,0:T(8,128)(2,1)S(1)}, u32[]{:S(2)}, u32[]{:S(2)}) collective-permute-start(bf16[32,3584]{1,0:T(8,128)(2,1)S(1)} %get-tuple-element.48), channel_id=1, source_target_pairs={{0,1},{1,0},{2,3},{3,2},{4,5},{5,4},{6,7},{7,6},{8,9},{9,8},{10,11... | collective-permute-start | bytes 688136 | tf_op jit(solution)/shard_map/ppermute | solution.py:225
  28.8 8.9 %collective-permute-start.16 = (bf16[8,3584]{1,0:T(8,128)(2,1)S(1)}, bf16[8,3584]{1,0:T(8,128)(2,1)S(1)}, u32[]{:S(2)}, u32[]{:S(2)}) collective-permute-start(bf16[8,3584]{1,0:T(8,128)(2,1)S(1)} %get-tuple-element.43), channel_id=1, source_target_pairs={{0,8},{1,9},{2,10},{3,11},{4,12},{5,13},{6,14},{7,15},{8,0},{9,1},... | collective-permute-start | bytes 172040 | tf_op jit(solution)/shard_map/ppermute | solution.py:150
  31.4 9.2 %collective-permute-start.17 = (bf16[8,3584]{1,0:T(8,128)(2,1)S(1)}, bf16[8,3584]{1,0:T(8,128)(2,1)S(1)}, u32[]{:S(2)}, u32[]{:S(2)}) collective-permute-start(bf16[8,3584]{1,0:T(8,128)(2,1)S(1)} %get-tuple-element.44), channel_id=1, source_target_pairs={{0,10},{1,11},{2,8},{3,9},{4,14},{5,15},{6,12},{7,13},{8,2},{9,3},... | collective-permute-start | bytes 172040 | tf_op jit(solution)/shard_map/ppermute | solution.py:150
  32.3 8.2 %collective-permute-start.18 = (bf16[8,3584]{1,0:T(8,128)(2,1)S(1)}, bf16[8,3584]{1,0:T(8,128)(2,1)S(1)}, u32[]{:S(2)}, u32[]{:S(2)}) collective-permute-start(bf16[8,3584]{1,0:T(8,128)(2,1)S(1)} %get-tuple-element.45), channel_id=1, source_target_pairs={{0,12},{1,13},{2,14},{3,15},{4,8},{5,9},{6,10},{7,11},{8,4},{9,5},... | collective-permute-start | bytes 172040 | tf_op jit(solution)/shard_map/ppermute | solution.py:150
  34.9 7.1 %collective-permute-start.19 = (bf16[8,3584]{1,0:T(8,128)(2,1)S(1)}, bf16[8,3584]{1,0:T(8,128)(2,1)S(1)}, u32[]{:S(2)}, u32[]{:S(2)}) collective-permute-start(bf16[8,3584]{1,0:T(8,128)(2,1)S(1)} %get-tuple-element.46), channel_id=1, source_target_pairs={{0,14},{1,15},{2,12},{3,13},{4,10},{5,11},{6,8},{7,9},{8,6},{9,7},... | collective-permute-start | bytes 172040 | tf_op jit(solution)/shard_map/ppermute | solution.py:150
  36.6 5.4 %collective-permute-start.21 = (bf16[8,3584]{1,0:T(8,128)(2,1)S(1)}, bf16[8,3584]{1,0:T(8,128)(2,1)S(1)}, u32[]{:S(2)}, u32[]{:S(2)}) collective-permute-start(bf16[8,3584]{1,0:T(8,128)(2,1)S(1)} %get-tuple-element.49), channel_id=1, source_target_pairs={{0,2},{1,3},{2,0},{3,1},{4,6},{5,7},{6,4},{7,5},{8,10},{9,11},{10,... | collective-permute-start | bytes 172040 | tf_op jit(solution)/shard_map/ppermute | solution.py:150
  37.7 4.6 %collective-permute-start.22 = (bf16[8,3584]{1,0:T(8,128)(2,1)S(1)}, bf16[8,3584]{1,0:T(8,128)(2,1)S(1)}, u32[]{:S(2)}, u32[]{:S(2)}) collective-permute-start(bf16[8,3584]{1,0:T(8,128)(2,1)S(1)} %get-tuple-element.50), channel_id=1, source_target_pairs={{0,4},{1,5},{2,6},{3,7},{4,0},{5,1},{6,2},{7,3},{8,12},{9,13},{10,... | collective-permute-start | bytes 172040 | tf_op jit(solution)/shard_map/ppermute | solution.py:150
  40.6 5.1 %collective-permute-start.23 = (bf16[8,3584]{1,0:T(8,128)(2,1)S(1)}, bf16[8,3584]{1,0:T(8,128)(2,1)S(1)}, u32[]{:S(2)}, u32[]{:S(2)}) collective-permute-start(bf16[8,3584]{1,0:T(8,128)(2,1)S(1)} %get-tuple-element.51), channel_id=1, source_target_pairs={{0,6},{1,7},{2,4},{3,5},{4,2},{5,3},{6,0},{7,1},{8,14},{9,15},{10,... | collective-permute-start | bytes 172040 | tf_op jit(solution)/shard_map/ppermute | solution.py:150

commit v6 on v5

--- a/solution.py
+++ b/solution.py
@@ -9,6 +9,7 @@
 
 SLOTS = 8
 CHUNKS = 4
+PIECES = 4
 
 VMEM = pl.BlockSpec(memory_space=pltpu.VMEM)
 HBM = pl.BlockSpec(memory_space=pltpu.HBM)
@@ -24,7 +25,11 @@
 
 def block_order(flight):
     far = list(range(flight // 2, flight))
-    return far + list(range(1, flight // 2)) + [0]
+    return far[:1] + list(range(1, flight // 2)) + far[1:] + [0]
+
+
+def group(items, flight, far):
+    return [x for x, r in zip(items, block_order(flight)) if (r >= flight // 2) == far]
 
 
 def dispatch_kernel(
@@ -90,32 +95,37 @@
     weights.wait()
 
 
-def stage_kernel(source, target, sem):
-    copy = pltpu.make_async_copy(source, target, sem)
-    copy.start()
-    copy.wait()
+def stage_kernel(source, target, sems):
+    rows = source.shape[0] // PIECES
+    copies = [
+        pltpu.make_async_copy(
+            source.at[pl.ds(i * rows, rows)], target.at[pl.ds(i * rows, rows)], sems.at[i]
+        )
+        for i in range(PIECES)
+    ]
+    for copy in copies:
+        copy.start()
+    for copy in copies:
+        copy.wait()
 
 
 def together(refs):
     return jnp.concatenate([b[...].astype(jnp.float32) for b in refs], axis=0).astype(jnp.bfloat16)
 
 
-def expert_kernel(flight, *refs):
-    blocks = refs[: 2 * flight]
-    gate_ref, up_ref, down_hbm = refs[2 * flight : 2 * flight + 3]
-    outs = refs[2 * flight + 3 : 2 * flight + 7]
-    down, sem = refs[2 * flight + 7 :]
-    copy = pltpu.make_async_copy(down_hbm, down, sem)
-    copy.start()
-    x = together(blocks)
+def gather_kernel(*refs):
+    refs[-1][...] = together(refs[:-1])
+
+
+def expert_kernel(own_ref, other_ref, gate_ref, up_ref, down_ref, own_out, other_out):
+    rows = own_ref.shape[0]
+    x = jnp.concatenate([own_ref[...], other_ref[...]], axis=0)
     gate_v = jnp.dot(x, gate_ref[...], preferred_element_type=jnp.float32)
     up_v = jnp.dot(x, up_ref[...], preferred_element_type=jnp.float32)
     hidden = (gate_v / (1.0 + jnp.exp(-gate_v)) * up_v).astype(jnp.bfloat16)
-    copy.wait()
-    part = jnp.dot(hidden, down[...], preferred_element_type=jnp.float32).astype(jnp.bfloat16)
-    rows = outs[0].shape[0]
-    for i, out in enumerate(outs):
-        out[...] = part[i * rows : (i + 1) * rows]
+    part = jnp.dot(hidden, down_ref[...], preferred_element_type=jnp.float32).astype(jnp.bfloat16)
+    own_out[...] = part[:rows]
+    other_out[...] = part[rows:]
 
 
 def join_kernel(mine_ref, got_ref, *outs):
@@ -141,7 +151,6 @@
     order = block_order(flight)
     block = jax.ShapeDtypeStruct((SLOTS, width), jnp.bfloat16)
     half = jax.ShapeDtypeStruct((packed // 2, width), jnp.bfloat16)
-    pairs = [(i, i ^ 1) for i in range(owners)]
     few = relative(flight)
 
     def exchange(blocks):
@@ -157,11 +166,57 @@
         )
         return [got[r] for r in order]
 
-    def swap(blocks):
-        if few:
-            return [lax.ppermute(b, "exp", pairs) for b in blocks]
-        got = lax.ppermute(jnp.stack(blocks), "exp", pairs)
-        return [got[r] for r in range(flight)]
+    def swap(rows):
+        return lax.ppermute(rows, "exp", [(i, i ^ 1) for i in range(owners)])
+
+    def stage(weights):
+        return pl.pallas_call(
+            stage_kernel,
+            out_shape=jax.ShapeDtypeStruct(weights.shape, weights.dtype),
+            in_specs=[HBM],
+            out_specs=VMEM,
+            scratch_shapes=[pltpu.SemaphoreType.DMA((PIECES,))],
+            compiler_params=pltpu.CompilerParams(vmem_limit_bytes=16 * 2**20),
+            cost_estimate=pl.CostEstimate(
+                flops=0, bytes_accessed=4 * width * hidden, transcendentals=0
+            ),
+            name="stage",
+        )(*in_hbm(weights))
+
+    def gather(blocks):
+        return pl.pallas_call(
+            gather_kernel,
+            out_shape=half,
+            in_specs=[VMEM] * (flight // 2),
+            out_specs=VMEM,
+            compiler_params=pltpu.CompilerParams(vmem_limit_bytes=16 * 2**20),
+            name="gather",
+        )(*blocks)
+
+    def experts(own, other, weights):
+        return pl.pallas_call(
+            expert_kernel,
+            out_shape=(half, half),
+            in_specs=[VMEM] * 5,
+            out_specs=(VMEM, VMEM),
+            compiler_params=pltpu.CompilerParams(vmem_limit_bytes=24 * 2**20),
+            cost_estimate=pl.CostEstimate(
+                flops=6 * packed * width * hidden,
+                bytes_accessed=6 * width * hidden,
+                transcendentals=0,
+            ),
+            name="experts",
+        )(own, other, *weights)
+
+    def join(mine, theirs):
+        return pl.pallas_call(
+            join_kernel,
+            out_shape=(block,) * (flight // 2),
+            in_specs=[VMEM] * 2,
+            out_specs=(VMEM,) * (flight // 2),
+            compiler_params=pltpu.CompilerParams(vmem_limit_bytes=16 * 2**20),
+            name="join",
+        )(mine, swap(theirs))
 
     mix, gate, *outgoing = pl.pallas_call(
         functools.partial(dispatch_kernel, flight),
@@ -184,47 +239,22 @@
         name="dispatch",
     )(*in_hbm(tokens, norm_gain, expert_ids.T, gate_weights.T, w_gate[0]))
 
-    up = pl.pallas_call(
-        stage_kernel,
-        out_shape=jax.ShapeDtypeStruct(w_up.shape[1:], w_up.dtype),
-        in_specs=[HBM],
-        out_specs=VMEM,
-        scratch_shapes=[pltpu.SemaphoreType.DMA],
-        compiler_params=pltpu.CompilerParams(vmem_limit_bytes=16 * 2**20),
-        cost_estimate=pl.CostEstimate(flops=0, bytes_accessed=4 * width * hidden, transcendentals=0),
-        name="stage",
-    )(*in_hbm(w_up[0]))
-
-    own = exchange(outgoing)
-    last = flight // 2 - 1
-    own[last], up = lax.optimization_barrier((own[last], up))
-    other = swap(own)
-    own_far, own_near, other_far, other_near = pl.pallas_call(
-        functools.partial(expert_kernel, flight),
-        out_shape=(half,) * 4,
-        in_specs=[VMEM] * (2 * flight + 2) + [HBM],
-        out_specs=(VMEM,) * 4,
-        scratch_shapes=[pltpu.VMEM(w_down.shape[1:], w_down.dtype), pltpu.SemaphoreType.DMA],
-        compiler_params=pltpu.CompilerParams(vmem_limit_bytes=32 * 2**20),
-        cost_estimate=pl.CostEstimate(
-            flops=12 * packed * width * hidden,
-            bytes_accessed=6 * width * hidden,
-            transcendentals=0,
-        ),
-        name="experts",
-    )(*own, *other, gate, up, *in_hbm(w_down[0]))
-
-    def join(mine, theirs):
-        return pl.pallas_call(
-            join_kernel,
-            out_shape=(block,) * (flight // 2),
-            in_specs=[VMEM] * 2,
-            out_specs=(VMEM,) * (flight // 2),
-            compiler_params=pltpu.CompilerParams(vmem_limit_bytes=24 * 2**20),
-            name="join",
-        )(mine, lax.ppermute(theirs, "exp", pairs))
-
-    returned = exchange([*join(own_far, other_far), *join(own_near, other_near)])
+    up, down = stage(w_up[0]), stage(w_down[0])
+    arrived = exchange(outgoing)
+    *held, up, down = lax.optimization_barrier((*arrived[:-2], up, down))
+    arrived = held + arrived[-2:]
+    weights = (gate, up, down)
+
+    near_own = gather(group(arrived, flight, False))
+    near_other = swap(near_own)
+    far_own = gather(group(arrived, flight, True))
+    far_own, near_own, near_other = lax.optimization_barrier((far_own, near_own, near_other))
+    far_other = swap(far_own)
+    near_mine, near_theirs = experts(near_own, near_other, weights)
+    far_mine, far_theirs = experts(far_own, far_other, weights)
+    far_rows = iter(join(far_mine, far_theirs))
+    near_rows = iter(join(near_mine, near_theirs))
+    returned = exchange([next(far_rows if r >= flight // 2 else near_rows) for r in order])
     return pl.pallas_call(
         functools.partial(combine_kernel, flight),
         out_shape=jax.ShapeDtypeStruct((count, width), jnp.bfloat16),

time: 47.2 us -> 48.2 us (1.021)
  waiting for transfers between devices: 14.3 us -> 9.25 us
  starting transfers between devices: 22.9 us -> 26.4 us
  Pallas kernels: 9.73 us -> 12.3 us
    ppermute x14, starting transfers between devices: 20.6 us -> 25.6 us  [exchange(): lax.ppermute(b, 'exp', [(i, i ^ 2 * r) for i in range(owners)])]
    ppermute x14, waiting for transfers between devices: 12.2 us -> 9.24 us  [exchange(): lax.ppermute(b, 'exp', [(i, i ^ 2 * r) for i in range(owners)])]
    pallas_call x2 -> x6, Pallas kernels: 5.7 us -> 8.29 us  [the longest x2 4.17 us: experts(): pl.pallas_call(expert_kernel, out_shape=(half, half), in_specs=[VMEM] * 5...]
    ppermute x10 -> x4, waiting for transfers between devices: 2.14 us -> 0.01 us  [swap(): return lax.ppermute(rows, 'exp', [(i, i ^ 1) for i in range(owners)])]
    ppermute x10 -> x4, starting transfers between devices: 2.25 us -> 0.79 us  [swap(): return lax.ppermute(rows, 'exp', [(i, i ^ 1) for i in range(owners)])]
  transfers between devices with their start and end apart: 24 -> 18, of which waited for: 11 -> 4; matrix products, arithmetic and copies ran while one was open for 0% -> 0% of each run, Pallas kernels for 5% -> 17%
where the time goes in v6:
time: 48.2 us; the launch traced here: 48.1 us
  starting transfers between devices  26.4 us (55%)
  Pallas kernels  12.3 us (26%)
  waiting for transfers between devices  9.25 us (19%)
    ppermute x14, starting transfers between devices, exchange(): lax.ppermute(b, 'exp', [(i, i ^ 2 * r) for i in range(owners)])  25.6 us
    ppermute x14, waiting for transfers between devices, exchange(): lax.ppermute(b, 'exp', [(i, i ^ 2 * r) for i in range(owners)])  9.24 us
    pallas_call x2, Pallas kernels, experts(): pl.pallas_call(expert_kernel, out_shape=(half, half), in_specs=[VMEM] * 5...  4.17 us
    pallas_call x2, Pallas kernels, stage(): pl.pallas_call(stage_kernel, out_shape=jax.ShapeDtypeStruct(weights.shape...  4.09 us
    pallas_call x1, Pallas kernels, per_device(): pl.pallas_call(functools.partial(dispatch_kernel, flight), out_shape=(jax...  2.57 us
    pallas_call x1, Pallas kernels, per_device(): pl.pallas_call(functools.partial(combine_kernel, flight), out_shape=jax.S...  1.35 us
  transfers between devices with their start and end apart: 18, of which 4 were waited for; matrix products, arithmetic and copies ran while one was open for 0% of the time, Pallas kernels for 17%

profile of v6, /device:TPU:0, one launch (start us, length us, event | category | flops | bytes accessed | tf_op | source)
XLA Modules:
  0.0 48.1 jit_solution(15906579424828001343)
XLA Ops:
  0.0 2.6 %dispatch.1 = (bf16[128,128]{1,0:T(8,128)(2,1)S(1)}, bf16[3584,512]{1,0:T(8,128)(2,1)S(1)}, bf16[8,3584]{1,0:T(8,128)(2,1)S(1)}, bf16[8,3584]{1,0:T(8,128)(2,1)S...) custom-call(bf16[128,3584]{1,0:T(8,128)(2,1)} %tok_hbm.1, ...), custom_call_target="tpu_custom_call" | custom-call | tf_op jit(solution)/shard_map/dispatch/pallas_call | solution.py:221
  2.6 4.1 %collective-permute-start = (bf16[8,3584]{1,0:T(8,128)(2,1)S(1)}, bf16[8,3584]{1,0:T(8,128)(2,1)S(1)}, u32[]{:S(2)}, u32[]{:S(2)}) collective-permute-start(bf16[8,3584]{1,0:T(8,128)(2,1)S(1)} %get-tuple-element.39), channel_id=1, source_target_pairs={{0,8},{1,9},{2,10},{3,11},{4,12},{5,13},{6,14},{7,15},{8,0},{9,1},... | collective-permute-start | bytes 172040 | tf_op jit(solution)/shard_map/ppermute | solution.py:159
  6.7 1.5 %collective-permute-start.1 = (bf16[8,3584]{1,0:T(8,128)(2,1)S(1)}, bf16[8,3584]{1,0:T(8,128)(2,1)S(1)}, u32[]{:S(2)}, u32[]{:S(2)}) collective-permute-start(bf16[8,3584]{1,0:T(8,128)(2,1)S(1)} %get-tuple-element.40), channel_id=1, source_target_pairs={{0,2},{1,3},{2,0},{3,1},{4,6},{5,7},{6,4},{7,5},{8,10},{9,11},{10,... | collective-permute-start | bytes 172040 | tf_op jit(solution)/shard_map/ppermute | solution.py:159
  8.2 1.6 %collective-permute-start.2 = (bf16[8,3584]{1,0:T(8,128)(2,1)S(1)}, bf16[8,3584]{1,0:T(8,128)(2,1)S(1)}, u32[]{:S(2)}, u32[]{:S(2)}) collective-permute-start(bf16[8,3584]{1,0:T(8,128)(2,1)S(1)} %get-tuple-element.41), channel_id=1, source_target_pairs={{0,4},{1,5},{2,6},{3,7},{4,0},{5,1},{6,2},{7,3},{8,12},{9,13},{10,... | collective-permute-start | bytes 172040 | tf_op jit(solution)/shard_map/ppermute | solution.py:159
  9.8 0.4 collective-permute-start.3
  10.2 1.3 %collective-permute-start.4 = (bf16[8,3584]{1,0:T(8,128)(2,1)S(1)}, bf16[8,3584]{1,0:T(8,128)(2,1)S(1)}, u32[]{:S(2)}, u32[]{:S(2)}) collective-permute-start(bf16[8,3584]{1,0:T(8,128)(2,1)S(1)} %get-tuple-element.43), channel_id=1, source_target_pairs={{0,10},{1,11},{2,8},{3,9},{4,14},{5,15},{6,12},{7,13},{8,2},{9,3},... | collective-permute-start | bytes 172040 | tf_op jit(solution)/shard_map/ppermute | solution.py:159
  11.5 0.0 collective-permute-done.refs_0_
  11.5 3.6 %collective-permute-start.5 = (bf16[8,3584]{1,0:T(8,128)(2,1)S(1)}, bf16[8,3584]{1,0:T(8,128)(2,1)S(1)}, u32[]{:S(2)}, u32[]{:S(2)}) collective-permute-start(bf16[8,3584]{1,0:T(8,128)(2,1)S(1)} %get-tuple-element.44), channel_id=1, source_target_pairs={{0,12},{1,13},{2,14},{3,15},{4,8},{5,9},{6,10},{7,11},{8,4},{9,5},... | collective-permute-start | bytes 172040 | tf_op jit(solution)/shard_map/ppermute | solution.py:159
  15.1 2.0 %stage.2.up_ref = bf16[3584,512]{1,0:T(8,128)(2,1)S(1)} custom-call(bf16[3584,512]{1,0:T(8,128)(2,1)} %bitcast.5), custom_call_target="tpu_custom_call" | custom-call | bytes 7340032 | tf_op jit(solution)/shard_map/stage/pallas_call | solution.py:173
  17.1 2.0 %stage.3.down_ref = bf16[512,3584]{1,0:T(8,128)(2,1)S(1)} custom-call(bf16[512,3584]{1,0:T(8,128)(2,1)} %bitcast.6), custom_call_target="tpu_custom_call" | custom-call | bytes 7340032 | tf_op jit(solution)/shard_map/stage/pallas_call | solution.py:173
  19.2 0.0 collective-permute-done.3.refs_2_
  19.2 0.1 collective-permute-start.7
  19.3 1.8 %collective-permute-start.6 = (bf16[8,3584]{1,0:T(8,128)(2,1)S(1)}, bf16[8,3584]{1,0:T(8,128)(2,1)S(1)}, u32[]{:S(2)}, u32[]{:S(2)}) collective-permute-start(bf16[8,3584]{1,0:T(8,128)(2,1)S(1)} %get-tuple-element.48), channel_id=1, source_target_pairs={{0,14},{1,15},{2,12},{3,13},{4,10},{5,11},{6,8},{7,9},{8,6},{9,7},... | collective-permute-start | bytes 172040 | tf_op jit(solution)/shard_map/ppermute | solution.py:159
  21.1 5.2 %collective-permute-done.6.refs_3_ = bf16[8,3584]{1,0:T(8,128)(2,1)S(1)} collective-permute-done((bf16[8,3584]{1,0:T(8,128)(2,1)S(1)}, bf16[8,3584]{1,0:T(8,128)(2,1)S(1)}, u32[]{:S(2)}, u32[]{:S(2)}) %collective-permute-start.6) | collective-permute-done | bytes 57376 | tf_op jit(solution)/shard_map/ppermute | solution.py:159
  26.4 0.0 collective-permute-done.7.other_ref
  26.4 0.1 collective-permute-start.8
  26.5 2.1 %experts.3 = (bf16[32,3584]{1,0:T(8,128)(2,1)S(1)}, bf16[32,3584]{1,0:T(8,128)(2,1)S(1)}) custom-call(bf16[32,3584]{1,0:T(8,128)(2,1)S(1)} %gather.3.own_ref, bf16[32,3584]{1,0:T(8,128)(2,1)S(1)} %collective-permute-done.7.other_ref, bf16[3584,512]{1,0:T(8,128)(2,1)S(1)} %get-tuple-element.54.gate_ref, bf16[3584,512]{1,0:T(8,128)(2,1)S(1)} %stage.2.up_ref, ...), custom_call_target="tpu_custom_call" | custom-call | flops 704643072 | bytes 11010048 | tf_op jit(solution)/shard_map/experts/pallas_call | solution.py:197
  28.6 0.6 %collective-permute-start.11 = (bf16[32,3584]{1,0:T(8,128)(2,1)S(1)}, bf16[32,3584]{1,0:T(8,128)(2,1)S(1)}, u32[]{:S(2)}, u32[]{:S(2)}) collective-permute-start(bf16[32,3584]{1,0:T(8,128)(2,1)S(1)} %get-tuple-element.63), channel_id=1, source_target_pairs={{0,1},{1,0},{2,3},{3,2},{4,5},{5,4},{6,7},{7,6},{8,9},{9,8},{10,11... | collective-permute-start | bytes 688136 | tf_op jit(solution)/shard_map/ppermute | solution.py:170
  29.1 2.1 %experts.2 = (bf16[32,3584]{1,0:T(8,128)(2,1)S(1)}, bf16[32,3584]{1,0:T(8,128)(2,1)S(1)}) custom-call(bf16[32,3584]{1,0:T(8,128)(2,1)S(1)} %gather.2.own_ref, bf16[32,3584]{1,0:T(8,128)(2,1)S(1)} %collective-permute-done.8.other_ref, bf16[3584,512]{1,0:T(8,128)(2,1)S(1)} %get-tuple-element.54.gate_ref, bf16[3584,512]{1,0:T(8,128)(2,1)S(1)} %stage.2.up_ref, ...), custom_call_target="tpu_custom_call" | custom-call | flops 704643072 | bytes 11010048 | tf_op jit(solution)/shard_map/experts/pallas_call | solution.py:197
  31.2 0.1 collective-permute-start.9
  31.3 0.1 join.3
  31.4 0.6 %collective-permute-start.12 = (bf16[8,3584]{1,0:T(8,128)(2,1)S(1)}, bf16[8,3584]{1,0:T(8,128)(2,1)S(1)}, u32[]{:S(2)}, u32[]{:S(2)}) collective-permute-start(bf16[8,3584]{1,0:T(8,128)(2,1)S(1)} %get-tuple-element.64), channel_id=1, source_target_pairs={{0,2},{1,3},{2,0},{3,1},{4,6},{5,7},{6,4},{7,5},{8,10},{9,11},{10,... | collective-permute-start | bytes 172040 | tf_op jit(solution)/shard_map/ppermute | solution.py:159
  31.9 3.0 %collective-permute-start.14 = (bf16[8,3584]{1,0:T(8,128)(2,1)S(1)}, bf16[8,3584]{1,0:T(8,128)(2,1)S(1)}, u32[]{:S(2)}, u32[]{:S(2)}) collective-permute-start(bf16[8,3584]{1,0:T(8,128)(2,1)S(1)} %get-tuple-element.66), channel_id=1, source_target_pairs={{0,6},{1,7},{2,4},{3,5},{4,2},{5,3},{6,0},{7,1},{8,14},{9,15},{10,... | collective-permute-start | bytes 172040 | tf_op jit(solution)/shard_map/ppermute | solution.py:159
  34.9 0.1 join.2
  35.0 0.4 collective-permute-start.10
  35.4 2.5 %collective-permute-start.15 = (bf16[8,3584]{1,0:T(8,128)(2,1)S(1)}, bf16[8,3584]{1,0:T(8,128)(2,1)S(1)}, u32[]{:S(2)}, u32[]{:S(2)}) collective-permute-start(bf16[8,3584]{1,0:T(8,128)(2,1)S(1)} %get-tuple-element.67), channel_id=1, source_target_pairs={{0,10},{1,11},{2,8},{3,9},{4,14},{5,15},{6,12},{7,13},{8,2},{9,3},... | collective-permute-start | bytes 172040 | tf_op jit(solution)/shard_map/ppermute | solution.py:159
  37.9 1.8 %collective-permute-start.16 = (bf16[8,3584]{1,0:T(8,128)(2,1)S(1)}, bf16[8,3584]{1,0:T(8,128)(2,1)S(1)}, u32[]{:S(2)}, u32[]{:S(2)}) collective-permute-start(bf16[8,3584]{1,0:T(8,128)(2,1)S(1)} %get-tuple-element.68), channel_id=1, source_target_pairs={{0,12},{1,13},{2,14},{3,15},{4,8},{5,9},{6,10},{7,11},{8,4},{9,5},... | collective-permute-start | bytes 172040 | tf_op jit(solution)/shard_map/ppermute | solution.py:159
  39.7 3.0 %collective-permute-start.17 = (bf16[8,3584]{1,0:T(8,128)(2,1)S(1)}, bf16[8,3584]{1,0:T(8,128)(2,1)S(1)}, u32[]{:S(2)}, u32[]{:S(2)}) collective-permute-start(bf16[8,3584]{1,0:T(8,128)(2,1)S(1)} %get-tuple-element.69), channel_id=1, source_target_pairs={{0,14},{1,15},{2,12},{3,13},{4,10},{5,11},{6,8},{7,9},{8,6},{9,7},... | collective-permute-start | bytes 172040 | tf_op jit(solution)/shard_map/ppermute | solution.py:159
  42.7 0.1 collective-permute-done.10.refs_0_
  42.9 2.4 %collective-permute-done.15.refs_4_ = bf16[8,3584]{1,0:T(8,128)(2,1)S(1)} collective-permute-done((bf16[8,3584]{1,0:T(8,128)(2,1)S(1)}, bf16[8,3584]{1,0:T(8,128)(2,1)S(1)}, u32[]{:S(2)}, u32[]{:S(2)}) %collective-permute-start.15) | collective-permute-done | bytes 57376 | tf_op jit(solution)/shard_map/ppermute | solution.py:159
  45.3 1.4 %collective-permute-done.17.refs_6_ = bf16[8,3584]{1,0:T(8,128)(2,1)S(1)} collective-permute-done((bf16[8,3584]{1,0:T(8,128)(2,1)S(1)}, bf16[8,3584]{1,0:T(8,128)(2,1)S(1)}, u32[]{:S(2)}, u32[]{:S(2)}) %collective-permute-start.17) | collective-permute-done | bytes 57376 | tf_op jit(solution)/shard_map/ppermute | solution.py:159
  46.7 1.3 %combine.1 = bf16[128,3584]{1,0:T(8,128)(2,1)} custom-call(bf16[128,128]{1,0:T(8,128)(2,1)S(1)} %get-tuple-element.38.mix_ref, bf16[8,3584]{1,0:T(8,128)(2,1)S(1)} %collective-permute-done.10.refs_0_, bf16[8,3584]{1,0:T(8,128)(2,1)S(1)} %collective-permute-done.12.refs_1_, bf16[8,3584]{1,0:T(8,128)(2,1)S(1)} %collective-permute-done.13.refs_2_, ...), custom_call_target="tpu_custom_call" | custom-call | tf_op jit(solution)/shard_map/combine/pallas_call | solution.py:258
  (14 shorter events, 0.1 us)
Async XLA Ops:
  2.6 8.9 %collective-permute-start = (bf16[8,3584]{1,0:T(8,128)(2,1)S(1)}, bf16[8,3584]{1,0:T(8,128)(2,1)S(1)}, u32[]{:S(2)}, u32[]{:S(2)}) collective-permute-start(bf16[8,3584]{1,0:T(8,128)(2,1)S(1)} %get-tuple-element.39), channel_id=1, source_target_pairs={{0,8},{1,9},{2,10},{3,11},{4,12},{5,13},{6,14},{7,15},{8,0},{9,1},... | collective-permute-start | bytes 172040 | tf_op jit(solution)/shard_map/ppermute | solution.py:159
  6.7 12.5 %collective-permute-start.1 = (bf16[8,3584]{1,0:T(8,128)(2,1)S(1)}, bf16[8,3584]{1,0:T(8,128)(2,1)S(1)}, u32[]{:S(2)}, u32[]{:S(2)}) collective-permute-start(bf16[8,3584]{1,0:T(8,128)(2,1)S(1)} %get-tuple-element.40), channel_id=1, source_target_pairs={{0,2},{1,3},{2,0},{3,1},{4,6},{5,7},{6,4},{7,5},{8,10},{9,11},{10,... | collective-permute-start | bytes 172040 | tf_op jit(solution)/shard_map/ppermute | solution.py:159
  8.2 11.0 %collective-permute-start.2 = (bf16[8,3584]{1,0:T(8,128)(2,1)S(1)}, bf16[8,3584]{1,0:T(8,128)(2,1)S(1)}, u32[]{:S(2)}, u32[]{:S(2)}) collective-permute-start(bf16[8,3584]{1,0:T(8,128)(2,1)S(1)} %get-tuple-element.41), channel_id=1, source_target_pairs={{0,4},{1,5},{2,6},{3,7},{4,0},{5,1},{6,2},{7,3},{8,12},{9,13},{10,... | collective-permute-start | bytes 172040 | tf_op jit(solution)/shard_map/ppermute | solution.py:159
  9.8 9.4 %collective-permute-start.3 = (bf16[8,3584]{1,0:T(8,128)(2,1)S(1)}, bf16[8,3584]{1,0:T(8,128)(2,1)S(1)}, u32[]{:S(2)}, u32[]{:S(2)}) collective-permute-start(bf16[8,3584]{1,0:T(8,128)(2,1)S(1)} %get-tuple-element.42), channel_id=1, source_target_pairs={{0,6},{1,7},{2,4},{3,5},{4,2},{5,3},{6,0},{7,1},{8,14},{9,15},{10,... | collective-permute-start | bytes 172040 | tf_op jit(solution)/shard_map/ppermute | solution.py:159
  10.2 9.0 %collective-permute-start.4 = (bf16[8,3584]{1,0:T(8,128)(2,1)S(1)}, bf16[8,3584]{1,0:T(8,128)(2,1)S(1)}, u32[]{:S(2)}, u32[]{:S(2)}) collective-permute-start(bf16[8,3584]{1,0:T(8,128)(2,1)S(1)} %get-tuple-element.43), channel_id=1, source_target_pairs={{0,10},{1,11},{2,8},{3,9},{4,14},{5,15},{6,12},{7,13},{8,2},{9,3},... | collective-permute-start | bytes 172040 | tf_op jit(solution)/shard_map/ppermute | solution.py:159
  11.5 7.7 %collective-permute-start.5 = (bf16[8,3584]{1,0:T(8,128)(2,1)S(1)}, bf16[8,3584]{1,0:T(8,128)(2,1)S(1)}, u32[]{:S(2)}, u32[]{:S(2)}) collective-permute-start(bf16[8,3584]{1,0:T(8,128)(2,1)S(1)} %get-tuple-element.44), channel_id=1, source_target_pairs={{0,12},{1,13},{2,14},{3,15},{4,8},{5,9},{6,10},{7,11},{8,4},{9,5},... | collective-permute-start | bytes 172040 | tf_op jit(solution)/shard_map/ppermute | solution.py:159
  19.2 7.1 %collective-permute-start.7 = (bf16[32,3584]{1,0:T(8,128)(2,1)S(1)}, bf16[32,3584]{1,0:T(8,128)(2,1)S(1)}, u32[]{:S(2)}, u32[]{:S(2)}) collective-permute-start(bf16[32,3584]{1,0:T(8,128)(2,1)S(1)} %gather.3.own_ref), channel_id=1, source_target_pairs={{0,1},{1,0},{2,3},{3,2},{4,5},{5,4},{6,7},{7,6},{8,9},{9,8},{10,11... | collective-permute-start | bytes 688136 | tf_op jit(solution)/shard_map/ppermute | solution.py:170
  19.3 7.0 %collective-permute-start.6 = (bf16[8,3584]{1,0:T(8,128)(2,1)S(1)}, bf16[8,3584]{1,0:T(8,128)(2,1)S(1)}, u32[]{:S(2)}, u32[]{:S(2)}) collective-permute-start(bf16[8,3584]{1,0:T(8,128)(2,1)S(1)} %get-tuple-element.48), channel_id=1, source_target_pairs={{0,14},{1,15},{2,12},{3,13},{4,10},{5,11},{6,8},{7,9},{8,6},{9,7},... | collective-permute-start | bytes 172040 | tf_op jit(solution)/shard_map/ppermute | solution.py:159
  26.4 2.7 %collective-permute-start.8 = (bf16[32,3584]{1,0:T(8,128)(2,1)S(1)}, bf16[32,3584]{1,0:T(8,128)(2,1)S(1)}, u32[]{:S(2)}, u32[]{:S(2)}) collective-permute-start(bf16[32,3584]{1,0:T(8,128)(2,1)S(1)} %gather.2.own_ref), channel_id=1, source_target_pairs={{0,1},{1,0},{2,3},{3,2},{4,5},{5,4},{6,7},{7,6},{8,9},{9,8},{10,11... | collective-permute-start | bytes 688136 | tf_op jit(solution)/shard_map/ppermute | solution.py:170
  28.6 2.7 %collective-permute-start.11 = (bf16[32,3584]{1,0:T(8,128)(2,1)S(1)}, bf16[32,3584]{1,0:T(8,128)(2,1)S(1)}, u32[]{:S(2)}, u32[]{:S(2)}) collective-permute-start(bf16[32,3584]{1,0:T(8,128)(2,1)S(1)} %get-tuple-element.63), channel_id=1, source_target_pairs={{0,1},{1,0},{2,3},{3,2},{4,5},{5,4},{6,7},{7,6},{8,9},{9,8},{10,11... | collective-permute-start | bytes 688136 | tf_op jit(solution)/shard_map/ppermute | solution.py:170
  31.2 3.7 %collective-permute-start.9 = (bf16[32,3584]{1,0:T(8,128)(2,1)S(1)}, bf16[32,3584]{1,0:T(8,128)(2,1)S(1)}, u32[]{:S(2)}, u32[]{:S(2)}) collective-permute-start(bf16[32,3584]{1,0:T(8,128)(2,1)S(1)} %get-tuple-element.58), channel_id=1, source_target_pairs={{0,1},{1,0},{2,3},{3,2},{4,5},{5,4},{6,7},{7,6},{8,9},{9,8},{10,11... | collective-permute-start | bytes 688136 | tf_op jit(solution)/shard_map/ppermute | solution.py:170
  31.4 6.6 %collective-permute-start.12 = (bf16[8,3584]{1,0:T(8,128)(2,1)S(1)}, bf16[8,3584]{1,0:T(8,128)(2,1)S(1)}, u32[]{:S(2)}, u32[]{:S(2)}) collective-permute-start(bf16[8,3584]{1,0:T(8,128)(2,1)S(1)} %get-tuple-element.64), channel_id=1, source_target_pairs={{0,2},{1,3},{2,0},{3,1},{4,6},{5,7},{6,4},{7,5},{8,10},{9,11},{10,... | collective-permute-start | bytes 172040 | tf_op jit(solution)/shard_map/ppermute | solution.py:159
  31.9 7.8 %collective-permute-start.13 = (bf16[8,3584]{1,0:T(8,128)(2,1)S(1)}, bf16[8,3584]{1,0:T(8,128)(2,1)S(1)}, u32[]{:S(2)}, u32[]{:S(2)}) collective-permute-start(bf16[8,3584]{1,0:T(8,128)(2,1)S(1)} %get-tuple-element.65), channel_id=1, source_target_pairs={{0,4},{1,5},{2,6},{3,7},{4,0},{5,1},{6,2},{7,3},{8,12},{9,13},{10,... | collective-permute-start | bytes 172040 | tf_op jit(solution)/shard_map/ppermute | solution.py:159
  31.9 10.8 %collective-permute-start.14 = (bf16[8,3584]{1,0:T(8,128)(2,1)S(1)}, bf16[8,3584]{1,0:T(8,128)(2,1)S(1)}, u32[]{:S(2)}, u32[]{:S(2)}) collective-permute-start(bf16[8,3584]{1,0:T(8,128)(2,1)S(1)} %get-tuple-element.66), channel_id=1, source_target_pairs={{0,6},{1,7},{2,4},{3,5},{4,2},{5,3},{6,0},{7,1},{8,14},{9,15},{10,... | collective-permute-start | bytes 172040 | tf_op jit(solution)/shard_map/ppermute | solution.py:159
  35.0 7.9 %collective-permute-start.10 = (bf16[8,3584]{1,0:T(8,128)(2,1)S(1)}, bf16[8,3584]{1,0:T(8,128)(2,1)S(1)}, u32[]{:S(2)}, u32[]{:S(2)}) collective-permute-start(bf16[8,3584]{1,0:T(8,128)(2,1)S(1)} %get-tuple-element.59), channel_id=1, source_target_pairs={{0,8},{1,9},{2,10},{3,11},{4,12},{5,13},{6,14},{7,15},{8,0},{9,1},... | collective-permute-start | bytes 172040 | tf_op jit(solution)/shard_map/ppermute | solution.py:159
  35.4 9.9 %collective-permute-start.15 = (bf16[8,3584]{1,0:T(8,128)(2,1)S(1)}, bf16[8,3584]{1,0:T(8,128)(2,1)S(1)}, u32[]{:S(2)}, u32[]{:S(2)}) collective-permute-start(bf16[8,3584]{1,0:T(8,128)(2,1)S(1)} %get-tuple-element.67), channel_id=1, source_target_pairs={{0,10},{1,11},{2,8},{3,9},{4,14},{5,15},{6,12},{7,13},{8,2},{9,3},... | collective-permute-start | bytes 172040 | tf_op jit(solution)/shard_map/ppermute | solution.py:159
  37.9 7.4 %collective-permute-start.16 = (bf16[8,3584]{1,0:T(8,128)(2,1)S(1)}, bf16[8,3584]{1,0:T(8,128)(2,1)S(1)}, u32[]{:S(2)}, u32[]{:S(2)}) collective-permute-start(bf16[8,3584]{1,0:T(8,128)(2,1)S(1)} %get-tuple-element.68), channel_id=1, source_target_pairs={{0,12},{1,13},{2,14},{3,15},{4,8},{5,9},{6,10},{7,11},{8,4},{9,5},... | collective-permute-start | bytes 172040 | tf_op jit(solution)/shard_map/ppermute | solution.py:159
  39.7 7.0 %collective-permute-start.17 = (bf16[8,3584]{1,0:T(8,128)(2,1)S(1)}, bf16[8,3584]{1,0:T(8,128)(2,1)S(1)}, u32[]{:S(2)}, u32[]{:S(2)}) collective-permute-start(bf16[8,3584]{1,0:T(8,128)(2,1)S(1)} %get-tuple-element.69), channel_id=1, source_target_pairs={{0,14},{1,15},{2,12},{3,13},{4,10},{5,11},{6,8},{7,9},{8,6},{9,7},... | collective-permute-start | bytes 172040 | tf_op jit(solution)/shard_map/ppermute | solution.py:159

commit v7 on v6

--- a/solution.py
+++ b/solution.py
@@ -24,12 +24,10 @@
 
 
 def block_order(flight):
-    far = list(range(flight // 2, flight))
-    return far[:1] + list(range(1, flight // 2)) + far[1:] + [0]
-
-
-def group(items, flight, far):
-    return [x for x, r in zip(items, block_order(flight)) if (r >= flight // 2) == far]
+    far = range(flight // 2, flight)
+    near = range(1, flight // 2)
+    mixed = [r for pair in zip(far, near) for r in pair]
+    return mixed + [flight - 1, 0]
 
 
 def dispatch_kernel(
@@ -150,7 +148,7 @@
     packed = flight * SLOTS
     order = block_order(flight)
     block = jax.ShapeDtypeStruct((SLOTS, width), jnp.bfloat16)
-    half = jax.ShapeDtypeStruct((packed // 2, width), jnp.bfloat16)
+    whole = jax.ShapeDtypeStruct((packed, width), jnp.bfloat16)
     few = relative(flight)
 
     def exchange(blocks):
@@ -182,41 +180,6 @@
             ),
             name="stage",
         )(*in_hbm(weights))
-
-    def gather(blocks):
-        return pl.pallas_call(
-            gather_kernel,
-            out_shape=half,
-            in_specs=[VMEM] * (flight // 2),
-            out_specs=VMEM,
-            compiler_params=pltpu.CompilerParams(vmem_limit_bytes=16 * 2**20),
-            name="gather",
-        )(*blocks)
-
-    def experts(own, other, weights):
-        return pl.pallas_call(
-            expert_kernel,
-            out_shape=(half, half),
-            in_specs=[VMEM] * 5,
-            out_specs=(VMEM, VMEM),
-            compiler_params=pltpu.CompilerParams(vmem_limit_bytes=24 * 2**20),
-            cost_estimate=pl.CostEstimate(
-                flops=6 * packed * width * hidden,
-                bytes_accessed=6 * width * hidden,
-                transcendentals=0,
-            ),
-            name="experts",
-        )(own, other, *weights)
-
-    def join(mine, theirs):
-        return pl.pallas_call(
-            join_kernel,
-            out_shape=(block,) * (flight // 2),
-            in_specs=[VMEM] * 2,
-            out_specs=(VMEM,) * (flight // 2),
-            compiler_params=pltpu.CompilerParams(vmem_limit_bytes=16 * 2**20),
-            name="join",
-        )(mine, swap(theirs))
 
     mix, gate, *outgoing = pl.pallas_call(
         functools.partial(dispatch_kernel, flight),
@@ -240,21 +203,37 @@
     )(*in_hbm(tokens, norm_gain, expert_ids.T, gate_weights.T, w_gate[0]))
 
     up, down = stage(w_up[0]), stage(w_down[0])
-    arrived = exchange(outgoing)
-    *held, up, down = lax.optimization_barrier((*arrived[:-2], up, down))
-    arrived = held + arrived[-2:]
-    weights = (gate, up, down)
-
-    near_own = gather(group(arrived, flight, False))
-    near_other = swap(near_own)
-    far_own = gather(group(arrived, flight, True))
-    far_own, near_own, near_other = lax.optimization_barrier((far_own, near_own, near_other))
-    far_other = swap(far_own)
-    near_mine, near_theirs = experts(near_own, near_other, weights)
-    far_mine, far_theirs = experts(far_own, far_other, weights)
-    far_rows = iter(join(far_mine, far_theirs))
-    near_rows = iter(join(near_mine, near_theirs))
-    returned = exchange([next(far_rows if r >= flight // 2 else near_rows) for r in order])
+    *arrived, up = lax.optimization_barrier((*exchange(outgoing), up))
+    own = pl.pallas_call(
+        gather_kernel,
+        out_shape=whole,
+        in_specs=[VMEM] * flight,
+        out_specs=VMEM,
+        compiler_params=pltpu.CompilerParams(vmem_limit_bytes=16 * 2**20),
+        name="gather",
+    )(*arrived)
+    mine, theirs = pl.pallas_call(
+        expert_kernel,
+        out_shape=(whole, whole),
+        in_specs=[VMEM] * 5,
+        out_specs=(VMEM, VMEM),
+        compiler_params=pltpu.CompilerParams(vmem_limit_bytes=24 * 2**20),
+        cost_estimate=pl.CostEstimate(
+            flops=12 * packed * width * hidden,
+            bytes_accessed=6 * width * hidden,
+            transcendentals=0,
+        ),
+        name="experts",
+    )(own, swap(own), gate, up, down)
+    joined = pl.pallas_call(
+        join_kernel,
+        out_shape=(block,) * flight,
+        in_specs=[VMEM] * 2,
+        out_specs=(VMEM,) * flight,
+        compiler_params=pltpu.CompilerParams(vmem_limit_bytes=16 * 2**20),
+        name="join",
+    )(mine, swap(theirs))
+    returned = exchange(joined)
     return pl.pallas_call(
         functools.partial(combine_kernel, flight),
         out_shape=jax.ShapeDtypeStruct((count, width), jnp.bfloat16),

time: 48.2 us -> 43.2 us (0.90)
  Pallas kernels: 12.3 us -> 9.86 us
  starting transfers between devices: 26.4 us -> 24.5 us
  waiting for transfers between devices: 9.25 us -> 8.51 us
    pallas_call x6 -> x3, Pallas kernels: 4.31 us -> 1.86 us  [the longest x1 1.72 us: per_device(): pl.pallas_call(expert_kernel, out_shape=(whole, whole), in_specs=[VMEM] *...]
    ppermute x14, waiting for transfers between devices: 9.24 us -> 7.06 us  [exchange(): lax.ppermute(b, 'exp', [(i, i ^ 2 * r) for i in range(owners)])]
    ppermute x14, starting transfers between devices: 25.6 us -> 23.9 us  [exchange(): lax.ppermute(b, 'exp', [(i, i ^ 2 * r) for i in range(owners)])]
    ppermute x4 -> x2, waiting for transfers between devices: 0.01 us -> 1.45 us  [swap(): return lax.ppermute(rows, 'exp', [(i, i ^ 1) for i in range(owners)])]
  transfers between devices with their start and end apart: 18 -> 16, of which waited for: 4 -> 5; matrix products, arithmetic and copies ran while one was open for 0% -> 0% of each run, Pallas kernels for 17% -> 10%
where the time goes in v7:
time: 43.2 us; the launch traced here: 43 us
  starting transfers between devices  24.5 us (57%)
  Pallas kernels  9.86 us (23%)
  waiting for transfers between devices  8.51 us (20%)
    ppermute x14, starting transfers between devices, exchange(): lax.ppermute(b, 'exp', [(i, i ^ 2 * r) for i in range(owners)])  23.9 us
    ppermute x14, waiting for transfers between devices, exchange(): lax.ppermute(b, 'exp', [(i, i ^ 2 * r) for i in range(owners)])  7.06 us
    pallas_call x2, Pallas kernels, stage(): pl.pallas_call(stage_kernel, out_shape=jax.ShapeDtypeStruct(weights.shape...  4.09 us
    pallas_call x1, Pallas kernels, per_device(): pl.pallas_call(functools.partial(dispatch_kernel, flight), out_shape=(jax...  2.57 us
    pallas_call x1, Pallas kernels, per_device(): pl.pallas_call(expert_kernel, out_shape=(whole, whole), in_specs=[VMEM] *...  1.72 us
    ppermute x2, waiting for transfers between devices, swap(): return lax.ppermute(rows, 'exp', [(i, i ^ 1) for i in range(owners)])  1.45 us
    pallas_call x1, Pallas kernels, per_device(): pl.pallas_call(functools.partial(combine_kernel, flight), out_shape=jax.S...  1.35 us
  transfers between devices with their start and end apart: 16, of which 5 were waited for; matrix products, arithmetic and copies ran while one was open for 0% of the time, Pallas kernels for 10%

profile of v7, /device:TPU:0, one launch (start us, length us, event | category | flops | bytes accessed | tf_op | source)
XLA Modules:
  0.0 43.0 jit_solution(5433154045503137218)
XLA Ops:
  0.0 2.6 %dispatch.1 = (bf16[128,128]{1,0:T(8,128)(2,1)S(1)}, bf16[3584,512]{1,0:T(8,128)(2,1)S(1)}, bf16[8,3584]{1,0:T(8,128)(2,1)S(1)}, bf16[8,3584]{1,0:T(8,128)(2,1)S...) custom-call(bf16[128,3584]{1,0:T(8,128)(2,1)} %tok_hbm.1, ...), custom_call_target="tpu_custom_call" | custom-call | tf_op jit(solution)/shard_map/dispatch/pallas_call | solution.py:184
  2.6 4.1 %collective-permute-start = (bf16[8,3584]{1,0:T(8,128)(2,1)S(1)}, bf16[8,3584]{1,0:T(8,128)(2,1)S(1)}, u32[]{:S(2)}, u32[]{:S(2)}) collective-permute-start(bf16[8,3584]{1,0:T(8,128)(2,1)S(1)} %get-tuple-element.35), channel_id=1, source_target_pairs={{0,8},{1,9},{2,10},{3,11},{4,12},{5,13},{6,14},{7,15},{8,0},{9,1},... | collective-permute-start | bytes 172040 | tf_op jit(solution)/shard_map/ppermute | solution.py:157
  6.7 1.5 %collective-permute-start.1 = (bf16[8,3584]{1,0:T(8,128)(2,1)S(1)}, bf16[8,3584]{1,0:T(8,128)(2,1)S(1)}, u32[]{:S(2)}, u32[]{:S(2)}) collective-permute-start(bf16[8,3584]{1,0:T(8,128)(2,1)S(1)} %get-tuple-element.36), channel_id=1, source_target_pairs={{0,2},{1,3},{2,0},{3,1},{4,6},{5,7},{6,4},{7,5},{8,10},{9,11},{10,... | collective-permute-start | bytes 172040 | tf_op jit(solution)/shard_map/ppermute | solution.py:157
  8.2 0.0 collective-permute-start.2
  8.2 1.8 %collective-permute-start.3 = (bf16[8,3584]{1,0:T(8,128)(2,1)S(1)}, bf16[8,3584]{1,0:T(8,128)(2,1)S(1)}, u32[]{:S(2)}, u32[]{:S(2)}) collective-permute-start(bf16[8,3584]{1,0:T(8,128)(2,1)S(1)} %get-tuple-element.38), channel_id=1, source_target_pairs={{0,4},{1,5},{2,6},{3,7},{4,0},{5,1},{6,2},{7,3},{8,12},{9,13},{10,... | collective-permute-start | bytes 172040 | tf_op jit(solution)/shard_map/ppermute | solution.py:157
  10.1 2.5 %collective-permute-start.4 = (bf16[8,3584]{1,0:T(8,128)(2,1)S(1)}, bf16[8,3584]{1,0:T(8,128)(2,1)S(1)}, u32[]{:S(2)}, u32[]{:S(2)}) collective-permute-start(bf16[8,3584]{1,0:T(8,128)(2,1)S(1)} %get-tuple-element.39), channel_id=1, source_target_pairs={{0,12},{1,13},{2,14},{3,15},{4,8},{5,9},{6,10},{7,11},{8,4},{9,5},... | collective-permute-start | bytes 172040 | tf_op jit(solution)/shard_map/ppermute | solution.py:157
  12.5 0.0 collective-permute-done.refs_0_
  12.5 1.6 %collective-permute-start.5 = (bf16[8,3584]{1,0:T(8,128)(2,1)S(1)}, bf16[8,3584]{1,0:T(8,128)(2,1)S(1)}, u32[]{:S(2)}, u32[]{:S(2)}) collective-permute-start(bf16[8,3584]{1,0:T(8,128)(2,1)S(1)} %get-tuple-element.40), channel_id=1, source_target_pairs={{0,6},{1,7},{2,4},{3,5},{4,2},{5,3},{6,0},{7,1},{8,14},{9,15},{10,... | collective-permute-start | bytes 172040 | tf_op jit(solution)/shard_map/ppermute | solution.py:157
  14.2 0.0 collective-permute-done.1.refs_1_
  14.2 2.0 %collective-permute-start.6 = (bf16[8,3584]{1,0:T(8,128)(2,1)S(1)}, bf16[8,3584]{1,0:T(8,128)(2,1)S(1)}, u32[]{:S(2)}, u32[]{:S(2)}) collective-permute-start(bf16[8,3584]{1,0:T(8,128)(2,1)S(1)} %get-tuple-element.41), channel_id=1, source_target_pairs={{0,14},{1,15},{2,12},{3,13},{4,10},{5,11},{6,8},{7,9},{8,6},{9,7},... | collective-permute-start | bytes 172040 | tf_op jit(solution)/shard_map/ppermute | solution.py:157
  16.2 2.0 %stage.2.up_ref = bf16[3584,512]{1,0:T(8,128)(2,1)S(1)} custom-call(bf16[3584,512]{1,0:T(8,128)(2,1)} %bitcast.5), custom_call_target="tpu_custom_call" | custom-call | bytes 7340032 | tf_op jit(solution)/shard_map/stage/pallas_call | solution.py:171
  18.2 0.0 collective-permute-done.2.refs_2_
  18.2 0.0 collective-permute-done.4.refs_4_
  18.2 0.0 collective-permute-done.5.refs_5_
  18.3 2.8 %collective-permute-done.6.refs_6_ = bf16[8,3584]{1,0:T(8,128)(2,1)S(1)} collective-permute-done((bf16[8,3584]{1,0:T(8,128)(2,1)S(1)}, bf16[8,3584]{1,0:T(8,128)(2,1)S(1)}, u32[]{:S(2)}, u32[]{:S(2)}) %collective-permute-start.6) | collective-permute-done | bytes 57376 | tf_op jit(solution)/shard_map/ppermute | solution.py:157
  21.1 0.1 collective-permute-start.7
  21.2 2.0 %stage.3.down_ref = bf16[512,3584]{1,0:T(8,128)(2,1)S(1)} custom-call(bf16[512,3584]{1,0:T(8,128)(2,1)} %bitcast.6), custom_call_target="tpu_custom_call" | custom-call | bytes 7340032 | tf_op jit(solution)/shard_map/stage/pallas_call | solution.py:171
  23.2 1.7 %experts.1 = (bf16[64,3584]{1,0:T(8,128)(2,1)S(1)}, bf16[64,3584]{1,0:T(8,128)(2,1)S(1)}) custom-call(bf16[64,3584]{1,0:T(8,128)(2,1)S(1)} %gather.1.own_ref, bf16[64,3584]{1,0:T(8,128)(2,1)S(1)} %collective-permute-done.7.other_ref, bf16[3584,512]{1,0:T(8,128)(2,1)S(1)} %get-tuple-element.51.gate_ref, bf16[3584,512]{1,0:T(8,128)(2,1)S(1)} %stage.2.up_ref, ...), custom_call_target="tpu_custom_call" | custom-call | flops 1409286144 | bytes 11010048 | tf_op jit(solution)/shard_map/experts/pallas_call | solution.py:215
  25.0 0.6 %collective-permute-start.8 = (bf16[64,3584]{1,0:T(8,128)(2,1)S(1)}, bf16[64,3584]{1,0:T(8,128)(2,1)S(1)}, u32[]{:S(2)}, u32[]{:S(2)}) collective-permute-start(bf16[64,3584]{1,0:T(8,128)(2,1)S(1)} %get-tuple-element.54), channel_id=1, source_target_pairs={{0,1},{1,0},{2,3},{3,2},{4,5},{5,4},{6,7},{7,6},{8,9},{9,8},{10,11... | collective-permute-start | bytes 1376264 | tf_op jit(solution)/shard_map/ppermute | solution.py:168
  25.5 1.4 %collective-permute-done.8.got_ref = bf16[64,3584]{1,0:T(8,128)(2,1)S(1)} collective-permute-done((bf16[64,3584]{1,0:T(8,128)(2,1)S(1)}, bf16[64,3584]{1,0:T(8,128)(2,1)S(1)}, u32[]{:S(2)}, u32[]{:S(2)}) %collective-permute-start.8) | collective-permute-done | bytes 458784 | tf_op jit(solution)/shard_map/ppermute | solution.py:168
  26.9 0.1 join.1
  27.1 0.9 %collective-permute-start.9 = (bf16[8,3584]{1,0:T(8,128)(2,1)S(1)}, bf16[8,3584]{1,0:T(8,128)(2,1)S(1)}, u32[]{:S(2)}, u32[]{:S(2)}) collective-permute-start(bf16[8,3584]{1,0:T(8,128)(2,1)S(1)} %get-tuple-element.55), channel_id=1, source_target_pairs={{0,8},{1,9},{2,10},{3,11},{4,12},{5,13},{6,14},{7,15},{8,0},{9,1},... | collective-permute-start | bytes 172040 | tf_op jit(solution)/shard_map/ppermute | solution.py:157
  27.9 1.1 %collective-permute-start.10 = (bf16[8,3584]{1,0:T(8,128)(2,1)S(1)}, bf16[8,3584]{1,0:T(8,128)(2,1)S(1)}, u32[]{:S(2)}, u32[]{:S(2)}) collective-permute-start(bf16[8,3584]{1,0:T(8,128)(2,1)S(1)} %get-tuple-element.56), channel_id=1, source_target_pairs={{0,2},{1,3},{2,0},{3,1},{4,6},{5,7},{6,4},{7,5},{8,10},{9,11},{10,... | collective-permute-start | bytes 172040 | tf_op jit(solution)/shard_map/ppermute | solution.py:157
  29.1 2.5 %collective-permute-start.11 = (bf16[8,3584]{1,0:T(8,128)(2,1)S(1)}, bf16[8,3584]{1,0:T(8,128)(2,1)S(1)}, u32[]{:S(2)}, u32[]{:S(2)}) collective-permute-start(bf16[8,3584]{1,0:T(8,128)(2,1)S(1)} %get-tuple-element.57), channel_id=1, source_target_pairs={{0,10},{1,11},{2,8},{3,9},{4,14},{5,15},{6,12},{7,13},{8,2},{9,3},... | collective-permute-start | bytes 172040 | tf_op jit(solution)/shard_map/ppermute | solution.py:157
  31.5 2.3 %collective-permute-start.13 = (bf16[8,3584]{1,0:T(8,128)(2,1)S(1)}, bf16[8,3584]{1,0:T(8,128)(2,1)S(1)}, u32[]{:S(2)}, u32[]{:S(2)}) collective-permute-start(bf16[8,3584]{1,0:T(8,128)(2,1)S(1)} %get-tuple-element.59), channel_id=1, source_target_pairs={{0,12},{1,13},{2,14},{3,15},{4,8},{5,9},{6,10},{7,11},{8,4},{9,5},... | collective-permute-start | bytes 172040 | tf_op jit(solution)/shard_map/ppermute | solution.py:157
  33.8 1.0 %collective-permute-start.14 = (bf16[8,3584]{1,0:T(8,128)(2,1)S(1)}, bf16[8,3584]{1,0:T(8,128)(2,1)S(1)}, u32[]{:S(2)}, u32[]{:S(2)}) collective-permute-start(bf16[8,3584]{1,0:T(8,128)(2,1)S(1)} %get-tuple-element.60), channel_id=1, source_target_pairs={{0,6},{1,7},{2,4},{3,5},{4,2},{5,3},{6,0},{7,1},{8,14},{9,15},{10,... | collective-permute-start | bytes 172040 | tf_op jit(solution)/shard_map/ppermute | solution.py:157
  34.8 0.0 collective-permute-done.10.refs_1_
  34.8 2.6 %collective-permute-start.15 = (bf16[8,3584]{1,0:T(8,128)(2,1)S(1)}, bf16[8,3584]{1,0:T(8,128)(2,1)S(1)}, u32[]{:S(2)}, u32[]{:S(2)}) collective-permute-start(bf16[8,3584]{1,0:T(8,128)(2,1)S(1)} %get-tuple-element.61), channel_id=1, source_target_pairs={{0,14},{1,15},{2,12},{3,13},{4,10},{5,11},{6,8},{7,9},{8,6},{9,7},... | collective-permute-start | bytes 172040 | tf_op jit(solution)/shard_map/ppermute | solution.py:157
  37.4 0.4 collective-permute-done.13.refs_4_
  37.8 1.7 %collective-permute-done.14.refs_5_ = bf16[8,3584]{1,0:T(8,128)(2,1)S(1)} collective-permute-done((bf16[8,3584]{1,0:T(8,128)(2,1)S(1)}, bf16[8,3584]{1,0:T(8,128)(2,1)S(1)}, u32[]{:S(2)}, u32[]{:S(2)}) %collective-permute-start.14) | collective-permute-done | bytes 57376 | tf_op jit(solution)/shard_map/ppermute | solution.py:157
  39.4 2.2 %collective-permute-done.15.refs_6_ = bf16[8,3584]{1,0:T(8,128)(2,1)S(1)} collective-permute-done((bf16[8,3584]{1,0:T(8,128)(2,1)S(1)}, bf16[8,3584]{1,0:T(8,128)(2,1)S(1)}, u32[]{:S(2)}, u32[]{:S(2)}) %collective-permute-start.15) | collective-permute-done | bytes 57376 | tf_op jit(solution)/shard_map/ppermute | solution.py:157
  41.6 1.3 %combine.1 = bf16[128,3584]{1,0:T(8,128)(2,1)} custom-call(bf16[128,128]{1,0:T(8,128)(2,1)S(1)} %get-tuple-element.34.mix_ref, bf16[8,3584]{1,0:T(8,128)(2,1)S(1)} %collective-permute-done.9.refs_0_, bf16[8,3584]{1,0:T(8,128)(2,1)S(1)} %collective-permute-done.10.refs_1_, bf16[8,3584]{1,0:T(8,128)(2,1)S(1)} %collective-permute-done.11.refs_2_, ...), custom_call_target="tpu_custom_call" | custom-call | tf_op jit(solution)/shard_map/combine/pallas_call | solution.py:237
  (7 shorter events, 0.0 us)
Async XLA Ops:
  2.6 10.0 %collective-permute-start = (bf16[8,3584]{1,0:T(8,128)(2,1)S(1)}, bf16[8,3584]{1,0:T(8,128)(2,1)S(1)}, u32[]{:S(2)}, u32[]{:S(2)}) collective-permute-start(bf16[8,3584]{1,0:T(8,128)(2,1)S(1)} %get-tuple-element.35), channel_id=1, source_target_pairs={{0,8},{1,9},{2,10},{3,11},{4,12},{5,13},{6,14},{7,15},{8,0},{9,1},... | collective-permute-start | bytes 172040 | tf_op jit(solution)/shard_map/ppermute | solution.py:157
  6.7 7.5 %collective-permute-start.1 = (bf16[8,3584]{1,0:T(8,128)(2,1)S(1)}, bf16[8,3584]{1,0:T(8,128)(2,1)S(1)}, u32[]{:S(2)}, u32[]{:S(2)}) collective-permute-start(bf16[8,3584]{1,0:T(8,128)(2,1)S(1)} %get-tuple-element.36), channel_id=1, source_target_pairs={{0,2},{1,3},{2,0},{3,1},{4,6},{5,7},{6,4},{7,5},{8,10},{9,11},{10,... | collective-permute-start | bytes 172040 | tf_op jit(solution)/shard_map/ppermute | solution.py:157
  8.2 10.0 %collective-permute-start.2 = (bf16[8,3584]{1,0:T(8,128)(2,1)S(1)}, bf16[8,3584]{1,0:T(8,128)(2,1)S(1)}, u32[]{:S(2)}, u32[]{:S(2)}) collective-permute-start(bf16[8,3584]{1,0:T(8,128)(2,1)S(1)} %get-tuple-element.37), channel_id=1, source_target_pairs={{0,10},{1,11},{2,8},{3,9},{4,14},{5,15},{6,12},{7,13},{8,2},{9,3},... | collective-permute-start | bytes 172040 | tf_op jit(solution)/shard_map/ppermute | solution.py:157
  8.2 10.0 %collective-permute-start.3 = (bf16[8,3584]{1,0:T(8,128)(2,1)S(1)}, bf16[8,3584]{1,0:T(8,128)(2,1)S(1)}, u32[]{:S(2)}, u32[]{:S(2)}) collective-permute-start(bf16[8,3584]{1,0:T(8,128)(2,1)S(1)} %get-tuple-element.38), channel_id=1, source_target_pairs={{0,4},{1,5},{2,6},{3,7},{4,0},{5,1},{6,2},{7,3},{8,12},{9,13},{10,... | collective-permute-start | bytes 172040 | tf_op jit(solution)/shard_map/ppermute | solution.py:157
  10.1 8.2 %collective-permute-start.4 = (bf16[8,3584]{1,0:T(8,128)(2,1)S(1)}, bf16[8,3584]{1,0:T(8,128)(2,1)S(1)}, u32[]{:S(2)}, u32[]{:S(2)}) collective-permute-start(bf16[8,3584]{1,0:T(8,128)(2,1)S(1)} %get-tuple-element.39), channel_id=1, source_target_pairs={{0,12},{1,13},{2,14},{3,15},{4,8},{5,9},{6,10},{7,11},{8,4},{9,5},... | collective-permute-start | bytes 172040 | tf_op jit(solution)/shard_map/ppermute | solution.py:157
  12.5 5.7 %collective-permute-start.5 = (bf16[8,3584]{1,0:T(8,128)(2,1)S(1)}, bf16[8,3584]{1,0:T(8,128)(2,1)S(1)}, u32[]{:S(2)}, u32[]{:S(2)}) collective-permute-start(bf16[8,3584]{1,0:T(8,128)(2,1)S(1)} %get-tuple-element.40), channel_id=1, source_target_pairs={{0,6},{1,7},{2,4},{3,5},{4,2},{5,3},{6,0},{7,1},{8,14},{9,15},{10,... | collective-permute-start | bytes 172040 | tf_op jit(solution)/shard_map/ppermute | solution.py:157
  14.2 6.9 %collective-permute-start.6 = (bf16[8,3584]{1,0:T(8,128)(2,1)S(1)}, bf16[8,3584]{1,0:T(8,128)(2,1)S(1)}, u32[]{:S(2)}, u32[]{:S(2)}) collective-permute-start(bf16[8,3584]{1,0:T(8,128)(2,1)S(1)} %get-tuple-element.41), channel_id=1, source_target_pairs={{0,14},{1,15},{2,12},{3,13},{4,10},{5,11},{6,8},{7,9},{8,6},{9,7},... | collective-permute-start | bytes 172040 | tf_op jit(solution)/shard_map/ppermute | solution.py:157
  21.1 2.1 %collective-permute-start.7 = (bf16[64,3584]{1,0:T(8,128)(2,1)S(1)}, bf16[64,3584]{1,0:T(8,128)(2,1)S(1)}, u32[]{:S(2)}, u32[]{:S(2)}) collective-permute-start(bf16[64,3584]{1,0:T(8,128)(2,1)S(1)} %gather.1.own_ref), channel_id=1, source_target_pairs={{0,1},{1,0},{2,3},{3,2},{4,5},{5,4},{6,7},{7,6},{8,9},{9,8},{10,11... | collective-permute-start | bytes 1376264 | tf_op jit(solution)/shard_map/ppermute | solution.py:168
  25.0 2.0 %collective-permute-start.8 = (bf16[64,3584]{1,0:T(8,128)(2,1)S(1)}, bf16[64,3584]{1,0:T(8,128)(2,1)S(1)}, u32[]{:S(2)}, u32[]{:S(2)}) collective-permute-start(bf16[64,3584]{1,0:T(8,128)(2,1)S(1)} %get-tuple-element.54), channel_id=1, source_target_pairs={{0,1},{1,0},{2,3},{3,2},{4,5},{5,4},{6,7},{7,6},{8,9},{9,8},{10,11... | collective-permute-start | bytes 1376264 | tf_op jit(solution)/shard_map/ppermute | solution.py:168
  27.1 6.7 %collective-permute-start.9 = (bf16[8,3584]{1,0:T(8,128)(2,1)S(1)}, bf16[8,3584]{1,0:T(8,128)(2,1)S(1)}, u32[]{:S(2)}, u32[]{:S(2)}) collective-permute-start(bf16[8,3584]{1,0:T(8,128)(2,1)S(1)} %get-tuple-element.55), channel_id=1, source_target_pairs={{0,8},{1,9},{2,10},{3,11},{4,12},{5,13},{6,14},{7,15},{8,0},{9,1},... | collective-permute-start | bytes 172040 | tf_op jit(solution)/shard_map/ppermute | solution.py:157
  27.9 6.8 %collective-permute-start.10 = (bf16[8,3584]{1,0:T(8,128)(2,1)S(1)}, bf16[8,3584]{1,0:T(8,128)(2,1)S(1)}, u32[]{:S(2)}, u32[]{:S(2)}) collective-permute-start(bf16[8,3584]{1,0:T(8,128)(2,1)S(1)} %get-tuple-element.56), channel_id=1, source_target_pairs={{0,2},{1,3},{2,0},{3,1},{4,6},{5,7},{6,4},{7,5},{8,10},{9,11},{10,... | collective-permute-start | bytes 172040 | tf_op jit(solution)/shard_map/ppermute | solution.py:157
  29.1 8.3 %collective-permute-start.11 = (bf16[8,3584]{1,0:T(8,128)(2,1)S(1)}, bf16[8,3584]{1,0:T(8,128)(2,1)S(1)}, u32[]{:S(2)}, u32[]{:S(2)}) collective-permute-start(bf16[8,3584]{1,0:T(8,128)(2,1)S(1)} %get-tuple-element.57), channel_id=1, source_target_pairs={{0,10},{1,11},{2,8},{3,9},{4,14},{5,15},{6,12},{7,13},{8,2},{9,3},... | collective-permute-start | bytes 172040 | tf_op jit(solution)/shard_map/ppermute | solution.py:157
  31.5 5.9 %collective-permute-start.12 = (bf16[8,3584]{1,0:T(8,128)(2,1)S(1)}, bf16[8,3584]{1,0:T(8,128)(2,1)S(1)}, u32[]{:S(2)}, u32[]{:S(2)}) collective-permute-start(bf16[8,3584]{1,0:T(8,128)(2,1)S(1)} %get-tuple-element.58), channel_id=1, source_target_pairs={{0,4},{1,5},{2,6},{3,7},{4,0},{5,1},{6,2},{7,3},{8,12},{9,13},{10,... | collective-permute-start | bytes 172040 | tf_op jit(solution)/shard_map/ppermute | solution.py:157
  31.5 6.3 %collective-permute-start.13 = (bf16[8,3584]{1,0:T(8,128)(2,1)S(1)}, bf16[8,3584]{1,0:T(8,128)(2,1)S(1)}, u32[]{:S(2)}, u32[]{:S(2)}) collective-permute-start(bf16[8,3584]{1,0:T(8,128)(2,1)S(1)} %get-tuple-element.59), channel_id=1, source_target_pairs={{0,12},{1,13},{2,14},{3,15},{4,8},{5,9},{6,10},{7,11},{8,4},{9,5},... | collective-permute-start | bytes 172040 | tf_op jit(solution)/shard_map/ppermute | solution.py:157
  33.8 5.6 %collective-permute-start.14 = (bf16[8,3584]{1,0:T(8,128)(2,1)S(1)}, bf16[8,3584]{1,0:T(8,128)(2,1)S(1)}, u32[]{:S(2)}, u32[]{:S(2)}) collective-permute-start(bf16[8,3584]{1,0:T(8,128)(2,1)S(1)} %get-tuple-element.60), channel_id=1, source_target_pairs={{0,6},{1,7},{2,4},{3,5},{4,2},{5,3},{6,0},{7,1},{8,14},{9,15},{10,... | collective-permute-start | bytes 172040 | tf_op jit(solution)/shard_map/ppermute | solution.py:157
  34.8 6.9 %collective-permute-start.15 = (bf16[8,3584]{1,0:T(8,128)(2,1)S(1)}, bf16[8,3584]{1,0:T(8,128)(2,1)S(1)}, u32[]{:S(2)}, u32[]{:S(2)}) collective-permute-start(bf16[8,3584]{1,0:T(8,128)(2,1)S(1)} %get-tuple-element.61), channel_id=1, source_target_pairs={{0,14},{1,15},{2,12},{3,13},{4,10},{5,11},{6,8},{7,9},{8,6},{9,7},... | collective-permute-start | bytes 172040 | tf_op jit(solution)/shard_map/ppermute | solution.py:157

commit v8 on v7

--- a/solution.py
+++ b/solution.py
@@ -23,11 +23,13 @@
     return flight <= 8
 
 
-def block_order(flight):
-    far = range(flight // 2, flight)
-    near = range(1, flight // 2)
-    mixed = [r for pair in zip(far, near) for r in pair]
-    return mixed + [flight - 1, 0]
+def block_order(flight, core):
+    if not relative(flight):
+        return list(range(flight))
+    far = list(range(flight // 2, flight))
+    near = list(range(1, flight // 2))
+    turns = zip(far, near) if core == 0 else zip(near, far)
+    return [r for pair in turns for r in pair] + [flight - 1, 0]
 
 
 def dispatch_kernel(
@@ -53,11 +55,12 @@
         copy.start()
     small[0].wait()
     small[1].wait()
-    chip = lax.axis_index("exp") // 2 if relative(flight) else 0
-    where = lax.broadcasted_iota(jnp.int32, (flight, count), 0)
-    experts = jnp.zeros((flight, count), jnp.int32)
-    for i, r in enumerate(block_order(flight)):
-        experts = jnp.where(where == i, r ^ chip, experts)
+    experts = lax.broadcasted_iota(jnp.int32, (flight, count), 0)
+    if relative(flight):
+        place = experts
+        me = lax.axis_index("exp")
+        for i, (even, odd) in enumerate(zip(block_order(flight, 0), block_order(flight, 1))):
+            experts = jnp.where(place == i, jnp.where(me % 2 == 0, even, odd) ^ (me // 2), experts)
     chosen = jnp.zeros((flight, count), jnp.float32)
     gates = jnp.zeros((flight, count), jnp.float32)
     for k in range(ids.shape[0]):
@@ -146,23 +149,25 @@
     count, width = tokens.shape
     hidden = w_gate.shape[2]
     packed = flight * SLOTS
-    order = block_order(flight)
     block = jax.ShapeDtypeStruct((SLOTS, width), jnp.bfloat16)
     whole = jax.ShapeDtypeStruct((packed, width), jnp.bfloat16)
     few = relative(flight)
 
     def exchange(blocks):
         if few:
-            return [
-                lax.ppermute(b, "exp", [(i, i ^ (2 * r)) for i in range(owners)]) if r else b
-                for b, r in zip(blocks, order)
+            orders = block_order(flight, 0), block_order(flight, 1)
+            got = [
+                lax.ppermute(
+                    blocks[i], "exp", [(n, n ^ (2 * orders[n % 2][i])) for n in range(owners)]
+                )
+                for i in range(flight - 1)
             ]
+            return got + [blocks[-1]]
         groups = [list(range(core, owners, 2)) for core in range(2)]
-        stacked = jnp.stack([blocks[order.index(r)] for r in range(flight)])
         got = lax.all_to_all(
-            stacked, "exp", split_axis=0, concat_axis=0, axis_index_groups=groups, tiled=True
-        )
-        return [got[r] for r in order]
+            jnp.stack(blocks), "exp", split_axis=0, concat_axis=0, axis_index_groups=groups, tiled=True
+        )
+        return [got[i] for i in range(flight)]
 
     def swap(rows):
         return lax.ppermute(rows, "exp", [(i, i ^ 1) for i in range(owners)])

time: 43.2 us -> 43.1 us (level)
  no operation moved by 1% of the time
where the time goes in v8:
time: 43.1 us; the launch traced here: 42.9 us
  starting transfers between devices  24.4 us (57%)
  Pallas kernels  9.86 us (23%)
  waiting for transfers between devices  8.53 us (20%)
    ppermute x14, starting transfers between devices, exchange(): lax.ppermute(blocks[i], 'exp', [(n, n ^ 2 * orders[n % 2][i]) for n in ra...  23.8 us
    ppermute x14, waiting for transfers between devices, exchange(): lax.ppermute(blocks[i], 'exp', [(n, n ^ 2 * orders[n % 2][i]) for n in ra...  7.08 us
    pallas_call x2, Pallas kernels, stage(): pl.pallas_call(stage_kernel, out_shape=jax.ShapeDtypeStruct(weights.shape...  4.09 us
    pallas_call x1, Pallas kernels, per_device(): pl.pallas_call(functools.partial(dispatch_kernel, flight), out_shape=(jax...  2.57 us
    pallas_call x1, Pallas kernels, per_device(): pl.pallas_call(expert_kernel, out_shape=(whole, whole), in_specs=[VMEM] *...  1.72 us
    ppermute x2, waiting for transfers between devices, swap(): return lax.ppermute(rows, 'exp', [(i, i ^ 1) for i in range(owners)])  1.45 us
    pallas_call x1, Pallas kernels, per_device(): pl.pallas_call(functools.partial(combine_kernel, flight), out_shape=jax.S...  1.35 us
  transfers between devices with their start and end apart: 16, of which 5 were waited for; matrix products, arithmetic and copies ran while one was open for 0% of the time, Pallas kernels for 10%

profile of v8, /device:TPU:0, one launch (start us, length us, event | category | flops | bytes accessed | tf_op | source)
XLA Modules:
  0.0 42.9 jit_solution(1785758135306744407)
XLA Ops:
  0.0 2.6 %dispatch.1 = (bf16[128,128]{1,0:T(8,128)(2,1)S(1)}, bf16[3584,512]{1,0:T(8,128)(2,1)S(1)}, bf16[8,3584]{1,0:T(8,128)(2,1)S(1)}, bf16[8,3584]{1,0:T(8,128)(2,1)S...) custom-call(bf16[128,3584]{1,0:T(8,128)(2,1)} %tok_hbm.1, ...), custom_call_target="tpu_custom_call" | custom-call | tf_op jit(solution)/shard_map/dispatch/pallas_call | solution.py:189
  2.6 4.1 %collective-permute-start = (bf16[8,3584]{1,0:T(8,128)(2,1)S(1)}, bf16[8,3584]{1,0:T(8,128)(2,1)S(1)}, u32[]{:S(2)}, u32[]{:S(2)}) collective-permute-start(bf16[8,3584]{1,0:T(8,128)(2,1)S(1)} %get-tuple-element.35), channel_id=1, source_target_pairs={{0,8},{1,3},{2,10},{3,1},{4,12},{5,7},{6,14},{7,5},{8,0},{9,11},{1... | collective-permute-start | bytes 172040 | tf_op jit(solution)/shard_map/ppermute | solution.py:160
  6.7 1.5 %collective-permute-start.1 = (bf16[8,3584]{1,0:T(8,128)(2,1)S(1)}, bf16[8,3584]{1,0:T(8,128)(2,1)S(1)}, u32[]{:S(2)}, u32[]{:S(2)}) collective-permute-start(bf16[8,3584]{1,0:T(8,128)(2,1)S(1)} %get-tuple-element.36), channel_id=1, source_target_pairs={{0,2},{1,9},{2,0},{3,11},{4,6},{5,13},{6,4},{7,15},{8,10},{9,1},{1... | collective-permute-start | bytes 172040 | tf_op jit(solution)/shard_map/ppermute | solution.py:160
  8.2 0.0 collective-permute-start.2
  8.2 1.8 %collective-permute-start.3 = (bf16[8,3584]{1,0:T(8,128)(2,1)S(1)}, bf16[8,3584]{1,0:T(8,128)(2,1)S(1)}, u32[]{:S(2)}, u32[]{:S(2)}) collective-permute-start(bf16[8,3584]{1,0:T(8,128)(2,1)S(1)} %get-tuple-element.38), channel_id=1, source_target_pairs={{0,4},{1,11},{2,6},{3,9},{4,0},{5,15},{6,2},{7,13},{8,12},{9,3},{1... | collective-permute-start | bytes 172040 | tf_op jit(solution)/shard_map/ppermute | solution.py:160
  10.1 2.5 %collective-permute-start.4 = (bf16[8,3584]{1,0:T(8,128)(2,1)S(1)}, bf16[8,3584]{1,0:T(8,128)(2,1)S(1)}, u32[]{:S(2)}, u32[]{:S(2)}) collective-permute-start(bf16[8,3584]{1,0:T(8,128)(2,1)S(1)} %get-tuple-element.39), channel_id=1, source_target_pairs={{0,12},{1,7},{2,14},{3,5},{4,8},{5,3},{6,10},{7,1},{8,4},{9,15},{1... | collective-permute-start | bytes 172040 | tf_op jit(solution)/shard_map/ppermute | solution.py:160
  12.5 0.0 collective-permute-done.refs_0_
  12.5 1.6 %collective-permute-start.5 = (bf16[8,3584]{1,0:T(8,128)(2,1)S(1)}, bf16[8,3584]{1,0:T(8,128)(2,1)S(1)}, u32[]{:S(2)}, u32[]{:S(2)}) collective-permute-start(bf16[8,3584]{1,0:T(8,128)(2,1)S(1)} %get-tuple-element.40), channel_id=1, source_target_pairs={{0,6},{1,13},{2,4},{3,15},{4,2},{5,9},{6,0},{7,11},{8,14},{9,5},{1... | collective-permute-start | bytes 172040 | tf_op jit(solution)/shard_map/ppermute | solution.py:160
  14.2 0.0 collective-permute-done.1.refs_1_
  14.2 1.9 %collective-permute-start.6 = (bf16[8,3584]{1,0:T(8,128)(2,1)S(1)}, bf16[8,3584]{1,0:T(8,128)(2,1)S(1)}, u32[]{:S(2)}, u32[]{:S(2)}) collective-permute-start(bf16[8,3584]{1,0:T(8,128)(2,1)S(1)} %get-tuple-element.41), channel_id=1, source_target_pairs={{0,14},{1,15},{2,12},{3,13},{4,10},{5,11},{6,8},{7,9},{8,6},{9,7},... | collective-permute-start | bytes 172040 | tf_op jit(solution)/shard_map/ppermute | solution.py:160
  16.1 2.0 %stage.2.up_ref = bf16[3584,512]{1,0:T(8,128)(2,1)S(1)} custom-call(bf16[3584,512]{1,0:T(8,128)(2,1)} %bitcast.5), custom_call_target="tpu_custom_call" | custom-call | bytes 7340032 | tf_op jit(solution)/shard_map/stage/pallas_call | solution.py:176
  18.1 0.0 collective-permute-done.2.refs_2_
  18.2 0.0 collective-permute-done.5.refs_5_
  18.2 2.9 %collective-permute-done.6.refs_6_ = bf16[8,3584]{1,0:T(8,128)(2,1)S(1)} collective-permute-done((bf16[8,3584]{1,0:T(8,128)(2,1)S(1)}, bf16[8,3584]{1,0:T(8,128)(2,1)S(1)}, u32[]{:S(2)}, u32[]{:S(2)}) %collective-permute-start.6) | collective-permute-done | bytes 57376 | tf_op jit(solution)/shard_map/ppermute | solution.py:160
  21.1 0.1 collective-permute-start.7
  21.2 2.0 %stage.3.down_ref = bf16[512,3584]{1,0:T(8,128)(2,1)S(1)} custom-call(bf16[512,3584]{1,0:T(8,128)(2,1)} %bitcast.6), custom_call_target="tpu_custom_call" | custom-call | bytes 7340032 | tf_op jit(solution)/shard_map/stage/pallas_call | solution.py:176
  23.2 0.0 collective-permute-done.7.other_ref
  23.2 1.7 %experts.1 = (bf16[64,3584]{1,0:T(8,128)(2,1)S(1)}, bf16[64,3584]{1,0:T(8,128)(2,1)S(1)}) custom-call(bf16[64,3584]{1,0:T(8,128)(2,1)S(1)} %gather.1.own_ref, bf16[64,3584]{1,0:T(8,128)(2,1)S(1)} %collective-permute-done.7.other_ref, bf16[3584,512]{1,0:T(8,128)(2,1)S(1)} %get-tuple-element.51.gate_ref, bf16[3584,512]{1,0:T(8,128)(2,1)S(1)} %stage.2.up_ref, ...), custom_call_target="tpu_custom_call" | custom-call | flops 1409286144 | bytes 11010048 | tf_op jit(solution)/shard_map/experts/pallas_call | solution.py:220
  25.0 0.6 %collective-permute-start.8 = (bf16[64,3584]{1,0:T(8,128)(2,1)S(1)}, bf16[64,3584]{1,0:T(8,128)(2,1)S(1)}, u32[]{:S(2)}, u32[]{:S(2)}) collective-permute-start(bf16[64,3584]{1,0:T(8,128)(2,1)S(1)} %get-tuple-element.54), channel_id=1, source_target_pairs={{0,1},{1,0},{2,3},{3,2},{4,5},{5,4},{6,7},{7,6},{8,9},{9,8},{10,11... | collective-permute-start | bytes 1376264 | tf_op jit(solution)/shard_map/ppermute | solution.py:173
  25.5 1.4 %collective-permute-done.8.got_ref = bf16[64,3584]{1,0:T(8,128)(2,1)S(1)} collective-permute-done((bf16[64,3584]{1,0:T(8,128)(2,1)S(1)}, bf16[64,3584]{1,0:T(8,128)(2,1)S(1)}, u32[]{:S(2)}, u32[]{:S(2)}) %collective-permute-start.8) | collective-permute-done | bytes 458784 | tf_op jit(solution)/shard_map/ppermute | solution.py:173
  26.9 0.1 join.1
  27.1 1.3 %collective-permute-start.9 = (bf16[8,3584]{1,0:T(8,128)(2,1)S(1)}, bf16[8,3584]{1,0:T(8,128)(2,1)S(1)}, u32[]{:S(2)}, u32[]{:S(2)}) collective-permute-start(bf16[8,3584]{1,0:T(8,128)(2,1)S(1)} %get-tuple-element.55), channel_id=1, source_target_pairs={{0,8},{1,3},{2,10},{3,1},{4,12},{5,7},{6,14},{7,5},{8,0},{9,11},{1... | collective-permute-start | bytes 172040 | tf_op jit(solution)/shard_map/ppermute | solution.py:160
  28.4 0.9 %collective-permute-start.10 = (bf16[8,3584]{1,0:T(8,128)(2,1)S(1)}, bf16[8,3584]{1,0:T(8,128)(2,1)S(1)}, u32[]{:S(2)}, u32[]{:S(2)}) collective-permute-start(bf16[8,3584]{1,0:T(8,128)(2,1)S(1)} %get-tuple-element.56), channel_id=1, source_target_pairs={{0,2},{1,9},{2,0},{3,11},{4,6},{5,13},{6,4},{7,15},{8,10},{9,1},{1... | collective-permute-start | bytes 172040 | tf_op jit(solution)/shard_map/ppermute | solution.py:160
  29.3 2.2 %collective-permute-start.11 = (bf16[8,3584]{1,0:T(8,128)(2,1)S(1)}, bf16[8,3584]{1,0:T(8,128)(2,1)S(1)}, u32[]{:S(2)}, u32[]{:S(2)}) collective-permute-start(bf16[8,3584]{1,0:T(8,128)(2,1)S(1)} %get-tuple-element.57), channel_id=1, source_target_pairs={{0,10},{1,5},{2,8},{3,7},{4,14},{5,1},{6,12},{7,3},{8,2},{9,13},{1... | collective-permute-start | bytes 172040 | tf_op jit(solution)/shard_map/ppermute | solution.py:160
  31.5 2.7 %collective-permute-start.13 = (bf16[8,3584]{1,0:T(8,128)(2,1)S(1)}, bf16[8,3584]{1,0:T(8,128)(2,1)S(1)}, u32[]{:S(2)}, u32[]{:S(2)}) collective-permute-start(bf16[8,3584]{1,0:T(8,128)(2,1)S(1)} %get-tuple-element.59), channel_id=1, source_target_pairs={{0,12},{1,7},{2,14},{3,5},{4,8},{5,3},{6,10},{7,1},{8,4},{9,15},{1... | collective-permute-start | bytes 172040 | tf_op jit(solution)/shard_map/ppermute | solution.py:160
  34.3 0.0 collective-permute-done.9.refs_0_
  34.3 0.3 collective-permute-start.14
  34.6 2.8 %collective-permute-start.15 = (bf16[8,3584]{1,0:T(8,128)(2,1)S(1)}, bf16[8,3584]{1,0:T(8,128)(2,1)S(1)}, u32[]{:S(2)}, u32[]{:S(2)}) collective-permute-start(bf16[8,3584]{1,0:T(8,128)(2,1)S(1)} %get-tuple-element.61), channel_id=1, source_target_pairs={{0,14},{1,15},{2,12},{3,13},{4,10},{5,11},{6,8},{7,9},{8,6},{9,7},... | collective-permute-start | bytes 172040 | tf_op jit(solution)/shard_map/ppermute | solution.py:160
  37.4 0.8 %collective-permute-done.13.refs_4_ = bf16[8,3584]{1,0:T(8,128)(2,1)S(1)} collective-permute-done((bf16[8,3584]{1,0:T(8,128)(2,1)S(1)}, bf16[8,3584]{1,0:T(8,128)(2,1)S(1)}, u32[]{:S(2)}, u32[]{:S(2)}) %collective-permute-start.13) | collective-permute-done | bytes 57376 | tf_op jit(solution)/shard_map/ppermute | solution.py:160
  38.2 1.1 %collective-permute-done.14.refs_5_ = bf16[8,3584]{1,0:T(8,128)(2,1)S(1)} collective-permute-done((bf16[8,3584]{1,0:T(8,128)(2,1)S(1)}, bf16[8,3584]{1,0:T(8,128)(2,1)S(1)}, u32[]{:S(2)}, u32[]{:S(2)}) %collective-permute-start.14) | collective-permute-done | bytes 57376 | tf_op jit(solution)/shard_map/ppermute | solution.py:160
  39.3 2.2 %collective-permute-done.15.refs_6_ = bf16[8,3584]{1,0:T(8,128)(2,1)S(1)} collective-permute-done((bf16[8,3584]{1,0:T(8,128)(2,1)S(1)}, bf16[8,3584]{1,0:T(8,128)(2,1)S(1)}, u32[]{:S(2)}, u32[]{:S(2)}) %collective-permute-start.15) | collective-permute-done | bytes 57376 | tf_op jit(solution)/shard_map/ppermute | solution.py:160
  41.6 1.3 %combine.1 = bf16[128,3584]{1,0:T(8,128)(2,1)} custom-call(bf16[128,128]{1,0:T(8,128)(2,1)S(1)} %get-tuple-element.34.mix_ref, bf16[8,3584]{1,0:T(8,128)(2,1)S(1)} %collective-permute-done.9.refs_0_, bf16[8,3584]{1,0:T(8,128)(2,1)S(1)} %collective-permute-done.10.refs_1_, bf16[8,3584]{1,0:T(8,128)(2,1)S(1)} %collective-permute-done.11.refs_2_, ...), custom_call_target="tpu_custom_call" | custom-call | tf_op jit(solution)/shard_map/combine/pallas_call | solution.py:242
  (7 shorter events, 0.0 us)
Async XLA Ops:
  2.6 10.0 %collective-permute-start = (bf16[8,3584]{1,0:T(8,128)(2,1)S(1)}, bf16[8,3584]{1,0:T(8,128)(2,1)S(1)}, u32[]{:S(2)}, u32[]{:S(2)}) collective-permute-start(bf16[8,3584]{1,0:T(8,128)(2,1)S(1)} %get-tuple-element.35), channel_id=1, source_target_pairs={{0,8},{1,3},{2,10},{3,1},{4,12},{5,7},{6,14},{7,5},{8,0},{9,11},{1... | collective-permute-start | bytes 172040 | tf_op jit(solution)/shard_map/ppermute | solution.py:160
  6.7 7.5 %collective-permute-start.1 = (bf16[8,3584]{1,0:T(8,128)(2,1)S(1)}, bf16[8,3584]{1,0:T(8,128)(2,1)S(1)}, u32[]{:S(2)}, u32[]{:S(2)}) collective-permute-start(bf16[8,3584]{1,0:T(8,128)(2,1)S(1)} %get-tuple-element.36), channel_id=1, source_target_pairs={{0,2},{1,9},{2,0},{3,11},{4,6},{5,13},{6,4},{7,15},{8,10},{9,1},{1... | collective-permute-start | bytes 172040 | tf_op jit(solution)/shard_map/ppermute | solution.py:160
  8.2 9.9 %collective-permute-start.2 = (bf16[8,3584]{1,0:T(8,128)(2,1)S(1)}, bf16[8,3584]{1,0:T(8,128)(2,1)S(1)}, u32[]{:S(2)}, u32[]{:S(2)}) collective-permute-start(bf16[8,3584]{1,0:T(8,128)(2,1)S(1)} %get-tuple-element.37), channel_id=1, source_target_pairs={{0,10},{1,5},{2,8},{3,7},{4,14},{5,1},{6,12},{7,3},{8,2},{9,13},{1... | collective-permute-start | bytes 172040 | tf_op jit(solution)/shard_map/ppermute | solution.py:160
  8.2 9.9 %collective-permute-start.3 = (bf16[8,3584]{1,0:T(8,128)(2,1)S(1)}, bf16[8,3584]{1,0:T(8,128)(2,1)S(1)}, u32[]{:S(2)}, u32[]{:S(2)}) collective-permute-start(bf16[8,3584]{1,0:T(8,128)(2,1)S(1)} %get-tuple-element.38), channel_id=1, source_target_pairs={{0,4},{1,11},{2,6},{3,9},{4,0},{5,15},{6,2},{7,13},{8,12},{9,3},{1... | collective-permute-start | bytes 172040 | tf_op jit(solution)/shard_map/ppermute | solution.py:160
  10.1 8.1 %collective-permute-start.4 = (bf16[8,3584]{1,0:T(8,128)(2,1)S(1)}, bf16[8,3584]{1,0:T(8,128)(2,1)S(1)}, u32[]{:S(2)}, u32[]{:S(2)}) collective-permute-start(bf16[8,3584]{1,0:T(8,128)(2,1)S(1)} %get-tuple-element.39), channel_id=1, source_target_pairs={{0,12},{1,7},{2,14},{3,5},{4,8},{5,3},{6,10},{7,1},{8,4},{9,15},{1... | collective-permute-start | bytes 172040 | tf_op jit(solution)/shard_map/ppermute | solution.py:160
  12.5 5.6 %collective-permute-start.5 = (bf16[8,3584]{1,0:T(8,128)(2,1)S(1)}, bf16[8,3584]{1,0:T(8,128)(2,1)S(1)}, u32[]{:S(2)}, u32[]{:S(2)}) collective-permute-start(bf16[8,3584]{1,0:T(8,128)(2,1)S(1)} %get-tuple-element.40), channel_id=1, source_target_pairs={{0,6},{1,13},{2,4},{3,15},{4,2},{5,9},{6,0},{7,11},{8,14},{9,5},{1... | collective-permute-start | bytes 172040 | tf_op jit(solution)/shard_map/ppermute | solution.py:160
  14.2 6.9 %collective-permute-start.6 = (bf16[8,3584]{1,0:T(8,128)(2,1)S(1)}, bf16[8,3584]{1,0:T(8,128)(2,1)S(1)}, u32[]{:S(2)}, u32[]{:S(2)}) collective-permute-start(bf16[8,3584]{1,0:T(8,128)(2,1)S(1)} %get-tuple-element.41), channel_id=1, source_target_pairs={{0,14},{1,15},{2,12},{3,13},{4,10},{5,11},{6,8},{7,9},{8,6},{9,7},... | collective-permute-start | bytes 172040 | tf_op jit(solution)/shard_map/ppermute | solution.py:160
  21.1 2.1 %collective-permute-start.7 = (bf16[64,3584]{1,0:T(8,128)(2,1)S(1)}, bf16[64,3584]{1,0:T(8,128)(2,1)S(1)}, u32[]{:S(2)}, u32[]{:S(2)}) collective-permute-start(bf16[64,3584]{1,0:T(8,128)(2,1)S(1)} %gather.1.own_ref), channel_id=1, source_target_pairs={{0,1},{1,0},{2,3},{3,2},{4,5},{5,4},{6,7},{7,6},{8,9},{9,8},{10,11... | collective-permute-start | bytes 1376264 | tf_op jit(solution)/shard_map/ppermute | solution.py:173
  25.0 2.0 %collective-permute-start.8 = (bf16[64,3584]{1,0:T(8,128)(2,1)S(1)}, bf16[64,3584]{1,0:T(8,128)(2,1)S(1)}, u32[]{:S(2)}, u32[]{:S(2)}) collective-permute-start(bf16[64,3584]{1,0:T(8,128)(2,1)S(1)} %get-tuple-element.54), channel_id=1, source_target_pairs={{0,1},{1,0},{2,3},{3,2},{4,5},{5,4},{6,7},{7,6},{8,9},{9,8},{10,11... | collective-permute-start | bytes 1376264 | tf_op jit(solution)/shard_map/ppermute | solution.py:173
  27.1 7.2 %collective-permute-start.9 = (bf16[8,3584]{1,0:T(8,128)(2,1)S(1)}, bf16[8,3584]{1,0:T(8,128)(2,1)S(1)}, u32[]{:S(2)}, u32[]{:S(2)}) collective-permute-start(bf16[8,3584]{1,0:T(8,128)(2,1)S(1)} %get-tuple-element.55), channel_id=1, source_target_pairs={{0,8},{1,3},{2,10},{3,1},{4,12},{5,7},{6,14},{7,5},{8,0},{9,11},{1... | collective-permute-start | bytes 172040 | tf_op jit(solution)/shard_map/ppermute | solution.py:160
  28.4 6.2 %collective-permute-start.10 = (bf16[8,3584]{1,0:T(8,128)(2,1)S(1)}, bf16[8,3584]{1,0:T(8,128)(2,1)S(1)}, u32[]{:S(2)}, u32[]{:S(2)}) collective-permute-start(bf16[8,3584]{1,0:T(8,128)(2,1)S(1)} %get-tuple-element.56), channel_id=1, source_target_pairs={{0,2},{1,9},{2,0},{3,11},{4,6},{5,13},{6,4},{7,15},{8,10},{9,1},{1... | collective-permute-start | bytes 172040 | tf_op jit(solution)/shard_map/ppermute | solution.py:160
  29.3 8.1 %collective-permute-start.11 = (bf16[8,3584]{1,0:T(8,128)(2,1)S(1)}, bf16[8,3584]{1,0:T(8,128)(2,1)S(1)}, u32[]{:S(2)}, u32[]{:S(2)}) collective-permute-start(bf16[8,3584]{1,0:T(8,128)(2,1)S(1)} %get-tuple-element.57), channel_id=1, source_target_pairs={{0,10},{1,5},{2,8},{3,7},{4,14},{5,1},{6,12},{7,3},{8,2},{9,13},{1... | collective-permute-start | bytes 172040 | tf_op jit(solution)/shard_map/ppermute | solution.py:160
  31.5 5.9 %collective-permute-start.12 = (bf16[8,3584]{1,0:T(8,128)(2,1)S(1)}, bf16[8,3584]{1,0:T(8,128)(2,1)S(1)}, u32[]{:S(2)}, u32[]{:S(2)}) collective-permute-start(bf16[8,3584]{1,0:T(8,128)(2,1)S(1)} %get-tuple-element.58), channel_id=1, source_target_pairs={{0,4},{1,11},{2,6},{3,9},{4,0},{5,15},{6,2},{7,13},{8,12},{9,3},{1... | collective-permute-start | bytes 172040 | tf_op jit(solution)/shard_map/ppermute | solution.py:160
  31.5 6.7 %collective-permute-start.13 = (bf16[8,3584]{1,0:T(8,128)(2,1)S(1)}, bf16[8,3584]{1,0:T(8,128)(2,1)S(1)}, u32[]{:S(2)}, u32[]{:S(2)}) collective-permute-start(bf16[8,3584]{1,0:T(8,128)(2,1)S(1)} %get-tuple-element.59), channel_id=1, source_target_pairs={{0,12},{1,7},{2,14},{3,5},{4,8},{5,3},{6,10},{7,1},{8,4},{9,15},{1... | collective-permute-start | bytes 172040 | tf_op jit(solution)/shard_map/ppermute | solution.py:160
  34.3 5.1 %collective-permute-start.14 = (bf16[8,3584]{1,0:T(8,128)(2,1)S(1)}, bf16[8,3584]{1,0:T(8,128)(2,1)S(1)}, u32[]{:S(2)}, u32[]{:S(2)}) collective-permute-start(bf16[8,3584]{1,0:T(8,128)(2,1)S(1)} %get-tuple-element.60), channel_id=1, source_target_pairs={{0,6},{1,13},{2,4},{3,15},{4,2},{5,9},{6,0},{7,11},{8,14},{9,5},{1... | collective-permute-start | bytes 172040 | tf_op jit(solution)/shard_map/ppermute | solution.py:160
  34.6 7.0 %collective-permute-start.15 = (bf16[8,3584]{1,0:T(8,128)(2,1)S(1)}, bf16[8,3584]{1,0:T(8,128)(2,1)S(1)}, u32[]{:S(2)}, u32[]{:S(2)}) collective-permute-start(bf16[8,3584]{1,0:T(8,128)(2,1)S(1)} %get-tuple-element.61), channel_id=1, source_target_pairs={{0,14},{1,15},{2,12},{3,13},{4,10},{5,11},{6,8},{7,9},{8,6},{9,7},... | collective-permute-start | bytes 172040 | tf_op jit(solution)/shard_map/ppermute | solution.py:160

commit v9 on v8

--- a/solution.py
+++ b/solution.py
@@ -10,6 +10,7 @@
 SLOTS = 8
 CHUNKS = 4
 PIECES = 4
+LANES = 128
 
 VMEM = pl.BlockSpec(memory_space=pltpu.VMEM)
 HBM = pl.BlockSpec(memory_space=pltpu.HBM)
@@ -20,23 +21,62 @@
 
 
 def relative(flight):
-    return flight <= 8
+    return 4 <= flight <= 8
 
 
 def block_order(flight, core):
     if not relative(flight):
         return list(range(flight))
     far = list(range(flight // 2, flight))
-    near = list(range(1, flight // 2))
-    turns = zip(far, near) if core == 0 else zip(near, far)
-    return [r for pair in turns for r in pair] + [flight - 1, 0]
+    cut = len(far) // 2
+    carried, given = (far[:cut], far[cut:]) if core == 0 else (far[cut:], far[:cut])
+    return carried + given + list(range(1, flight // 2)) + [0]
+
+
+def packed_width(width):
+    return width // 7 * 6 + LANES
+
+
+def pack(rows):
+    blocks = rows.reshape(-1, SLOTS, rows.shape[1])
+    tail = rows.shape[1] // 7
+    main = blocks[:, :, : 6 * tail]
+    moved = jnp.concatenate([blocks[:, j : j + 1, 6 * tail :] for j in range(6)], axis=2)
+    row = lax.broadcasted_iota(jnp.int32, main.shape, 1)
+    main = jnp.where(row == SLOTS - 1, moved, main)
+    row = row[:, :, :LANES]
+    extra = jnp.zeros(row.shape, rows.dtype)
+    for k in range(tail // LANES):
+        start = 6 * tail + k * LANES
+        extra = jnp.where(row == k, blocks[:, 6:7, start : start + LANES], extra)
+    return jnp.concatenate([main, extra], axis=2).reshape(rows.shape[0], -1)
+
+
+def unpack(packed):
+    blocks = packed.reshape(-1, SLOTS, packed.shape[1])
+    tail = (packed.shape[1] - LANES) // 6
+    main = blocks[:, :, : 6 * tail]
+    last = jnp.concatenate(
+        [blocks[:, k : k + 1, 6 * tail :] for k in range(tail // LANES)], axis=2
+    )
+    row = lax.broadcasted_iota(jnp.int32, (blocks.shape[0], SLOTS, tail), 1)
+    end = jnp.where(row == 6, last, 0.0)
+    for j in range(6):
+        end = jnp.where(row == j, blocks[:, 7:8, j * tail : (j + 1) * tail], end)
+    return jnp.concatenate([main, end], axis=2).reshape(packed.shape[0], -1)
+
+
+def store(refs, rows):
+    at = 0
+    for ref in refs:
+        ref[...] = rows[at : at + ref.shape[0]].astype(ref.dtype)
+        at += ref.shape[0]
 
 
 def dispatch_kernel(
     flight, tok_hbm, gain_hbm, ids_hbm, gw_hbm, gate_hbm, mix_ref, gate_ref, *rest
 ):
-    outs = rest[:flight]
-    tok, gain, ids, gw, normed, sems = rest[flight:]
+    *outs, tok, gain, ids, gw, normed, sems = rest
     count = tok.shape[0]
     part = count // CHUNKS
     small = [
@@ -91,8 +131,7 @@
             wide * lax.rsqrt(mean_square + 1e-06) * gain[...]
         ).astype(jnp.bfloat16)
     rows = jnp.dot(pick, normed[...], preferred_element_type=jnp.float32)
-    for i in range(flight):
-        outs[i][...] = rows[i * SLOTS : (i + 1) * SLOTS].astype(jnp.bfloat16)
+    store(outs, pack(rows))
     weights.wait()
 
 
@@ -111,11 +150,18 @@
 
 
 def together(refs):
-    return jnp.concatenate([b[...].astype(jnp.float32) for b in refs], axis=0).astype(jnp.bfloat16)
+    return jnp.concatenate([b[...].astype(jnp.float32) for b in refs], axis=0)
+
+
+def merge_kernel(kept_ref, got_ref, *outs):
+    kept, got = kept_ref[...].astype(jnp.float32), got_ref[...].astype(jnp.float32)
+    for i, out in enumerate(outs):
+        here = slice(i * SLOTS, (i + 1) * SLOTS)
+        out[...] = jnp.concatenate([kept[here], got[here]], axis=0).astype(jnp.bfloat16)
 
 
 def gather_kernel(*refs):
-    refs[-1][...] = together(refs[:-1])
+    refs[-1][...] = unpack(together(refs[:-1])).astype(jnp.bfloat16)
 
 
 def expert_kernel(own_ref, other_ref, gate_ref, up_ref, down_ref, own_out, other_out):
@@ -130,15 +176,22 @@
 
 
 def join_kernel(mine_ref, got_ref, *outs):
-    joined = mine_ref[...].astype(jnp.float32) + got_ref[...].astype(jnp.float32)
-    for i, out in enumerate(outs):
-        out[...] = joined[i * SLOTS : (i + 1) * SLOTS].astype(jnp.bfloat16)
-
-
-def combine_kernel(flight, mix_ref, *refs):
-    rows = together(refs[:flight])
+    store(outs, pack(mine_ref[...].astype(jnp.float32) + got_ref[...].astype(jnp.float32)))
+
+
+def combine_kernel(carried, mix_ref, *refs):
+    *refs, out_ref = refs
+    blocks = []
+    for i, ref in enumerate(refs):
+        rows = ref[...].astype(jnp.float32)
+        if i < carried:
+            rows = rows[:SLOTS]
+        elif i < 2 * carried:
+            rows = rows[SLOTS:]
+        blocks.append(rows)
+    rows = unpack(jnp.concatenate(blocks, axis=0)).astype(jnp.bfloat16)
     both = jnp.concatenate([rows, rows], axis=0)
-    refs[flight][...] = lax.dot_general(
+    out_ref[...] = lax.dot_general(
         mix_ref[...], both, (((0,), (0,)), ((), ())), preferred_element_type=jnp.float32
     ).astype(jnp.bfloat16)
 
@@ -149,25 +202,33 @@
     count, width = tokens.shape
     hidden = w_gate.shape[2]
     packed = flight * SLOTS
-    block = jax.ShapeDtypeStruct((SLOTS, width), jnp.bfloat16)
     whole = jax.ShapeDtypeStruct((packed, width), jnp.bfloat16)
     few = relative(flight)
-
-    def exchange(blocks):
+    carried = flight // 4 if few else 0
+    near = flight // 2 - 1
+    routes = []
+    for core in range(2):
+        order = block_order(flight, core)
+        routes.append(order[:1] + order[2 * carried : -1] + order[1:carried])
+
+    def blocks(*counts):
+        return tuple(
+            jax.ShapeDtypeStruct((n * SLOTS, packed_width(width)), jnp.bfloat16) for n in counts
+        )
+
+    def exchange(arrays):
         if few:
-            orders = block_order(flight, 0), block_order(flight, 1)
-            got = [
-                lax.ppermute(
-                    blocks[i], "exp", [(n, n ^ (2 * orders[n % 2][i])) for n in range(owners)]
-                )
-                for i in range(flight - 1)
-            ]
-            return got + [blocks[-1]]
+            got = []
+            for i, a in enumerate(arrays[:-1]):
+                pairs = [(n, n ^ (2 * routes[n % 2][i])) for n in range(owners)]
+                got.append(lax.ppermute(a, "exp", pairs))
+            return got + [arrays[-1]]
         groups = [list(range(core, owners, 2)) for core in range(2)]
-        got = lax.all_to_all(
-            jnp.stack(blocks), "exp", split_axis=0, concat_axis=0, axis_index_groups=groups, tiled=True
-        )
-        return [got[i] for i in range(flight)]
+        return [
+            lax.all_to_all(
+                arrays[0], "exp", split_axis=0, concat_axis=0, axis_index_groups=groups, tiled=True
+            )
+        ]
 
     def swap(rows):
         return lax.ppermute(rows, "exp", [(i, i ^ 1) for i in range(owners)])
@@ -186,15 +247,17 @@
             name="stage",
         )(*in_hbm(weights))
 
+    first = blocks(carried, carried, *[1] * (near + 1)) if few else blocks(flight)
+    sent = blocks(2, *[1] * near, *[2] * (carried - 1), 1) if few else blocks(flight)
     mix, gate, *outgoing = pl.pallas_call(
         functools.partial(dispatch_kernel, flight),
         out_shape=(
             jax.ShapeDtypeStruct((2 * packed, count), jnp.bfloat16),
             jax.ShapeDtypeStruct(w_gate.shape[1:], w_gate.dtype),
         )
-        + (block,) * flight,
+        + first,
         in_specs=[HBM] * 5,
-        out_specs=(VMEM,) * (flight + 2),
+        out_specs=(VMEM,) * (len(first) + 2),
         scratch_shapes=[
             pltpu.VMEM((count, width), jnp.bfloat16),
             pltpu.VMEM((1, width), jnp.float32),
@@ -207,12 +270,24 @@
         name="dispatch",
     )(*in_hbm(tokens, norm_gain, expert_ids.T, gate_weights.T, w_gate[0]))
 
+    if few:
+        kept, given, *others = outgoing
+        merged = pl.pallas_call(
+            merge_kernel,
+            out_shape=sent[:1] * carried,
+            in_specs=[VMEM] * 2,
+            out_specs=(VMEM,) * carried,
+            compiler_params=pltpu.CompilerParams(vmem_limit_bytes=16 * 2**20),
+            name="merge",
+        )(kept, swap(given))
+        outgoing = [merged[0], *others[:-1], *merged[1:], others[-1]]
+
     up, down = stage(w_up[0]), stage(w_down[0])
     *arrived, up = lax.optimization_barrier((*exchange(outgoing), up))
     own = pl.pallas_call(
         gather_kernel,
         out_shape=whole,
-        in_specs=[VMEM] * flight,
+        in_specs=[VMEM] * len(arrived),
         out_specs=VMEM,
         compiler_params=pltpu.CompilerParams(vmem_limit_bytes=16 * 2**20),
         name="gather",
@@ -232,17 +307,21 @@
     )(own, swap(own), gate, up, down)
     joined = pl.pallas_call(
         join_kernel,
-        out_shape=(block,) * flight,
+        out_shape=sent,
         in_specs=[VMEM] * 2,
-        out_specs=(VMEM,) * flight,
+        out_specs=(VMEM,) * len(sent),
         compiler_params=pltpu.CompilerParams(vmem_limit_bytes=16 * 2**20),
         name="join",
     )(mine, swap(theirs))
     returned = exchange(joined)
+    if few:
+        pair, *close = lax.optimization_barrier(returned[: near + 1])
+        pairs = [pair, *returned[near + 1 : -1]]
+        returned = [*pairs, *[swap(a) for a in pairs], *close, returned[-1]]
     return pl.pallas_call(
-        functools.partial(combine_kernel, flight),
+        functools.partial(combine_kernel, carried),
         out_shape=jax.ShapeDtypeStruct((count, width), jnp.bfloat16),
-        in_specs=[VMEM] * (flight + 1),
+        in_specs=[VMEM] * (len(returned) + 1),
         out_specs=VMEM,
         compiler_params=pltpu.CompilerParams(vmem_limit_bytes=24 * 2**20),
         name="combine",

time: 43.1 us -> 40.7 us (0.944)
  starting transfers between devices: 24.4 us -> 16.9 us
  waiting for transfers between devices: 8.53 us -> 13.6 us
    ppermute x14 -> x10, starting transfers between devices: 23.8 us -> 15.2 us  [exchange(): got.append(lax.ppermute(a, 'exp', pairs))]
    ppermute x14 -> x10, waiting for transfers between devices: 7.08 us -> 10.2 us  [exchange(): got.append(lax.ppermute(a, 'exp', pairs))]
    ppermute x2 -> x5, waiting for transfers between devices: 1.45 us -> 3.34 us  [swap(): return lax.ppermute(rows, 'exp', [(i, i ^ 1) for i in range(owners)])]
    ppermute x2 -> x5, starting transfers between devices: 0.62 us -> 1.66 us  [swap(): return lax.ppermute(rows, 'exp', [(i, i ^ 1) for i in range(owners)])]
    pallas_call x3 -> x4, Pallas kernels: 1.49 us -> 1.67 us  [the longest x1 1.37 us: per_device(): pl.pallas_call(functools.partial(combine_kernel, carried), out_shape=jax....]
  transfers between devices with their start and end apart: 16 -> 15, of which waited for: 5 -> 10; matrix products, arithmetic and copies ran while one was open for 0% -> 0% of each run, Pallas kernels for 10% -> 10%
where the time goes in v9:
time: 40.7 us; the launch traced here: 40.6 us
  starting transfers between devices  16.9 us (42%)
  waiting for transfers between devices  13.6 us (33%)
  Pallas kernels  10 us (25%)
    ppermute x10, starting transfers between devices, exchange(): got.append(lax.ppermute(a, 'exp', pairs))  15.2 us
    ppermute x10, waiting for transfers between devices, exchange(): got.append(lax.ppermute(a, 'exp', pairs))  10.2 us
    pallas_call x2, Pallas kernels, stage(): pl.pallas_call(stage_kernel, out_shape=jax.ShapeDtypeStruct(weights.shape...  4.09 us
    ppermute x5, waiting for transfers between devices, swap(): return lax.ppermute(rows, 'exp', [(i, i ^ 1) for i in range(owners)])  3.34 us
    pallas_call x1, Pallas kernels, per_device(): pl.pallas_call(functools.partial(dispatch_kernel, flight), out_shape=(jax...  2.57 us
    pallas_call x1, Pallas kernels, per_device(): pl.pallas_call(expert_kernel, out_shape=(whole, whole), in_specs=[VMEM] *...  1.71 us
    ppermute x5, starting transfers between devices, swap(): return lax.ppermute(rows, 'exp', [(i, i ^ 1) for i in range(owners)])  1.66 us
    pallas_call x1, Pallas kernels, per_device(): pl.pallas_call(functools.partial(combine_kernel, carried), out_shape=jax....  1.37 us
  transfers between devices with their start and end apart: 15, of which 10 were waited for; matrix products, arithmetic and copies ran while one was open for 0% of the time, Pallas kernels for 10%

profile of v9, /device:TPU:0, one launch (start us, length us, event | category | flops | bytes accessed | tf_op | source)
XLA Modules:
  0.0 40.6 jit_solution(15568063032578343163)
XLA Ops:
  0.0 2.6 %dispatch.1 = (bf16[128,128]{1,0:T(8,128)(2,1)S(1)}, bf16[3584,512]{1,0:T(8,128)(2,1)S(1)}, bf16[16,3200]{1,0:T(8,128)(2,1)S(1)}, bf16[16,3200]{1,0:T(8,128)(2,1...) custom-call(bf16[128,3584]{1,0:T(8,128)(2,1)} %tok_hbm.1, ...), custom_call_target="tpu_custom_call" | custom-call | tf_op jit(solution)/shard_map/dispatch/pallas_call | solution.py:252
  2.6 0.5 %collective-permute-start = (bf16[16,3200]{1,0:T(8,128)(2,1)S(1)}, bf16[16,3200]{1,0:T(8,128)(2,1)S(1)}, u32[]{:S(2)}, u32[]{:S(2)}) collective-permute-start(bf16[16,3200]{1,0:T(8,128)(2,1)S(1)} %get-tuple-element.36), channel_id=1, source_target_pairs={{0,1},{1,0},{2,3},{3,2},{4,5},{5,4},{6,7},{7,6},{8,9},{9,8},{10,11... | collective-permute-start | bytes 307208 | tf_op jit(solution)/shard_map/ppermute | solution.py:234
  3.1 0.9 %collective-permute-done.got_ref = bf16[16,3200]{1,0:T(8,128)(2,1)S(1)} collective-permute-done((bf16[16,3200]{1,0:T(8,128)(2,1)S(1)}, bf16[16,3200]{1,0:T(8,128)(2,1)S(1)}, u32[]{:S(2)}, u32[]{:S(2)}) %collective-permute-start) | collective-permute-done | bytes 102432 | tf_op jit(solution)/shard_map/ppermute | solution.py:234
  4.1 4.0 %collective-permute-start.1 = (bf16[16,3200]{1,0:T(8,128)(2,1)S(1)}, bf16[16,3200]{1,0:T(8,128)(2,1)S(1)}, u32[]{:S(2)}, u32[]{:S(2)}) collective-permute-start(bf16[16,3200]{1,0:T(8,128)(2,1)S(1)} %get-tuple-element.37), channel_id=1, source_target_pairs={{0,8},{1,13},{2,10},{3,15},{4,12},{5,9},{6,14},{7,11},{8,0},{9,5},... | collective-permute-start | bytes 307208 | tf_op jit(solution)/shard_map/ppermute | solution.py:224
  8.1 1.3 %collective-permute-start.5 = (bf16[16,3200]{1,0:T(8,128)(2,1)S(1)}, bf16[16,3200]{1,0:T(8,128)(2,1)S(1)}, u32[]{:S(2)}, u32[]{:S(2)}) collective-permute-start(bf16[16,3200]{1,0:T(8,128)(2,1)S(1)} %get-tuple-element.41), channel_id=1, source_target_pairs={{0,10},{1,15},{2,8},{3,13},{4,14},{5,11},{6,12},{7,9},{8,2},{9,7},... | collective-permute-start | bytes 307208 | tf_op jit(solution)/shard_map/ppermute | solution.py:224
  9.4 0.2 collective-permute-start.2
  9.6 1.8 %collective-permute-start.3 = (bf16[8,3200]{1,0:T(8,128)(2,1)S(1)}, bf16[8,3200]{1,0:T(8,128)(2,1)S(1)}, u32[]{:S(2)}, u32[]{:S(2)}) collective-permute-start(bf16[8,3200]{1,0:T(8,128)(2,1)S(1)} %get-tuple-element.39), channel_id=1, source_target_pairs={{0,4},{1,5},{2,6},{3,7},{4,0},{5,1},{6,2},{7,3},{8,12},{9,13},{10,... | collective-permute-start | bytes 153608 | tf_op jit(solution)/shard_map/ppermute | solution.py:224
  11.4 1.4 %collective-permute-start.4 = (bf16[8,3200]{1,0:T(8,128)(2,1)S(1)}, bf16[8,3200]{1,0:T(8,128)(2,1)S(1)}, u32[]{:S(2)}, u32[]{:S(2)}) collective-permute-start(bf16[8,3200]{1,0:T(8,128)(2,1)S(1)} %get-tuple-element.40), channel_id=1, source_target_pairs={{0,6},{1,7},{2,4},{3,5},{4,2},{5,3},{6,0},{7,1},{8,14},{9,15},{10,... | collective-permute-start | bytes 153608 | tf_op jit(solution)/shard_map/ppermute | solution.py:224
  12.9 2.0 %stage.2.up_ref = bf16[3584,512]{1,0:T(8,128)(2,1)S(1)} custom-call(bf16[3584,512]{1,0:T(8,128)(2,1)} %bitcast.5), custom_call_target="tpu_custom_call" | custom-call | bytes 7340032 | tf_op jit(solution)/shard_map/stage/pallas_call | solution.py:237
  14.9 0.0 collective-permute-done.2.refs_1_
  14.9 0.6 %collective-permute-done.3.refs_2_ = bf16[8,3200]{1,0:T(8,128)(2,1)S(1)} collective-permute-done((bf16[8,3200]{1,0:T(8,128)(2,1)S(1)}, bf16[8,3200]{1,0:T(8,128)(2,1)S(1)}, u32[]{:S(2)}, u32[]{:S(2)}) %collective-permute-start.3) | collective-permute-done | bytes 51232 | tf_op jit(solution)/shard_map/ppermute | solution.py:224
  15.6 2.6 %collective-permute-done.4.refs_3_ = bf16[8,3200]{1,0:T(8,128)(2,1)S(1)} collective-permute-done((bf16[8,3200]{1,0:T(8,128)(2,1)S(1)}, bf16[8,3200]{1,0:T(8,128)(2,1)S(1)}, u32[]{:S(2)}, u32[]{:S(2)}) %collective-permute-start.4) | collective-permute-done | bytes 51232 | tf_op jit(solution)/shard_map/ppermute | solution.py:224
  18.2 0.8 %collective-permute-done.5.refs_4_ = bf16[16,3200]{1,0:T(8,128)(2,1)S(1)} collective-permute-done((bf16[16,3200]{1,0:T(8,128)(2,1)S(1)}, bf16[16,3200]{1,0:T(8,128)(2,1)S(1)}, u32[]{:S(2)}, u32[]{:S(2)}) %collective-permute-start.5) | collective-permute-done | bytes 102432 | tf_op jit(solution)/shard_map/ppermute | solution.py:224
  19.0 0.1 gather.1.own_ref
  19.1 0.1 collective-permute-start.6
  19.2 2.0 %stage.3.down_ref = bf16[512,3584]{1,0:T(8,128)(2,1)S(1)} custom-call(bf16[512,3584]{1,0:T(8,128)(2,1)} %bitcast.6), custom_call_target="tpu_custom_call" | custom-call | bytes 7340032 | tf_op jit(solution)/shard_map/stage/pallas_call | solution.py:237
  21.2 1.7 %experts.1 = (bf16[64,3584]{1,0:T(8,128)(2,1)S(1)}, bf16[64,3584]{1,0:T(8,128)(2,1)S(1)}) custom-call(bf16[64,3584]{1,0:T(8,128)(2,1)S(1)} %gather.1.own_ref, bf16[64,3584]{1,0:T(8,128)(2,1)S(1)} %collective-permute-done.6.other_ref, bf16[3584,512]{1,0:T(8,128)(2,1)S(1)} %get-tuple-element.49.gate_ref, bf16[3584,512]{1,0:T(8,128)(2,1)S(1)} %stage.2.up_ref, ...), custom_call_target="tpu_custom_call" | custom-call | flops 1409286144 | bytes 11010048 | tf_op jit(solution)/shard_map/experts/pallas_call | solution.py:295
  22.9 0.6 %collective-permute-start.7 = (bf16[64,3584]{1,0:T(8,128)(2,1)S(1)}, bf16[64,3584]{1,0:T(8,128)(2,1)S(1)}, u32[]{:S(2)}, u32[]{:S(2)}) collective-permute-start(bf16[64,3584]{1,0:T(8,128)(2,1)S(1)} %get-tuple-element.52), channel_id=1, source_target_pairs={{0,1},{1,0},{2,3},{3,2},{4,5},{5,4},{6,7},{7,6},{8,9},{9,8},{10,11... | collective-permute-start | bytes 1376264 | tf_op jit(solution)/shard_map/ppermute | solution.py:234
  23.5 1.4 %collective-permute-done.7.got_ref = bf16[64,3584]{1,0:T(8,128)(2,1)S(1)} collective-permute-done((bf16[64,3584]{1,0:T(8,128)(2,1)S(1)}, bf16[64,3584]{1,0:T(8,128)(2,1)S(1)}, u32[]{:S(2)}, u32[]{:S(2)}) %collective-permute-start.7) | collective-permute-done | bytes 458784 | tf_op jit(solution)/shard_map/ppermute | solution.py:234
  25.0 0.2 join.1
  25.1 0.8 %collective-permute-start.8 = (bf16[16,3200]{1,0:T(8,128)(2,1)S(1)}, bf16[16,3200]{1,0:T(8,128)(2,1)S(1)}, u32[]{:S(2)}, u32[]{:S(2)}) collective-permute-start(bf16[16,3200]{1,0:T(8,128)(2,1)S(1)} %get-tuple-element.53), channel_id=1, source_target_pairs={{0,8},{1,13},{2,10},{3,15},{4,12},{5,9},{6,14},{7,11},{8,0},{9,5},... | collective-permute-start | bytes 307208 | tf_op jit(solution)/shard_map/ppermute | solution.py:224
  25.9 2.2 %collective-permute-start.12 = (bf16[16,3200]{1,0:T(8,128)(2,1)S(1)}, bf16[16,3200]{1,0:T(8,128)(2,1)S(1)}, u32[]{:S(2)}, u32[]{:S(2)}) collective-permute-start(bf16[16,3200]{1,0:T(8,128)(2,1)S(1)} %get-tuple-element.58), channel_id=1, source_target_pairs={{0,10},{1,15},{2,8},{3,13},{4,14},{5,11},{6,12},{7,9},{8,2},{9,7},... | collective-permute-start | bytes 307208 | tf_op jit(solution)/shard_map/ppermute | solution.py:224
  28.1 1.5 %collective-permute-start.9 = (bf16[8,3200]{1,0:T(8,128)(2,1)S(1)}, bf16[8,3200]{1,0:T(8,128)(2,1)S(1)}, u32[]{:S(2)}, u32[]{:S(2)}) collective-permute-start(bf16[8,3200]{1,0:T(8,128)(2,1)S(1)} %get-tuple-element.54), channel_id=1, source_target_pairs={{0,2},{1,3},{2,0},{3,1},{4,6},{5,7},{6,4},{7,5},{8,10},{9,11},{10,... | collective-permute-start | bytes 153608 | tf_op jit(solution)/shard_map/ppermute | solution.py:224
  29.6 1.3 %collective-permute-start.10 = (bf16[8,3200]{1,0:T(8,128)(2,1)S(1)}, bf16[8,3200]{1,0:T(8,128)(2,1)S(1)}, u32[]{:S(2)}, u32[]{:S(2)}) collective-permute-start(bf16[8,3200]{1,0:T(8,128)(2,1)S(1)} %get-tuple-element.55), channel_id=1, source_target_pairs={{0,4},{1,5},{2,6},{3,7},{4,0},{5,1},{6,2},{7,3},{8,12},{9,13},{10,... | collective-permute-start | bytes 153608 | tf_op jit(solution)/shard_map/ppermute | solution.py:224
  30.9 0.7 %collective-permute-start.11 = (bf16[8,3200]{1,0:T(8,128)(2,1)S(1)}, bf16[8,3200]{1,0:T(8,128)(2,1)S(1)}, u32[]{:S(2)}, u32[]{:S(2)}) collective-permute-start(bf16[8,3200]{1,0:T(8,128)(2,1)S(1)} %get-tuple-element.56), channel_id=1, source_target_pairs={{0,6},{1,7},{2,4},{3,5},{4,2},{5,3},{6,0},{7,1},{8,14},{9,15},{10,... | collective-permute-start | bytes 153608 | tf_op jit(solution)/shard_map/ppermute | solution.py:224
  31.6 1.0 %collective-permute-done.9.refs_4_ = bf16[8,3200]{1,0:T(8,128)(2,1)S(1)} collective-permute-done((bf16[8,3200]{1,0:T(8,128)(2,1)S(1)}, bf16[8,3200]{1,0:T(8,128)(2,1)S(1)}, u32[]{:S(2)}, u32[]{:S(2)}) %collective-permute-start.9) | collective-permute-done | bytes 51232 | tf_op jit(solution)/shard_map/ppermute | solution.py:224
  32.6 2.7 %collective-permute-done.10.refs_5_ = bf16[8,3200]{1,0:T(8,128)(2,1)S(1)} collective-permute-done((bf16[8,3200]{1,0:T(8,128)(2,1)S(1)}, bf16[8,3200]{1,0:T(8,128)(2,1)S(1)}, u32[]{:S(2)}, u32[]{:S(2)}) %collective-permute-start.10) | collective-permute-done | bytes 51232 | tf_op jit(solution)/shard_map/ppermute | solution.py:224
  35.3 2.4 %collective-permute-done.11.refs_6_ = bf16[8,3200]{1,0:T(8,128)(2,1)S(1)} collective-permute-done((bf16[8,3200]{1,0:T(8,128)(2,1)S(1)}, bf16[8,3200]{1,0:T(8,128)(2,1)S(1)}, u32[]{:S(2)}, u32[]{:S(2)}) %collective-permute-start.11) | collective-permute-done | bytes 51232 | tf_op jit(solution)/shard_map/ppermute | solution.py:224
  37.7 0.5 %collective-permute-start.14 = (bf16[16,3200]{1,0:T(8,128)(2,1)S(1)}, bf16[16,3200]{1,0:T(8,128)(2,1)S(1)}, u32[]{:S(2)}, u32[]{:S(2)}) collective-permute-start(bf16[16,3200]{1,0:T(8,128)(2,1)S(1)} %collective-permute-done.12.refs_1_), channel_id=1, source_target_pairs={{0,1},{1,0},{2,3},{3,2},{4,5},{5,4},{6,7},{7,6},{8,9},{9,8},{10,11... | collective-permute-start | bytes 307208 | tf_op jit(solution)/shard_map/ppermute | solution.py:234
  38.2 0.8 %collective-permute-done.13.refs_2_ = bf16[16,3200]{1,0:T(8,128)(2,1)S(1)} collective-permute-done((bf16[16,3200]{1,0:T(8,128)(2,1)S(1)}, bf16[16,3200]{1,0:T(8,128)(2,1)S(1)}, u32[]{:S(2)}, u32[]{:S(2)}) %collective-permute-start.13) | collective-permute-done | bytes 102432 | tf_op jit(solution)/shard_map/ppermute | solution.py:234
  39.0 0.2 collective-permute-done.14.refs_3_
  39.2 1.4 %combine.1 = bf16[128,3584]{1,0:T(8,128)(2,1)} custom-call(bf16[128,128]{1,0:T(8,128)(2,1)S(1)} %get-tuple-element.34.mix_ref, bf16[16,3200]{1,0:T(8,128)(2,1)S(1)} %collective-permute-done.8.refs_0_, bf16[16,3200]{1,0:T(8,128)(2,1)S(1)} %collective-permute-done.12.refs_1_, bf16[16,3200]{1,0:T(8,128)(2,1)S(1)} %collective-permute-done.13.refs_2_, ...), custom_call_target="tpu_custom_call" | custom-call | tf_op jit(solution)/shard_map/combine/pallas_call | solution.py:321
  (6 shorter events, 0.0 us)
Async XLA Ops:
  2.6 1.5 %collective-permute-start = (bf16[16,3200]{1,0:T(8,128)(2,1)S(1)}, bf16[16,3200]{1,0:T(8,128)(2,1)S(1)}, u32[]{:S(2)}, u32[]{:S(2)}) collective-permute-start(bf16[16,3200]{1,0:T(8,128)(2,1)S(1)} %get-tuple-element.36), channel_id=1, source_target_pairs={{0,1},{1,0},{2,3},{3,2},{4,5},{5,4},{6,7},{7,6},{8,9},{9,8},{10,11... | collective-permute-start | bytes 307208 | tf_op jit(solution)/shard_map/ppermute | solution.py:234
  4.1 14.1 %collective-permute-start.1 = (bf16[16,3200]{1,0:T(8,128)(2,1)S(1)}, bf16[16,3200]{1,0:T(8,128)(2,1)S(1)}, u32[]{:S(2)}, u32[]{:S(2)}) collective-permute-start(bf16[16,3200]{1,0:T(8,128)(2,1)S(1)} %get-tuple-element.37), channel_id=1, source_target_pairs={{0,8},{1,13},{2,10},{3,15},{4,12},{5,9},{6,14},{7,11},{8,0},{9,5},... | collective-permute-start | bytes 307208 | tf_op jit(solution)/shard_map/ppermute | solution.py:224
  8.1 10.9 %collective-permute-start.5 = (bf16[16,3200]{1,0:T(8,128)(2,1)S(1)}, bf16[16,3200]{1,0:T(8,128)(2,1)S(1)}, u32[]{:S(2)}, u32[]{:S(2)}) collective-permute-start(bf16[16,3200]{1,0:T(8,128)(2,1)S(1)} %get-tuple-element.41), channel_id=1, source_target_pairs={{0,10},{1,15},{2,8},{3,13},{4,14},{5,11},{6,12},{7,9},{8,2},{9,7},... | collective-permute-start | bytes 307208 | tf_op jit(solution)/shard_map/ppermute | solution.py:224
  9.4 5.5 %collective-permute-start.2 = (bf16[8,3200]{1,0:T(8,128)(2,1)S(1)}, bf16[8,3200]{1,0:T(8,128)(2,1)S(1)}, u32[]{:S(2)}, u32[]{:S(2)}) collective-permute-start(bf16[8,3200]{1,0:T(8,128)(2,1)S(1)} %get-tuple-element.38), channel_id=1, source_target_pairs={{0,2},{1,3},{2,0},{3,1},{4,6},{5,7},{6,4},{7,5},{8,10},{9,11},{10,... | collective-permute-start | bytes 153608 | tf_op jit(solution)/shard_map/ppermute | solution.py:224
  9.6 5.9 %collective-permute-start.3 = (bf16[8,3200]{1,0:T(8,128)(2,1)S(1)}, bf16[8,3200]{1,0:T(8,128)(2,1)S(1)}, u32[]{:S(2)}, u32[]{:S(2)}) collective-permute-start(bf16[8,3200]{1,0:T(8,128)(2,1)S(1)} %get-tuple-element.39), channel_id=1, source_target_pairs={{0,4},{1,5},{2,6},{3,7},{4,0},{5,1},{6,2},{7,3},{8,12},{9,13},{10,... | collective-permute-start | bytes 153608 | tf_op jit(solution)/shard_map/ppermute | solution.py:224
  11.4 6.7 %collective-permute-start.4 = (bf16[8,3200]{1,0:T(8,128)(2,1)S(1)}, bf16[8,3200]{1,0:T(8,128)(2,1)S(1)}, u32[]{:S(2)}, u32[]{:S(2)}) collective-permute-start(bf16[8,3200]{1,0:T(8,128)(2,1)S(1)} %get-tuple-element.40), channel_id=1, source_target_pairs={{0,6},{1,7},{2,4},{3,5},{4,2},{5,3},{6,0},{7,1},{8,14},{9,15},{10,... | collective-permute-start | bytes 153608 | tf_op jit(solution)/shard_map/ppermute | solution.py:224
  19.1 2.1 %collective-permute-start.6 = (bf16[64,3584]{1,0:T(8,128)(2,1)S(1)}, bf16[64,3584]{1,0:T(8,128)(2,1)S(1)}, u32[]{:S(2)}, u32[]{:S(2)}) collective-permute-start(bf16[64,3584]{1,0:T(8,128)(2,1)S(1)} %gather.1.own_ref), channel_id=1, source_target_pairs={{0,1},{1,0},{2,3},{3,2},{4,5},{5,4},{6,7},{7,6},{8,9},{9,8},{10,11... | collective-permute-start | bytes 1376264 | tf_op jit(solution)/shard_map/ppermute | solution.py:234
  22.9 2.0 %collective-permute-start.7 = (bf16[64,3584]{1,0:T(8,128)(2,1)S(1)}, bf16[64,3584]{1,0:T(8,128)(2,1)S(1)}, u32[]{:S(2)}, u32[]{:S(2)}) collective-permute-start(bf16[64,3584]{1,0:T(8,128)(2,1)S(1)} %get-tuple-element.52), channel_id=1, source_target_pairs={{0,1},{1,0},{2,3},{3,2},{4,5},{5,4},{6,7},{7,6},{8,9},{9,8},{10,11... | collective-permute-start | bytes 1376264 | tf_op jit(solution)/shard_map/ppermute | solution.py:234
  25.1 12.6 %collective-permute-start.8 = (bf16[16,3200]{1,0:T(8,128)(2,1)S(1)}, bf16[16,3200]{1,0:T(8,128)(2,1)S(1)}, u32[]{:S(2)}, u32[]{:S(2)}) collective-permute-start(bf16[16,3200]{1,0:T(8,128)(2,1)S(1)} %get-tuple-element.53), channel_id=1, source_target_pairs={{0,8},{1,13},{2,10},{3,15},{4,12},{5,9},{6,14},{7,11},{8,0},{9,5},... | collective-permute-start | bytes 307208 | tf_op jit(solution)/shard_map/ppermute | solution.py:224
  25.9 11.8 %collective-permute-start.12 = (bf16[16,3200]{1,0:T(8,128)(2,1)S(1)}, bf16[16,3200]{1,0:T(8,128)(2,1)S(1)}, u32[]{:S(2)}, u32[]{:S(2)}) collective-permute-start(bf16[16,3200]{1,0:T(8,128)(2,1)S(1)} %get-tuple-element.58), channel_id=1, source_target_pairs={{0,10},{1,15},{2,8},{3,13},{4,14},{5,11},{6,12},{7,9},{8,2},{9,7},... | collective-permute-start | bytes 307208 | tf_op jit(solution)/shard_map/ppermute | solution.py:224
  28.1 4.5 %collective-permute-start.9 = (bf16[8,3200]{1,0:T(8,128)(2,1)S(1)}, bf16[8,3200]{1,0:T(8,128)(2,1)S(1)}, u32[]{:S(2)}, u32[]{:S(2)}) collective-permute-start(bf16[8,3200]{1,0:T(8,128)(2,1)S(1)} %get-tuple-element.54), channel_id=1, source_target_pairs={{0,2},{1,3},{2,0},{3,1},{4,6},{5,7},{6,4},{7,5},{8,10},{9,11},{10,... | collective-permute-start | bytes 153608 | tf_op jit(solution)/shard_map/ppermute | solution.py:224
  29.6 5.7 %collective-permute-start.10 = (bf16[8,3200]{1,0:T(8,128)(2,1)S(1)}, bf16[8,3200]{1,0:T(8,128)(2,1)S(1)}, u32[]{:S(2)}, u32[]{:S(2)}) collective-permute-start(bf16[8,3200]{1,0:T(8,128)(2,1)S(1)} %get-tuple-element.55), channel_id=1, source_target_pairs={{0,4},{1,5},{2,6},{3,7},{4,0},{5,1},{6,2},{7,3},{8,12},{9,13},{10,... | collective-permute-start | bytes 153608 | tf_op jit(solution)/shard_map/ppermute | solution.py:224
  30.9 6.8 %collective-permute-start.11 = (bf16[8,3200]{1,0:T(8,128)(2,1)S(1)}, bf16[8,3200]{1,0:T(8,128)(2,1)S(1)}, u32[]{:S(2)}, u32[]{:S(2)}) collective-permute-start(bf16[8,3200]{1,0:T(8,128)(2,1)S(1)} %get-tuple-element.56), channel_id=1, source_target_pairs={{0,6},{1,7},{2,4},{3,5},{4,2},{5,3},{6,0},{7,1},{8,14},{9,15},{10,... | collective-permute-start | bytes 153608 | tf_op jit(solution)/shard_map/ppermute | solution.py:224
  37.7 1.3 %collective-permute-start.13 = (bf16[16,3200]{1,0:T(8,128)(2,1)S(1)}, bf16[16,3200]{1,0:T(8,128)(2,1)S(1)}, u32[]{:S(2)}, u32[]{:S(2)}) collective-permute-start(bf16[16,3200]{1,0:T(8,128)(2,1)S(1)} %collective-permute-done.8.refs_0_), channel_id=1, source_target_pairs={{0,1},{1,0},{2,3},{3,2},{4,5},{5,4},{6,7},{7,6},{8,9},{9,8},{10,11... | collective-permute-start | bytes 307208 | tf_op jit(solution)/shard_map/ppermute | solution.py:234
  37.7 1.5 %collective-permute-start.14 = (bf16[16,3200]{1,0:T(8,128)(2,1)S(1)}, bf16[16,3200]{1,0:T(8,128)(2,1)S(1)}, u32[]{:S(2)}, u32[]{:S(2)}) collective-permute-start(bf16[16,3200]{1,0:T(8,128)(2,1)S(1)} %collective-permute-done.12.refs_1_), channel_id=1, source_target_pairs={{0,1},{1,0},{2,3},{3,2},{4,5},{5,4},{6,7},{7,6},{8,9},{9,8},{10,11... | collective-permute-start | bytes 307208 | tf_op jit(solution)/shard_map/ppermute | solution.py:234

commit v10 on v9

v10 whole, which is shorter than its diff:
```python
import functools

import jax
import jax.numpy as jnp
from jax import lax
from jax.experimental import pallas as pl
from jax.experimental.pallas import tpu as pltpu
from jax.sharding import PartitionSpec as P

SLOTS = 8
CHUNKS = 4
PIECES = 4
LANES = 128

VMEM = pl.BlockSpec(memory_space=pltpu.VMEM)
SMALL = pl.CostEstimate(flops=1, bytes_accessed=1, transcendentals=0)
HBM = pl.BlockSpec(memory_space=pltpu.HBM)


def in_hbm(*arrays):
    return [pltpu.with_memory_space_constraint(a, pltpu.HBM) for a in arrays]


def relative(flight):
    return flight == 8


CARRIED = ((4, 5), (6, 7))
NEAR = (1, 2, 3)


def block_order(flight, core):
    if not relative(flight):
        return range(flight)
    return CARRIED[core] + CARRIED[1 - core] + NEAR + (0,)


def packed_width(width):
    return width // 7 * 6 + LANES


def pack(rows):
    blocks = rows.reshape(-1, SLOTS, rows.shape[1])
    tail = rows.shape[1] // 7
    main = blocks[:, :, : 6 * tail]
    moved = jnp.concatenate([blocks[:, j : j + 1, 6 * tail :] for j in range(6)], axis=2)
    row = lax.broadcasted_iota(jnp.int32, main.shape, 1)
    main = jnp.where(row == SLOTS - 1, moved, main)
    row = row[:, :, :LANES]
    extra = jnp.zeros(row.shape, rows.dtype)
    for k in range(tail // LANES):
        start = 6 * tail + k * LANES
        extra = jnp.where(row == k, blocks[:, 6:7, start : start + LANES], extra)
    return jnp.concatenate([main, extra], axis=2).reshape(rows.shape[0], -1)


def unpack(packed):
    blocks = packed.reshape(-1, SLOTS, packed.shape[1])
    tail = (packed.shape[1] - LANES) // 6
    main = blocks[:, :, : 6 * tail]
    last = jnp.concatenate(
        [blocks[:, k : k + 1, 6 * tail :] for k in range(tail // LANES)], axis=2
    )
    row = lax.broadcasted_iota(jnp.int32, (blocks.shape[0], SLOTS, tail), 1)
    end = jnp.where(row == 6, last, 0.0)
    for j in range(6):
        end = jnp.where(row == j, blocks[:, 7:8, j * tail : (j + 1) * tail], end)
    return jnp.concatenate([main, end], axis=2).reshape(packed.shape[0], -1)


def store(refs, rows):
    at = 0
    for ref in refs:
        ref[...] = rows[at : at + ref.shape[0]].astype(ref.dtype)
        at += ref.shape[0]


def dispatch_kernel(flight, tok_hbm, gain_hbm, ids_hbm, gw_hbm, mix_ref, *rest):
    *outs, tok, gain, ids, gw, normed, sems = rest
    count = tok.shape[0]
    part = count // CHUNKS
    small = [
        pltpu.make_async_copy(ids_hbm, ids, sems.at[0]),
        pltpu.make_async_copy(gw_hbm, gw, sems.at[1]),
        pltpu.make_async_copy(gain_hbm, gain.at[0], sems.at[2]),
    ]
    large = [
        pltpu.make_async_copy(
            tok_hbm.at[pl.ds(i * part, part)], tok.at[pl.ds(i * part, part)], sems.at[3 + i]
        )
        for i in range(CHUNKS)
    ]
    for copy in small + large:
        copy.start()
    small[0].wait()
    small[1].wait()
    experts = lax.broadcasted_iota(jnp.int32, (flight, count), 0)
    if relative(flight):
        place = experts
        me = lax.axis_index("exp")
        for i, (even, odd) in enumerate(zip(block_order(flight, 0), block_order(flight, 1))):
            experts = jnp.where(place == i, jnp.where(me % 2 == 0, even, odd) ^ (me // 2), experts)
    chosen = jnp.zeros((flight, count), jnp.float32)
    gates = jnp.zeros((flight, count), jnp.float32)
    for k in range(ids.shape[0]):
        hit = ids[k : k + 1, :] == experts
        chosen = jnp.where(hit, 1.0, chosen)
        gates = jnp.where(hit, gw[k : k + 1, :], gates)
    before = (
        lax.broadcasted_iota(jnp.int32, (count, count), 0)
        < lax.broadcasted_iota(jnp.int32, (count, count), 1)
    ).astype(jnp.bfloat16)
    rank = jnp.dot(chosen.astype(jnp.bfloat16), before, preferred_element_type=jnp.float32)
    rank = jnp.where(chosen > 0.0, rank, -1.0)

    slot = lax.broadcasted_iota(jnp.int32, (flight, SLOTS, count), 1).astype(jnp.float32)
    taken = rank[:, None, :] == slot
    pick = jnp.where(taken, 1.0, 0.0).reshape(flight * SLOTS, count).astype(jnp.bfloat16)
    mix = jnp.where(taken, gates[:, None, :], 0.0).reshape(flight * SLOTS, count)
    high = mix.astype(jnp.bfloat16)
    mix_ref[: flight * SLOTS, :] = high
    mix_ref[flight * SLOTS :, :] = (mix - high.astype(jnp.float32)).astype(jnp.bfloat16)

    small[2].wait()
    for i in range(CHUNKS):
        large[i].wait()
        wide = tok[pl.ds(i * part, part), :].astype(jnp.float32)
        mean_square = jnp.mean(wide * wide, axis=1, keepdims=True)
        normed[pl.ds(i * part, part), :] = (
            wide * lax.rsqrt(mean_square + 1e-06) * gain[...]
        ).astype(jnp.bfloat16)
    rows = jnp.dot(pick, normed[...], preferred_element_type=jnp.float32)
    store(outs, pack(rows))


def stage_kernel(source, *refs):
    target, sems = refs[-2:]
    rows = source.shape[0] // PIECES
    copies = [
        pltpu.make_async_copy(
            source.at[pl.ds(i * rows, rows)], target.at[pl.ds(i * rows, rows)], sems.at[i]
        )
        for i in range(PIECES)
    ]
    for copy in copies:
        copy.start()
    for copy in copies:
        copy.wait()


def together(refs):
    return jnp.concatenate([b[...].astype(jnp.float32) for b in refs], axis=0)


def merge_kernel(kept_ref, got_ref, *outs):
    kept, got = kept_ref[...].astype(jnp.float32), got_ref[...].astype(jnp.float32)
    for i, out in enumerate(outs):
        here = slice(i * SLOTS, (i + 1) * SLOTS)
        out[...] = jnp.concatenate([kept[here], got[here]], axis=0).astype(jnp.bfloat16)


def gather_kernel(*refs):
    refs[-1][...] = unpack(together(refs[:-1])).astype(jnp.bfloat16)


def expert_kernel(count, *refs):
    rows, weights, outs = refs[: 2 * count], refs[2 * count : 2 * count + 3], refs[2 * count + 3 :]
    gate_ref, up_ref, down_ref = weights
    x = jnp.concatenate([r[...] for r in rows], axis=0)
    gate_v = jnp.dot(x, gate_ref[...], preferred_element_type=jnp.float32)
    up_v = jnp.dot(x, up_ref[...], preferred_element_type=jnp.float32)
    hidden = (gate_v / (1.0 + jnp.exp(-gate_v)) * up_v).astype(jnp.bfloat16)
    store(outs, jnp.dot(hidden, down_ref[...], preferred_element_type=jnp.float32))


def join_kernel(mine_ref, got_ref, *outs):
    store(outs, pack(mine_ref[...].astype(jnp.float32) + got_ref[...].astype(jnp.float32)))


def weigh(mix, rows):
    rows = unpack(rows).astype(jnp.bfloat16)
    both = jnp.concatenate([rows, rows], axis=0)
    return lax.dot_general(mix, both, (((0,), (0,)), ((), ())), preferred_element_type=jnp.float32)


def mix_rows(mix_ref, start, count):
    half = mix_ref.shape[0] // 2
    return jnp.concatenate([mix_ref[at + start : at + start + count, :] for at in (0, half)], axis=0)


def close_kernel(mix_ref, *refs):
    *refs, out_ref = refs
    rows = together(refs)
    out_ref[...] = weigh(mix_rows(mix_ref, mix_ref.shape[0] // 2 - rows.shape[0], rows.shape[0]), rows)


def far_kernel(first, mix_ref, close_ref, *refs):
    *refs, out_ref = refs
    blocks = [
        r[...].astype(jnp.float32)[at * SLOTS : (at + 1) * SLOTS] for r, at in zip(refs, first)
    ]
    rows = jnp.concatenate(blocks, axis=0)
    out_ref[...] = (
        close_ref[...] + weigh(mix_rows(mix_ref, 0, rows.shape[0]), rows)
    ).astype(jnp.bfloat16)


def combine_kernel(mix_ref, rows_ref, out_ref):
    out_ref[...] = weigh(mix_ref[...], rows_ref[...].astype(jnp.float32)).astype(jnp.bfloat16)


def per_device(tokens, norm_gain, expert_ids, gate_weights, w_gate, w_up, w_down):
    owners = lax.axis_size("exp")
    flight = owners // 2
    count, width = tokens.shape
    hidden = w_gate.shape[2]
    few = relative(flight)

    def local(kernel, outs, name, *args, limit=16):
        return pl.pallas_call(
            kernel,
            out_shape=outs,
            in_specs=[VMEM] * len(args),
            out_specs=(VMEM,) * len(outs),
            compiler_params=pltpu.CompilerParams(vmem_limit_bytes=limit * 2**20),
            cost_estimate=SMALL,
            name=name,
        )(*args)

    def full(*counts):
        return tuple(jax.ShapeDtypeStruct((n * SLOTS, width), jnp.bfloat16) for n in counts)

    def packed(*counts):
        shapes = [(n * SLOTS, packed_width(width)) for n in counts]
        return tuple(jax.ShapeDtypeStruct(shape, jnp.bfloat16) for shape in shapes)

    def swap(rows):
        return lax.ppermute(rows, "exp", [(n, n ^ 1) for n in range(owners)])

    def travel(rows, distances, cross=0):
        pairs = [(n, n ^ (2 * distances[n % 2]) ^ cross) for n in range(owners)]
        return lax.ppermute(rows, "exp", pairs)

    def stage(weights, *after):
        return pl.pallas_call(
            stage_kernel,
            out_shape=jax.ShapeDtypeStruct(weights.shape, weights.dtype),
            in_specs=[HBM] + [pl.BlockSpec(memory_space=pl.ANY)] * len(after),
            out_specs=VMEM,
            scratch_shapes=[pltpu.SemaphoreType.DMA((PIECES,))],
            compiler_params=pltpu.CompilerParams(vmem_limit_bytes=16 * 2**20),
            cost_estimate=SMALL,
            name="stage",
        )(*in_hbm(weights), *after)

    def experts(own, other, weights, outs):
        return local(
            functools.partial(expert_kernel, len(own)),
            outs,
            "experts",
            *own,
            *other,
            *weights,
            limit=24,
        )

    result = (jax.ShapeDtypeStruct((count, width), jnp.bfloat16),)
    first = packed(2, 2, 1, 1, 1, 1) if few else packed(flight)
    mix, *outgoing = pl.pallas_call(
        functools.partial(dispatch_kernel, flight),
        out_shape=(jax.ShapeDtypeStruct((2 * flight * SLOTS, count), jnp.bfloat16),) + first,
        in_specs=[HBM] * 4,
        out_specs=(VMEM,) * (len(first) + 1),
        scratch_shapes=[
            pltpu.VMEM((count, width), jnp.bfloat16),
            pltpu.VMEM((1, width), jnp.float32),
            pltpu.VMEM(expert_ids.shape[::-1], jnp.int32),
            pltpu.VMEM(gate_weights.shape[::-1], jnp.float32),
            pltpu.VMEM((count, width), jnp.bfloat16),
            pltpu.SemaphoreType.DMA((3 + CHUNKS,)),
        ],
        compiler_params=pltpu.CompilerParams(vmem_limit_bytes=24 * 2**20),
        name="dispatch",
    )(*in_hbm(tokens, norm_gain, expert_ids.T, gate_weights.T))
    down = stage(w_down[0])

    if not few:
        gate, up = stage(w_gate[0]), stage(w_up[0])
        groups = [list(range(core, owners, 2)) for core in range(2)]
        exchange = functools.partial(
            lax.all_to_all,
            axis_name="exp",
            split_axis=0,
            concat_axis=0,
            axis_index_groups=groups,
            tiled=True,
        )
        (own,) = local(gather_kernel, full(flight), "gather", exchange(outgoing[0]))
        mine, theirs = experts([own], [swap(own)], (gate, up, down), full(flight, flight))
        (joined,) = local(join_kernel, packed(flight), "join", mine, swap(theirs))
        return local(combine_kernel, result, "combine", mix, exchange(joined), limit=24)[0]

    near = [(r, r) for r in NEAR]
    one, two = zip(*CARRIED)
    kept, given, *close, own = outgoing
    far = local(merge_kernel, packed(2, 2), "merge", kept, swap(given))
    gate = stage(w_gate[0], far[0])
    far_one = travel(far[0], one)
    close = [travel(a, r) for a, r in zip(close, near)]
    far_two, gate, *close = lax.optimization_barrier((far[1], gate, *close))
    up = stage(w_up[0], far_one)
    far_two = travel(far_two, two)
    far_two, up = lax.optimization_barrier((far_two, up))
    (own,) = local(gather_kernel, full(8), "gather", far_one, *close, own, far_two)
    mine_one, mine, theirs_one, theirs = experts(
        [own], [swap(own)], (gate, up, down), full(2, 6, 2, 6)
    )
    (far_one,) = local(join_kernel, packed(2), "join", mine_one, swap(theirs_one))
    far_one = travel(far_one, one)
    *close, own, far_two = local(join_kernel, packed(1, 1, 1, 1, 2), "join", mine, swap(theirs))
    close = [travel(a, r) for a, r in zip(close, near)]
    far_two, *close = lax.optimization_barrier((far_two, *close))
    far_two = travel(far_two, two)
    total = (jax.ShapeDtypeStruct((count, width), jnp.float32),)
    (total,) = local(close_kernel, total, "combine_close", mix, *close, own, limit=24)
    far_one, total = lax.optimization_barrier((far_one, total))
    arrays = [far_one, far_two, swap(far_one), swap(far_two)]
    kernel = functools.partial(far_kernel, (0, 0, 1, 1))
    return local(kernel, result, "combine_far", mix, total, *arrays, limit=24)[0]


def solution(mesh):
    placed = (
        P(("group", "exp"), None),
        P(),
        P(("group", "exp"), None),
        P(("group", "exp"), None),
        P("exp", None, None),
        P("exp", None, None),
        P("exp", None, None),
    )
    return jax.shard_map(
        per_device, mesh=mesh, in_specs=placed, out_specs=P(("group", "exp"), None), check_vma=False
    )
```

time: 40.7 us -> 45.6 us (1.12)
  starting transfers between devices: 16.9 us -> 20.1 us
  Pallas kernels: 10 us -> 11.9 us
    ppermute x15 -> x16, starting transfers between devices: 16.9 us -> 20.1 us  [the longest x10 18.9 us: travel(): return lax.ppermute(rows, 'exp', pairs)]
    pallas_call x2 -> x3, Pallas kernels: 4.09 us -> 6.13 us  [stage(): pl.pallas_call(stage_kernel, out_shape=jax.ShapeDtypeStruct(weights.shape...]
    pallas_call x1, Pallas kernels: 2.57 us -> 2.03 us  [per_device(): pl.pallas_call(functools.partial(dispatch_kernel, flight), out_shape=(jax...]
    pallas_call x5 -> x7, Pallas kernels: 3.38 us -> 3.78 us  [local(): pl.pallas_call(kernel, out_shape=outs, in_specs=[VMEM] * len(args), out_s...]
    ppermute x15 -> x16, waiting for transfers between devices: 13.6 us -> 13.3 us  [the longest x10 10.8 us: travel(): return lax.ppermute(rows, 'exp', pairs)]
  transfers between devices with their start and end apart: 15 -> 16, of which waited for: 10 -> 7; matrix products, arithmetic and copies ran while one was open for 0% -> 0% of each run, Pallas kernels for 10% -> 15%
where the time goes in v10:
time: 45.6 us; the launch traced here: 45.4 us
  starting transfers between devices  20.1 us (44%)
  waiting for transfers between devices  13.3 us (29%)
  Pallas kernels  11.9 us (26%)
    ppermute x10, starting transfers between devices, travel(): return lax.ppermute(rows, 'exp', pairs)  18.9 us
    ppermute x10, waiting for transfers between devices, travel(): return lax.ppermute(rows, 'exp', pairs)  10.8 us
    pallas_call x3, Pallas kernels, stage(): pl.pallas_call(stage_kernel, out_shape=jax.ShapeDtypeStruct(weights.shape...  6.13 us
    pallas_call x7, Pallas kernels, local(): pl.pallas_call(kernel, out_shape=outs, in_specs=[VMEM] * len(args), out_s...  3.78 us
    ppermute x6, waiting for transfers between devices, swap(): return lax.ppermute(rows, 'exp', [(n, n ^ 1) for n in range(owners)])  2.51 us
    pallas_call x1, Pallas kernels, per_device(): pl.pallas_call(functools.partial(dispatch_kernel, flight), out_shape=(jax...  2.03 us
    ppermute x6, starting transfers between devices, swap(): return lax.ppermute(rows, 'exp', [(n, n ^ 1) for n in range(owners)])  1.23 us
  transfers between devices with their start and end apart: 16, of which 7 were waited for; matrix products, arithmetic and copies ran while one was open for 0% of the time, Pallas kernels for 15%

profile of v10, /device:TPU:0, one launch (start us, length us, event | category | flops | bytes accessed | tf_op | source)
XLA Modules:
  0.0 45.4 jit_solution(8643943137606828374)
XLA Ops:
  0.0 2.0 %dispatch.1 = (bf16[128,128]{1,0:T(8,128)(2,1)S(1)}, bf16[16,3200]{1,0:T(8,128)(2,1)S(1)}, bf16[16,3200]{1,0:T(8,128)(2,1)S(1)}, bf16[8,3200]{1,0:T(8,128)(2,1)S...) custom-call(bf16[128,3584]{1,0:T(8,128)(2,1)} %tok_hbm.1, ...), custom_call_target="tpu_custom_call" | custom-call | tf_op jit(solution)/shard_map/dispatch/pallas_call | solution.py:269
  2.0 0.5 %collective-permute-start = (bf16[16,3200]{1,0:T(8,128)(2,1)S(1)}, bf16[16,3200]{1,0:T(8,128)(2,1)S(1)}, u32[]{:S(2)}, u32[]{:S(2)}) collective-permute-start(bf16[16,3200]{1,0:T(8,128)(2,1)S(1)} %get-tuple-element.38), channel_id=1, source_target_pairs={{0,1},{1,0},{2,3},{3,2},{4,5},{5,4},{6,7},{7,6},{8,9},{9,8},{10,11... | collective-permute-start | bytes 307208 | tf_op jit(solution)/shard_map/ppermute | solution.py:238
  2.6 2.6 %collective-permute-start.2 = (bf16[8,3200]{1,0:T(8,128)(2,1)S(1)}, bf16[8,3200]{1,0:T(8,128)(2,1)S(1)}, u32[]{:S(2)}, u32[]{:S(2)}) collective-permute-start(bf16[8,3200]{1,0:T(8,128)(2,1)S(1)} %get-tuple-element.41), channel_id=1, source_target_pairs={{0,2},{1,3},{2,0},{3,1},{4,6},{5,7},{6,4},{7,5},{8,10},{9,11},{10,... | collective-permute-start | bytes 153608 | tf_op jit(solution)/shard_map/ppermute | solution.py:242
  5.2 1.6 %collective-permute-start.3 = (bf16[8,3200]{1,0:T(8,128)(2,1)S(1)}, bf16[8,3200]{1,0:T(8,128)(2,1)S(1)}, u32[]{:S(2)}, u32[]{:S(2)}) collective-permute-start(bf16[8,3200]{1,0:T(8,128)(2,1)S(1)} %get-tuple-element.42), channel_id=1, source_target_pairs={{0,4},{1,5},{2,6},{3,7},{4,0},{5,1},{6,2},{7,3},{8,12},{9,13},{10,... | collective-permute-start | bytes 153608 | tf_op jit(solution)/shard_map/ppermute | solution.py:242
  6.7 0.0 collective-permute-start.4
  6.7 0.0 collective-permute-done.got_ref
  6.8 3.1 %collective-permute-start.1 = (bf16[16,3200]{1,0:T(8,128)(2,1)S(1)}, bf16[16,3200]{1,0:T(8,128)(2,1)S(1)}, u32[]{:S(2)}, u32[]{:S(2)}) collective-permute-start(bf16[16,3200]{1,0:T(8,128)(2,1)S(1)} %get-tuple-element.39.refs_0_), channel_id=1, source_target_pairs={{0,8},{1,13},{2,10},{3,15},{4,12},{5,9},{6,14},{7,11},{8,0},{9,5},... | collective-permute-start | bytes 307208 | tf_op jit(solution)/shard_map/ppermute | solution.py:242
  9.8 2.0 %stage.3.refs_2_ = bf16[3584,512]{1,0:T(8,128)(2,1)S(1)} custom-call(bf16[3584,512]{1,0:T(8,128)(2,1)} %bitcast.5, bf16[16,3200]{1,0:T(8,128)(2,1)S(1)} %get-tuple-element.39.refs_0_), custom_call_target="tpu_custom_call" | custom-call | flops 1 | bytes 1 | tf_op jit(solution)/shard_map/stage/pallas_call | solution.py:245
  11.9 0.0 collective-permute-done.2.refs_1_
  11.9 3.0 %collective-permute-start.5 = (bf16[16,3200]{1,0:T(8,128)(2,1)S(1)}, bf16[16,3200]{1,0:T(8,128)(2,1)S(1)}, u32[]{:S(2)}, u32[]{:S(2)}) collective-permute-start(bf16[16,3200]{1,0:T(8,128)(2,1)S(1)} %get-tuple-element.48), channel_id=1, source_target_pairs={{0,10},{1,15},{2,8},{3,13},{4,14},{5,11},{6,12},{7,9},{8,2},{9,7},... | collective-permute-start | bytes 307208 | tf_op jit(solution)/shard_map/ppermute | solution.py:242
  14.8 2.0 %stage.4.refs_3_ = bf16[3584,512]{1,0:T(8,128)(2,1)S(1)} custom-call(bf16[3584,512]{1,0:T(8,128)(2,1)} %bitcast.6, bf16[16,3200]{1,0:T(8,128)(2,1)S(1)} %collective-permute-done.1.refs_0_), custom_call_target="tpu_custom_call" | custom-call | flops 1 | bytes 1 | tf_op jit(solution)/shard_map/stage/pallas_call | solution.py:245
  16.9 3.7 %collective-permute-done.5.refs_5_ = bf16[16,3200]{1,0:T(8,128)(2,1)S(1)} collective-permute-done((bf16[16,3200]{1,0:T(8,128)(2,1)S(1)}, bf16[16,3200]{1,0:T(8,128)(2,1)S(1)}, u32[]{:S(2)}, u32[]{:S(2)}) %collective-permute-start.5) | collective-permute-done | bytes 102432 | tf_op jit(solution)/shard_map/ppermute | solution.py:242
  20.6 0.1 gather.1.refs_0_
  20.7 0.1 collective-permute-start.6
  20.8 2.0 %stage.5.refs_4_ = bf16[512,3584]{1,0:T(8,128)(2,1)S(1)} custom-call(bf16[512,3584]{1,0:T(8,128)(2,1)} %bitcast.7), custom_call_target="tpu_custom_call" | custom-call | flops 1 | bytes 1 | tf_op jit(solution)/shard_map/stage/pallas_call | solution.py:245
  22.9 1.7 %experts.1 = (bf16[16,3584]{1,0:T(8,128)(2,1)S(1)}, bf16[48,3584]{1,0:T(8,128)(2,1)S(1)}, bf16[16,3584]{1,0:T(8,128)(2,1)S(1)}, bf16[48,3584]{1,0:T(8,128)(2,1)S(1)}) custom-call(bf16[64,3584]{1,0:T(8,128)(2,1)S(1)} %gather.1.refs_0_, bf16[64,3584]{1,0:T(8,128)(2,1)S(1)} %collective-permute-done.6.refs_1_, bf16[3584,512]{1,0:T(8,128)(2,1)S(1)} %stage.3.refs_2_, ...), custom_call_target="tpu_custom_call" | custom-call | flops 1 | bytes 1 | tf_op jit(solution)/shard_map/experts/pallas_call | solution.py:220
  24.6 0.6 %collective-permute-start.9 = (bf16[48,3584]{1,0:T(8,128)(2,1)S(1)}, bf16[48,3584]{1,0:T(8,128)(2,1)S(1)}, u32[]{:S(2)}, u32[]{:S(2)}) collective-permute-start(bf16[48,3584]{1,0:T(8,128)(2,1)S(1)} %get-tuple-element.55), channel_id=1, source_target_pairs={{0,1},{1,0},{2,3},{3,2},{4,5},{5,4},{6,7},{7,6},{8,9},{9,8},{10,11... | collective-permute-start | bytes 1032200 | tf_op jit(solution)/shard_map/ppermute | solution.py:238
  25.1 0.1 collective-permute-start.7
  25.2 1.2 %collective-permute-done.9.got_ref = bf16[48,3584]{1,0:T(8,128)(2,1)S(1)} collective-permute-done((bf16[48,3584]{1,0:T(8,128)(2,1)S(1)}, bf16[48,3584]{1,0:T(8,128)(2,1)S(1)}, u32[]{:S(2)}, u32[]{:S(2)}) %collective-permute-start.9) | collective-permute-done | bytes 344096 | tf_op jit(solution)/shard_map/ppermute | solution.py:238
  26.4 0.1 join.3
  26.6 1.6 %collective-permute-start.10 = (bf16[8,3200]{1,0:T(8,128)(2,1)S(1)}, bf16[8,3200]{1,0:T(8,128)(2,1)S(1)}, u32[]{:S(2)}, u32[]{:S(2)}) collective-permute-start(bf16[8,3200]{1,0:T(8,128)(2,1)S(1)} %get-tuple-element.57), channel_id=1, source_target_pairs={{0,2},{1,3},{2,0},{3,1},{4,6},{5,7},{6,4},{7,5},{8,10},{9,11},{10,... | collective-permute-start | bytes 153608 | tf_op jit(solution)/shard_map/ppermute | solution.py:242
  28.2 2.0 %collective-permute-start.12 = (bf16[8,3200]{1,0:T(8,128)(2,1)S(1)}, bf16[8,3200]{1,0:T(8,128)(2,1)S(1)}, u32[]{:S(2)}, u32[]{:S(2)}) collective-permute-start(bf16[8,3200]{1,0:T(8,128)(2,1)S(1)} %get-tuple-element.59), channel_id=1, source_target_pairs={{0,6},{1,7},{2,4},{3,5},{4,2},{5,3},{6,0},{7,1},{8,14},{9,15},{10,... | collective-permute-start | bytes 153608 | tf_op jit(solution)/shard_map/ppermute | solution.py:242
  30.1 0.1 join.2
  30.2 1.5 %collective-permute-start.8 = (bf16[16,3200]{1,0:T(8,128)(2,1)S(1)}, bf16[16,3200]{1,0:T(8,128)(2,1)S(1)}, u32[]{:S(2)}, u32[]{:S(2)}) collective-permute-start(bf16[16,3200]{1,0:T(8,128)(2,1)S(1)} %join.2), channel_id=1, source_target_pairs={{0,8},{1,13},{2,10},{3,15},{4,12},{5,9},{6,14},{7,11},{8,0},{9,5},... | collective-permute-start | bytes 307208 | tf_op jit(solution)/shard_map/ppermute | solution.py:242
  31.6 0.8 %collective-permute-done.11.refs_1_ = bf16[8,3200]{1,0:T(8,128)(2,1)S(1)} collective-permute-done((bf16[8,3200]{1,0:T(8,128)(2,1)S(1)}, bf16[8,3200]{1,0:T(8,128)(2,1)S(1)}, u32[]{:S(2)}, u32[]{:S(2)}) %collective-permute-start.11) | collective-permute-done | bytes 51232 | tf_op jit(solution)/shard_map/ppermute | solution.py:242
  32.5 0.8 %collective-permute-done.12.refs_2_ = bf16[8,3200]{1,0:T(8,128)(2,1)S(1)} collective-permute-done((bf16[8,3200]{1,0:T(8,128)(2,1)S(1)}, bf16[8,3200]{1,0:T(8,128)(2,1)S(1)}, u32[]{:S(2)}, u32[]{:S(2)}) %collective-permute-start.12) | collective-permute-done | bytes 51232 | tf_op jit(solution)/shard_map/ppermute | solution.py:242
  33.3 3.7 %collective-permute-start.13 = (bf16[16,3200]{1,0:T(8,128)(2,1)S(1)}, bf16[16,3200]{1,0:T(8,128)(2,1)S(1)}, u32[]{:S(2)}, u32[]{:S(2)}) collective-permute-start(bf16[16,3200]{1,0:T(8,128)(2,1)S(1)} %get-tuple-element.66), channel_id=1, source_target_pairs={{0,10},{1,15},{2,8},{3,13},{4,14},{5,11},{6,12},{7,9},{8,2},{9,7},... | collective-permute-start | bytes 307208 | tf_op jit(solution)/shard_map/ppermute | solution.py:242
  37.0 0.4 combine_close.1.close_ref
  37.4 3.0 %collective-permute-done.8.refs_0_ = bf16[16,3200]{1,0:T(8,128)(2,1)S(1)} collective-permute-done((bf16[16,3200]{1,0:T(8,128)(2,1)S(1)}, bf16[16,3200]{1,0:T(8,128)(2,1)S(1)}, u32[]{:S(2)}, u32[]{:S(2)}) %collective-permute-start.8) | collective-permute-done | bytes 102432 | tf_op jit(solution)/shard_map/ppermute | solution.py:242
  40.4 2.4 %collective-permute-done.13.refs_1_ = bf16[16,3200]{1,0:T(8,128)(2,1)S(1)} collective-permute-done((bf16[16,3200]{1,0:T(8,128)(2,1)S(1)}, bf16[16,3200]{1,0:T(8,128)(2,1)S(1)}, u32[]{:S(2)}, u32[]{:S(2)}) %collective-permute-start.13) | collective-permute-done | bytes 102432 | tf_op jit(solution)/shard_map/ppermute | solution.py:242
  42.8 1.3 %collective-permute-done.15.refs_3_ = bf16[16,3200]{1,0:T(8,128)(2,1)S(1)} collective-permute-done((bf16[16,3200]{1,0:T(8,128)(2,1)S(1)}, bf16[16,3200]{1,0:T(8,128)(2,1)S(1)}, u32[]{:S(2)}, u32[]{:S(2)}) %collective-permute-start.15) | collective-permute-done | bytes 102432 | tf_op jit(solution)/shard_map/ppermute | solution.py:238
  44.1 1.3 %combine_far.1 = bf16[128,3584]{1,0:T(8,128)(2,1)} custom-call(bf16[128,128]{1,0:T(8,128)(2,1)S(1)} %get-tuple-element.36.mix_ref, f32[128,3584]{1,0:T(8,128)S(1)} %combine_close.1.close_ref, bf16[16,3200]{1,0:T(8,128)(2,1)S(1)} %collective-permute-done.8.refs_0_, bf16[16,3200]{1,0:T(8,128)(2,1)S(1)} %collective-permute-done.13.refs_1_, ...), custom_call_target="tpu_custom_call" | custom-call | flops 1 | bytes 1 | tf_op jit(solution)/shard_map/combine_far/pallas_call | solution.py:220
  (11 shorter events, 0.0 us)
Async XLA Ops:
  2.0 4.7 %collective-permute-start = (bf16[16,3200]{1,0:T(8,128)(2,1)S(1)}, bf16[16,3200]{1,0:T(8,128)(2,1)S(1)}, u32[]{:S(2)}, u32[]{:S(2)}) collective-permute-start(bf16[16,3200]{1,0:T(8,128)(2,1)S(1)} %get-tuple-element.38), channel_id=1, source_target_pairs={{0,1},{1,0},{2,3},{3,2},{4,5},{5,4},{6,7},{7,6},{8,9},{9,8},{10,11... | collective-permute-start | bytes 307208 | tf_op jit(solution)/shard_map/ppermute | solution.py:238
  2.6 9.3 %collective-permute-start.2 = (bf16[8,3200]{1,0:T(8,128)(2,1)S(1)}, bf16[8,3200]{1,0:T(8,128)(2,1)S(1)}, u32[]{:S(2)}, u32[]{:S(2)}) collective-permute-start(bf16[8,3200]{1,0:T(8,128)(2,1)S(1)} %get-tuple-element.41), channel_id=1, source_target_pairs={{0,2},{1,3},{2,0},{3,1},{4,6},{5,7},{6,4},{7,5},{8,10},{9,11},{10,... | collective-permute-start | bytes 153608 | tf_op jit(solution)/shard_map/ppermute | solution.py:242
  5.2 6.7 %collective-permute-start.3 = (bf16[8,3200]{1,0:T(8,128)(2,1)S(1)}, bf16[8,3200]{1,0:T(8,128)(2,1)S(1)}, u32[]{:S(2)}, u32[]{:S(2)}) collective-permute-start(bf16[8,3200]{1,0:T(8,128)(2,1)S(1)} %get-tuple-element.42), channel_id=1, source_target_pairs={{0,4},{1,5},{2,6},{3,7},{4,0},{5,1},{6,2},{7,3},{8,12},{9,13},{10,... | collective-permute-start | bytes 153608 | tf_op jit(solution)/shard_map/ppermute | solution.py:242
  6.7 5.2 %collective-permute-start.4 = (bf16[8,3200]{1,0:T(8,128)(2,1)S(1)}, bf16[8,3200]{1,0:T(8,128)(2,1)S(1)}, u32[]{:S(2)}, u32[]{:S(2)}) collective-permute-start(bf16[8,3200]{1,0:T(8,128)(2,1)S(1)} %get-tuple-element.43), channel_id=1, source_target_pairs={{0,6},{1,7},{2,4},{3,5},{4,2},{5,3},{6,0},{7,1},{8,14},{9,15},{10,... | collective-permute-start | bytes 153608 | tf_op jit(solution)/shard_map/ppermute | solution.py:242
  6.8 8.1 %collective-permute-start.1 = (bf16[16,3200]{1,0:T(8,128)(2,1)S(1)}, bf16[16,3200]{1,0:T(8,128)(2,1)S(1)}, u32[]{:S(2)}, u32[]{:S(2)}) collective-permute-start(bf16[16,3200]{1,0:T(8,128)(2,1)S(1)} %get-tuple-element.39.refs_0_), channel_id=1, source_target_pairs={{0,8},{1,13},{2,10},{3,15},{4,12},{5,9},{6,14},{7,11},{8,0},{9,5},... | collective-permute-start | bytes 307208 | tf_op jit(solution)/shard_map/ppermute | solution.py:242
  11.9 8.7 %collective-permute-start.5 = (bf16[16,3200]{1,0:T(8,128)(2,1)S(1)}, bf16[16,3200]{1,0:T(8,128)(2,1)S(1)}, u32[]{:S(2)}, u32[]{:S(2)}) collective-permute-start(bf16[16,3200]{1,0:T(8,128)(2,1)S(1)} %get-tuple-element.48), channel_id=1, source_target_pairs={{0,10},{1,15},{2,8},{3,13},{4,14},{5,11},{6,12},{7,9},{8,2},{9,7},... | collective-permute-start | bytes 307208 | tf_op jit(solution)/shard_map/ppermute | solution.py:242
  20.7 2.1 %collective-permute-start.6 = (bf16[64,3584]{1,0:T(8,128)(2,1)S(1)}, bf16[64,3584]{1,0:T(8,128)(2,1)S(1)}, u32[]{:S(2)}, u32[]{:S(2)}) collective-permute-start(bf16[64,3584]{1,0:T(8,128)(2,1)S(1)} %gather.1.refs_0_), channel_id=1, source_target_pairs={{0,1},{1,0},{2,3},{3,2},{4,5},{5,4},{6,7},{7,6},{8,9},{9,8},{10,11... | collective-permute-start | bytes 1376264 | tf_op jit(solution)/shard_map/ppermute | solution.py:238
  24.6 1.8 %collective-permute-start.9 = (bf16[48,3584]{1,0:T(8,128)(2,1)S(1)}, bf16[48,3584]{1,0:T(8,128)(2,1)S(1)}, u32[]{:S(2)}, u32[]{:S(2)}) collective-permute-start(bf16[48,3584]{1,0:T(8,128)(2,1)S(1)} %get-tuple-element.55), channel_id=1, source_target_pairs={{0,1},{1,0},{2,3},{3,2},{4,5},{5,4},{6,7},{7,6},{8,9},{9,8},{10,11... | collective-permute-start | bytes 1032200 | tf_op jit(solution)/shard_map/ppermute | solution.py:238
  25.1 5.0 %collective-permute-start.7 = (bf16[16,3584]{1,0:T(8,128)(2,1)S(1)}, bf16[16,3584]{1,0:T(8,128)(2,1)S(1)}, u32[]{:S(2)}, u32[]{:S(2)}) collective-permute-start(bf16[16,3584]{1,0:T(8,128)(2,1)S(1)} %get-tuple-element.53), channel_id=1, source_target_pairs={{0,1},{1,0},{2,3},{3,2},{4,5},{5,4},{6,7},{7,6},{8,9},{9,8},{10,11... | collective-permute-start | bytes 344072 | tf_op jit(solution)/shard_map/ppermute | solution.py:238
  26.6 5.1 %collective-permute-start.10 = (bf16[8,3200]{1,0:T(8,128)(2,1)S(1)}, bf16[8,3200]{1,0:T(8,128)(2,1)S(1)}, u32[]{:S(2)}, u32[]{:S(2)}) collective-permute-start(bf16[8,3200]{1,0:T(8,128)(2,1)S(1)} %get-tuple-element.57), channel_id=1, source_target_pairs={{0,2},{1,3},{2,0},{3,1},{4,6},{5,7},{6,4},{7,5},{8,10},{9,11},{10,... | collective-permute-start | bytes 153608 | tf_op jit(solution)/shard_map/ppermute | solution.py:242
  28.2 4.3 %collective-permute-start.11 = (bf16[8,3200]{1,0:T(8,128)(2,1)S(1)}, bf16[8,3200]{1,0:T(8,128)(2,1)S(1)}, u32[]{:S(2)}, u32[]{:S(2)}) collective-permute-start(bf16[8,3200]{1,0:T(8,128)(2,1)S(1)} %get-tuple-element.58), channel_id=1, source_target_pairs={{0,4},{1,5},{2,6},{3,7},{4,0},{5,1},{6,2},{7,3},{8,12},{9,13},{10,... | collective-permute-start | bytes 153608 | tf_op jit(solution)/shard_map/ppermute | solution.py:242
  28.2 5.2 %collective-permute-start.12 = (bf16[8,3200]{1,0:T(8,128)(2,1)S(1)}, bf16[8,3200]{1,0:T(8,128)(2,1)S(1)}, u32[]{:S(2)}, u32[]{:S(2)}) collective-permute-start(bf16[8,3200]{1,0:T(8,128)(2,1)S(1)} %get-tuple-element.59), channel_id=1, source_target_pairs={{0,6},{1,7},{2,4},{3,5},{4,2},{5,3},{6,0},{7,1},{8,14},{9,15},{10,... | collective-permute-start | bytes 153608 | tf_op jit(solution)/shard_map/ppermute | solution.py:242
  30.2 10.2 %collective-permute-start.8 = (bf16[16,3200]{1,0:T(8,128)(2,1)S(1)}, bf16[16,3200]{1,0:T(8,128)(2,1)S(1)}, u32[]{:S(2)}, u32[]{:S(2)}) collective-permute-start(bf16[16,3200]{1,0:T(8,128)(2,1)S(1)} %join.2), channel_id=1, source_target_pairs={{0,8},{1,13},{2,10},{3,15},{4,12},{5,9},{6,14},{7,11},{8,0},{9,5},... | collective-permute-start | bytes 307208 | tf_op jit(solution)/shard_map/ppermute | solution.py:242
  33.3 9.5 %collective-permute-start.13 = (bf16[16,3200]{1,0:T(8,128)(2,1)S(1)}, bf16[16,3200]{1,0:T(8,128)(2,1)S(1)}, u32[]{:S(2)}, u32[]{:S(2)}) collective-permute-start(bf16[16,3200]{1,0:T(8,128)(2,1)S(1)} %get-tuple-element.66), channel_id=1, source_target_pairs={{0,10},{1,15},{2,8},{3,13},{4,14},{5,11},{6,12},{7,9},{8,2},{9,7},... | collective-permute-start | bytes 307208 | tf_op jit(solution)/shard_map/ppermute | solution.py:242
  40.4 2.4 %collective-permute-start.14 = (bf16[16,3200]{1,0:T(8,128)(2,1)S(1)}, bf16[16,3200]{1,0:T(8,128)(2,1)S(1)}, u32[]{:S(2)}, u32[]{:S(2)}) collective-permute-start(bf16[16,3200]{1,0:T(8,128)(2,1)S(1)} %collective-permute-done.8.refs_0_), channel_id=1, source_target_pairs={{0,1},{1,0},{2,3},{3,2},{4,5},{5,4},{6,7},{7,6},{8,9},{9,8},{10,11... | collective-permute-start | bytes 307208 | tf_op jit(solution)/shard_map/ppermute | solution.py:238
  42.8 1.3 %collective-permute-start.15 = (bf16[16,3200]{1,0:T(8,128)(2,1)S(1)}, bf16[16,3200]{1,0:T(8,128)(2,1)S(1)}, u32[]{:S(2)}, u32[]{:S(2)}) collective-permute-start(bf16[16,3200]{1,0:T(8,128)(2,1)S(1)} %collective-permute-done.13.refs_1_), channel_id=1, source_target_pairs={{0,1},{1,0},{2,3},{3,2},{4,5},{5,4},{6,7},{7,6},{8,9},{9,8},{10,11... | collective-permute-start | bytes 307208 | tf_op jit(solution)/shard_map/ppermute | solution.py:238

commit v11 on v10

--- a/solution.py
+++ b/solution.py
@@ -10,6 +10,7 @@
 SLOTS = 8
 CHUNKS = 4
 PIECES = 4
+OUT_PIECES = 4
 LANES = 128
 
 VMEM = pl.BlockSpec(memory_space=pltpu.VMEM)
@@ -25,14 +26,14 @@
     return flight == 8
 
 
-CARRIED = ((4, 5), (6, 7))
-NEAR = (1, 2, 3)
+CARRIED = ((4, 1, 5), (6, 2, 7))
+SHARED = 3
 
 
 def block_order(flight, core):
     if not relative(flight):
         return range(flight)
-    return CARRIED[core] + CARRIED[1 - core] + NEAR + (0,)
+    return CARRIED[core] + CARRIED[1 - core] + (SHARED, 0)
 
 
 def packed_width(width):
@@ -177,36 +178,28 @@
     store(outs, pack(mine_ref[...].astype(jnp.float32) + got_ref[...].astype(jnp.float32)))
 
 
-def weigh(mix, rows):
-    rows = unpack(rows).astype(jnp.bfloat16)
+def combine_kernel(first, mix_ref, *refs):
+    *refs, out_hbm, out, sems = refs
+    blocks = [r[...].astype(jnp.float32) for r in refs]
+    if first:
+        blocks = [b[at * SLOTS : (at + 1) * SLOTS] for b, at in zip(blocks, first)]
+    rows = unpack(jnp.concatenate(blocks, axis=0)).astype(jnp.bfloat16)
     both = jnp.concatenate([rows, rows], axis=0)
-    return lax.dot_general(mix, both, (((0,), (0,)), ((), ())), preferred_element_type=jnp.float32)
-
-
-def mix_rows(mix_ref, start, count):
-    half = mix_ref.shape[0] // 2
-    return jnp.concatenate([mix_ref[at + start : at + start + count, :] for at in (0, half)], axis=0)
-
-
-def close_kernel(mix_ref, *refs):
-    *refs, out_ref = refs
-    rows = together(refs)
-    out_ref[...] = weigh(mix_rows(mix_ref, mix_ref.shape[0] // 2 - rows.shape[0], rows.shape[0]), rows)
-
-
-def far_kernel(first, mix_ref, close_ref, *refs):
-    *refs, out_ref = refs
-    blocks = [
-        r[...].astype(jnp.float32)[at * SLOTS : (at + 1) * SLOTS] for r, at in zip(refs, first)
-    ]
-    rows = jnp.concatenate(blocks, axis=0)
-    out_ref[...] = (
-        close_ref[...] + weigh(mix_rows(mix_ref, 0, rows.shape[0]), rows)
-    ).astype(jnp.bfloat16)
-
-
-def combine_kernel(mix_ref, rows_ref, out_ref):
-    out_ref[...] = weigh(mix_ref[...], rows_ref[...].astype(jnp.float32)).astype(jnp.bfloat16)
+    mix = mix_ref[...]
+    part = out.shape[1] // OUT_PIECES
+    copies = []
+    for i in range(OUT_PIECES):
+        here = pl.ds(i * part, part)
+        out[:, here] = lax.dot_general(
+            mix,
+            both[:, i * part : (i + 1) * part],
+            (((0,), (0,)), ((), ())),
+            preferred_element_type=jnp.float32,
+        ).astype(jnp.bfloat16)
+        copies.append(pltpu.make_async_copy(out.at[:, here], out_hbm.at[:, here], sems.at[i]))
+        copies[-1].start()
+    for copy in copies:
+        copy.wait()
 
 
 def per_device(tokens, norm_gain, expert_ids, gate_weights, w_gate, w_up, w_down):
@@ -264,8 +257,21 @@
             limit=24,
         )
 
-    result = (jax.ShapeDtypeStruct((count, width), jnp.bfloat16),)
-    first = packed(2, 2, 1, 1, 1, 1) if few else packed(flight)
+    def combine(mix, arrays, first):
+        return pl.pallas_call(
+            functools.partial(combine_kernel, first),
+            out_shape=jax.ShapeDtypeStruct((count, width), jnp.bfloat16),
+            in_specs=[VMEM] * (len(arrays) + 1),
+            out_specs=HBM,
+            scratch_shapes=[
+                pltpu.VMEM((count, width), jnp.bfloat16),
+                pltpu.SemaphoreType.DMA((OUT_PIECES,)),
+            ],
+            compiler_params=pltpu.CompilerParams(vmem_limit_bytes=24 * 2**20),
+            name="combine",
+        )(mix, *arrays)
+
+    first = packed(3, 3, 1, 1) if few else packed(flight)
     mix, *outgoing = pl.pallas_call(
         functools.partial(dispatch_kernel, flight),
         out_shape=(jax.ShapeDtypeStruct((2 * flight * SLOTS, count), jnp.bfloat16),) + first,
@@ -282,10 +288,9 @@
         compiler_params=pltpu.CompilerParams(vmem_limit_bytes=24 * 2**20),
         name="dispatch",
     )(*in_hbm(tokens, norm_gain, expert_ids.T, gate_weights.T))
-    down = stage(w_down[0])
+    gate, up, down = stage(w_gate[0]), stage(w_up[0]), stage(w_down[0])
 
     if not few:
-        gate, up = stage(w_gate[0]), stage(w_up[0])
         groups = [list(range(core, owners, 2)) for core in range(2)]
         exchange = functools.partial(
             lax.all_to_all,
@@ -298,35 +303,28 @@
         (own,) = local(gather_kernel, full(flight), "gather", exchange(outgoing[0]))
         mine, theirs = experts([own], [swap(own)], (gate, up, down), full(flight, flight))
         (joined,) = local(join_kernel, packed(flight), "join", mine, swap(theirs))
-        return local(combine_kernel, result, "combine", mix, exchange(joined), limit=24)[0]
-
-    near = [(r, r) for r in NEAR]
-    one, two = zip(*CARRIED)
-    kept, given, *close, own = outgoing
-    far = local(merge_kernel, packed(2, 2), "merge", kept, swap(given))
-    gate = stage(w_gate[0], far[0])
-    far_one = travel(far[0], one)
-    close = [travel(a, r) for a, r in zip(close, near)]
-    far_two, gate, *close = lax.optimization_barrier((far[1], gate, *close))
-    up = stage(w_up[0], far_one)
-    far_two = travel(far_two, two)
-    far_two, up = lax.optimization_barrier((far_two, up))
-    (own,) = local(gather_kernel, full(8), "gather", far_one, *close, own, far_two)
-    mine_one, mine, theirs_one, theirs = experts(
-        [own], [swap(own)], (gate, up, down), full(2, 6, 2, 6)
+        return combine(mix, [exchange(joined)], None)
+
+    one, two, three = zip(*CARRIED)
+    four = (SHARED, SHARED)
+    kept, given, shared, own = outgoing
+    pairs = local(merge_kernel, packed(2, 2, 2), "merge", kept, swap(given))
+    arrived = [travel(a, r) for a, r in zip((*pairs, shared), (one, two, three, four))]
+    *arrived, gate, up = lax.optimization_barrier((*arrived, gate, up))
+    (own,) = local(gather_kernel, full(8), "gather", *arrived, own)
+
+    mine_one, mine_two, theirs_one, theirs_two = experts(
+        [own], [swap(own)], (gate, up, down), full(4, 4, 4, 4)
     )
-    (far_one,) = local(join_kernel, packed(2), "join", mine_one, swap(theirs_one))
-    far_one = travel(far_one, one)
-    *close, own, far_two = local(join_kernel, packed(1, 1, 1, 1, 2), "join", mine, swap(theirs))
-    close = [travel(a, r) for a, r in zip(close, near)]
-    far_two, *close = lax.optimization_barrier((far_two, *close))
-    far_two = travel(far_two, two)
-    total = (jax.ShapeDtypeStruct((count, width), jnp.float32),)
-    (total,) = local(close_kernel, total, "combine_close", mix, *close, own, limit=24)
-    far_one, total = lax.optimization_barrier((far_one, total))
-    arrays = [far_one, far_two, swap(far_one), swap(far_two)]
-    kernel = functools.partial(far_kernel, (0, 0, 1, 1))
-    return local(kernel, result, "combine_far", mix, total, *arrays, limit=24)[0]
+    first, second = local(join_kernel, packed(2, 2), "join", mine_one, swap(theirs_one))
+    third, shared, own = local(join_kernel, packed(2, 1, 1), "join", mine_two, swap(theirs_two))
+    returned = [
+        travel(a, r) for a, r in zip((first, second, third, shared), (one, two, three, four))
+    ]
+    *pairs, shared = returned
+    pairs[0], shared = lax.optimization_barrier((pairs[0], shared))
+    arrays = [*pairs, *[swap(a) for a in pairs], shared, own]
+    return combine(mix, arrays, (0, 0, 0, 1, 1, 1, 0, 0))
 
 
 def solution(mesh):

time: 45.6 us -> 38.9 us (0.85)
  starting transfers between devices: 20.1 us -> 15.5 us
  waiting for transfers between devices: 13.3 us -> 11.7 us
  Pallas kernels: 11.9 us -> 11.4 us
    ppermute x10 -> x8, starting transfers between devices: 18.9 us -> 13.7 us  [travel(): return lax.ppermute(rows, 'exp', pairs)]
    ppermute x10 -> x8, waiting for transfers between devices: 10.8 us -> 8.48 us  [travel(): return lax.ppermute(rows, 'exp', pairs)]
    pallas_call x7 -> x5, Pallas kernels: 3.78 us -> 2.05 us  [local(): pl.pallas_call(kernel, out_shape=outs, in_specs=[VMEM] * len(args), out_s...]
    pallas_call x0 -> x1, Pallas kernels: none -> 1.21 us  [combine(): pl.pallas_call(functools.partial(combine_kernel, first), out_shape=jax.Sh...]
    ppermute x6 -> x7, waiting for transfers between devices: 2.51 us -> 3.23 us  [swap(): return lax.ppermute(rows, 'exp', [(n, n ^ 1) for n in range(owners)])]
    ppermute x6 -> x7, starting transfers between devices: 1.23 us -> 1.85 us  [swap(): return lax.ppermute(rows, 'exp', [(n, n ^ 1) for n in range(owners)])]
  transfers between devices with their start and end apart: 16 -> 15, of which waited for: 7 -> 8; matrix products, arithmetic and copies ran while one was open for 0% -> 0% of each run, Pallas kernels for 15% -> 16%
where the time goes in v11:
time: 38.9 us; the launch traced here: 38.7 us
  starting transfers between devices  15.5 us (40%)
  waiting for transfers between devices  11.7 us (30%)
  Pallas kernels  11.4 us (29%)
    ppermute x8, starting transfers between devices, travel(): return lax.ppermute(rows, 'exp', pairs)  13.7 us
    ppermute x8, waiting for transfers between devices, travel(): return lax.ppermute(rows, 'exp', pairs)  8.48 us
    pallas_call x3, Pallas kernels, stage(): pl.pallas_call(stage_kernel, out_shape=jax.ShapeDtypeStruct(weights.shape...  6.13 us
    ppermute x7, waiting for transfers between devices, swap(): return lax.ppermute(rows, 'exp', [(n, n ^ 1) for n in range(owners)])  3.23 us
    pallas_call x5, Pallas kernels, local(): pl.pallas_call(kernel, out_shape=outs, in_specs=[VMEM] * len(args), out_s...  2.05 us
    pallas_call x1, Pallas kernels, per_device(): pl.pallas_call(functools.partial(dispatch_kernel, flight), out_shape=(jax...  2.03 us
    ppermute x7, starting transfers between devices, swap(): return lax.ppermute(rows, 'exp', [(n, n ^ 1) for n in range(owners)])  1.85 us
    pallas_call x1, Pallas kernels, combine(): pl.pallas_call(functools.partial(combine_kernel, first), out_shape=jax.Sh...  1.21 us
  transfers between devices with their start and end apart: 15, of which 8 were waited for; matrix products, arithmetic and copies ran while one was open for 0% of the time, Pallas kernels for 16%

profile of v11, /device:TPU:0, one launch (start us, length us, event | category | flops | bytes accessed | tf_op | source)
XLA Modules:
  0.0 38.7 jit_solution(14264958786418996759)
XLA Ops:
  0.0 2.0 %dispatch.1 = (bf16[128,128]{1,0:T(8,128)(2,1)S(1)}, bf16[24,3200]{1,0:T(8,128)(2,1)S(1)}, bf16[24,3200]{1,0:T(8,128)(2,1)S(1)}, bf16[8,3200]{1,0:T(8,128)(2,1)S(1)}, bf16[8,3200]{1,0:T(8,128)(2,1)S(1)}) custom-call(bf16[128,3584]{1,0:T(8,128)(2,1)} %tok_hbm.1, f32[3584]{0:T(1024)} %gain_hbm.1, s32[8,128]{1,0:T(8,128)} %bitcast.8, f32[8,128]{1,0:T(8,128)} %bitcast.9), custom_call_target="tpu_custom_call" | custom-call | tf_op jit(solution)/shard_map/dispatch/pallas_call | solution.py:275
  2.0 0.5 %collective-permute-start = (bf16[24,3200]{1,0:T(8,128)(2,1)S(1)}, bf16[24,3200]{1,0:T(8,128)(2,1)S(1)}, u32[]{:S(2)}, u32[]{:S(2)}) collective-permute-start(bf16[24,3200]{1,0:T(8,128)(2,1)S(1)} %get-tuple-element.32), channel_id=1, source_target_pairs={{0,1},{1,0},{2,3},{3,2},{4,5},{5,4},{6,7},{7,6},{8,9},{9,8},{10,11... | collective-permute-start | bytes 460808 | tf_op jit(solution)/shard_map/ppermute | solution.py:231
  2.6 1.0 %collective-permute-done.got_ref = bf16[24,3200]{1,0:T(8,128)(2,1)S(1)} collective-permute-done((bf16[24,3200]{1,0:T(8,128)(2,1)S(1)}, bf16[24,3200]{1,0:T(8,128)(2,1)S(1)}, u32[]{:S(2)}, u32[]{:S(2)}) %collective-permute-start) | collective-permute-done | bytes 153632 | tf_op jit(solution)/shard_map/ppermute | solution.py:231
  3.6 4.0 %collective-permute-start.1 = (bf16[16,3200]{1,0:T(8,128)(2,1)S(1)}, bf16[16,3200]{1,0:T(8,128)(2,1)S(1)}, u32[]{:S(2)}, u32[]{:S(2)}) collective-permute-start(bf16[16,3200]{1,0:T(8,128)(2,1)S(1)} %get-tuple-element.33), channel_id=1, source_target_pairs={{0,8},{1,13},{2,10},{3,15},{4,12},{5,9},{6,14},{7,11},{8,0},{9,5},... | collective-permute-start | bytes 307208 | tf_op jit(solution)/shard_map/ppermute | solution.py:235
  7.6 1.5 %collective-permute-start.2 = (bf16[16,3200]{1,0:T(8,128)(2,1)S(1)}, bf16[16,3200]{1,0:T(8,128)(2,1)S(1)}, u32[]{:S(2)}, u32[]{:S(2)}) collective-permute-start(bf16[16,3200]{1,0:T(8,128)(2,1)S(1)} %get-tuple-element.34), channel_id=1, source_target_pairs={{0,2},{1,5},{2,0},{3,7},{4,6},{5,1},{6,4},{7,3},{8,10},{9,13},{10,... | collective-permute-start | bytes 307208 | tf_op jit(solution)/shard_map/ppermute | solution.py:235
  9.1 0.0 collective-permute-start.3
  9.2 2.8 %collective-permute-start.4 = (bf16[8,3200]{1,0:T(8,128)(2,1)S(1)}, bf16[8,3200]{1,0:T(8,128)(2,1)S(1)}, u32[]{:S(2)}, u32[]{:S(2)}) collective-permute-start(bf16[8,3200]{1,0:T(8,128)(2,1)S(1)} %get-tuple-element.36), channel_id=1, source_target_pairs={{0,6},{1,7},{2,4},{3,5},{4,2},{5,3},{6,0},{7,1},{8,14},{9,15},{10,... | collective-permute-start | bytes 153608 | tf_op jit(solution)/shard_map/ppermute | solution.py:235
  11.9 2.0 %stage.3.refs_2_ = bf16[3584,512]{1,0:T(8,128)(2,1)S(1)} custom-call(bf16[3584,512]{1,0:T(8,128)(2,1)} %bitcast.5), custom_call_target="tpu_custom_call" | custom-call | flops 1 | bytes 1 | tf_op jit(solution)/shard_map/stage/pallas_call | solution.py:238
  14.0 2.0 %stage.4.refs_3_ = bf16[3584,512]{1,0:T(8,128)(2,1)S(1)} custom-call(bf16[3584,512]{1,0:T(8,128)(2,1)} %bitcast.6), custom_call_target="tpu_custom_call" | custom-call | flops 1 | bytes 1 | tf_op jit(solution)/shard_map/stage/pallas_call | solution.py:238
  16.1 0.3 collective-permute-done.4.refs_3_
  16.3 2.2 %collective-permute-done.3.refs_2_ = bf16[16,3200]{1,0:T(8,128)(2,1)S(1)} collective-permute-done((bf16[16,3200]{1,0:T(8,128)(2,1)S(1)}, bf16[16,3200]{1,0:T(8,128)(2,1)S(1)}, u32[]{:S(2)}, u32[]{:S(2)}) %collective-permute-start.3) | collective-permute-done | bytes 102432 | tf_op jit(solution)/shard_map/ppermute | solution.py:235
  18.6 0.1 gather.1.refs_0_
  18.7 0.1 collective-permute-start.5
  18.7 2.0 %stage.5.refs_4_ = bf16[512,3584]{1,0:T(8,128)(2,1)S(1)} custom-call(bf16[512,3584]{1,0:T(8,128)(2,1)} %bitcast.7), custom_call_target="tpu_custom_call" | custom-call | flops 1 | bytes 1 | tf_op jit(solution)/shard_map/stage/pallas_call | solution.py:238
  20.8 1.7 %experts.1 = (bf16[32,3584]{1,0:T(8,128)(2,1)S(1)}, bf16[32,3584]{1,0:T(8,128)(2,1)S(1)}, bf16[32,3584]{1,0:T(8,128)(2,1)S(1)}, bf16[32,3584]{1,0:T(8,128)(2,1)S(1)}) custom-call(bf16[64,3584]{1,0:T(8,128)(2,1)S(1)} %gather.1.refs_0_, bf16[64,3584]{1,0:T(8,128)(2,1)S(1)} %collective-permute-done.5.refs_1_, bf16[3584,512]{1,0:T(8,128)(2,1)S(1)} %stage.3.refs_2_, ...), custom_call_target="tpu_custom_call" | custom-call | flops 1 | bytes 1 | tf_op jit(solution)/shard_map/experts/pallas_call | solution.py:213
  22.5 0.5 %collective-permute-start.6 = (bf16[32,3584]{1,0:T(8,128)(2,1)S(1)}, bf16[32,3584]{1,0:T(8,128)(2,1)S(1)}, u32[]{:S(2)}, u32[]{:S(2)}) collective-permute-start(bf16[32,3584]{1,0:T(8,128)(2,1)S(1)} %get-tuple-element.45), channel_id=1, source_target_pairs={{0,1},{1,0},{2,3},{3,2},{4,5},{5,4},{6,7},{7,6},{8,9},{9,8},{10,11... | collective-permute-start | bytes 688136 | tf_op jit(solution)/shard_map/ppermute | solution.py:231
  23.1 0.1 collective-permute-start.8
  23.2 1.0 %collective-permute-done.6.got_ref = bf16[32,3584]{1,0:T(8,128)(2,1)S(1)} collective-permute-done((bf16[32,3584]{1,0:T(8,128)(2,1)S(1)}, bf16[32,3584]{1,0:T(8,128)(2,1)S(1)}, u32[]{:S(2)}, u32[]{:S(2)}) %collective-permute-start.6) | collective-permute-done | bytes 229408 | tf_op jit(solution)/shard_map/ppermute | solution.py:231
  24.2 0.1 join.2
  24.3 0.8 %collective-permute-start.7 = (bf16[16,3200]{1,0:T(8,128)(2,1)S(1)}, bf16[16,3200]{1,0:T(8,128)(2,1)S(1)}, u32[]{:S(2)}, u32[]{:S(2)}) collective-permute-start(bf16[16,3200]{1,0:T(8,128)(2,1)S(1)} %get-tuple-element.46), channel_id=1, source_target_pairs={{0,8},{1,13},{2,10},{3,15},{4,12},{5,9},{6,14},{7,11},{8,0},{9,5},... | collective-permute-start | bytes 307208 | tf_op jit(solution)/shard_map/ppermute | solution.py:235
  25.1 0.5 %collective-permute-start.10 = (bf16[16,3200]{1,0:T(8,128)(2,1)S(1)}, bf16[16,3200]{1,0:T(8,128)(2,1)S(1)}, u32[]{:S(2)}, u32[]{:S(2)}) collective-permute-start(bf16[16,3200]{1,0:T(8,128)(2,1)S(1)} %get-tuple-element.51), channel_id=1, source_target_pairs={{0,2},{1,5},{2,0},{3,7},{4,6},{5,1},{6,4},{7,3},{8,10},{9,13},{10,... | collective-permute-start | bytes 307208 | tf_op jit(solution)/shard_map/ppermute | solution.py:235
  25.7 0.1 join.3
  25.8 3.1 %collective-permute-start.11 = (bf16[16,3200]{1,0:T(8,128)(2,1)S(1)}, bf16[16,3200]{1,0:T(8,128)(2,1)S(1)}, u32[]{:S(2)}, u32[]{:S(2)}) collective-permute-start(bf16[16,3200]{1,0:T(8,128)(2,1)S(1)} %get-tuple-element.52), channel_id=1, source_target_pairs={{0,10},{1,15},{2,8},{3,13},{4,14},{5,11},{6,12},{7,9},{8,2},{9,7},... | collective-permute-start | bytes 307208 | tf_op jit(solution)/shard_map/ppermute | solution.py:235
  28.9 0.8 %collective-permute-start.9 = (bf16[8,3200]{1,0:T(8,128)(2,1)S(1)}, bf16[8,3200]{1,0:T(8,128)(2,1)S(1)}, u32[]{:S(2)}, u32[]{:S(2)}) collective-permute-start(bf16[8,3200]{1,0:T(8,128)(2,1)S(1)} %get-tuple-element.49), channel_id=1, source_target_pairs={{0,6},{1,7},{2,4},{3,5},{4,2},{5,3},{6,0},{7,1},{8,14},{9,15},{10,... | collective-permute-start | bytes 153608 | tf_op jit(solution)/shard_map/ppermute | solution.py:235
  29.7 5.8 %collective-permute-done.9.refs_6_ = bf16[8,3200]{1,0:T(8,128)(2,1)S(1)} collective-permute-done((bf16[8,3200]{1,0:T(8,128)(2,1)S(1)}, bf16[8,3200]{1,0:T(8,128)(2,1)S(1)}, u32[]{:S(2)}, u32[]{:S(2)}) %collective-permute-start.9) | collective-permute-done | bytes 51232 | tf_op jit(solution)/shard_map/ppermute | solution.py:235
  35.6 0.3 collective-permute-start.12
  35.8 0.2 collective-permute-start.13
  36.1 0.1 collective-permute-done.11.refs_2_
  36.2 0.1 collective-permute-start.14
  36.3 0.8 %collective-permute-done.13.refs_4_ = bf16[16,3200]{1,0:T(8,128)(2,1)S(1)} collective-permute-done((bf16[16,3200]{1,0:T(8,128)(2,1)S(1)}, bf16[16,3200]{1,0:T(8,128)(2,1)S(1)}, u32[]{:S(2)}, u32[]{:S(2)}) %collective-permute-start.13) | collective-permute-done | bytes 102432 | tf_op jit(solution)/shard_map/ppermute | solution.py:231
  37.1 0.4 collective-permute-done.14.refs_5_
  37.5 1.2 %combine.1 = bf16[128,3584]{1,0:T(8,128)(2,1)} custom-call(bf16[128,128]{1,0:T(8,128)(2,1)S(1)} %get-tuple-element.30.mix_ref, bf16[16,3200]{1,0:T(8,128)(2,1)S(1)} %collective-permute-done.7.refs_0_, bf16[16,3200]{1,0:T(8,128)(2,1)S(1)} %collective-permute-done.10.refs_1_, bf16[16,3200]{1,0:T(8,128)(2,1)S(1)} %collective-permute-done.11.refs_2_, ...), custom_call_target="tpu_custom_call" | custom-call | tf_op jit(solution)/shard_map/combine/pallas_call | solution.py:261
  (8 shorter events, 0.0 us)
Async XLA Ops:
  2.0 1.5 %collective-permute-start = (bf16[24,3200]{1,0:T(8,128)(2,1)S(1)}, bf16[24,3200]{1,0:T(8,128)(2,1)S(1)}, u32[]{:S(2)}, u32[]{:S(2)}) collective-permute-start(bf16[24,3200]{1,0:T(8,128)(2,1)S(1)} %get-tuple-element.32), channel_id=1, source_target_pairs={{0,1},{1,0},{2,3},{3,2},{4,5},{5,4},{6,7},{7,6},{8,9},{9,8},{10,11... | collective-permute-start | bytes 460808 | tf_op jit(solution)/shard_map/ppermute | solution.py:231
  3.6 12.7 %collective-permute-start.1 = (bf16[16,3200]{1,0:T(8,128)(2,1)S(1)}, bf16[16,3200]{1,0:T(8,128)(2,1)S(1)}, u32[]{:S(2)}, u32[]{:S(2)}) collective-permute-start(bf16[16,3200]{1,0:T(8,128)(2,1)S(1)} %get-tuple-element.33), channel_id=1, source_target_pairs={{0,8},{1,13},{2,10},{3,15},{4,12},{5,9},{6,14},{7,11},{8,0},{9,5},... | collective-permute-start | bytes 307208 | tf_op jit(solution)/shard_map/ppermute | solution.py:235
  7.6 8.7 %collective-permute-start.2 = (bf16[16,3200]{1,0:T(8,128)(2,1)S(1)}, bf16[16,3200]{1,0:T(8,128)(2,1)S(1)}, u32[]{:S(2)}, u32[]{:S(2)}) collective-permute-start(bf16[16,3200]{1,0:T(8,128)(2,1)S(1)} %get-tuple-element.34), channel_id=1, source_target_pairs={{0,2},{1,5},{2,0},{3,7},{4,6},{5,1},{6,4},{7,3},{8,10},{9,13},{10,... | collective-permute-start | bytes 307208 | tf_op jit(solution)/shard_map/ppermute | solution.py:235
  9.1 9.4 %collective-permute-start.3 = (bf16[16,3200]{1,0:T(8,128)(2,1)S(1)}, bf16[16,3200]{1,0:T(8,128)(2,1)S(1)}, u32[]{:S(2)}, u32[]{:S(2)}) collective-permute-start(bf16[16,3200]{1,0:T(8,128)(2,1)S(1)} %get-tuple-element.35), channel_id=1, source_target_pairs={{0,10},{1,15},{2,8},{3,13},{4,14},{5,11},{6,12},{7,9},{8,2},{9,7},... | collective-permute-start | bytes 307208 | tf_op jit(solution)/shard_map/ppermute | solution.py:235
  9.2 7.1 %collective-permute-start.4 = (bf16[8,3200]{1,0:T(8,128)(2,1)S(1)}, bf16[8,3200]{1,0:T(8,128)(2,1)S(1)}, u32[]{:S(2)}, u32[]{:S(2)}) collective-permute-start(bf16[8,3200]{1,0:T(8,128)(2,1)S(1)} %get-tuple-element.36), channel_id=1, source_target_pairs={{0,6},{1,7},{2,4},{3,5},{4,2},{5,3},{6,0},{7,1},{8,14},{9,15},{10,... | collective-permute-start | bytes 153608 | tf_op jit(solution)/shard_map/ppermute | solution.py:235
  18.7 2.1 %collective-permute-start.5 = (bf16[64,3584]{1,0:T(8,128)(2,1)S(1)}, bf16[64,3584]{1,0:T(8,128)(2,1)S(1)}, u32[]{:S(2)}, u32[]{:S(2)}) collective-permute-start(bf16[64,3584]{1,0:T(8,128)(2,1)S(1)} %gather.1.refs_0_), channel_id=1, source_target_pairs={{0,1},{1,0},{2,3},{3,2},{4,5},{5,4},{6,7},{7,6},{8,9},{9,8},{10,11... | collective-permute-start | bytes 1376264 | tf_op jit(solution)/shard_map/ppermute | solution.py:231
  22.5 1.7 %collective-permute-start.6 = (bf16[32,3584]{1,0:T(8,128)(2,1)S(1)}, bf16[32,3584]{1,0:T(8,128)(2,1)S(1)}, u32[]{:S(2)}, u32[]{:S(2)}) collective-permute-start(bf16[32,3584]{1,0:T(8,128)(2,1)S(1)} %get-tuple-element.45), channel_id=1, source_target_pairs={{0,1},{1,0},{2,3},{3,2},{4,5},{5,4},{6,7},{7,6},{8,9},{9,8},{10,11... | collective-permute-start | bytes 688136 | tf_op jit(solution)/shard_map/ppermute | solution.py:231
  23.1 2.6 %collective-permute-start.8 = (bf16[32,3584]{1,0:T(8,128)(2,1)S(1)}, bf16[32,3584]{1,0:T(8,128)(2,1)S(1)}, u32[]{:S(2)}, u32[]{:S(2)}) collective-permute-start(bf16[32,3584]{1,0:T(8,128)(2,1)S(1)} %get-tuple-element.48), channel_id=1, source_target_pairs={{0,1},{1,0},{2,3},{3,2},{4,5},{5,4},{6,7},{7,6},{8,9},{9,8},{10,11... | collective-permute-start | bytes 688136 | tf_op jit(solution)/shard_map/ppermute | solution.py:231
  24.3 11.3 %collective-permute-start.7 = (bf16[16,3200]{1,0:T(8,128)(2,1)S(1)}, bf16[16,3200]{1,0:T(8,128)(2,1)S(1)}, u32[]{:S(2)}, u32[]{:S(2)}) collective-permute-start(bf16[16,3200]{1,0:T(8,128)(2,1)S(1)} %get-tuple-element.46), channel_id=1, source_target_pairs={{0,8},{1,13},{2,10},{3,15},{4,12},{5,9},{6,14},{7,11},{8,0},{9,5},... | collective-permute-start | bytes 307208 | tf_op jit(solution)/shard_map/ppermute | solution.py:235
  25.1 10.7 %collective-permute-start.10 = (bf16[16,3200]{1,0:T(8,128)(2,1)S(1)}, bf16[16,3200]{1,0:T(8,128)(2,1)S(1)}, u32[]{:S(2)}, u32[]{:S(2)}) collective-permute-start(bf16[16,3200]{1,0:T(8,128)(2,1)S(1)} %get-tuple-element.51), channel_id=1, source_target_pairs={{0,2},{1,5},{2,0},{3,7},{4,6},{5,1},{6,4},{7,3},{8,10},{9,13},{10,... | collective-permute-start | bytes 307208 | tf_op jit(solution)/shard_map/ppermute | solution.py:235
  25.8 10.4 %collective-permute-start.11 = (bf16[16,3200]{1,0:T(8,128)(2,1)S(1)}, bf16[16,3200]{1,0:T(8,128)(2,1)S(1)}, u32[]{:S(2)}, u32[]{:S(2)}) collective-permute-start(bf16[16,3200]{1,0:T(8,128)(2,1)S(1)} %get-tuple-element.52), channel_id=1, source_target_pairs={{0,10},{1,15},{2,8},{3,13},{4,14},{5,11},{6,12},{7,9},{8,2},{9,7},... | collective-permute-start | bytes 307208 | tf_op jit(solution)/shard_map/ppermute | solution.py:235
  28.9 6.6 %collective-permute-start.9 = (bf16[8,3200]{1,0:T(8,128)(2,1)S(1)}, bf16[8,3200]{1,0:T(8,128)(2,1)S(1)}, u32[]{:S(2)}, u32[]{:S(2)}) collective-permute-start(bf16[8,3200]{1,0:T(8,128)(2,1)S(1)} %get-tuple-element.49), channel_id=1, source_target_pairs={{0,6},{1,7},{2,4},{3,5},{4,2},{5,3},{6,0},{7,1},{8,14},{9,15},{10,... | collective-permute-start | bytes 153608 | tf_op jit(solution)/shard_map/ppermute | solution.py:235
  35.6 1.6 %collective-permute-start.12 = (bf16[16,3200]{1,0:T(8,128)(2,1)S(1)}, bf16[16,3200]{1,0:T(8,128)(2,1)S(1)}, u32[]{:S(2)}, u32[]{:S(2)}) collective-permute-start(bf16[16,3200]{1,0:T(8,128)(2,1)S(1)} %collective-permute-done.7.refs_0_), channel_id=1, source_target_pairs={{0,1},{1,0},{2,3},{3,2},{4,5},{5,4},{6,7},{7,6},{8,9},{9,8},{10,11... | collective-permute-start | bytes 307208 | tf_op jit(solution)/shard_map/ppermute | solution.py:231
  35.8 1.3 %collective-permute-start.13 = (bf16[16,3200]{1,0:T(8,128)(2,1)S(1)}, bf16[16,3200]{1,0:T(8,128)(2,1)S(1)}, u32[]{:S(2)}, u32[]{:S(2)}) collective-permute-start(bf16[16,3200]{1,0:T(8,128)(2,1)S(1)} %collective-permute-done.10.refs_1_), channel_id=1, source_target_pairs={{0,1},{1,0},{2,3},{3,2},{4,5},{5,4},{6,7},{7,6},{8,9},{9,8},{10,11... | collective-permute-start | bytes 307208 | tf_op jit(solution)/shard_map/ppermute | solution.py:231
  36.2 1.3 %collective-permute-start.14 = (bf16[16,3200]{1,0:T(8,128)(2,1)S(1)}, bf16[16,3200]{1,0:T(8,128)(2,1)S(1)}, u32[]{:S(2)}, u32[]{:S(2)}) collective-permute-start(bf16[16,3200]{1,0:T(8,128)(2,1)S(1)} %collective-permute-done.11.refs_2_), channel_id=1, source_target_pairs={{0,1},{1,0},{2,3},{3,2},{4,5},{5,4},{6,7},{7,6},{8,9},{9,8},{10,11... | collective-permute-start | bytes 307208 | tf_op jit(solution)/shard_map/ppermute | solution.py:231

commit v12 on v11

--- a/solution.py
+++ b/solution.py
@@ -131,18 +131,26 @@
             wide * lax.rsqrt(mean_square + 1e-06) * gain[...]
         ).astype(jnp.bfloat16)
     rows = jnp.dot(pick, normed[...], preferred_element_type=jnp.float32)
-    store(outs, pack(rows))
-
-
-def stage_kernel(source, *refs):
-    target, sems = refs[-2:]
-    rows = source.shape[0] // PIECES
-    copies = [
-        pltpu.make_async_copy(
-            source.at[pl.ds(i * rows, rows)], target.at[pl.ds(i * rows, rows)], sems.at[i]
-        )
-        for i in range(PIECES)
-    ]
+    blocks = pack(rows)
+    if len(outs) == 1:
+        store(outs, blocks)
+    else:
+        kept, given = 3 * SLOTS, 6 * SLOTS
+        store(outs[:1], blocks[:kept])
+        store(outs[1:2], jnp.concatenate([blocks[kept:given], blocks[given + SLOTS :]], axis=0))
+        store(outs[2:], blocks[given:])
+
+
+def stage_kernel(*refs):
+    sources, targets, sems = refs[:3], refs[-4:-1], refs[-1]
+    copies = []
+    for at, (source, target) in enumerate(zip(sources, targets)):
+        rows = source.shape[0] // PIECES
+        for i in range(PIECES):
+            here = pl.ds(i * rows, rows)
+            copies.append(
+                pltpu.make_async_copy(source.at[here], target.at[here], sems.at[at * PIECES + i])
+            )
     for copy in copies:
         copy.start()
     for copy in copies:
@@ -154,24 +162,22 @@
 
 
 def merge_kernel(kept_ref, got_ref, *outs):
+    *outs, own_out = outs
     kept, got = kept_ref[...].astype(jnp.float32), got_ref[...].astype(jnp.float32)
     for i, out in enumerate(outs):
         here = slice(i * SLOTS, (i + 1) * SLOTS)
         out[...] = jnp.concatenate([kept[here], got[here]], axis=0).astype(jnp.bfloat16)
-
-
-def gather_kernel(*refs):
-    refs[-1][...] = unpack(together(refs[:-1])).astype(jnp.bfloat16)
-
-
-def expert_kernel(count, *refs):
-    rows, weights, outs = refs[: 2 * count], refs[2 * count : 2 * count + 3], refs[2 * count + 3 :]
-    gate_ref, up_ref, down_ref = weights
-    x = jnp.concatenate([r[...] for r in rows], axis=0)
+    own_out[...] = got[len(outs) * SLOTS :].astype(jnp.bfloat16)
+
+
+def expert_kernel(*refs):
+    *rows, gate_ref, up_ref, down_ref, own_one, own_two, other_one, other_two = refs
+    x = unpack(together(rows)).astype(jnp.bfloat16)
     gate_v = jnp.dot(x, gate_ref[...], preferred_element_type=jnp.float32)
     up_v = jnp.dot(x, up_ref[...], preferred_element_type=jnp.float32)
     hidden = (gate_v / (1.0 + jnp.exp(-gate_v)) * up_v).astype(jnp.bfloat16)
-    store(outs, jnp.dot(hidden, down_ref[...], preferred_element_type=jnp.float32))
+    part = jnp.dot(hidden, down_ref[...], preferred_element_type=jnp.float32)
+    store((own_one, own_two, other_one, other_two), part)
 
 
 def join_kernel(mine_ref, got_ref, *outs):
@@ -206,7 +212,6 @@
     owners = lax.axis_size("exp")
     flight = owners // 2
     count, width = tokens.shape
-    hidden = w_gate.shape[2]
     few = relative(flight)
 
     def local(kernel, outs, name, *args, limit=16):
@@ -234,28 +239,25 @@
         pairs = [(n, n ^ (2 * distances[n % 2]) ^ cross) for n in range(owners)]
         return lax.ppermute(rows, "exp", pairs)
 
-    def stage(weights, *after):
+    def stage(*after):
+        weights = w_gate[0], w_up[0], w_down[0]
         return pl.pallas_call(
             stage_kernel,
-            out_shape=jax.ShapeDtypeStruct(weights.shape, weights.dtype),
-            in_specs=[HBM] + [pl.BlockSpec(memory_space=pl.ANY)] * len(after),
-            out_specs=VMEM,
-            scratch_shapes=[pltpu.SemaphoreType.DMA((PIECES,))],
+            out_shape=tuple(jax.ShapeDtypeStruct(w.shape, w.dtype) for w in weights),
+            in_specs=[HBM] * 3 + [pl.BlockSpec(memory_space=pl.ANY)] * len(after),
+            out_specs=(VMEM,) * 3,
+            scratch_shapes=[pltpu.SemaphoreType.DMA((3 * PIECES,))],
             compiler_params=pltpu.CompilerParams(vmem_limit_bytes=16 * 2**20),
             cost_estimate=SMALL,
             name="stage",
-        )(*in_hbm(weights), *after)
-
-    def experts(own, other, weights, outs):
-        return local(
-            functools.partial(expert_kernel, len(own)),
-            outs,
-            "experts",
-            *own,
-            *other,
-            *weights,
-            limit=24,
-        )
+        )(*in_hbm(*weights), *after)
+
+    def experts(rows, weights):
+        outs = full(*[flight // 2] * 4)
+        return local(expert_kernel, outs, "experts", *rows, *weights, limit=24)
+
+    def join(outs, mine, theirs):
+        return local(join_kernel, packed(*outs), "join", mine, swap(theirs))
 
     def combine(mix, arrays, first):
         return pl.pallas_call(
@@ -271,7 +273,7 @@
             name="combine",
         )(mix, *arrays)
 
-    first = packed(3, 3, 1, 1) if few else packed(flight)
+    first = packed(3, 4, 1, 1) if few else packed(flight)
     mix, *outgoing = pl.pallas_call(
         functools.partial(dispatch_kernel, flight),
         out_shape=(jax.ShapeDtypeStruct((2 * flight * SLOTS, count), jnp.bfloat16),) + first,
@@ -288,9 +290,8 @@
         compiler_params=pltpu.CompilerParams(vmem_limit_bytes=24 * 2**20),
         name="dispatch",
     )(*in_hbm(tokens, norm_gain, expert_ids.T, gate_weights.T))
-    gate, up, down = stage(w_gate[0]), stage(w_up[0]), stage(w_down[0])
-
     if not few:
+        weights = stage()
         groups = [list(range(core, owners, 2)) for core in range(2)]
         exchange = functools.partial(
             lax.all_to_all,
@@ -300,29 +301,34 @@
             axis_index_groups=groups,
             tiled=True,
         )
-        (own,) = local(gather_kernel, full(flight), "gather", exchange(outgoing[0]))
-        mine, theirs = experts([own], [swap(own)], (gate, up, down), full(flight, flight))
-        (joined,) = local(join_kernel, packed(flight), "join", mine, swap(theirs))
-        return combine(mix, [exchange(joined)], None)
+        own = exchange(outgoing[0])
+        mine_one, mine_two, theirs_one, theirs_two = experts([own, swap(own)], weights)
+        half = flight // 2
+        (joined_one,) = join([half], mine_one, theirs_one)
+        (joined_two,) = join([half], mine_two, theirs_two)
+        return combine(mix, [exchange(jnp.concatenate([joined_one, joined_two]))], None)
 
     one, two, three = zip(*CARRIED)
     four = (SHARED, SHARED)
     kept, given, shared, own = outgoing
-    pairs = local(merge_kernel, packed(2, 2, 2), "merge", kept, swap(given))
-    arrived = [travel(a, r) for a, r in zip((*pairs, shared), (one, two, three, four))]
-    *arrived, gate, up = lax.optimization_barrier((*arrived, gate, up))
-    (own,) = local(gather_kernel, full(8), "gather", *arrived, own)
-
+    *pairs, other_own = local(merge_kernel, packed(2, 2, 2, 1), "merge", kept, swap(given))
+    shared = travel(shared, four)
+    *pairs[1:], shared = lax.optimization_barrier((*pairs[1:], shared))
+    pairs = [travel(a, r) for a, r in zip(pairs, (one, two, three))]
+    weights = stage(pairs[0])
+    pairs[1], *weights = lax.optimization_barrier((pairs[1], *weights))
+    others = [swap(pairs[0]), swap(pairs[1]), swap(shared)]
+    pairs[2], others[0], others[2] = lax.optimization_barrier((pairs[2], others[0], others[2]))
+    rows = [*pairs, shared, own, *others[:2], swap(pairs[2]), others[2], other_own]
     mine_one, mine_two, theirs_one, theirs_two = experts(
-        [own], [swap(own)], (gate, up, down), full(4, 4, 4, 4)
+        [rows[i] for i in (0, 3, 4, 1, 2, 5, 8, 9, 6, 7)], weights
     )
-    first, second = local(join_kernel, packed(2, 2), "join", mine_one, swap(theirs_one))
-    third, shared, own = local(join_kernel, packed(2, 1, 1), "join", mine_two, swap(theirs_two))
-    returned = [
-        travel(a, r) for a, r in zip((first, second, third, shared), (one, two, three, four))
-    ]
-    *pairs, shared = returned
-    pairs[0], shared = lax.optimization_barrier((pairs[0], shared))
+
+    first, shared, own = join((2, 1, 1), mine_one, theirs_one)
+    second, third = join((2, 2), mine_two, theirs_two)
+    first, shared = travel(first, one), travel(shared, four)
+    second, third, shared = lax.optimization_barrier((second, third, shared))
+    pairs = [first, travel(second, two), travel(third, three)]
     arrays = [*pairs, *[swap(a) for a in pairs], shared, own]
     return combine(mix, arrays, (0, 0, 0, 1, 1, 1, 0, 0))
 

time: 38.9 us -> 44.8 us (1.15)
  waiting for transfers between devices: 11.7 us -> 22.8 us
  starting transfers between devices: 15.5 us -> 12.2 us
  Pallas kernels: 11.4 us -> 9.57 us
    ppermute x8, waiting for transfers between devices: 8.48 us -> 18.1 us  [travel(): return lax.ppermute(rows, 'exp', pairs)]
    ppermute x8, starting transfers between devices: 13.7 us -> 10.6 us  [travel(): return lax.ppermute(rows, 'exp', pairs)]
    pallas_call x3 -> x1, Pallas kernels: 6.13 us -> 4.24 us  [stage(): pl.pallas_call(stage_kernel, out_shape=tuple((jax.ShapeDtypeStruct(w.shap...]
    ppermute x7 -> x10, waiting for transfers between devices: 3.23 us -> 4.67 us  [swap(): return lax.ppermute(rows, 'exp', [(n, n ^ 1) for n in range(owners)])]
    ppermute x7 -> x10, starting transfers between devices: 1.85 us -> 1.69 us  [swap(): return lax.ppermute(rows, 'exp', [(n, n ^ 1) for n in range(owners)])]
    pallas_call x5 -> x4, Pallas kernels: 2.05 us -> 2.08 us  [local(): pl.pallas_call(kernel, out_shape=outs, in_specs=[VMEM] * len(args), out_s...]
  transfers between devices with their start and end apart: 15 -> 18, of which waited for: 8 -> 10; matrix products, arithmetic and copies ran while one was open for 0% -> 0% of each run, Pallas kernels for 16% -> 10%
where the time goes in v12:
time: 44.8 us; the launch traced here: 44.7 us
  waiting for transfers between devices  22.8 us (51%)
  starting transfers between devices  12.2 us (27%)
  Pallas kernels  9.57 us (21%)
    ppermute x8, waiting for transfers between devices, travel(): return lax.ppermute(rows, 'exp', pairs)  18.1 us
    ppermute x8, starting transfers between devices, travel(): return lax.ppermute(rows, 'exp', pairs)  10.6 us
    ppermute x10, waiting for transfers between devices, swap(): return lax.ppermute(rows, 'exp', [(n, n ^ 1) for n in range(owners)])  4.67 us
    pallas_call x1, Pallas kernels, stage(): pl.pallas_call(stage_kernel, out_shape=tuple((jax.ShapeDtypeStruct(w.shap...  4.24 us
    pallas_call x4, Pallas kernels, local(): pl.pallas_call(kernel, out_shape=outs, in_specs=[VMEM] * len(args), out_s...  2.08 us
    pallas_call x1, Pallas kernels, per_device(): pl.pallas_call(functools.partial(dispatch_kernel, flight), out_shape=(jax...  2.04 us
    ppermute x10, starting transfers between devices, swap(): return lax.ppermute(rows, 'exp', [(n, n ^ 1) for n in range(owners)])  1.69 us
    pallas_call x1, Pallas kernels, combine(): pl.pallas_call(functools.partial(combine_kernel, first), out_shape=jax.Sh...  1.21 us
  transfers between devices with their start and end apart: 18, of which 10 were waited for; matrix products, arithmetic and copies ran while one was open for 0% of the time, Pallas kernels for 10%

profile of v12, /device:TPU:0, one launch (start us, length us, event | category | flops | bytes accessed | tf_op | source)
XLA Modules:
  0.0 44.7 jit_solution(8481201638432870950)
XLA Ops:
  0.0 2.0 %dispatch.1 = (bf16[128,128]{1,0:T(8,128)(2,1)S(1)}, bf16[24,3200]{1,0:T(8,128)(2,1)S(1)}, bf16[32,3200]{1,0:T(8,128)(2,1)S(1)}, bf16[8,3200]{1,0:T(8,128)(2,1)S(1)}, bf16[8,3200]{1,0:T(8,128)(2,1)S(1)}) custom-call(bf16[128,3584]{1,0:T(8,128)(2,1)} %tok_hbm.1, f32[3584]{0:T(1024)} %gain_hbm.1, s32[8,128]{1,0:T(8,128)} %bitcast.8, f32[8,128]{1,0:T(8,128)} %bitcast.9), custom_call_target="tpu_custom_call" | custom-call | tf_op jit(solution)/shard_map/dispatch/pallas_call | solution.py:277
  2.0 0.5 %collective-permute-start = (bf16[32,3200]{1,0:T(8,128)(2,1)S(1)}, bf16[32,3200]{1,0:T(8,128)(2,1)S(1)}, u32[]{:S(2)}, u32[]{:S(2)}) collective-permute-start(bf16[32,3200]{1,0:T(8,128)(2,1)S(1)} %get-tuple-element.41), channel_id=1, source_target_pairs={{0,1},{1,0},{2,3},{3,2},{4,5},{5,4},{6,7},{7,6},{8,9},{9,8},{10,11... | collective-permute-start | bytes 614408 | tf_op jit(solution)/shard_map/ppermute | solution.py:236
  2.6 1.1 %collective-permute-done.got_ref = bf16[32,3200]{1,0:T(8,128)(2,1)S(1)} collective-permute-done((bf16[32,3200]{1,0:T(8,128)(2,1)S(1)}, bf16[32,3200]{1,0:T(8,128)(2,1)S(1)}, u32[]{:S(2)}, u32[]{:S(2)}) %collective-permute-start) | collective-permute-done | bytes 204832 | tf_op jit(solution)/shard_map/ppermute | solution.py:236
  3.7 4.0 %collective-permute-start.1 = (bf16[16,3200]{1,0:T(8,128)(2,1)S(1)}, bf16[16,3200]{1,0:T(8,128)(2,1)S(1)}, u32[]{:S(2)}, u32[]{:S(2)}) collective-permute-start(bf16[16,3200]{1,0:T(8,128)(2,1)S(1)} %get-tuple-element.42), channel_id=1, source_target_pairs={{0,8},{1,13},{2,10},{3,15},{4,12},{5,9},{6,14},{7,11},{8,0},{9,5},... | collective-permute-start | bytes 307208 | tf_op jit(solution)/shard_map/ppermute | solution.py:240
  7.7 2.5 %collective-permute-start.2 = (bf16[8,3200]{1,0:T(8,128)(2,1)S(1)}, bf16[8,3200]{1,0:T(8,128)(2,1)S(1)}, u32[]{:S(2)}, u32[]{:S(2)}) collective-permute-start(bf16[8,3200]{1,0:T(8,128)(2,1)S(1)} %get-tuple-element.45), channel_id=1, source_target_pairs={{0,6},{1,7},{2,4},{3,5},{4,2},{5,3},{6,0},{7,1},{8,14},{9,15},{10,... | collective-permute-start | bytes 153608 | tf_op jit(solution)/shard_map/ppermute | solution.py:240
  10.2 3.2 %collective-permute-done.2.refs_1_ = bf16[8,3200]{1,0:T(8,128)(2,1)S(1)} collective-permute-done((bf16[8,3200]{1,0:T(8,128)(2,1)S(1)}, bf16[8,3200]{1,0:T(8,128)(2,1)S(1)}, u32[]{:S(2)}, u32[]{:S(2)}) %collective-permute-start.2) | collective-permute-done | bytes 51232 | tf_op jit(solution)/shard_map/ppermute | solution.py:240
  13.4 1.8 %collective-permute-start.3 = (bf16[16,3200]{1,0:T(8,128)(2,1)S(1)}, bf16[16,3200]{1,0:T(8,128)(2,1)S(1)}, u32[]{:S(2)}, u32[]{:S(2)}) collective-permute-start(bf16[16,3200]{1,0:T(8,128)(2,1)S(1)} %get-tuple-element.48), channel_id=1, source_target_pairs={{0,2},{1,5},{2,0},{3,7},{4,6},{5,1},{6,4},{7,3},{8,10},{9,13},{10,... | collective-permute-start | bytes 307208 | tf_op jit(solution)/shard_map/ppermute | solution.py:240
  15.2 0.8 %collective-permute-start.4 = (bf16[16,3200]{1,0:T(8,128)(2,1)S(1)}, bf16[16,3200]{1,0:T(8,128)(2,1)S(1)}, u32[]{:S(2)}, u32[]{:S(2)}) collective-permute-start(bf16[16,3200]{1,0:T(8,128)(2,1)S(1)} %get-tuple-element.53), channel_id=1, source_target_pairs={{0,10},{1,15},{2,8},{3,13},{4,14},{5,11},{6,12},{7,9},{8,2},{9,7},... | collective-permute-start | bytes 307208 | tf_op jit(solution)/shard_map/ppermute | solution.py:240
  16.0 0.0 collective-permute-done.1.refs_3_.refs_0_
  16.0 0.0 collective-permute-start.5
  16.0 0.5 %collective-permute-start.6 = (bf16[8,3200]{1,0:T(8,128)(2,1)S(1)}, bf16[8,3200]{1,0:T(8,128)(2,1)S(1)}, u32[]{:S(2)}, u32[]{:S(2)}) collective-permute-start(bf16[8,3200]{1,0:T(8,128)(2,1)S(1)} %collective-permute-done.2.refs_1_), channel_id=1, source_target_pairs={{0,1},{1,0},{2,3},{3,2},{4,5},{5,4},{6,7},{7,6},{8,9},{9,8},{10,11... | collective-permute-start | bytes 153608 | tf_op jit(solution)/shard_map/ppermute | solution.py:236
  16.5 4.2 %stage.1 = (bf16[3584,512]{1,0:T(8,128)(2,1)S(1)}, bf16[3584,512]{1,0:T(8,128)(2,1)S(1)}, bf16[512,3584]{1,0:T(8,128)(2,1)S(1)}) custom-call(bf16[3584,512]{1,0:T(8,128)(2,1)} %bitcast.5, bf16[3584,512]{1,0:T(8,128)(2,1)} %bitcast.6, bf16[512,3584]{1,0:T(8,128)(2,1)} %bitcast.7, bf16[16,3200]{1,0:T(8,128)(2,1)S(1)} %collective-permute-done.1.refs_3_.refs_0_), custom_call_target="tpu_custom_call" | custom-call | flops 1 | bytes 1 | tf_op jit(solution)/shard_map/stage/pallas_call | solution.py:244
  20.8 0.1 collective-permute-start.7
  20.9 0.0 collective-permute-done.6.refs_6_
  20.9 2.9 %collective-permute-done.4.refs_4_ = bf16[16,3200]{1,0:T(8,128)(2,1)S(1)} collective-permute-done((bf16[16,3200]{1,0:T(8,128)(2,1)S(1)}, bf16[16,3200]{1,0:T(8,128)(2,1)S(1)}, u32[]{:S(2)}, u32[]{:S(2)}) %collective-permute-start.4) | collective-permute-done | bytes 102432 | tf_op jit(solution)/shard_map/ppermute | solution.py:240
  23.8 1.3 %collective-permute-done.8.refs_9_ = bf16[16,3200]{1,0:T(8,128)(2,1)S(1)} collective-permute-done((bf16[16,3200]{1,0:T(8,128)(2,1)S(1)}, bf16[16,3200]{1,0:T(8,128)(2,1)S(1)}, u32[]{:S(2)}, u32[]{:S(2)}) %collective-permute-start.8) | collective-permute-done | bytes 102432 | tf_op jit(solution)/shard_map/ppermute | solution.py:236
  25.1 1.9 %experts.1 = (bf16[32,3584]{1,0:T(8,128)(2,1)S(1)}, bf16[32,3584]{1,0:T(8,128)(2,1)S(1)}, bf16[32,3584]{1,0:T(8,128)(2,1)S(1)}, bf16[32,3584]{1,0:T(8,128)(2,1)S(1)}) custom-call(bf16[16,3200]{1,0:T(8,128)(2,1)S(1)} %collective-permute-done.1.refs_3_.refs_0_, bf16[8,3200]{1,0:T(8,128)(2,1)S(1)} %collective-permute-done.2.refs_1_, ...), custom_call_target="tpu_custom_call" | custom-call | flops 1 | bytes 1 | tf_op jit(solution)/shard_map/experts/pallas_call | solution.py:218
  27.0 0.2 collective-permute-start.9
  27.1 0.4 collective-permute-start.11
  27.5 1.0 %collective-permute-done.9.got_ref = bf16[32,3584]{1,0:T(8,128)(2,1)S(1)} collective-permute-done((bf16[32,3584]{1,0:T(8,128)(2,1)S(1)}, bf16[32,3584]{1,0:T(8,128)(2,1)S(1)}, u32[]{:S(2)}, u32[]{:S(2)}) %collective-permute-start.9) | collective-permute-done | bytes 229408 | tf_op jit(solution)/shard_map/ppermute | solution.py:236
  28.5 0.1 join.2
  28.6 0.1 collective-permute-start.12
  28.7 1.3 %collective-permute-start.10 = (bf16[16,3200]{1,0:T(8,128)(2,1)S(1)}, bf16[16,3200]{1,0:T(8,128)(2,1)S(1)}, u32[]{:S(2)}, u32[]{:S(2)}) collective-permute-start(bf16[16,3200]{1,0:T(8,128)(2,1)S(1)} %get-tuple-element.63), channel_id=1, source_target_pairs={{0,8},{1,13},{2,10},{3,15},{4,12},{5,9},{6,14},{7,11},{8,0},{9,5},... | collective-permute-start | bytes 307208 | tf_op jit(solution)/shard_map/ppermute | solution.py:240
  30.0 0.0 collective-permute-done.11.got_ref
  30.0 0.1 join.3
  30.1 5.0 %collective-permute-done.12.refs_6_ = bf16[8,3200]{1,0:T(8,128)(2,1)S(1)} collective-permute-done((bf16[8,3200]{1,0:T(8,128)(2,1)S(1)}, bf16[8,3200]{1,0:T(8,128)(2,1)S(1)}, u32[]{:S(2)}, u32[]{:S(2)}) %collective-permute-start.12) | collective-permute-done | bytes 51232 | tf_op jit(solution)/shard_map/ppermute | solution.py:240
  35.1 0.0 collective-permute-start.13
  35.1 3.2 %collective-permute-done.10.refs_0_ = bf16[16,3200]{1,0:T(8,128)(2,1)S(1)} collective-permute-done((bf16[16,3200]{1,0:T(8,128)(2,1)S(1)}, bf16[16,3200]{1,0:T(8,128)(2,1)S(1)}, u32[]{:S(2)}, u32[]{:S(2)}) %collective-permute-start.10) | collective-permute-done | bytes 102432 | tf_op jit(solution)/shard_map/ppermute | solution.py:240
  38.3 1.8 %collective-permute-done.13.refs_1_ = bf16[16,3200]{1,0:T(8,128)(2,1)S(1)} collective-permute-done((bf16[16,3200]{1,0:T(8,128)(2,1)S(1)}, bf16[16,3200]{1,0:T(8,128)(2,1)S(1)}, u32[]{:S(2)}, u32[]{:S(2)}) %collective-permute-start.13) | collective-permute-done | bytes 102432 | tf_op jit(solution)/shard_map/ppermute | solution.py:240
  40.2 2.0 %collective-permute-done.14.refs_2_ = bf16[16,3200]{1,0:T(8,128)(2,1)S(1)} collective-permute-done((bf16[16,3200]{1,0:T(8,128)(2,1)S(1)}, bf16[16,3200]{1,0:T(8,128)(2,1)S(1)}, u32[]{:S(2)}, u32[]{:S(2)}) %collective-permute-start.14) | collective-permute-done | bytes 102432 | tf_op jit(solution)/shard_map/ppermute | solution.py:240
  42.2 1.3 %collective-permute-done.17.refs_5_ = bf16[16,3200]{1,0:T(8,128)(2,1)S(1)} collective-permute-done((bf16[16,3200]{1,0:T(8,128)(2,1)S(1)}, bf16[16,3200]{1,0:T(8,128)(2,1)S(1)}, u32[]{:S(2)}, u32[]{:S(2)}) %collective-permute-start.17) | collective-permute-done | bytes 102432 | tf_op jit(solution)/shard_map/ppermute | solution.py:236
  43.5 1.2 %combine.1 = bf16[128,3584]{1,0:T(8,128)(2,1)} custom-call(bf16[128,128]{1,0:T(8,128)(2,1)S(1)} %get-tuple-element.39.mix_ref, bf16[16,3200]{1,0:T(8,128)(2,1)S(1)} %collective-permute-done.10.refs_0_, bf16[16,3200]{1,0:T(8,128)(2,1)S(1)} %collective-permute-done.13.refs_1_, bf16[16,3200]{1,0:T(8,128)(2,1)S(1)} %collective-permute-done.14.refs_2_, ...), custom_call_target="tpu_custom_call" | custom-call | tf_op jit(solution)/shard_map/combine/pallas_call | solution.py:263
  (11 shorter events, 0.1 us)
Async XLA Ops:
  2.0 1.6 %collective-permute-start = (bf16[32,3200]{1,0:T(8,128)(2,1)S(1)}, bf16[32,3200]{1,0:T(8,128)(2,1)S(1)}, u32[]{:S(2)}, u32[]{:S(2)}) collective-permute-start(bf16[32,3200]{1,0:T(8,128)(2,1)S(1)} %get-tuple-element.41), channel_id=1, source_target_pairs={{0,1},{1,0},{2,3},{3,2},{4,5},{5,4},{6,7},{7,6},{8,9},{9,8},{10,11... | collective-permute-start | bytes 614408 | tf_op jit(solution)/shard_map/ppermute | solution.py:236
  3.7 12.4 %collective-permute-start.1 = (bf16[16,3200]{1,0:T(8,128)(2,1)S(1)}, bf16[16,3200]{1,0:T(8,128)(2,1)S(1)}, u32[]{:S(2)}, u32[]{:S(2)}) collective-permute-start(bf16[16,3200]{1,0:T(8,128)(2,1)S(1)} %get-tuple-element.42), channel_id=1, source_target_pairs={{0,8},{1,13},{2,10},{3,15},{4,12},{5,9},{6,14},{7,11},{8,0},{9,5},... | collective-permute-start | bytes 307208 | tf_op jit(solution)/shard_map/ppermute | solution.py:240
  7.7 5.7 %collective-permute-start.2 = (bf16[8,3200]{1,0:T(8,128)(2,1)S(1)}, bf16[8,3200]{1,0:T(8,128)(2,1)S(1)}, u32[]{:S(2)}, u32[]{:S(2)}) collective-permute-start(bf16[8,3200]{1,0:T(8,128)(2,1)S(1)} %get-tuple-element.45), channel_id=1, source_target_pairs={{0,6},{1,7},{2,4},{3,5},{4,2},{5,3},{6,0},{7,1},{8,14},{9,15},{10,... | collective-permute-start | bytes 153608 | tf_op jit(solution)/shard_map/ppermute | solution.py:240
  13.4 7.4 %collective-permute-start.3 = (bf16[16,3200]{1,0:T(8,128)(2,1)S(1)}, bf16[16,3200]{1,0:T(8,128)(2,1)S(1)}, u32[]{:S(2)}, u32[]{:S(2)}) collective-permute-start(bf16[16,3200]{1,0:T(8,128)(2,1)S(1)} %get-tuple-element.48), channel_id=1, source_target_pairs={{0,2},{1,5},{2,0},{3,7},{4,6},{5,1},{6,4},{7,3},{8,10},{9,13},{10,... | collective-permute-start | bytes 307208 | tf_op jit(solution)/shard_map/ppermute | solution.py:240
  15.2 8.5 %collective-permute-start.4 = (bf16[16,3200]{1,0:T(8,128)(2,1)S(1)}, bf16[16,3200]{1,0:T(8,128)(2,1)S(1)}, u32[]{:S(2)}, u32[]{:S(2)}) collective-permute-start(bf16[16,3200]{1,0:T(8,128)(2,1)S(1)} %get-tuple-element.53), channel_id=1, source_target_pairs={{0,10},{1,15},{2,8},{3,13},{4,14},{5,11},{6,12},{7,9},{8,2},{9,7},... | collective-permute-start | bytes 307208 | tf_op jit(solution)/shard_map/ppermute | solution.py:240
  16.0 7.7 %collective-permute-start.5 = (bf16[16,3200]{1,0:T(8,128)(2,1)S(1)}, bf16[16,3200]{1,0:T(8,128)(2,1)S(1)}, u32[]{:S(2)}, u32[]{:S(2)}) collective-permute-start(bf16[16,3200]{1,0:T(8,128)(2,1)S(1)} %collective-permute-done.1.refs_3_.refs_0_), channel_id=1, source_target_pairs={{0,1},{1,0},{2,3},{3,2},{4,5},{5,4},{6,7},{7,6},{8,9},{9,8},{10,11... | collective-permute-start | bytes 307208 | tf_op jit(solution)/shard_map/ppermute | solution.py:236
  16.0 4.9 %collective-permute-start.6 = (bf16[8,3200]{1,0:T(8,128)(2,1)S(1)}, bf16[8,3200]{1,0:T(8,128)(2,1)S(1)}, u32[]{:S(2)}, u32[]{:S(2)}) collective-permute-start(bf16[8,3200]{1,0:T(8,128)(2,1)S(1)} %collective-permute-done.2.refs_1_), channel_id=1, source_target_pairs={{0,1},{1,0},{2,3},{3,2},{4,5},{5,4},{6,7},{7,6},{8,9},{9,8},{10,11... | collective-permute-start | bytes 153608 | tf_op jit(solution)/shard_map/ppermute | solution.py:236
  20.8 3.0 %collective-permute-start.7 = (bf16[16,3200]{1,0:T(8,128)(2,1)S(1)}, bf16[16,3200]{1,0:T(8,128)(2,1)S(1)}, u32[]{:S(2)}, u32[]{:S(2)}) collective-permute-start(bf16[16,3200]{1,0:T(8,128)(2,1)S(1)} %collective-permute-done.3.refs_3_), channel_id=1, source_target_pairs={{0,1},{1,0},{2,3},{3,2},{4,5},{5,4},{6,7},{7,6},{8,9},{9,8},{10,11... | collective-permute-start | bytes 307208 | tf_op jit(solution)/shard_map/ppermute | solution.py:236
  23.8 1.3 %collective-permute-start.8 = (bf16[16,3200]{1,0:T(8,128)(2,1)S(1)}, bf16[16,3200]{1,0:T(8,128)(2,1)S(1)}, u32[]{:S(2)}, u32[]{:S(2)}) collective-permute-start(bf16[16,3200]{1,0:T(8,128)(2,1)S(1)} %collective-permute-done.4.refs_4_), channel_id=1, source_target_pairs={{0,1},{1,0},{2,3},{3,2},{4,5},{5,4},{6,7},{7,6},{8,9},{9,8},{10,11... | collective-permute-start | bytes 307208 | tf_op jit(solution)/shard_map/ppermute | solution.py:236
  27.0 1.6 %collective-permute-start.9 = (bf16[32,3584]{1,0:T(8,128)(2,1)S(1)}, bf16[32,3584]{1,0:T(8,128)(2,1)S(1)}, u32[]{:S(2)}, u32[]{:S(2)}) collective-permute-start(bf16[32,3584]{1,0:T(8,128)(2,1)S(1)} %get-tuple-element.62), channel_id=1, source_target_pairs={{0,1},{1,0},{2,3},{3,2},{4,5},{5,4},{6,7},{7,6},{8,9},{9,8},{10,11... | collective-permute-start | bytes 688136 | tf_op jit(solution)/shard_map/ppermute | solution.py:236
  27.1 2.9 %collective-permute-start.11 = (bf16[32,3584]{1,0:T(8,128)(2,1)S(1)}, bf16[32,3584]{1,0:T(8,128)(2,1)S(1)}, u32[]{:S(2)}, u32[]{:S(2)}) collective-permute-start(bf16[32,3584]{1,0:T(8,128)(2,1)S(1)} %get-tuple-element.65), channel_id=1, source_target_pairs={{0,1},{1,0},{2,3},{3,2},{4,5},{5,4},{6,7},{7,6},{8,9},{9,8},{10,11... | collective-permute-start | bytes 688136 | tf_op jit(solution)/shard_map/ppermute | solution.py:236
  28.6 6.5 %collective-permute-start.12 = (bf16[8,3200]{1,0:T(8,128)(2,1)S(1)}, bf16[8,3200]{1,0:T(8,128)(2,1)S(1)}, u32[]{:S(2)}, u32[]{:S(2)}) collective-permute-start(bf16[8,3200]{1,0:T(8,128)(2,1)S(1)} %get-tuple-element.68), channel_id=1, source_target_pairs={{0,6},{1,7},{2,4},{3,5},{4,2},{5,3},{6,0},{7,1},{8,14},{9,15},{10,... | collective-permute-start | bytes 153608 | tf_op jit(solution)/shard_map/ppermute | solution.py:240
  28.7 9.6 %collective-permute-start.10 = (bf16[16,3200]{1,0:T(8,128)(2,1)S(1)}, bf16[16,3200]{1,0:T(8,128)(2,1)S(1)}, u32[]{:S(2)}, u32[]{:S(2)}) collective-permute-start(bf16[16,3200]{1,0:T(8,128)(2,1)S(1)} %get-tuple-element.63), channel_id=1, source_target_pairs={{0,8},{1,13},{2,10},{3,15},{4,12},{5,9},{6,14},{7,11},{8,0},{9,5},... | collective-permute-start | bytes 307208 | tf_op jit(solution)/shard_map/ppermute | solution.py:240
  35.1 5.1 %collective-permute-start.13 = (bf16[16,3200]{1,0:T(8,128)(2,1)S(1)}, bf16[16,3200]{1,0:T(8,128)(2,1)S(1)}, u32[]{:S(2)}, u32[]{:S(2)}) collective-permute-start(bf16[16,3200]{1,0:T(8,128)(2,1)S(1)} %get-tuple-element.69), channel_id=1, source_target_pairs={{0,2},{1,5},{2,0},{3,7},{4,6},{5,1},{6,4},{7,3},{8,10},{9,13},{10,... | collective-permute-start | bytes 307208 | tf_op jit(solution)/shard_map/ppermute | solution.py:240
  35.1 7.0 %collective-permute-start.14 = (bf16[16,3200]{1,0:T(8,128)(2,1)S(1)}, bf16[16,3200]{1,0:T(8,128)(2,1)S(1)}, u32[]{:S(2)}, u32[]{:S(2)}) collective-permute-start(bf16[16,3200]{1,0:T(8,128)(2,1)S(1)} %get-tuple-element.70), channel_id=1, source_target_pairs={{0,10},{1,15},{2,8},{3,13},{4,14},{5,11},{6,12},{7,9},{8,2},{9,7},... | collective-permute-start | bytes 307208 | tf_op jit(solution)/shard_map/ppermute | solution.py:240
  38.3 3.8 %collective-permute-start.15 = (bf16[16,3200]{1,0:T(8,128)(2,1)S(1)}, bf16[16,3200]{1,0:T(8,128)(2,1)S(1)}, u32[]{:S(2)}, u32[]{:S(2)}) collective-permute-start(bf16[16,3200]{1,0:T(8,128)(2,1)S(1)} %collective-permute-done.10.refs_0_), channel_id=1, source_target_pairs={{0,1},{1,0},{2,3},{3,2},{4,5},{5,4},{6,7},{7,6},{8,9},{9,8},{10,11... | collective-permute-start | bytes 307208 | tf_op jit(solution)/shard_map/ppermute | solution.py:236
  40.2 2.0 %collective-permute-start.16 = (bf16[16,3200]{1,0:T(8,128)(2,1)S(1)}, bf16[16,3200]{1,0:T(8,128)(2,1)S(1)}, u32[]{:S(2)}, u32[]{:S(2)}) collective-permute-start(bf16[16,3200]{1,0:T(8,128)(2,1)S(1)} %collective-permute-done.13.refs_1_), channel_id=1, source_target_pairs={{0,1},{1,0},{2,3},{3,2},{4,5},{5,4},{6,7},{7,6},{8,9},{9,8},{10,11... | collective-permute-start | bytes 307208 | tf_op jit(solution)/shard_map/ppermute | solution.py:236
  42.1 1.3 %collective-permute-start.17 = (bf16[16,3200]{1,0:T(8,128)(2,1)S(1)}, bf16[16,3200]{1,0:T(8,128)(2,1)S(1)}, u32[]{:S(2)}, u32[]{:S(2)}) collective-permute-start(bf16[16,3200]{1,0:T(8,128)(2,1)S(1)} %collective-permute-done.14.refs_2_), channel_id=1, source_target_pairs={{0,1},{1,0},{2,3},{3,2},{4,5},{5,4},{6,7},{7,6},{8,9},{9,8},{10,11... | collective-permute-start | bytes 307208 | tf_op jit(solution)/shard_map/ppermute | solution.py:236

commit v13 on v12

--- a/solution.py
+++ b/solution.py
@@ -142,7 +142,8 @@
 
 
 def stage_kernel(*refs):
-    sources, targets, sems = refs[:3], refs[-4:-1], refs[-1]
+    *refs, sems = refs
+    sources, targets = refs[:3], refs[3:]
     copies = []
     for at, (source, target) in enumerate(zip(sources, targets)):
         rows = source.shape[0] // PIECES
@@ -170,6 +171,16 @@
     own_out[...] = got[len(outs) * SLOTS :].astype(jnp.bfloat16)
 
 
+def gather_kernel(*refs):
+    refs[-1][...] = together(refs[:-1]).astype(jnp.bfloat16)
+
+
+def sift_kernel(*refs):
+    *refs, out_ref = refs
+    blocks = [r[...].astype(jnp.float32)[SLOTS:] for r in refs]
+    out_ref[...] = jnp.concatenate(blocks, axis=0).astype(jnp.bfloat16)
+
+
 def expert_kernel(*refs):
     *rows, gate_ref, up_ref, down_ref, own_one, own_two, other_one, other_two = refs
     x = unpack(together(rows)).astype(jnp.bfloat16)
@@ -184,11 +195,11 @@
     store(outs, pack(mine_ref[...].astype(jnp.float32) + got_ref[...].astype(jnp.float32)))
 
 
-def combine_kernel(first, mix_ref, *refs):
+def combine_kernel(paired, mix_ref, *refs):
     *refs, out_hbm, out, sems = refs
     blocks = [r[...].astype(jnp.float32) for r in refs]
-    if first:
-        blocks = [b[at * SLOTS : (at + 1) * SLOTS] for b, at in zip(blocks, first)]
+    if paired:
+        blocks[:3] = [b[:SLOTS] for b in blocks[:3]]
     rows = unpack(jnp.concatenate(blocks, axis=0)).astype(jnp.bfloat16)
     both = jnp.concatenate([rows, rows], axis=0)
     mix = mix_ref[...]
@@ -239,18 +250,18 @@
         pairs = [(n, n ^ (2 * distances[n % 2]) ^ cross) for n in range(owners)]
         return lax.ppermute(rows, "exp", pairs)
 
-    def stage(*after):
+    def stage():
         weights = w_gate[0], w_up[0], w_down[0]
         return pl.pallas_call(
             stage_kernel,
             out_shape=tuple(jax.ShapeDtypeStruct(w.shape, w.dtype) for w in weights),
-            in_specs=[HBM] * 3 + [pl.BlockSpec(memory_space=pl.ANY)] * len(after),
+            in_specs=[HBM] * 3,
             out_specs=(VMEM,) * 3,
             scratch_shapes=[pltpu.SemaphoreType.DMA((3 * PIECES,))],
             compiler_params=pltpu.CompilerParams(vmem_limit_bytes=16 * 2**20),
             cost_estimate=SMALL,
             name="stage",
-        )(*in_hbm(*weights), *after)
+        )(*in_hbm(*weights))
 
     def experts(rows, weights):
         outs = full(*[flight // 2] * 4)
@@ -259,9 +270,9 @@
     def join(outs, mine, theirs):
         return local(join_kernel, packed(*outs), "join", mine, swap(theirs))
 
-    def combine(mix, arrays, first):
+    def combine(mix, arrays, paired):
         return pl.pallas_call(
-            functools.partial(combine_kernel, first),
+            functools.partial(combine_kernel, paired),
             out_shape=jax.ShapeDtypeStruct((count, width), jnp.bfloat16),
             in_specs=[VMEM] * (len(arrays) + 1),
             out_specs=HBM,
@@ -306,31 +317,28 @@
         half = flight // 2
         (joined_one,) = join([half], mine_one, theirs_one)
         (joined_two,) = join([half], mine_two, theirs_two)
-        return combine(mix, [exchange(jnp.concatenate([joined_one, joined_two]))], None)
+        return combine(mix, [exchange(jnp.concatenate([joined_one, joined_two]))], False)
 
     one, two, three = zip(*CARRIED)
     four = (SHARED, SHARED)
     kept, given, shared, own = outgoing
     *pairs, other_own = local(merge_kernel, packed(2, 2, 2, 1), "merge", kept, swap(given))
     shared = travel(shared, four)
-    *pairs[1:], shared = lax.optimization_barrier((*pairs[1:], shared))
-    pairs = [travel(a, r) for a, r in zip(pairs, (one, two, three))]
-    weights = stage(pairs[0])
-    pairs[1], *weights = lax.optimization_barrier((pairs[1], *weights))
-    others = [swap(pairs[0]), swap(pairs[1]), swap(shared)]
-    pairs[2], others[0], others[2] = lax.optimization_barrier((pairs[2], others[0], others[2]))
-    rows = [*pairs, shared, own, *others[:2], swap(pairs[2]), others[2], other_own]
+    arrived = [travel(a, r) for a, r in zip(pairs, (one, two, three))] + [shared]
+    *arrived, gate, up, down = lax.optimization_barrier((*arrived, *stage()))
+    (rows,) = local(gather_kernel, packed(7), "gather", *arrived)
     mine_one, mine_two, theirs_one, theirs_two = experts(
-        [rows[i] for i in (0, 3, 4, 1, 2, 5, 8, 9, 6, 7)], weights
+        (rows, own, swap(rows), other_own), (gate, up, down)
     )
 
-    first, shared, own = join((2, 1, 1), mine_one, theirs_one)
-    second, third = join((2, 2), mine_two, theirs_two)
-    first, shared = travel(first, one), travel(shared, four)
-    second, third, shared = lax.optimization_barrier((second, third, shared))
-    pairs = [first, travel(second, two), travel(third, three)]
-    arrays = [*pairs, *[swap(a) for a in pairs], shared, own]
-    return combine(mix, arrays, (0, 0, 0, 1, 1, 1, 0, 0))
+    first, second = join((2, 2), mine_one, theirs_one)
+    third, shared, own = join((2, 1, 1), mine_two, theirs_two)
+    arrived = [
+        travel(a, r) for a, r in zip((first, second, third, shared), (one, two, three, four))
+    ]
+    *pairs, shared = lax.optimization_barrier(tuple(arrived))
+    (others,) = local(sift_kernel, packed(3), "sift", *pairs)
+    return combine(mix, [*pairs, swap(others), shared, own], True)
 
 
 def solution(mesh):

time: 44.8 us -> 38.8 us (0.87)
  waiting for transfers between devices: 22.8 us -> 14.1 us
  starting transfers between devices: 12.2 us -> 14.9 us
    ppermute x8, waiting for transfers between devices: 18.1 us -> 9.03 us  [travel(): return lax.ppermute(rows, 'exp', pairs)]
    ppermute x8, starting transfers between devices: 10.6 us -> 13.7 us  [travel(): return lax.ppermute(rows, 'exp', pairs)]
    ppermute x10 -> x5, starting transfers between devices: 1.69 us -> 1.24 us  [swap(): return lax.ppermute(rows, 'exp', [(n, n ^ 1) for n in range(owners)])]
    ppermute x10 -> x5, waiting for transfers between devices: 4.67 us -> 5.09 us  [swap(): return lax.ppermute(rows, 'exp', [(n, n ^ 1) for n in range(owners)])]
    pallas_call x4 -> x6, Pallas kernels: 2.08 us -> 2.01 us  [local(): pl.pallas_call(kernel, out_shape=outs, in_specs=[VMEM] * len(args), out_s...]
  transfers between devices with their start and end apart: 18 -> 13, of which waited for: 10 -> 8; matrix products, arithmetic and copies ran while one was open for 0% -> 0% of each run, Pallas kernels for 10% -> 11%
where the time goes in v13:
time: 38.8 us; the launch traced here: 38.6 us
  starting transfers between devices  14.9 us (38%)
  waiting for transfers between devices  14.1 us (36%)
  Pallas kernels  9.52 us (25%)
    ppermute x8, starting transfers between devices, travel(): return lax.ppermute(rows, 'exp', pairs)  13.7 us
    ppermute x8, waiting for transfers between devices, travel(): return lax.ppermute(rows, 'exp', pairs)  9.03 us
    ppermute x5, waiting for transfers between devices, swap(): return lax.ppermute(rows, 'exp', [(n, n ^ 1) for n in range(owners)])  5.09 us
    pallas_call x1, Pallas kernels, stage(): pl.pallas_call(stage_kernel, out_shape=tuple((jax.ShapeDtypeStruct(w.shap...  4.24 us
    pallas_call x1, Pallas kernels, per_device(): pl.pallas_call(functools.partial(dispatch_kernel, flight), out_shape=(jax...  2.04 us
    pallas_call x6, Pallas kernels, local(): pl.pallas_call(kernel, out_shape=outs, in_specs=[VMEM] * len(args), out_s...  2.01 us
    ppermute x5, starting transfers between devices, swap(): return lax.ppermute(rows, 'exp', [(n, n ^ 1) for n in range(owners)])  1.24 us
    pallas_call x1, Pallas kernels, combine(): pl.pallas_call(functools.partial(combine_kernel, paired), out_shape=jax.S...  1.23 us
  transfers between devices with their start and end apart: 13, of which 8 were waited for; matrix products, arithmetic and copies ran while one was open for 0% of the time, Pallas kernels for 11%

profile of v13, /device:TPU:0, one launch (start us, length us, event | category | flops | bytes accessed | tf_op | source)
XLA Modules:
  0.0 38.6 jit_solution(7480080162006748483)
XLA Ops:
  0.0 2.0 %dispatch.1 = (bf16[128,128]{1,0:T(8,128)(2,1)S(1)}, bf16[24,3200]{1,0:T(8,128)(2,1)S(1)}, bf16[32,3200]{1,0:T(8,128)(2,1)S(1)}, bf16[8,3200]{1,0:T(8,128)(2,1)S(1)}, bf16[8,3200]{1,0:T(8,128)(2,1)S(1)}) custom-call(bf16[128,3584]{1,0:T(8,128)(2,1)} %tok_hbm.1, f32[3584]{0:T(1024)} %gain_hbm.1, s32[8,128]{1,0:T(8,128)} %bitcast.8, f32[8,128]{1,0:T(8,128)} %bitcast.9), custom_call_target="tpu_custom_call" | custom-call | tf_op jit(solution)/shard_map/dispatch/pallas_call | solution.py:288
  2.0 0.5 %collective-permute-start = (bf16[32,3200]{1,0:T(8,128)(2,1)S(1)}, bf16[32,3200]{1,0:T(8,128)(2,1)S(1)}, u32[]{:S(2)}, u32[]{:S(2)}) collective-permute-start(bf16[32,3200]{1,0:T(8,128)(2,1)S(1)} %get-tuple-element.39), channel_id=1, source_target_pairs={{0,1},{1,0},{2,3},{3,2},{4,5},{5,4},{6,7},{7,6},{8,9},{9,8},{10,11... | collective-permute-start | bytes 614408 | tf_op jit(solution)/shard_map/ppermute | solution.py:247
  2.6 1.1 %collective-permute-done.got_ref = bf16[32,3200]{1,0:T(8,128)(2,1)S(1)} collective-permute-done((bf16[32,3200]{1,0:T(8,128)(2,1)S(1)}, bf16[32,3200]{1,0:T(8,128)(2,1)S(1)}, u32[]{:S(2)}, u32[]{:S(2)}) %collective-permute-start) | collective-permute-done | bytes 204832 | tf_op jit(solution)/shard_map/ppermute | solution.py:247
  3.7 4.0 %collective-permute-start.1 = (bf16[16,3200]{1,0:T(8,128)(2,1)S(1)}, bf16[16,3200]{1,0:T(8,128)(2,1)S(1)}, u32[]{:S(2)}, u32[]{:S(2)}) collective-permute-start(bf16[16,3200]{1,0:T(8,128)(2,1)S(1)} %get-tuple-element.40), channel_id=1, source_target_pairs={{0,8},{1,13},{2,10},{3,15},{4,12},{5,9},{6,14},{7,11},{8,0},{9,5},... | collective-permute-start | bytes 307208 | tf_op jit(solution)/shard_map/ppermute | solution.py:251
  7.7 1.5 %collective-permute-start.2 = (bf16[16,3200]{1,0:T(8,128)(2,1)S(1)}, bf16[16,3200]{1,0:T(8,128)(2,1)S(1)}, u32[]{:S(2)}, u32[]{:S(2)}) collective-permute-start(bf16[16,3200]{1,0:T(8,128)(2,1)S(1)} %get-tuple-element.41), channel_id=1, source_target_pairs={{0,2},{1,5},{2,0},{3,7},{4,6},{5,1},{6,4},{7,3},{8,10},{9,13},{10,... | collective-permute-start | bytes 307208 | tf_op jit(solution)/shard_map/ppermute | solution.py:251
  9.2 0.0 collective-permute-start.3
  9.2 2.8 %collective-permute-start.4 = (bf16[8,3200]{1,0:T(8,128)(2,1)S(1)}, bf16[8,3200]{1,0:T(8,128)(2,1)S(1)}, u32[]{:S(2)}, u32[]{:S(2)}) collective-permute-start(bf16[8,3200]{1,0:T(8,128)(2,1)S(1)} %get-tuple-element.43), channel_id=1, source_target_pairs={{0,6},{1,7},{2,4},{3,5},{4,2},{5,3},{6,0},{7,1},{8,14},{9,15},{10,... | collective-permute-start | bytes 153608 | tf_op jit(solution)/shard_map/ppermute | solution.py:251
  12.0 4.2 %stage.1 = (bf16[3584,512]{1,0:T(8,128)(2,1)S(1)}, bf16[3584,512]{1,0:T(8,128)(2,1)S(1)}, bf16[512,3584]{1,0:T(8,128)(2,1)S(1)}) custom-call(bf16[3584,512]{1,0:T(8,128)(2,1)} %bitcast.5, bf16[3584,512]{1,0:T(8,128)(2,1)} %bitcast.6, bf16[512,3584]{1,0:T(8,128)(2,1)} %bitcast.7), custom_call_target="tpu_custom_call" | custom-call | flops 1 | bytes 1 | tf_op jit(solution)/shard_map/stage/pallas_call | solution.py:255
  16.3 0.1 collective-permute-done.4.refs_3_
  16.4 0.0 collective-permute-done.1.refs_0_
  16.4 0.0 collective-permute-done.2.refs_1_
  16.4 2.2 %collective-permute-done.3.refs_2_ = bf16[16,3200]{1,0:T(8,128)(2,1)S(1)} collective-permute-done((bf16[16,3200]{1,0:T(8,128)(2,1)S(1)}, bf16[16,3200]{1,0:T(8,128)(2,1)S(1)}, u32[]{:S(2)}, u32[]{:S(2)}) %collective-permute-start.3) | collective-permute-done | bytes 102432 | tf_op jit(solution)/shard_map/ppermute | solution.py:251
  18.7 0.1 collective-permute-start.5
  18.7 1.7 %collective-permute-done.5.refs_2_ = bf16[56,3200]{1,0:T(8,128)(2,1)S(1)} collective-permute-done((bf16[56,3200]{1,0:T(8,128)(2,1)S(1)}, bf16[56,3200]{1,0:T(8,128)(2,1)S(1)}, u32[]{:S(2)}, u32[]{:S(2)}) %collective-permute-start.5) | collective-permute-done | bytes 358432 | tf_op jit(solution)/shard_map/ppermute | solution.py:247
  20.4 1.8 %experts.1 = (bf16[32,3584]{1,0:T(8,128)(2,1)S(1)}, bf16[32,3584]{1,0:T(8,128)(2,1)S(1)}, bf16[32,3584]{1,0:T(8,128)(2,1)S(1)}, bf16[32,3584]{1,0:T(8,128)(2,1)S(1)}) custom-call(bf16[56,3200]{1,0:T(8,128)(2,1)S(1)} %gather.1.refs_0_, bf16[8,3200]{1,0:T(8,128)(2,1)S(1)} %get-tuple-element.51.refs_1_, bf16[56,3200]{1,0:T(8,128)(2,1)S(1)} %collective-permute-done.5.refs_2_, ...), custom_call_target="tpu_custom_call" | custom-call | flops 1 | bytes 1 | tf_op jit(solution)/shard_map/experts/pallas_call | solution.py:229
  22.2 0.2 collective-permute-start.6
  22.4 0.4 collective-permute-start.9
  22.7 1.0 %collective-permute-done.6.got_ref = bf16[32,3584]{1,0:T(8,128)(2,1)S(1)} collective-permute-done((bf16[32,3584]{1,0:T(8,128)(2,1)S(1)}, bf16[32,3584]{1,0:T(8,128)(2,1)S(1)}, u32[]{:S(2)}, u32[]{:S(2)}) %collective-permute-start.6) | collective-permute-done | bytes 229408 | tf_op jit(solution)/shard_map/ppermute | solution.py:247
  23.7 0.1 join.2
  23.8 0.6 %collective-permute-start.7 = (bf16[16,3200]{1,0:T(8,128)(2,1)S(1)}, bf16[16,3200]{1,0:T(8,128)(2,1)S(1)}, u32[]{:S(2)}, u32[]{:S(2)}) collective-permute-start(bf16[16,3200]{1,0:T(8,128)(2,1)S(1)} %get-tuple-element.58), channel_id=1, source_target_pairs={{0,8},{1,13},{2,10},{3,15},{4,12},{5,9},{6,14},{7,11},{8,0},{9,5},... | collective-permute-start | bytes 307208 | tf_op jit(solution)/shard_map/ppermute | solution.py:251
  24.4 0.5 %collective-permute-start.8 = (bf16[16,3200]{1,0:T(8,128)(2,1)S(1)}, bf16[16,3200]{1,0:T(8,128)(2,1)S(1)}, u32[]{:S(2)}, u32[]{:S(2)}) collective-permute-start(bf16[16,3200]{1,0:T(8,128)(2,1)S(1)} %get-tuple-element.59), channel_id=1, source_target_pairs={{0,2},{1,5},{2,0},{3,7},{4,6},{5,1},{6,4},{7,3},{8,10},{9,13},{10,... | collective-permute-start | bytes 307208 | tf_op jit(solution)/shard_map/ppermute | solution.py:251
  25.0 0.0 collective-permute-done.9.got_ref
  25.0 0.1 join.3
  25.1 3.4 %collective-permute-start.10 = (bf16[16,3200]{1,0:T(8,128)(2,1)S(1)}, bf16[16,3200]{1,0:T(8,128)(2,1)S(1)}, u32[]{:S(2)}, u32[]{:S(2)}) collective-permute-start(bf16[16,3200]{1,0:T(8,128)(2,1)S(1)} %get-tuple-element.62), channel_id=1, source_target_pairs={{0,10},{1,15},{2,8},{3,13},{4,14},{5,11},{6,12},{7,9},{8,2},{9,7},... | collective-permute-start | bytes 307208 | tf_op jit(solution)/shard_map/ppermute | solution.py:251
  28.4 0.8 %collective-permute-start.11 = (bf16[8,3200]{1,0:T(8,128)(2,1)S(1)}, bf16[8,3200]{1,0:T(8,128)(2,1)S(1)}, u32[]{:S(2)}, u32[]{:S(2)}) collective-permute-start(bf16[8,3200]{1,0:T(8,128)(2,1)S(1)} %get-tuple-element.63), channel_id=1, source_target_pairs={{0,6},{1,7},{2,4},{3,5},{4,2},{5,3},{6,0},{7,1},{8,14},{9,15},{10,... | collective-permute-start | bytes 153608 | tf_op jit(solution)/shard_map/ppermute | solution.py:251
  29.2 5.6 %collective-permute-done.11.refs_4_ = bf16[8,3200]{1,0:T(8,128)(2,1)S(1)} collective-permute-done((bf16[8,3200]{1,0:T(8,128)(2,1)S(1)}, bf16[8,3200]{1,0:T(8,128)(2,1)S(1)}, u32[]{:S(2)}, u32[]{:S(2)}) %collective-permute-start.11) | collective-permute-done | bytes 51232 | tf_op jit(solution)/shard_map/ppermute | solution.py:251
  34.9 0.0 collective-permute-done.7.refs_0_
  34.9 0.0 collective-permute-done.8.refs_1_
  34.9 1.0 %collective-permute-done.10.refs_2_ = bf16[16,3200]{1,0:T(8,128)(2,1)S(1)} collective-permute-done((bf16[16,3200]{1,0:T(8,128)(2,1)S(1)}, bf16[16,3200]{1,0:T(8,128)(2,1)S(1)}, u32[]{:S(2)}, u32[]{:S(2)}) %collective-permute-start.10) | collective-permute-done | bytes 102432 | tf_op jit(solution)/shard_map/ppermute | solution.py:251
  35.9 0.1 collective-permute-start.12
  36.0 1.4 %collective-permute-done.12.refs_3_ = bf16[24,3200]{1,0:T(8,128)(2,1)S(1)} collective-permute-done((bf16[24,3200]{1,0:T(8,128)(2,1)S(1)}, bf16[24,3200]{1,0:T(8,128)(2,1)S(1)}, u32[]{:S(2)}, u32[]{:S(2)}) %collective-permute-start.12) | collective-permute-done | bytes 153632 | tf_op jit(solution)/shard_map/ppermute | solution.py:247
  37.4 1.2 %combine.1 = bf16[128,3584]{1,0:T(8,128)(2,1)} custom-call(bf16[128,128]{1,0:T(8,128)(2,1)S(1)} %get-tuple-element.37.mix_ref, bf16[16,3200]{1,0:T(8,128)(2,1)S(1)} %collective-permute-done.7.refs_0_, bf16[16,3200]{1,0:T(8,128)(2,1)S(1)} %collective-permute-done.8.refs_1_, bf16[16,3200]{1,0:T(8,128)(2,1)S(1)} %collective-permute-done.10.refs_2_, ...), custom_call_target="tpu_custom_call" | custom-call | tf_op jit(solution)/shard_map/combine/pallas_call | solution.py:274
  (3 shorter events, 0.1 us)
Async XLA Ops:
  2.0 1.6 %collective-permute-start = (bf16[32,3200]{1,0:T(8,128)(2,1)S(1)}, bf16[32,3200]{1,0:T(8,128)(2,1)S(1)}, u32[]{:S(2)}, u32[]{:S(2)}) collective-permute-start(bf16[32,3200]{1,0:T(8,128)(2,1)S(1)} %get-tuple-element.39), channel_id=1, source_target_pairs={{0,1},{1,0},{2,3},{3,2},{4,5},{5,4},{6,7},{7,6},{8,9},{9,8},{10,11... | collective-permute-start | bytes 614408 | tf_op jit(solution)/shard_map/ppermute | solution.py:247
  3.7 12.7 %collective-permute-start.1 = (bf16[16,3200]{1,0:T(8,128)(2,1)S(1)}, bf16[16,3200]{1,0:T(8,128)(2,1)S(1)}, u32[]{:S(2)}, u32[]{:S(2)}) collective-permute-start(bf16[16,3200]{1,0:T(8,128)(2,1)S(1)} %get-tuple-element.40), channel_id=1, source_target_pairs={{0,8},{1,13},{2,10},{3,15},{4,12},{5,9},{6,14},{7,11},{8,0},{9,5},... | collective-permute-start | bytes 307208 | tf_op jit(solution)/shard_map/ppermute | solution.py:251
  7.7 8.7 %collective-permute-start.2 = (bf16[16,3200]{1,0:T(8,128)(2,1)S(1)}, bf16[16,3200]{1,0:T(8,128)(2,1)S(1)}, u32[]{:S(2)}, u32[]{:S(2)}) collective-permute-start(bf16[16,3200]{1,0:T(8,128)(2,1)S(1)} %get-tuple-element.41), channel_id=1, source_target_pairs={{0,2},{1,5},{2,0},{3,7},{4,6},{5,1},{6,4},{7,3},{8,10},{9,13},{10,... | collective-permute-start | bytes 307208 | tf_op jit(solution)/shard_map/ppermute | solution.py:251
  9.2 9.4 %collective-permute-start.3 = (bf16[16,3200]{1,0:T(8,128)(2,1)S(1)}, bf16[16,3200]{1,0:T(8,128)(2,1)S(1)}, u32[]{:S(2)}, u32[]{:S(2)}) collective-permute-start(bf16[16,3200]{1,0:T(8,128)(2,1)S(1)} %get-tuple-element.42), channel_id=1, source_target_pairs={{0,10},{1,15},{2,8},{3,13},{4,14},{5,11},{6,12},{7,9},{8,2},{9,7},... | collective-permute-start | bytes 307208 | tf_op jit(solution)/shard_map/ppermute | solution.py:251
  9.2 7.1 %collective-permute-start.4 = (bf16[8,3200]{1,0:T(8,128)(2,1)S(1)}, bf16[8,3200]{1,0:T(8,128)(2,1)S(1)}, u32[]{:S(2)}, u32[]{:S(2)}) collective-permute-start(bf16[8,3200]{1,0:T(8,128)(2,1)S(1)} %get-tuple-element.43), channel_id=1, source_target_pairs={{0,6},{1,7},{2,4},{3,5},{4,2},{5,3},{6,0},{7,1},{8,14},{9,15},{10,... | collective-permute-start | bytes 153608 | tf_op jit(solution)/shard_map/ppermute | solution.py:251
  18.7 1.7 %collective-permute-start.5 = (bf16[56,3200]{1,0:T(8,128)(2,1)S(1)}, bf16[56,3200]{1,0:T(8,128)(2,1)S(1)}, u32[]{:S(2)}, u32[]{:S(2)}) collective-permute-start(bf16[56,3200]{1,0:T(8,128)(2,1)S(1)} %gather.1.refs_0_), channel_id=1, source_target_pairs={{0,1},{1,0},{2,3},{3,2},{4,5},{5,4},{6,7},{7,6},{8,9},{9,8},{10,11... | collective-permute-start | bytes 1075208 | tf_op jit(solution)/shard_map/ppermute | solution.py:247
  22.2 1.6 %collective-permute-start.6 = (bf16[32,3584]{1,0:T(8,128)(2,1)S(1)}, bf16[32,3584]{1,0:T(8,128)(2,1)S(1)}, u32[]{:S(2)}, u32[]{:S(2)}) collective-permute-start(bf16[32,3584]{1,0:T(8,128)(2,1)S(1)} %get-tuple-element.57), channel_id=1, source_target_pairs={{0,1},{1,0},{2,3},{3,2},{4,5},{5,4},{6,7},{7,6},{8,9},{9,8},{10,11... | collective-permute-start | bytes 688136 | tf_op jit(solution)/shard_map/ppermute | solution.py:247
  22.4 2.6 %collective-permute-start.9 = (bf16[32,3584]{1,0:T(8,128)(2,1)S(1)}, bf16[32,3584]{1,0:T(8,128)(2,1)S(1)}, u32[]{:S(2)}, u32[]{:S(2)}) collective-permute-start(bf16[32,3584]{1,0:T(8,128)(2,1)S(1)} %get-tuple-element.61), channel_id=1, source_target_pairs={{0,1},{1,0},{2,3},{3,2},{4,5},{5,4},{6,7},{7,6},{8,9},{9,8},{10,11... | collective-permute-start | bytes 688136 | tf_op jit(solution)/shard_map/ppermute | solution.py:247
  23.8 11.1 %collective-permute-start.7 = (bf16[16,3200]{1,0:T(8,128)(2,1)S(1)}, bf16[16,3200]{1,0:T(8,128)(2,1)S(1)}, u32[]{:S(2)}, u32[]{:S(2)}) collective-permute-start(bf16[16,3200]{1,0:T(8,128)(2,1)S(1)} %get-tuple-element.58), channel_id=1, source_target_pairs={{0,8},{1,13},{2,10},{3,15},{4,12},{5,9},{6,14},{7,11},{8,0},{9,5},... | collective-permute-start | bytes 307208 | tf_op jit(solution)/shard_map/ppermute | solution.py:251
  24.4 10.4 %collective-permute-start.8 = (bf16[16,3200]{1,0:T(8,128)(2,1)S(1)}, bf16[16,3200]{1,0:T(8,128)(2,1)S(1)}, u32[]{:S(2)}, u32[]{:S(2)}) collective-permute-start(bf16[16,3200]{1,0:T(8,128)(2,1)S(1)} %get-tuple-element.59), channel_id=1, source_target_pairs={{0,2},{1,5},{2,0},{3,7},{4,6},{5,1},{6,4},{7,3},{8,10},{9,13},{10,... | collective-permute-start | bytes 307208 | tf_op jit(solution)/shard_map/ppermute | solution.py:251
  25.1 10.9 %collective-permute-start.10 = (bf16[16,3200]{1,0:T(8,128)(2,1)S(1)}, bf16[16,3200]{1,0:T(8,128)(2,1)S(1)}, u32[]{:S(2)}, u32[]{:S(2)}) collective-permute-start(bf16[16,3200]{1,0:T(8,128)(2,1)S(1)} %get-tuple-element.62), channel_id=1, source_target_pairs={{0,10},{1,15},{2,8},{3,13},{4,14},{5,11},{6,12},{7,9},{8,2},{9,7},... | collective-permute-start | bytes 307208 | tf_op jit(solution)/shard_map/ppermute | solution.py:251
  28.4 6.4 %collective-permute-start.11 = (bf16[8,3200]{1,0:T(8,128)(2,1)S(1)}, bf16[8,3200]{1,0:T(8,128)(2,1)S(1)}, u32[]{:S(2)}, u32[]{:S(2)}) collective-permute-start(bf16[8,3200]{1,0:T(8,128)(2,1)S(1)} %get-tuple-element.63), channel_id=1, source_target_pairs={{0,6},{1,7},{2,4},{3,5},{4,2},{5,3},{6,0},{7,1},{8,14},{9,15},{10,... | collective-permute-start | bytes 153608 | tf_op jit(solution)/shard_map/ppermute | solution.py:251
  35.9 1.4 %collective-permute-start.12 = (bf16[24,3200]{1,0:T(8,128)(2,1)S(1)}, bf16[24,3200]{1,0:T(8,128)(2,1)S(1)}, u32[]{:S(2)}, u32[]{:S(2)}) collective-permute-start(bf16[24,3200]{1,0:T(8,128)(2,1)S(1)} %sift.1), channel_id=1, source_target_pairs={{0,1},{1,0},{2,3},{3,2},{4,5},{5,4},{6,7},{7,6},{8,9},{9,8},{10,11... | collective-permute-start | bytes 460808 | tf_op jit(solution)/shard_map/ppermute | solution.py:247

commit v14 on v13

--- a/solution.py
+++ b/solution.py
@@ -26,7 +26,7 @@
     return flight == 8
 
 
-CARRIED = ((4, 1, 5), (6, 2, 7))
+CARRIED = ((4, 5, 1), (2, 6, 7))
 SHARED = 3
 
 

time: 38.8 us -> 39.4 us (1.015)
  waiting for transfers between devices: 14.1 us -> 14.5 us
where the time goes in v14:
time: 39.4 us; the launch traced here: 39.3 us
  starting transfers between devices  15.2 us (39%)
  waiting for transfers between devices  14.5 us (37%)
  Pallas kernels  9.51 us (24%)
    ppermute x8, starting transfers between devices, travel(): return lax.ppermute(rows, 'exp', pairs)  13.9 us
    ppermute x8, waiting for transfers between devices, travel(): return lax.ppermute(rows, 'exp', pairs)  9.39 us
    ppermute x5, waiting for transfers between devices, swap(): return lax.ppermute(rows, 'exp', [(n, n ^ 1) for n in range(owners)])  5.09 us
    pallas_call x1, Pallas kernels, stage(): pl.pallas_call(stage_kernel, out_shape=tuple((jax.ShapeDtypeStruct(w.shap...  4.24 us
    pallas_call x1, Pallas kernels, per_device(): pl.pallas_call(functools.partial(dispatch_kernel, flight), out_shape=(jax...  2.04 us
    pallas_call x6, Pallas kernels, local(): pl.pallas_call(kernel, out_shape=outs, in_specs=[VMEM] * len(args), out_s...  2.01 us
    ppermute x5, starting transfers between devices, swap(): return lax.ppermute(rows, 'exp', [(n, n ^ 1) for n in range(owners)])  1.24 us
    pallas_call x1, Pallas kernels, combine(): pl.pallas_call(functools.partial(combine_kernel, paired), out_shape=jax.S...  1.22 us
  transfers between devices with their start and end apart: 13, of which 8 were waited for; matrix products, arithmetic and copies ran while one was open for 0% of the time, Pallas kernels for 11%

profile of v14, /device:TPU:0, one launch (start us, length us, event | category | flops | bytes accessed | tf_op | source)
XLA Modules:
  0.0 39.3 jit_solution(5374720872582546012)
XLA Ops:
  0.0 2.0 %dispatch.1 = (bf16[128,128]{1,0:T(8,128)(2,1)S(1)}, bf16[24,3200]{1,0:T(8,128)(2,1)S(1)}, bf16[32,3200]{1,0:T(8,128)(2,1)S(1)}, bf16[8,3200]{1,0:T(8,128)(2,1)S(1)}, bf16[8,3200]{1,0:T(8,128)(2,1)S(1)}) custom-call(bf16[128,3584]{1,0:T(8,128)(2,1)} %tok_hbm.1, f32[3584]{0:T(1024)} %gain_hbm.1, s32[8,128]{1,0:T(8,128)} %bitcast.8, f32[8,128]{1,0:T(8,128)} %bitcast.9), custom_call_target="tpu_custom_call" | custom-call | tf_op jit(solution)/shard_map/dispatch/pallas_call | solution.py:288
  2.0 0.5 %collective-permute-start = (bf16[32,3200]{1,0:T(8,128)(2,1)S(1)}, bf16[32,3200]{1,0:T(8,128)(2,1)S(1)}, u32[]{:S(2)}, u32[]{:S(2)}) collective-permute-start(bf16[32,3200]{1,0:T(8,128)(2,1)S(1)} %get-tuple-element.39), channel_id=1, source_target_pairs={{0,1},{1,0},{2,3},{3,2},{4,5},{5,4},{6,7},{7,6},{8,9},{9,8},{10,11... | collective-permute-start | bytes 614408 | tf_op jit(solution)/shard_map/ppermute | solution.py:247
  2.6 1.1 %collective-permute-done.got_ref = bf16[32,3200]{1,0:T(8,128)(2,1)S(1)} collective-permute-done((bf16[32,3200]{1,0:T(8,128)(2,1)S(1)}, bf16[32,3200]{1,0:T(8,128)(2,1)S(1)}, u32[]{:S(2)}, u32[]{:S(2)}) %collective-permute-start) | collective-permute-done | bytes 204832 | tf_op jit(solution)/shard_map/ppermute | solution.py:247
  3.7 4.0 %collective-permute-start.1 = (bf16[16,3200]{1,0:T(8,128)(2,1)S(1)}, bf16[16,3200]{1,0:T(8,128)(2,1)S(1)}, u32[]{:S(2)}, u32[]{:S(2)}) collective-permute-start(bf16[16,3200]{1,0:T(8,128)(2,1)S(1)} %get-tuple-element.40), channel_id=1, source_target_pairs={{0,8},{1,5},{2,10},{3,7},{4,12},{5,1},{6,14},{7,3},{8,0},{9,13},{1... | collective-permute-start | bytes 307208 | tf_op jit(solution)/shard_map/ppermute | solution.py:251
  7.7 1.3 %collective-permute-start.2 = (bf16[16,3200]{1,0:T(8,128)(2,1)S(1)}, bf16[16,3200]{1,0:T(8,128)(2,1)S(1)}, u32[]{:S(2)}, u32[]{:S(2)}) collective-permute-start(bf16[16,3200]{1,0:T(8,128)(2,1)S(1)} %get-tuple-element.41), channel_id=1, source_target_pairs={{0,10},{1,13},{2,8},{3,15},{4,14},{5,9},{6,12},{7,11},{8,2},{9,5},... | collective-permute-start | bytes 307208 | tf_op jit(solution)/shard_map/ppermute | solution.py:251
  9.0 0.3 collective-permute-start.3
  9.2 2.8 %collective-permute-start.4 = (bf16[8,3200]{1,0:T(8,128)(2,1)S(1)}, bf16[8,3200]{1,0:T(8,128)(2,1)S(1)}, u32[]{:S(2)}, u32[]{:S(2)}) collective-permute-start(bf16[8,3200]{1,0:T(8,128)(2,1)S(1)} %get-tuple-element.43), channel_id=1, source_target_pairs={{0,6},{1,7},{2,4},{3,5},{4,2},{5,3},{6,0},{7,1},{8,14},{9,15},{10,... | collective-permute-start | bytes 153608 | tf_op jit(solution)/shard_map/ppermute | solution.py:251
  12.0 4.2 %stage.1 = (bf16[3584,512]{1,0:T(8,128)(2,1)S(1)}, bf16[3584,512]{1,0:T(8,128)(2,1)S(1)}, bf16[512,3584]{1,0:T(8,128)(2,1)S(1)}) custom-call(bf16[3584,512]{1,0:T(8,128)(2,1)} %bitcast.5, bf16[3584,512]{1,0:T(8,128)(2,1)} %bitcast.6, bf16[512,3584]{1,0:T(8,128)(2,1)} %bitcast.7), custom_call_target="tpu_custom_call" | custom-call | flops 1 | bytes 1 | tf_op jit(solution)/shard_map/stage/pallas_call | solution.py:255
  16.3 0.0 collective-permute-done.4.refs_3_
  16.3 0.0 collective-permute-done.1.refs_0_
  16.3 2.7 %collective-permute-done.2.refs_1_ = bf16[16,3200]{1,0:T(8,128)(2,1)S(1)} collective-permute-done((bf16[16,3200]{1,0:T(8,128)(2,1)S(1)}, bf16[16,3200]{1,0:T(8,128)(2,1)S(1)}, u32[]{:S(2)}, u32[]{:S(2)}) %collective-permute-start.2) | collective-permute-done | bytes 102432 | tf_op jit(solution)/shard_map/ppermute | solution.py:251
  19.0 0.0 collective-permute-done.3.refs_2_
  19.0 0.1 collective-permute-start.5
  19.1 1.7 %collective-permute-done.5.refs_2_ = bf16[56,3200]{1,0:T(8,128)(2,1)S(1)} collective-permute-done((bf16[56,3200]{1,0:T(8,128)(2,1)S(1)}, bf16[56,3200]{1,0:T(8,128)(2,1)S(1)}, u32[]{:S(2)}, u32[]{:S(2)}) %collective-permute-start.5) | collective-permute-done | bytes 358432 | tf_op jit(solution)/shard_map/ppermute | solution.py:247
  20.7 1.8 %experts.1 = (bf16[32,3584]{1,0:T(8,128)(2,1)S(1)}, bf16[32,3584]{1,0:T(8,128)(2,1)S(1)}, bf16[32,3584]{1,0:T(8,128)(2,1)S(1)}, bf16[32,3584]{1,0:T(8,128)(2,1)S(1)}) custom-call(bf16[56,3200]{1,0:T(8,128)(2,1)S(1)} %gather.1.refs_0_, bf16[8,3200]{1,0:T(8,128)(2,1)S(1)} %get-tuple-element.51.refs_1_, bf16[56,3200]{1,0:T(8,128)(2,1)S(1)} %collective-permute-done.5.refs_2_, ...), custom_call_target="tpu_custom_call" | custom-call | flops 1 | bytes 1 | tf_op jit(solution)/shard_map/experts/pallas_call | solution.py:229
  22.5 0.2 collective-permute-start.6
  22.7 0.4 collective-permute-start.9
  23.1 1.0 %collective-permute-done.6.got_ref = bf16[32,3584]{1,0:T(8,128)(2,1)S(1)} collective-permute-done((bf16[32,3584]{1,0:T(8,128)(2,1)S(1)}, bf16[32,3584]{1,0:T(8,128)(2,1)S(1)}, u32[]{:S(2)}, u32[]{:S(2)}) %collective-permute-start.6) | collective-permute-done | bytes 229408 | tf_op jit(solution)/shard_map/ppermute | solution.py:247
  24.1 0.1 join.2
  24.2 1.6 %collective-permute-start.7 = (bf16[16,3200]{1,0:T(8,128)(2,1)S(1)}, bf16[16,3200]{1,0:T(8,128)(2,1)S(1)}, u32[]{:S(2)}, u32[]{:S(2)}) collective-permute-start(bf16[16,3200]{1,0:T(8,128)(2,1)S(1)} %get-tuple-element.58), channel_id=1, source_target_pairs={{0,8},{1,5},{2,10},{3,7},{4,12},{5,1},{6,14},{7,3},{8,0},{9,13},{1... | collective-permute-start | bytes 307208 | tf_op jit(solution)/shard_map/ppermute | solution.py:251
  25.7 1.0 %collective-permute-start.8 = (bf16[16,3200]{1,0:T(8,128)(2,1)S(1)}, bf16[16,3200]{1,0:T(8,128)(2,1)S(1)}, u32[]{:S(2)}, u32[]{:S(2)}) collective-permute-start(bf16[16,3200]{1,0:T(8,128)(2,1)S(1)} %get-tuple-element.59), channel_id=1, source_target_pairs={{0,10},{1,13},{2,8},{3,15},{4,14},{5,9},{6,12},{7,11},{8,2},{9,5},... | collective-permute-start | bytes 307208 | tf_op jit(solution)/shard_map/ppermute | solution.py:251
  26.7 0.0 collective-permute-done.9.got_ref
  26.7 0.1 join.3
  26.8 1.9 %collective-permute-start.10 = (bf16[16,3200]{1,0:T(8,128)(2,1)S(1)}, bf16[16,3200]{1,0:T(8,128)(2,1)S(1)}, u32[]{:S(2)}, u32[]{:S(2)}) collective-permute-start(bf16[16,3200]{1,0:T(8,128)(2,1)S(1)} %get-tuple-element.62), channel_id=1, source_target_pairs={{0,2},{1,15},{2,0},{3,13},{4,6},{5,11},{6,4},{7,9},{8,10},{9,7},{1... | collective-permute-start | bytes 307208 | tf_op jit(solution)/shard_map/ppermute | solution.py:251
  28.8 1.1 %collective-permute-start.11 = (bf16[8,3200]{1,0:T(8,128)(2,1)S(1)}, bf16[8,3200]{1,0:T(8,128)(2,1)S(1)}, u32[]{:S(2)}, u32[]{:S(2)}) collective-permute-start(bf16[8,3200]{1,0:T(8,128)(2,1)S(1)} %get-tuple-element.63), channel_id=1, source_target_pairs={{0,6},{1,7},{2,4},{3,5},{4,2},{5,3},{6,0},{7,1},{8,14},{9,15},{10,... | collective-permute-start | bytes 153608 | tf_op jit(solution)/shard_map/ppermute | solution.py:251
  29.8 4.5 %collective-permute-done.11.refs_4_ = bf16[8,3200]{1,0:T(8,128)(2,1)S(1)} collective-permute-done((bf16[8,3200]{1,0:T(8,128)(2,1)S(1)}, bf16[8,3200]{1,0:T(8,128)(2,1)S(1)}, u32[]{:S(2)}, u32[]{:S(2)}) %collective-permute-start.11) | collective-permute-done | bytes 51232 | tf_op jit(solution)/shard_map/ppermute | solution.py:251
  34.3 0.7 %collective-permute-done.7.refs_0_ = bf16[16,3200]{1,0:T(8,128)(2,1)S(1)} collective-permute-done((bf16[16,3200]{1,0:T(8,128)(2,1)S(1)}, bf16[16,3200]{1,0:T(8,128)(2,1)S(1)}, u32[]{:S(2)}, u32[]{:S(2)}) %collective-permute-start.7) | collective-permute-done | bytes 102432 | tf_op jit(solution)/shard_map/ppermute | solution.py:251
  35.0 1.5 %collective-permute-done.8.refs_1_ = bf16[16,3200]{1,0:T(8,128)(2,1)S(1)} collective-permute-done((bf16[16,3200]{1,0:T(8,128)(2,1)S(1)}, bf16[16,3200]{1,0:T(8,128)(2,1)S(1)}, u32[]{:S(2)}, u32[]{:S(2)}) %collective-permute-start.8) | collective-permute-done | bytes 102432 | tf_op jit(solution)/shard_map/ppermute | solution.py:251
  36.6 0.0 collective-permute-done.10.refs_2_
  36.6 0.1 collective-permute-start.12
  36.7 1.4 %collective-permute-done.12.refs_3_ = bf16[24,3200]{1,0:T(8,128)(2,1)S(1)} collective-permute-done((bf16[24,3200]{1,0:T(8,128)(2,1)S(1)}, bf16[24,3200]{1,0:T(8,128)(2,1)S(1)}, u32[]{:S(2)}, u32[]{:S(2)}) %collective-permute-start.12) | collective-permute-done | bytes 153632 | tf_op jit(solution)/shard_map/ppermute | solution.py:247
  38.0 1.2 %combine.1 = bf16[128,3584]{1,0:T(8,128)(2,1)} custom-call(bf16[128,128]{1,0:T(8,128)(2,1)S(1)} %get-tuple-element.37.mix_ref, bf16[16,3200]{1,0:T(8,128)(2,1)S(1)} %collective-permute-done.7.refs_0_, bf16[16,3200]{1,0:T(8,128)(2,1)S(1)} %collective-permute-done.8.refs_1_, bf16[16,3200]{1,0:T(8,128)(2,1)S(1)} %collective-permute-done.10.refs_2_, ...), custom_call_target="tpu_custom_call" | custom-call | tf_op jit(solution)/shard_map/combine/pallas_call | solution.py:274
  (3 shorter events, 0.1 us)
Async XLA Ops:
  2.0 1.6 %collective-permute-start = (bf16[32,3200]{1,0:T(8,128)(2,1)S(1)}, bf16[32,3200]{1,0:T(8,128)(2,1)S(1)}, u32[]{:S(2)}, u32[]{:S(2)}) collective-permute-start(bf16[32,3200]{1,0:T(8,128)(2,1)S(1)} %get-tuple-element.39), channel_id=1, source_target_pairs={{0,1},{1,0},{2,3},{3,2},{4,5},{5,4},{6,7},{7,6},{8,9},{9,8},{10,11... | collective-permute-start | bytes 614408 | tf_op jit(solution)/shard_map/ppermute | solution.py:247
  3.7 12.6 %collective-permute-start.1 = (bf16[16,3200]{1,0:T(8,128)(2,1)S(1)}, bf16[16,3200]{1,0:T(8,128)(2,1)S(1)}, u32[]{:S(2)}, u32[]{:S(2)}) collective-permute-start(bf16[16,3200]{1,0:T(8,128)(2,1)S(1)} %get-tuple-element.40), channel_id=1, source_target_pairs={{0,8},{1,5},{2,10},{3,7},{4,12},{5,1},{6,14},{7,3},{8,0},{9,13},{1... | collective-permute-start | bytes 307208 | tf_op jit(solution)/shard_map/ppermute | solution.py:251
  7.7 11.3 %collective-permute-start.2 = (bf16[16,3200]{1,0:T(8,128)(2,1)S(1)}, bf16[16,3200]{1,0:T(8,128)(2,1)S(1)}, u32[]{:S(2)}, u32[]{:S(2)}) collective-permute-start(bf16[16,3200]{1,0:T(8,128)(2,1)S(1)} %get-tuple-element.41), channel_id=1, source_target_pairs={{0,10},{1,13},{2,8},{3,15},{4,14},{5,9},{6,12},{7,11},{8,2},{9,5},... | collective-permute-start | bytes 307208 | tf_op jit(solution)/shard_map/ppermute | solution.py:251
  9.0 10.0 %collective-permute-start.3 = (bf16[16,3200]{1,0:T(8,128)(2,1)S(1)}, bf16[16,3200]{1,0:T(8,128)(2,1)S(1)}, u32[]{:S(2)}, u32[]{:S(2)}) collective-permute-start(bf16[16,3200]{1,0:T(8,128)(2,1)S(1)} %get-tuple-element.42), channel_id=1, source_target_pairs={{0,2},{1,15},{2,0},{3,13},{4,6},{5,11},{6,4},{7,9},{8,10},{9,7},{1... | collective-permute-start | bytes 307208 | tf_op jit(solution)/shard_map/ppermute | solution.py:251
  9.2 7.0 %collective-permute-start.4 = (bf16[8,3200]{1,0:T(8,128)(2,1)S(1)}, bf16[8,3200]{1,0:T(8,128)(2,1)S(1)}, u32[]{:S(2)}, u32[]{:S(2)}) collective-permute-start(bf16[8,3200]{1,0:T(8,128)(2,1)S(1)} %get-tuple-element.43), channel_id=1, source_target_pairs={{0,6},{1,7},{2,4},{3,5},{4,2},{5,3},{6,0},{7,1},{8,14},{9,15},{10,... | collective-permute-start | bytes 153608 | tf_op jit(solution)/shard_map/ppermute | solution.py:251
  19.0 1.7 %collective-permute-start.5 = (bf16[56,3200]{1,0:T(8,128)(2,1)S(1)}, bf16[56,3200]{1,0:T(8,128)(2,1)S(1)}, u32[]{:S(2)}, u32[]{:S(2)}) collective-permute-start(bf16[56,3200]{1,0:T(8,128)(2,1)S(1)} %gather.1.refs_0_), channel_id=1, source_target_pairs={{0,1},{1,0},{2,3},{3,2},{4,5},{5,4},{6,7},{7,6},{8,9},{9,8},{10,11... | collective-permute-start | bytes 1075208 | tf_op jit(solution)/shard_map/ppermute | solution.py:247
  22.5 1.6 %collective-permute-start.6 = (bf16[32,3584]{1,0:T(8,128)(2,1)S(1)}, bf16[32,3584]{1,0:T(8,128)(2,1)S(1)}, u32[]{:S(2)}, u32[]{:S(2)}) collective-permute-start(bf16[32,3584]{1,0:T(8,128)(2,1)S(1)} %get-tuple-element.57), channel_id=1, source_target_pairs={{0,1},{1,0},{2,3},{3,2},{4,5},{5,4},{6,7},{7,6},{8,9},{9,8},{10,11... | collective-permute-start | bytes 688136 | tf_op jit(solution)/shard_map/ppermute | solution.py:247
  22.7 4.0 %collective-permute-start.9 = (bf16[32,3584]{1,0:T(8,128)(2,1)S(1)}, bf16[32,3584]{1,0:T(8,128)(2,1)S(1)}, u32[]{:S(2)}, u32[]{:S(2)}) collective-permute-start(bf16[32,3584]{1,0:T(8,128)(2,1)S(1)} %get-tuple-element.61), channel_id=1, source_target_pairs={{0,1},{1,0},{2,3},{3,2},{4,5},{5,4},{6,7},{7,6},{8,9},{9,8},{10,11... | collective-permute-start | bytes 688136 | tf_op jit(solution)/shard_map/ppermute | solution.py:247
  24.2 10.9 %collective-permute-start.7 = (bf16[16,3200]{1,0:T(8,128)(2,1)S(1)}, bf16[16,3200]{1,0:T(8,128)(2,1)S(1)}, u32[]{:S(2)}, u32[]{:S(2)}) collective-permute-start(bf16[16,3200]{1,0:T(8,128)(2,1)S(1)} %get-tuple-element.58), channel_id=1, source_target_pairs={{0,8},{1,5},{2,10},{3,7},{4,12},{5,1},{6,14},{7,3},{8,0},{9,13},{1... | collective-permute-start | bytes 307208 | tf_op jit(solution)/shard_map/ppermute | solution.py:251
  25.7 10.9 %collective-permute-start.8 = (bf16[16,3200]{1,0:T(8,128)(2,1)S(1)}, bf16[16,3200]{1,0:T(8,128)(2,1)S(1)}, u32[]{:S(2)}, u32[]{:S(2)}) collective-permute-start(bf16[16,3200]{1,0:T(8,128)(2,1)S(1)} %get-tuple-element.59), channel_id=1, source_target_pairs={{0,10},{1,13},{2,8},{3,15},{4,14},{5,9},{6,12},{7,11},{8,2},{9,5},... | collective-permute-start | bytes 307208 | tf_op jit(solution)/shard_map/ppermute | solution.py:251
  26.8 9.7 %collective-permute-start.10 = (bf16[16,3200]{1,0:T(8,128)(2,1)S(1)}, bf16[16,3200]{1,0:T(8,128)(2,1)S(1)}, u32[]{:S(2)}, u32[]{:S(2)}) collective-permute-start(bf16[16,3200]{1,0:T(8,128)(2,1)S(1)} %get-tuple-element.62), channel_id=1, source_target_pairs={{0,2},{1,15},{2,0},{3,13},{4,6},{5,11},{6,4},{7,9},{8,10},{9,7},{1... | collective-permute-start | bytes 307208 | tf_op jit(solution)/shard_map/ppermute | solution.py:251
  28.8 5.6 %collective-permute-start.11 = (bf16[8,3200]{1,0:T(8,128)(2,1)S(1)}, bf16[8,3200]{1,0:T(8,128)(2,1)S(1)}, u32[]{:S(2)}, u32[]{:S(2)}) collective-permute-start(bf16[8,3200]{1,0:T(8,128)(2,1)S(1)} %get-tuple-element.63), channel_id=1, source_target_pairs={{0,6},{1,7},{2,4},{3,5},{4,2},{5,3},{6,0},{7,1},{8,14},{9,15},{10,... | collective-permute-start | bytes 153608 | tf_op jit(solution)/shard_map/ppermute | solution.py:251
  36.6 1.4 %collective-permute-start.12 = (bf16[24,3200]{1,0:T(8,128)(2,1)S(1)}, bf16[24,3200]{1,0:T(8,128)(2,1)S(1)}, u32[]{:S(2)}, u32[]{:S(2)}) collective-permute-start(bf16[24,3200]{1,0:T(8,128)(2,1)S(1)} %sift.1), channel_id=1, source_target_pairs={{0,1},{1,0},{2,3},{3,2},{4,5},{5,4},{6,7},{7,6},{8,9},{9,8},{10,11... | collective-permute-start | bytes 460808 | tf_op jit(solution)/shard_map/ppermute | solution.py:247

commit v15 on v13

--- a/solution.py
+++ b/solution.py
@@ -77,7 +77,7 @@
 
 
 def dispatch_kernel(flight, tok_hbm, gain_hbm, ids_hbm, gw_hbm, mix_ref, *rest):
-    *outs, tok, gain, ids, gw, normed, sems = rest
+    *outs, tok, gain, ids, gw, sems = rest
     count = tok.shape[0]
     part = count // CHUNKS
     small = [
@@ -122,15 +122,13 @@
     mix_ref[: flight * SLOTS, :] = high
     mix_ref[flight * SLOTS :, :] = (mix - high.astype(jnp.float32)).astype(jnp.bfloat16)
 
+    for copy in large:
+        copy.wait()
+    wide = jnp.dot(pick, tok[...], preferred_element_type=jnp.float32)
+    mean_square = jnp.mean(wide * wide, axis=1, keepdims=True)
     small[2].wait()
-    for i in range(CHUNKS):
-        large[i].wait()
-        wide = tok[pl.ds(i * part, part), :].astype(jnp.float32)
-        mean_square = jnp.mean(wide * wide, axis=1, keepdims=True)
-        normed[pl.ds(i * part, part), :] = (
-            wide * lax.rsqrt(mean_square + 1e-06) * gain[...]
-        ).astype(jnp.bfloat16)
-    rows = jnp.dot(pick, normed[...], preferred_element_type=jnp.float32)
+    rows = (wide * lax.rsqrt(mean_square + 1e-06) * gain[...]).astype(jnp.bfloat16)
+    rows = rows.astype(jnp.float32)
     blocks = pack(rows)
     if len(outs) == 1:
         store(outs, blocks)
@@ -295,7 +293,6 @@
             pltpu.VMEM((1, width), jnp.float32),
             pltpu.VMEM(expert_ids.shape[::-1], jnp.int32),
             pltpu.VMEM(gate_weights.shape[::-1], jnp.float32),
-            pltpu.VMEM((count, width), jnp.bfloat16),
             pltpu.SemaphoreType.DMA((3 + CHUNKS,)),
         ],
         compiler_params=pltpu.CompilerParams(vmem_limit_bytes=24 * 2**20),

time: 38.8 us -> 38.6 us (level)
  transfers between devices with their start and end apart: 13 -> 13, of which waited for: 8 -> 8; matrix products, arithmetic and copies ran while one was open for 0% -> 0% of each run, Pallas kernels for 11% -> 12%
where the time goes in v15:
time: 38.6 us; the launch traced here: 38.5 us
  starting transfers between devices  14.9 us (39%)
  waiting for transfers between devices  14.1 us (37%)
  Pallas kernels  9.37 us (24%)
    ppermute x8, starting transfers between devices, travel(): return lax.ppermute(rows, 'exp', pairs)  13.6 us
    ppermute x8, waiting for transfers between devices, travel(): return lax.ppermute(rows, 'exp', pairs)  9.03 us
    ppermute x5, waiting for transfers between devices, swap(): return lax.ppermute(rows, 'exp', [(n, n ^ 1) for n in range(owners)])  5.09 us
    pallas_call x1, Pallas kernels, stage(): pl.pallas_call(stage_kernel, out_shape=tuple((jax.ShapeDtypeStruct(w.shap...  4.24 us
    pallas_call x6, Pallas kernels, local(): pl.pallas_call(kernel, out_shape=outs, in_specs=[VMEM] * len(args), out_s...  2.01 us
    pallas_call x1, Pallas kernels, per_device(): pl.pallas_call(functools.partial(dispatch_kernel, flight), out_shape=(jax...  1.91 us
    ppermute x5, starting transfers between devices, swap(): return lax.ppermute(rows, 'exp', [(n, n ^ 1) for n in range(owners)])  1.24 us
    pallas_call x1, Pallas kernels, combine(): pl.pallas_call(functools.partial(combine_kernel, paired), out_shape=jax.S...  1.21 us
  transfers between devices with their start and end apart: 13, of which 8 were waited for; matrix products, arithmetic and copies ran while one was open for 0% of the time, Pallas kernels for 12%

profile of v15, /device:TPU:0, one launch (start us, length us, event | category | flops | bytes accessed | tf_op | source)
XLA Modules:
  0.0 38.5 jit_solution(8258665327346781705)
XLA Ops:
  0.0 1.9 %dispatch.1 = (bf16[128,128]{1,0:T(8,128)(2,1)S(1)}, bf16[24,3200]{1,0:T(8,128)(2,1)S(1)}, bf16[32,3200]{1,0:T(8,128)(2,1)S(1)}, bf16[8,3200]{1,0:T(8,128)(2,1)S(1)}, bf16[8,3200]{1,0:T(8,128)(2,1)S(1)}) custom-call(bf16[128,3584]{1,0:T(8,128)(2,1)} %tok_hbm.1, f32[3584]{0:T(1024)} %gain_hbm.1, s32[8,128]{1,0:T(8,128)} %bitcast.8, f32[8,128]{1,0:T(8,128)} %bitcast.9), custom_call_target="tpu_custom_call" | custom-call | tf_op jit(solution)/shard_map/dispatch/pallas_call | solution.py:286
  1.9 0.5 %collective-permute-start = (bf16[32,3200]{1,0:T(8,128)(2,1)S(1)}, bf16[32,3200]{1,0:T(8,128)(2,1)S(1)}, u32[]{:S(2)}, u32[]{:S(2)}) collective-permute-start(bf16[32,3200]{1,0:T(8,128)(2,1)S(1)} %get-tuple-element.39), channel_id=1, source_target_pairs={{0,1},{1,0},{2,3},{3,2},{4,5},{5,4},{6,7},{7,6},{8,9},{9,8},{10,11... | collective-permute-start | bytes 614408 | tf_op jit(solution)/shard_map/ppermute | solution.py:245
  2.4 1.1 %collective-permute-done.got_ref = bf16[32,3200]{1,0:T(8,128)(2,1)S(1)} collective-permute-done((bf16[32,3200]{1,0:T(8,128)(2,1)S(1)}, bf16[32,3200]{1,0:T(8,128)(2,1)S(1)}, u32[]{:S(2)}, u32[]{:S(2)}) %collective-permute-start) | collective-permute-done | bytes 204832 | tf_op jit(solution)/shard_map/ppermute | solution.py:245
  3.5 4.0 %collective-permute-start.1 = (bf16[16,3200]{1,0:T(8,128)(2,1)S(1)}, bf16[16,3200]{1,0:T(8,128)(2,1)S(1)}, u32[]{:S(2)}, u32[]{:S(2)}) collective-permute-start(bf16[16,3200]{1,0:T(8,128)(2,1)S(1)} %get-tuple-element.40), channel_id=1, source_target_pairs={{0,8},{1,13},{2,10},{3,15},{4,12},{5,9},{6,14},{7,11},{8,0},{9,5},... | collective-permute-start | bytes 307208 | tf_op jit(solution)/shard_map/ppermute | solution.py:249
  7.6 1.5 %collective-permute-start.2 = (bf16[16,3200]{1,0:T(8,128)(2,1)S(1)}, bf16[16,3200]{1,0:T(8,128)(2,1)S(1)}, u32[]{:S(2)}, u32[]{:S(2)}) collective-permute-start(bf16[16,3200]{1,0:T(8,128)(2,1)S(1)} %get-tuple-element.41), channel_id=1, source_target_pairs={{0,2},{1,5},{2,0},{3,7},{4,6},{5,1},{6,4},{7,3},{8,10},{9,13},{10,... | collective-permute-start | bytes 307208 | tf_op jit(solution)/shard_map/ppermute | solution.py:249
  9.1 0.0 collective-permute-start.3
  9.1 2.8 %collective-permute-start.4 = (bf16[8,3200]{1,0:T(8,128)(2,1)S(1)}, bf16[8,3200]{1,0:T(8,128)(2,1)S(1)}, u32[]{:S(2)}, u32[]{:S(2)}) collective-permute-start(bf16[8,3200]{1,0:T(8,128)(2,1)S(1)} %get-tuple-element.43), channel_id=1, source_target_pairs={{0,6},{1,7},{2,4},{3,5},{4,2},{5,3},{6,0},{7,1},{8,14},{9,15},{10,... | collective-permute-start | bytes 153608 | tf_op jit(solution)/shard_map/ppermute | solution.py:249
  11.9 4.2 %stage.1 = (bf16[3584,512]{1,0:T(8,128)(2,1)S(1)}, bf16[3584,512]{1,0:T(8,128)(2,1)S(1)}, bf16[512,3584]{1,0:T(8,128)(2,1)S(1)}) custom-call(bf16[3584,512]{1,0:T(8,128)(2,1)} %bitcast.5, bf16[3584,512]{1,0:T(8,128)(2,1)} %bitcast.6, bf16[512,3584]{1,0:T(8,128)(2,1)} %bitcast.7), custom_call_target="tpu_custom_call" | custom-call | flops 1 | bytes 1 | tf_op jit(solution)/shard_map/stage/pallas_call | solution.py:253
  16.2 0.1 collective-permute-done.4.refs_3_
  16.2 0.0 collective-permute-done.1.refs_0_
  16.2 0.0 collective-permute-done.2.refs_1_
  16.2 2.3 %collective-permute-done.3.refs_2_ = bf16[16,3200]{1,0:T(8,128)(2,1)S(1)} collective-permute-done((bf16[16,3200]{1,0:T(8,128)(2,1)S(1)}, bf16[16,3200]{1,0:T(8,128)(2,1)S(1)}, u32[]{:S(2)}, u32[]{:S(2)}) %collective-permute-start.3) | collective-permute-done | bytes 102432 | tf_op jit(solution)/shard_map/ppermute | solution.py:249
  18.5 0.1 collective-permute-start.5
  18.6 1.7 %collective-permute-done.5.refs_2_ = bf16[56,3200]{1,0:T(8,128)(2,1)S(1)} collective-permute-done((bf16[56,3200]{1,0:T(8,128)(2,1)S(1)}, bf16[56,3200]{1,0:T(8,128)(2,1)S(1)}, u32[]{:S(2)}, u32[]{:S(2)}) %collective-permute-start.5) | collective-permute-done | bytes 358432 | tf_op jit(solution)/shard_map/ppermute | solution.py:245
  20.3 1.8 %experts.1 = (bf16[32,3584]{1,0:T(8,128)(2,1)S(1)}, bf16[32,3584]{1,0:T(8,128)(2,1)S(1)}, bf16[32,3584]{1,0:T(8,128)(2,1)S(1)}, bf16[32,3584]{1,0:T(8,128)(2,1)S(1)}) custom-call(bf16[56,3200]{1,0:T(8,128)(2,1)S(1)} %gather.1.refs_0_, bf16[8,3200]{1,0:T(8,128)(2,1)S(1)} %get-tuple-element.51.refs_1_, bf16[56,3200]{1,0:T(8,128)(2,1)S(1)} %collective-permute-done.5.refs_2_, ...), custom_call_target="tpu_custom_call" | custom-call | flops 1 | bytes 1 | tf_op jit(solution)/shard_map/experts/pallas_call | solution.py:227
  22.0 0.2 collective-permute-start.6
  22.2 0.4 collective-permute-start.9
  22.6 1.0 %collective-permute-done.6.got_ref = bf16[32,3584]{1,0:T(8,128)(2,1)S(1)} collective-permute-done((bf16[32,3584]{1,0:T(8,128)(2,1)S(1)}, bf16[32,3584]{1,0:T(8,128)(2,1)S(1)}, u32[]{:S(2)}, u32[]{:S(2)}) %collective-permute-start.6) | collective-permute-done | bytes 229408 | tf_op jit(solution)/shard_map/ppermute | solution.py:245
  23.6 0.1 join.2
  23.7 0.6 %collective-permute-start.7 = (bf16[16,3200]{1,0:T(8,128)(2,1)S(1)}, bf16[16,3200]{1,0:T(8,128)(2,1)S(1)}, u32[]{:S(2)}, u32[]{:S(2)}) collective-permute-start(bf16[16,3200]{1,0:T(8,128)(2,1)S(1)} %get-tuple-element.58), channel_id=1, source_target_pairs={{0,8},{1,13},{2,10},{3,15},{4,12},{5,9},{6,14},{7,11},{8,0},{9,5},... | collective-permute-start | bytes 307208 | tf_op jit(solution)/shard_map/ppermute | solution.py:249
  24.3 0.5 %collective-permute-start.8 = (bf16[16,3200]{1,0:T(8,128)(2,1)S(1)}, bf16[16,3200]{1,0:T(8,128)(2,1)S(1)}, u32[]{:S(2)}, u32[]{:S(2)}) collective-permute-start(bf16[16,3200]{1,0:T(8,128)(2,1)S(1)} %get-tuple-element.59), channel_id=1, source_target_pairs={{0,2},{1,5},{2,0},{3,7},{4,6},{5,1},{6,4},{7,3},{8,10},{9,13},{10,... | collective-permute-start | bytes 307208 | tf_op jit(solution)/shard_map/ppermute | solution.py:249
  24.8 0.0 collective-permute-done.9.got_ref
  24.8 0.1 join.3
  24.9 3.4 %collective-permute-start.10 = (bf16[16,3200]{1,0:T(8,128)(2,1)S(1)}, bf16[16,3200]{1,0:T(8,128)(2,1)S(1)}, u32[]{:S(2)}, u32[]{:S(2)}) collective-permute-start(bf16[16,3200]{1,0:T(8,128)(2,1)S(1)} %get-tuple-element.62), channel_id=1, source_target_pairs={{0,10},{1,15},{2,8},{3,13},{4,14},{5,11},{6,12},{7,9},{8,2},{9,7},... | collective-permute-start | bytes 307208 | tf_op jit(solution)/shard_map/ppermute | solution.py:249
  28.3 0.8 %collective-permute-start.11 = (bf16[8,3200]{1,0:T(8,128)(2,1)S(1)}, bf16[8,3200]{1,0:T(8,128)(2,1)S(1)}, u32[]{:S(2)}, u32[]{:S(2)}) collective-permute-start(bf16[8,3200]{1,0:T(8,128)(2,1)S(1)} %get-tuple-element.63), channel_id=1, source_target_pairs={{0,6},{1,7},{2,4},{3,5},{4,2},{5,3},{6,0},{7,1},{8,14},{9,15},{10,... | collective-permute-start | bytes 153608 | tf_op jit(solution)/shard_map/ppermute | solution.py:249
  29.1 5.6 %collective-permute-done.11.refs_4_ = bf16[8,3200]{1,0:T(8,128)(2,1)S(1)} collective-permute-done((bf16[8,3200]{1,0:T(8,128)(2,1)S(1)}, bf16[8,3200]{1,0:T(8,128)(2,1)S(1)}, u32[]{:S(2)}, u32[]{:S(2)}) %collective-permute-start.11) | collective-permute-done | bytes 51232 | tf_op jit(solution)/shard_map/ppermute | solution.py:249
  34.7 0.0 collective-permute-done.7.refs_0_
  34.7 0.0 collective-permute-done.8.refs_1_
  34.7 1.0 %collective-permute-done.10.refs_2_ = bf16[16,3200]{1,0:T(8,128)(2,1)S(1)} collective-permute-done((bf16[16,3200]{1,0:T(8,128)(2,1)S(1)}, bf16[16,3200]{1,0:T(8,128)(2,1)S(1)}, u32[]{:S(2)}, u32[]{:S(2)}) %collective-permute-start.10) | collective-permute-done | bytes 102432 | tf_op jit(solution)/shard_map/ppermute | solution.py:249
  35.8 0.1 collective-permute-start.12
  35.9 1.4 %collective-permute-done.12.refs_3_ = bf16[24,3200]{1,0:T(8,128)(2,1)S(1)} collective-permute-done((bf16[24,3200]{1,0:T(8,128)(2,1)S(1)}, bf16[24,3200]{1,0:T(8,128)(2,1)S(1)}, u32[]{:S(2)}, u32[]{:S(2)}) %collective-permute-start.12) | collective-permute-done | bytes 153632 | tf_op jit(solution)/shard_map/ppermute | solution.py:245
  37.2 1.2 %combine.1 = bf16[128,3584]{1,0:T(8,128)(2,1)} custom-call(bf16[128,128]{1,0:T(8,128)(2,1)S(1)} %get-tuple-element.37.mix_ref, bf16[16,3200]{1,0:T(8,128)(2,1)S(1)} %collective-permute-done.7.refs_0_, bf16[16,3200]{1,0:T(8,128)(2,1)S(1)} %collective-permute-done.8.refs_1_, bf16[16,3200]{1,0:T(8,128)(2,1)S(1)} %collective-permute-done.10.refs_2_, ...), custom_call_target="tpu_custom_call" | custom-call | tf_op jit(solution)/shard_map/combine/pallas_call | solution.py:272
  (3 shorter events, 0.1 us)
Async XLA Ops:
  1.9 1.6 %collective-permute-start = (bf16[32,3200]{1,0:T(8,128)(2,1)S(1)}, bf16[32,3200]{1,0:T(8,128)(2,1)S(1)}, u32[]{:S(2)}, u32[]{:S(2)}) collective-permute-start(bf16[32,3200]{1,0:T(8,128)(2,1)S(1)} %get-tuple-element.39), channel_id=1, source_target_pairs={{0,1},{1,0},{2,3},{3,2},{4,5},{5,4},{6,7},{7,6},{8,9},{9,8},{10,11... | collective-permute-start | bytes 614408 | tf_op jit(solution)/shard_map/ppermute | solution.py:245
  3.5 12.7 %collective-permute-start.1 = (bf16[16,3200]{1,0:T(8,128)(2,1)S(1)}, bf16[16,3200]{1,0:T(8,128)(2,1)S(1)}, u32[]{:S(2)}, u32[]{:S(2)}) collective-permute-start(bf16[16,3200]{1,0:T(8,128)(2,1)S(1)} %get-tuple-element.40), channel_id=1, source_target_pairs={{0,8},{1,13},{2,10},{3,15},{4,12},{5,9},{6,14},{7,11},{8,0},{9,5},... | collective-permute-start | bytes 307208 | tf_op jit(solution)/shard_map/ppermute | solution.py:249
  7.6 8.7 %collective-permute-start.2 = (bf16[16,3200]{1,0:T(8,128)(2,1)S(1)}, bf16[16,3200]{1,0:T(8,128)(2,1)S(1)}, u32[]{:S(2)}, u32[]{:S(2)}) collective-permute-start(bf16[16,3200]{1,0:T(8,128)(2,1)S(1)} %get-tuple-element.41), channel_id=1, source_target_pairs={{0,2},{1,5},{2,0},{3,7},{4,6},{5,1},{6,4},{7,3},{8,10},{9,13},{10,... | collective-permute-start | bytes 307208 | tf_op jit(solution)/shard_map/ppermute | solution.py:249
  9.1 9.4 %collective-permute-start.3 = (bf16[16,3200]{1,0:T(8,128)(2,1)S(1)}, bf16[16,3200]{1,0:T(8,128)(2,1)S(1)}, u32[]{:S(2)}, u32[]{:S(2)}) collective-permute-start(bf16[16,3200]{1,0:T(8,128)(2,1)S(1)} %get-tuple-element.42), channel_id=1, source_target_pairs={{0,10},{1,15},{2,8},{3,13},{4,14},{5,11},{6,12},{7,9},{8,2},{9,7},... | collective-permute-start | bytes 307208 | tf_op jit(solution)/shard_map/ppermute | solution.py:249
  9.1 7.1 %collective-permute-start.4 = (bf16[8,3200]{1,0:T(8,128)(2,1)S(1)}, bf16[8,3200]{1,0:T(8,128)(2,1)S(1)}, u32[]{:S(2)}, u32[]{:S(2)}) collective-permute-start(bf16[8,3200]{1,0:T(8,128)(2,1)S(1)} %get-tuple-element.43), channel_id=1, source_target_pairs={{0,6},{1,7},{2,4},{3,5},{4,2},{5,3},{6,0},{7,1},{8,14},{9,15},{10,... | collective-permute-start | bytes 153608 | tf_op jit(solution)/shard_map/ppermute | solution.py:249
  18.5 1.7 %collective-permute-start.5 = (bf16[56,3200]{1,0:T(8,128)(2,1)S(1)}, bf16[56,3200]{1,0:T(8,128)(2,1)S(1)}, u32[]{:S(2)}, u32[]{:S(2)}) collective-permute-start(bf16[56,3200]{1,0:T(8,128)(2,1)S(1)} %gather.1.refs_0_), channel_id=1, source_target_pairs={{0,1},{1,0},{2,3},{3,2},{4,5},{5,4},{6,7},{7,6},{8,9},{9,8},{10,11... | collective-permute-start | bytes 1075208 | tf_op jit(solution)/shard_map/ppermute | solution.py:245
  22.0 1.6 %collective-permute-start.6 = (bf16[32,3584]{1,0:T(8,128)(2,1)S(1)}, bf16[32,3584]{1,0:T(8,128)(2,1)S(1)}, u32[]{:S(2)}, u32[]{:S(2)}) collective-permute-start(bf16[32,3584]{1,0:T(8,128)(2,1)S(1)} %get-tuple-element.57), channel_id=1, source_target_pairs={{0,1},{1,0},{2,3},{3,2},{4,5},{5,4},{6,7},{7,6},{8,9},{9,8},{10,11... | collective-permute-start | bytes 688136 | tf_op jit(solution)/shard_map/ppermute | solution.py:245
  22.2 2.6 %collective-permute-start.9 = (bf16[32,3584]{1,0:T(8,128)(2,1)S(1)}, bf16[32,3584]{1,0:T(8,128)(2,1)S(1)}, u32[]{:S(2)}, u32[]{:S(2)}) collective-permute-start(bf16[32,3584]{1,0:T(8,128)(2,1)S(1)} %get-tuple-element.61), channel_id=1, source_target_pairs={{0,1},{1,0},{2,3},{3,2},{4,5},{5,4},{6,7},{7,6},{8,9},{9,8},{10,11... | collective-permute-start | bytes 688136 | tf_op jit(solution)/shard_map/ppermute | solution.py:245
  23.7 11.0 %collective-permute-start.7 = (bf16[16,3200]{1,0:T(8,128)(2,1)S(1)}, bf16[16,3200]{1,0:T(8,128)(2,1)S(1)}, u32[]{:S(2)}, u32[]{:S(2)}) collective-permute-start(bf16[16,3200]{1,0:T(8,128)(2,1)S(1)} %get-tuple-element.58), channel_id=1, source_target_pairs={{0,8},{1,13},{2,10},{3,15},{4,12},{5,9},{6,14},{7,11},{8,0},{9,5},... | collective-permute-start | bytes 307208 | tf_op jit(solution)/shard_map/ppermute | solution.py:249
  24.3 10.4 %collective-permute-start.8 = (bf16[16,3200]{1,0:T(8,128)(2,1)S(1)}, bf16[16,3200]{1,0:T(8,128)(2,1)S(1)}, u32[]{:S(2)}, u32[]{:S(2)}) collective-permute-start(bf16[16,3200]{1,0:T(8,128)(2,1)S(1)} %get-tuple-element.59), channel_id=1, source_target_pairs={{0,2},{1,5},{2,0},{3,7},{4,6},{5,1},{6,4},{7,3},{8,10},{9,13},{10,... | collective-permute-start | bytes 307208 | tf_op jit(solution)/shard_map/ppermute | solution.py:249
  24.9 10.9 %collective-permute-start.10 = (bf16[16,3200]{1,0:T(8,128)(2,1)S(1)}, bf16[16,3200]{1,0:T(8,128)(2,1)S(1)}, u32[]{:S(2)}, u32[]{:S(2)}) collective-permute-start(bf16[16,3200]{1,0:T(8,128)(2,1)S(1)} %get-tuple-element.62), channel_id=1, source_target_pairs={{0,10},{1,15},{2,8},{3,13},{4,14},{5,11},{6,12},{7,9},{8,2},{9,7},... | collective-permute-start | bytes 307208 | tf_op jit(solution)/shard_map/ppermute | solution.py:249
  28.3 6.4 %collective-permute-start.11 = (bf16[8,3200]{1,0:T(8,128)(2,1)S(1)}, bf16[8,3200]{1,0:T(8,128)(2,1)S(1)}, u32[]{:S(2)}, u32[]{:S(2)}) collective-permute-start(bf16[8,3200]{1,0:T(8,128)(2,1)S(1)} %get-tuple-element.63), channel_id=1, source_target_pairs={{0,6},{1,7},{2,4},{3,5},{4,2},{5,3},{6,0},{7,1},{8,14},{9,15},{10,... | collective-permute-start | bytes 153608 | tf_op jit(solution)/shard_map/ppermute | solution.py:249
  35.8 1.4 %collective-permute-start.12 = (bf16[24,3200]{1,0:T(8,128)(2,1)S(1)}, bf16[24,3200]{1,0:T(8,128)(2,1)S(1)}, u32[]{:S(2)}, u32[]{:S(2)}) collective-permute-start(bf16[24,3200]{1,0:T(8,128)(2,1)S(1)} %sift.1), channel_id=1, source_target_pairs={{0,1},{1,0},{2,3},{3,2},{4,5},{5,4},{6,7},{7,6},{8,9},{9,8},{10,11... | collective-permute-start | bytes 460808 | tf_op jit(solution)/shard_map/ppermute | solution.py:245

commit v16 on v15

--- a/solution.py
+++ b/solution.py
@@ -26,7 +26,7 @@
     return flight == 8
 
 
-CARRIED = ((4, 1, 5), (6, 2, 7))
+CARRIED = ((4, 5, 1), (6, 7, 2))
 SHARED = 3
 
 
@@ -134,9 +134,9 @@
         store(outs, blocks)
     else:
         kept, given = 3 * SLOTS, 6 * SLOTS
-        store(outs[:1], blocks[:kept])
-        store(outs[1:2], jnp.concatenate([blocks[kept:given], blocks[given + SLOTS :]], axis=0))
-        store(outs[2:], blocks[given:])
+        store(outs[:2], blocks[:kept])
+        store(outs[2:3], jnp.concatenate([blocks[kept:given], blocks[given + SLOTS :]], axis=0))
+        store(outs[3:], blocks[given:])
 
 
 def stage_kernel(*refs):
@@ -160,13 +160,15 @@
     return jnp.concatenate([b[...].astype(jnp.float32) for b in refs], axis=0)
 
 
-def merge_kernel(kept_ref, got_ref, *outs):
+def merge_kernel(kept_ref, got_ref, first_out, *outs):
     *outs, own_out = outs
     kept, got = kept_ref[...].astype(jnp.float32), got_ref[...].astype(jnp.float32)
+    first_out[...] = got[:SLOTS].astype(jnp.bfloat16)
     for i, out in enumerate(outs):
-        here = slice(i * SLOTS, (i + 1) * SLOTS)
-        out[...] = jnp.concatenate([kept[here], got[here]], axis=0).astype(jnp.bfloat16)
-    own_out[...] = got[len(outs) * SLOTS :].astype(jnp.bfloat16)
+        one, two = i * SLOTS, (i + 1) * SLOTS
+        pair = [kept[one : one + SLOTS], got[two : two + SLOTS]]
+        out[...] = jnp.concatenate(pair, axis=0).astype(jnp.bfloat16)
+    own_out[...] = got[(len(outs) + 1) * SLOTS :].astype(jnp.bfloat16)
 
 
 def gather_kernel(*refs):
@@ -282,7 +284,7 @@
             name="combine",
         )(mix, *arrays)
 
-    first = packed(3, 4, 1, 1) if few else packed(flight)
+    first = packed(1, 2, 4, 1, 1) if few else packed(flight)
     mix, *outgoing = pl.pallas_call(
         functools.partial(dispatch_kernel, flight),
         out_shape=(jax.ShapeDtypeStruct((2 * flight * SLOTS, count), jnp.bfloat16),) + first,
@@ -318,10 +320,17 @@
 
     one, two, three = zip(*CARRIED)
     four = (SHARED, SHARED)
-    kept, given, shared, own = outgoing
-    *pairs, other_own = local(merge_kernel, packed(2, 2, 2, 1), "merge", kept, swap(given))
-    shared = travel(shared, four)
-    arrived = [travel(a, r) for a, r in zip(pairs, (one, two, three))] + [shared]
+    lead, kept, given, shared, own = outgoing
+    follow, second, third, other_own = local(
+        merge_kernel, packed(1, 2, 2, 1), "merge", kept, swap(given)
+    )
+    lead = travel(lead, one)
+    shared, lead = lax.optimization_barrier((shared, lead))
+    arrived = [
+        travel(a, r)
+        for a, r in zip((follow, second, third, shared), (one, two, three, four))
+    ]
+    arrived = [lead, *arrived]
     *arrived, gate, up, down = lax.optimization_barrier((*arrived, *stage()))
     (rows,) = local(gather_kernel, packed(7), "gather", *arrived)
     mine_one, mine_two, theirs_one, theirs_two = experts(

time: 38.6 us -> 40.9 us (1.060)
  starting transfers between devices: 14.9 us -> 20.1 us
  waiting for transfers between devices: 14.1 us -> 11.2 us
    ppermute x8 -> x9, starting transfers between devices: 13.6 us -> 18.7 us  [travel(): return lax.ppermute(rows, 'exp', pairs)]
    ppermute x8 -> x9, waiting for transfers between devices: 9.03 us -> 7.28 us  [travel(): return lax.ppermute(rows, 'exp', pairs)]
    ppermute x5, waiting for transfers between devices: 5.09 us -> 3.91 us  [swap(): return lax.ppermute(rows, 'exp', [(n, n ^ 1) for n in range(owners)])]
  transfers between devices with their start and end apart: 13 -> 14, of which waited for: 8 -> 5; matrix products, arithmetic and copies ran while one was open for 0% -> 0% of each run, Pallas kernels for 12% -> 11%
where the time goes in v16:
time: 40.9 us; the launch traced here: 40.7 us
  starting transfers between devices  20.1 us (49%)
  waiting for transfers between devices  11.2 us (27%)
  Pallas kernels  9.38 us (23%)
    ppermute x9, starting transfers between devices, travel(): return lax.ppermute(rows, 'exp', pairs)  18.7 us
    ppermute x9, waiting for transfers between devices, travel(): return lax.ppermute(rows, 'exp', pairs)  7.28 us
    pallas_call x1, Pallas kernels, stage(): pl.pallas_call(stage_kernel, out_shape=tuple((jax.ShapeDtypeStruct(w.shap...  4.24 us
    ppermute x5, waiting for transfers between devices, swap(): return lax.ppermute(rows, 'exp', [(n, n ^ 1) for n in range(owners)])  3.91 us
    pallas_call x6, Pallas kernels, local(): pl.pallas_call(kernel, out_shape=outs, in_specs=[VMEM] * len(args), out_s...  2 us
    pallas_call x1, Pallas kernels, per_device(): pl.pallas_call(functools.partial(dispatch_kernel, flight), out_shape=(jax...  1.91 us
    ppermute x5, starting transfers between devices, swap(): return lax.ppermute(rows, 'exp', [(n, n ^ 1) for n in range(owners)])  1.35 us
    pallas_call x1, Pallas kernels, combine(): pl.pallas_call(functools.partial(combine_kernel, paired), out_shape=jax.S...  1.22 us
  transfers between devices with their start and end apart: 14, of which 5 were waited for; matrix products, arithmetic and copies ran while one was open for 0% of the time, Pallas kernels for 11%

profile of v16, /device:TPU:0, one launch (start us, length us, event | category | flops | bytes accessed | tf_op | source)
XLA Modules:
  0.0 40.7 jit_solution(16712079827427777988)
XLA Ops:
  0.0 1.9 %dispatch.1 = (bf16[128,128]{1,0:T(8,128)(2,1)S(1)}, bf16[8,3200]{1,0:T(8,128)(2,1)S(1)}, bf16[16,3200]{1,0:T(8,128)(2,1)S(1)}, bf16[32,3200]{1,0:T(8,128)(2,1)S...) custom-call(bf16[128,3584]{1,0:T(8,128)(2,1)} %tok_hbm.1, f32[3584]{0:T(1024)} %gain_hbm.1, ...), custom_call_target="tpu_custom_call" | custom-call | tf_op jit(solution)/shard_map/dispatch/pallas_call | solution.py:288
  1.9 0.5 %collective-permute-start.1 = (bf16[32,3200]{1,0:T(8,128)(2,1)S(1)}, bf16[32,3200]{1,0:T(8,128)(2,1)S(1)}, u32[]{:S(2)}, u32[]{:S(2)}) collective-permute-start(bf16[32,3200]{1,0:T(8,128)(2,1)S(1)} %get-tuple-element.46), channel_id=1, source_target_pairs={{0,1},{1,0},{2,3},{3,2},{4,5},{5,4},{6,7},{7,6},{8,9},{9,8},{10,11... | collective-permute-start | bytes 614408 | tf_op jit(solution)/shard_map/ppermute | solution.py:247
  2.4 3.7 %collective-permute-start = (bf16[8,3200]{1,0:T(8,128)(2,1)S(1)}, bf16[8,3200]{1,0:T(8,128)(2,1)S(1)}, u32[]{:S(2)}, u32[]{:S(2)}) collective-permute-start(bf16[8,3200]{1,0:T(8,128)(2,1)S(1)} %get-tuple-element.43), channel_id=1, source_target_pairs={{0,8},{1,13},{2,10},{3,15},{4,12},{5,9},{6,14},{7,11},{8,0},{9,5},... | collective-permute-start | bytes 153608 | tf_op jit(solution)/shard_map/ppermute | solution.py:251
  6.1 0.0 collective-permute-done.1.got_ref
  6.1 2.4 %collective-permute-start.3 = (bf16[16,3200]{1,0:T(8,128)(2,1)S(1)}, bf16[16,3200]{1,0:T(8,128)(2,1)S(1)}, u32[]{:S(2)}, u32[]{:S(2)}) collective-permute-start(bf16[16,3200]{1,0:T(8,128)(2,1)S(1)} %get-tuple-element.48), channel_id=1, source_target_pairs={{0,10},{1,15},{2,8},{3,13},{4,14},{5,11},{6,12},{7,9},{8,2},{9,7},... | collective-permute-start | bytes 307208 | tf_op jit(solution)/shard_map/ppermute | solution.py:251
  8.5 0.5 %collective-permute-start.4 = (bf16[16,3200]{1,0:T(8,128)(2,1)S(1)}, bf16[16,3200]{1,0:T(8,128)(2,1)S(1)}, u32[]{:S(2)}, u32[]{:S(2)}) collective-permute-start(bf16[16,3200]{1,0:T(8,128)(2,1)S(1)} %get-tuple-element.49), channel_id=1, source_target_pairs={{0,2},{1,5},{2,0},{3,7},{4,6},{5,1},{6,4},{7,3},{8,10},{9,13},{10,... | collective-permute-start | bytes 307208 | tf_op jit(solution)/shard_map/ppermute | solution.py:251
  9.0 0.7 %collective-permute-done.refs_0_ = bf16[8,3200]{1,0:T(8,128)(2,1)S(1)} collective-permute-done((bf16[8,3200]{1,0:T(8,128)(2,1)S(1)}, bf16[8,3200]{1,0:T(8,128)(2,1)S(1)}, u32[]{:S(2)}, u32[]{:S(2)}) %collective-permute-start) | collective-permute-done | bytes 51232 | tf_op jit(solution)/shard_map/ppermute | solution.py:251
  9.7 4.3 %collective-permute-start.5 = (bf16[8,3200]{1,0:T(8,128)(2,1)S(1)}, bf16[8,3200]{1,0:T(8,128)(2,1)S(1)}, u32[]{:S(2)}, u32[]{:S(2)}) collective-permute-start(bf16[8,3200]{1,0:T(8,128)(2,1)S(1)} %get-tuple-element.50), channel_id=1, source_target_pairs={{0,6},{1,7},{2,4},{3,5},{4,2},{5,3},{6,0},{7,1},{8,14},{9,15},{10,... | collective-permute-start | bytes 153608 | tf_op jit(solution)/shard_map/ppermute | solution.py:251
  14.0 3.4 %collective-permute-start.2 = (bf16[8,3200]{1,0:T(8,128)(2,1)S(1)}, bf16[8,3200]{1,0:T(8,128)(2,1)S(1)}, u32[]{:S(2)}, u32[]{:S(2)}) collective-permute-start(bf16[8,3200]{1,0:T(8,128)(2,1)S(1)} %get-tuple-element.47), channel_id=1, source_target_pairs={{0,8},{1,13},{2,10},{3,15},{4,12},{5,9},{6,14},{7,11},{8,0},{9,5},... | collective-permute-start | bytes 153608 | tf_op jit(solution)/shard_map/ppermute | solution.py:251
  17.4 4.2 %stage.1 = (bf16[3584,512]{1,0:T(8,128)(2,1)S(1)}, bf16[3584,512]{1,0:T(8,128)(2,1)S(1)}, bf16[512,3584]{1,0:T(8,128)(2,1)S(1)}) custom-call(bf16[3584,512]{1,0:T(8,128)(2,1)} %bitcast.5, bf16[3584,512]{1,0:T(8,128)(2,1)} %bitcast.6, bf16[512,3584]{1,0:T(8,128)(2,1)} %bitcast.7), custom_call_target="tpu_custom_call" | custom-call | flops 1 | bytes 1 | tf_op jit(solution)/shard_map/stage/pallas_call | solution.py:255
  21.6 0.0 collective-permute-done.5.refs_4_
  21.6 0.0 collective-permute-done.2.refs_1_
  21.7 0.0 collective-permute-done.4.refs_3_
  21.7 0.1 collective-permute-start.6
  21.8 1.7 %collective-permute-done.6.refs_2_ = bf16[56,3200]{1,0:T(8,128)(2,1)S(1)} collective-permute-done((bf16[56,3200]{1,0:T(8,128)(2,1)S(1)}, bf16[56,3200]{1,0:T(8,128)(2,1)S(1)}, u32[]{:S(2)}, u32[]{:S(2)}) %collective-permute-start.6) | collective-permute-done | bytes 358432 | tf_op jit(solution)/shard_map/ppermute | solution.py:247
  23.4 1.7 %experts.1 = (bf16[32,3584]{1,0:T(8,128)(2,1)S(1)}, bf16[32,3584]{1,0:T(8,128)(2,1)S(1)}, bf16[32,3584]{1,0:T(8,128)(2,1)S(1)}, bf16[32,3584]{1,0:T(8,128)(2,1)S(1)}) custom-call(bf16[56,3200]{1,0:T(8,128)(2,1)S(1)} %gather.1.refs_0_, bf16[8,3200]{1,0:T(8,128)(2,1)S(1)} %get-tuple-element.59.refs_1_, bf16[56,3200]{1,0:T(8,128)(2,1)S(1)} %collective-permute-done.6.refs_2_, ...), custom_call_target="tpu_custom_call" | custom-call | flops 1 | bytes 1 | tf_op jit(solution)/shard_map/experts/pallas_call | solution.py:229
  25.2 0.2 collective-permute-start.7
  25.4 0.4 collective-permute-start.10
  25.8 1.0 %collective-permute-done.7.got_ref = bf16[32,3584]{1,0:T(8,128)(2,1)S(1)} collective-permute-done((bf16[32,3584]{1,0:T(8,128)(2,1)S(1)}, bf16[32,3584]{1,0:T(8,128)(2,1)S(1)}, u32[]{:S(2)}, u32[]{:S(2)}) %collective-permute-start.7) | collective-permute-done | bytes 229408 | tf_op jit(solution)/shard_map/ppermute | solution.py:247
  26.8 0.1 join.2
  26.9 0.8 %collective-permute-start.8 = (bf16[16,3200]{1,0:T(8,128)(2,1)S(1)}, bf16[16,3200]{1,0:T(8,128)(2,1)S(1)}, u32[]{:S(2)}, u32[]{:S(2)}) collective-permute-start(bf16[16,3200]{1,0:T(8,128)(2,1)S(1)} %get-tuple-element.66), channel_id=1, source_target_pairs={{0,8},{1,13},{2,10},{3,15},{4,12},{5,9},{6,14},{7,11},{8,0},{9,5},... | collective-permute-start | bytes 307208 | tf_op jit(solution)/shard_map/ppermute | solution.py:251
  27.6 0.0 collective-permute-start.9
  27.7 0.0 collective-permute-done.10.got_ref
  27.7 0.1 join.3
  27.8 3.7 %collective-permute-start.11 = (bf16[16,3200]{1,0:T(8,128)(2,1)S(1)}, bf16[16,3200]{1,0:T(8,128)(2,1)S(1)}, u32[]{:S(2)}, u32[]{:S(2)}) collective-permute-start(bf16[16,3200]{1,0:T(8,128)(2,1)S(1)} %get-tuple-element.70), channel_id=1, source_target_pairs={{0,2},{1,5},{2,0},{3,7},{4,6},{5,1},{6,4},{7,3},{8,10},{9,13},{10,... | collective-permute-start | bytes 307208 | tf_op jit(solution)/shard_map/ppermute | solution.py:251
  31.5 0.0 collective-permute-start.12
  31.5 6.5 %collective-permute-done.12.refs_4_ = bf16[8,3200]{1,0:T(8,128)(2,1)S(1)} collective-permute-done((bf16[8,3200]{1,0:T(8,128)(2,1)S(1)}, bf16[8,3200]{1,0:T(8,128)(2,1)S(1)}, u32[]{:S(2)}, u32[]{:S(2)}) %collective-permute-start.12) | collective-permute-done | bytes 51232 | tf_op jit(solution)/shard_map/ppermute | solution.py:251
  38.0 0.0 collective-permute-done.8.refs_0_
  38.0 0.0 collective-permute-done.9.refs_1_
  38.1 0.2 collective-permute-start.13
  38.3 1.3 %collective-permute-done.13.refs_3_ = bf16[24,3200]{1,0:T(8,128)(2,1)S(1)} collective-permute-done((bf16[24,3200]{1,0:T(8,128)(2,1)S(1)}, bf16[24,3200]{1,0:T(8,128)(2,1)S(1)}, u32[]{:S(2)}, u32[]{:S(2)}) %collective-permute-start.13) | collective-permute-done | bytes 153632 | tf_op jit(solution)/shard_map/ppermute | solution.py:247
  39.5 1.2 %combine.1 = bf16[128,3584]{1,0:T(8,128)(2,1)} custom-call(bf16[128,128]{1,0:T(8,128)(2,1)S(1)} %get-tuple-element.41.mix_ref, bf16[16,3200]{1,0:T(8,128)(2,1)S(1)} %collective-permute-done.8.refs_0_, bf16[16,3200]{1,0:T(8,128)(2,1)S(1)} %collective-permute-done.9.refs_1_, bf16[16,3200]{1,0:T(8,128)(2,1)S(1)} %collective-permute-done.11.refs_2_, ...), custom_call_target="tpu_custom_call" | custom-call | tf_op jit(solution)/shard_map/combine/pallas_call | solution.py:274
  (5 shorter events, 0.1 us)
Async XLA Ops:
  1.9 4.2 %collective-permute-start.1 = (bf16[32,3200]{1,0:T(8,128)(2,1)S(1)}, bf16[32,3200]{1,0:T(8,128)(2,1)S(1)}, u32[]{:S(2)}, u32[]{:S(2)}) collective-permute-start(bf16[32,3200]{1,0:T(8,128)(2,1)S(1)} %get-tuple-element.46), channel_id=1, source_target_pairs={{0,1},{1,0},{2,3},{3,2},{4,5},{5,4},{6,7},{7,6},{8,9},{9,8},{10,11... | collective-permute-start | bytes 614408 | tf_op jit(solution)/shard_map/ppermute | solution.py:247
  2.4 7.3 %collective-permute-start = (bf16[8,3200]{1,0:T(8,128)(2,1)S(1)}, bf16[8,3200]{1,0:T(8,128)(2,1)S(1)}, u32[]{:S(2)}, u32[]{:S(2)}) collective-permute-start(bf16[8,3200]{1,0:T(8,128)(2,1)S(1)} %get-tuple-element.43), channel_id=1, source_target_pairs={{0,8},{1,13},{2,10},{3,15},{4,12},{5,9},{6,14},{7,11},{8,0},{9,5},... | collective-permute-start | bytes 153608 | tf_op jit(solution)/shard_map/ppermute | solution.py:251
  6.1 15.5 %collective-permute-start.3 = (bf16[16,3200]{1,0:T(8,128)(2,1)S(1)}, bf16[16,3200]{1,0:T(8,128)(2,1)S(1)}, u32[]{:S(2)}, u32[]{:S(2)}) collective-permute-start(bf16[16,3200]{1,0:T(8,128)(2,1)S(1)} %get-tuple-element.48), channel_id=1, source_target_pairs={{0,10},{1,15},{2,8},{3,13},{4,14},{5,11},{6,12},{7,9},{8,2},{9,7},... | collective-permute-start | bytes 307208 | tf_op jit(solution)/shard_map/ppermute | solution.py:251
  8.5 13.1 %collective-permute-start.4 = (bf16[16,3200]{1,0:T(8,128)(2,1)S(1)}, bf16[16,3200]{1,0:T(8,128)(2,1)S(1)}, u32[]{:S(2)}, u32[]{:S(2)}) collective-permute-start(bf16[16,3200]{1,0:T(8,128)(2,1)S(1)} %get-tuple-element.49), channel_id=1, source_target_pairs={{0,2},{1,5},{2,0},{3,7},{4,6},{5,1},{6,4},{7,3},{8,10},{9,13},{10,... | collective-permute-start | bytes 307208 | tf_op jit(solution)/shard_map/ppermute | solution.py:251
  9.7 11.9 %collective-permute-start.5 = (bf16[8,3200]{1,0:T(8,128)(2,1)S(1)}, bf16[8,3200]{1,0:T(8,128)(2,1)S(1)}, u32[]{:S(2)}, u32[]{:S(2)}) collective-permute-start(bf16[8,3200]{1,0:T(8,128)(2,1)S(1)} %get-tuple-element.50), channel_id=1, source_target_pairs={{0,6},{1,7},{2,4},{3,5},{4,2},{5,3},{6,0},{7,1},{8,14},{9,15},{10,... | collective-permute-start | bytes 153608 | tf_op jit(solution)/shard_map/ppermute | solution.py:251
  14.0 7.6 %collective-permute-start.2 = (bf16[8,3200]{1,0:T(8,128)(2,1)S(1)}, bf16[8,3200]{1,0:T(8,128)(2,1)S(1)}, u32[]{:S(2)}, u32[]{:S(2)}) collective-permute-start(bf16[8,3200]{1,0:T(8,128)(2,1)S(1)} %get-tuple-element.47), channel_id=1, source_target_pairs={{0,8},{1,13},{2,10},{3,15},{4,12},{5,9},{6,14},{7,11},{8,0},{9,5},... | collective-permute-start | bytes 153608 | tf_op jit(solution)/shard_map/ppermute | solution.py:251
  21.7 1.7 %collective-permute-start.6 = (bf16[56,3200]{1,0:T(8,128)(2,1)S(1)}, bf16[56,3200]{1,0:T(8,128)(2,1)S(1)}, u32[]{:S(2)}, u32[]{:S(2)}) collective-permute-start(bf16[56,3200]{1,0:T(8,128)(2,1)S(1)} %gather.1.refs_0_), channel_id=1, source_target_pairs={{0,1},{1,0},{2,3},{3,2},{4,5},{5,4},{6,7},{7,6},{8,9},{9,8},{10,11... | collective-permute-start | bytes 1075208 | tf_op jit(solution)/shard_map/ppermute | solution.py:247
  25.2 1.6 %collective-permute-start.7 = (bf16[32,3584]{1,0:T(8,128)(2,1)S(1)}, bf16[32,3584]{1,0:T(8,128)(2,1)S(1)}, u32[]{:S(2)}, u32[]{:S(2)}) collective-permute-start(bf16[32,3584]{1,0:T(8,128)(2,1)S(1)} %get-tuple-element.65), channel_id=1, source_target_pairs={{0,1},{1,0},{2,3},{3,2},{4,5},{5,4},{6,7},{7,6},{8,9},{9,8},{10,11... | collective-permute-start | bytes 688136 | tf_op jit(solution)/shard_map/ppermute | solution.py:247
  25.4 2.2 %collective-permute-start.10 = (bf16[32,3584]{1,0:T(8,128)(2,1)S(1)}, bf16[32,3584]{1,0:T(8,128)(2,1)S(1)}, u32[]{:S(2)}, u32[]{:S(2)}) collective-permute-start(bf16[32,3584]{1,0:T(8,128)(2,1)S(1)} %get-tuple-element.69), channel_id=1, source_target_pairs={{0,1},{1,0},{2,3},{3,2},{4,5},{5,4},{6,7},{7,6},{8,9},{9,8},{10,11... | collective-permute-start | bytes 688136 | tf_op jit(solution)/shard_map/ppermute | solution.py:247
  26.9 11.2 %collective-permute-start.8 = (bf16[16,3200]{1,0:T(8,128)(2,1)S(1)}, bf16[16,3200]{1,0:T(8,128)(2,1)S(1)}, u32[]{:S(2)}, u32[]{:S(2)}) collective-permute-start(bf16[16,3200]{1,0:T(8,128)(2,1)S(1)} %get-tuple-element.66), channel_id=1, source_target_pairs={{0,8},{1,13},{2,10},{3,15},{4,12},{5,9},{6,14},{7,11},{8,0},{9,5},... | collective-permute-start | bytes 307208 | tf_op jit(solution)/shard_map/ppermute | solution.py:251
  27.6 10.4 %collective-permute-start.9 = (bf16[16,3200]{1,0:T(8,128)(2,1)S(1)}, bf16[16,3200]{1,0:T(8,128)(2,1)S(1)}, u32[]{:S(2)}, u32[]{:S(2)}) collective-permute-start(bf16[16,3200]{1,0:T(8,128)(2,1)S(1)} %get-tuple-element.67), channel_id=1, source_target_pairs={{0,10},{1,15},{2,8},{3,13},{4,14},{5,11},{6,12},{7,9},{8,2},{9,7},... | collective-permute-start | bytes 307208 | tf_op jit(solution)/shard_map/ppermute | solution.py:251
  27.8 10.3 %collective-permute-start.11 = (bf16[16,3200]{1,0:T(8,128)(2,1)S(1)}, bf16[16,3200]{1,0:T(8,128)(2,1)S(1)}, u32[]{:S(2)}, u32[]{:S(2)}) collective-permute-start(bf16[16,3200]{1,0:T(8,128)(2,1)S(1)} %get-tuple-element.70), channel_id=1, source_target_pairs={{0,2},{1,5},{2,0},{3,7},{4,6},{5,1},{6,4},{7,3},{8,10},{9,13},{10,... | collective-permute-start | bytes 307208 | tf_op jit(solution)/shard_map/ppermute | solution.py:251
  31.5 6.6 %collective-permute-start.12 = (bf16[8,3200]{1,0:T(8,128)(2,1)S(1)}, bf16[8,3200]{1,0:T(8,128)(2,1)S(1)}, u32[]{:S(2)}, u32[]{:S(2)}) collective-permute-start(bf16[8,3200]{1,0:T(8,128)(2,1)S(1)} %get-tuple-element.71), channel_id=1, source_target_pairs={{0,6},{1,7},{2,4},{3,5},{4,2},{5,3},{6,0},{7,1},{8,14},{9,15},{10,... | collective-permute-start | bytes 153608 | tf_op jit(solution)/shard_map/ppermute | solution.py:251
  38.1 1.4 %collective-permute-start.13 = (bf16[24,3200]{1,0:T(8,128)(2,1)S(1)}, bf16[24,3200]{1,0:T(8,128)(2,1)S(1)}, u32[]{:S(2)}, u32[]{:S(2)}) collective-permute-start(bf16[24,3200]{1,0:T(8,128)(2,1)S(1)} %sift.1), channel_id=1, source_target_pairs={{0,1},{1,0},{2,3},{3,2},{4,5},{5,4},{6,7},{7,6},{8,9},{9,8},{10,11... | collective-permute-start | bytes 460808 | tf_op jit(solution)/shard_map/ppermute | solution.py:247

commit v17 on v15

--- a/solution.py
+++ b/solution.py
@@ -217,8 +217,17 @@
         copy.wait()
 
 
-def per_device(tokens, norm_gain, expert_ids, gate_weights, w_gate, w_up, w_down):
+def per_device(*args):
+    groups = range(lax.axis_size("group"))
+    if not relative(lax.axis_size("exp") // 2):
+        return work(groups, *args)
+    branches = [functools.partial(work, [group]) for group in groups]
+    return lax.switch(lax.axis_index("group"), branches, *args)
+
+
+def work(groups, tokens, norm_gain, expert_ids, gate_weights, w_gate, w_up, w_down):
     owners = lax.axis_size("exp")
+    bases = [group * owners for group in groups]
     flight = owners // 2
     count, width = tokens.shape
     few = relative(flight)
@@ -242,11 +251,14 @@
         return tuple(jax.ShapeDtypeStruct(shape, jnp.bfloat16) for shape in shapes)
 
     def swap(rows):
-        return lax.ppermute(rows, "exp", [(n, n ^ 1) for n in range(owners)])
-
-    def travel(rows, distances, cross=0):
-        pairs = [(n, n ^ (2 * distances[n % 2]) ^ cross) for n in range(owners)]
-        return lax.ppermute(rows, "exp", pairs)
+        pairs = [(base + n, base + (n ^ 1)) for base in bases for n in range(owners)]
+        return lax.ppermute(rows, ("group", "exp"), pairs)
+
+    def travel(rows, distances):
+        pairs = [
+            (base + n, base + (n ^ (2 * distances[n % 2]))) for base in bases for n in range(owners)
+        ]
+        return lax.ppermute(rows, ("group", "exp"), pairs)
 
     def stage():
         weights = w_gate[0], w_up[0], w_down[0]
@@ -300,13 +312,13 @@
     )(*in_hbm(tokens, norm_gain, expert_ids.T, gate_weights.T))
     if not few:
         weights = stage()
-        groups = [list(range(core, owners, 2)) for core in range(2)]
+        cores = [list(range(core, owners, 2)) for core in range(2)]
         exchange = functools.partial(
             lax.all_to_all,
             axis_name="exp",
             split_axis=0,
             concat_axis=0,
-            axis_index_groups=groups,
+            axis_index_groups=cores,
             tiled=True,
         )
         own = exchange(outgoing[0])

time: 38.6 us -> 59.1 us (1.53)
  starting transfers between devices: 14.9 us -> 39.4 us
  waiting for transfers between devices: 14.1 us -> 8.76 us
  local copies, waits for them, and re-layouts: 0 us -> 0.92 us
    ppermute x13, starting transfers between devices: 14.9 us -> 39.4 us  [the longest x8 28.9 us: travel(): return lax.ppermute(rows, ('group', 'exp'), pairs)]
    ppermute x13, waiting for transfers between devices: 14.1 us -> 8.76 us  [the longest x8 4.71 us: travel(): return lax.ppermute(rows, ('group', 'exp'), pairs)]
    unnamed x0 -> x2, local copies, waits for them, and re-layouts: none -> 0.92 us
  transfers between devices with their start and end apart: 13 -> 13, of which waited for: 8 -> 4; matrix products, arithmetic and copies ran while one was open for 0% -> 0% of each run, Pallas kernels for 12% -> 8%
where the time goes in v17:
time: 59.1 us; the launch traced here: 58.6 us
  starting transfers between devices  39.4 us (67%)
  Pallas kernels  9.24 us (16%)
  waiting for transfers between devices  8.76 us (15%)
  local copies, waits for them, and re-layouts  0.92 us (2%)
    ppermute x8, starting transfers between devices, travel(): return lax.ppermute(rows, ('group', 'exp'), pairs)  28.9 us
    ppermute x5, starting transfers between devices, swap(): return lax.ppermute(rows, ('group', 'exp'), pairs)  10.5 us
    ppermute x8, waiting for transfers between devices, travel(): return lax.ppermute(rows, ('group', 'exp'), pairs)  4.71 us
    pallas_call x1, Pallas kernels, stage(): pl.pallas_call(stage_kernel, out_shape=tuple((jax.ShapeDtypeStruct(w.shap...  4.25 us
    ppermute x5, waiting for transfers between devices, swap(): return lax.ppermute(rows, ('group', 'exp'), pairs)  4.05 us
    pallas_call x6, Pallas kernels, local(): pl.pallas_call(kernel, out_shape=outs, in_specs=[VMEM] * len(args), out_s...  2.04 us
    pallas_call x1, Pallas kernels, work(): pl.pallas_call(functools.partial(dispatch_kernel, flight), out_shape=(jax...  1.91 us
  transfers between devices with their start and end apart: 13, of which 4 were waited for; matrix products, arithmetic and copies ran while one was open for 0% of the time, Pallas kernels for 8%

profile of v17, /device:TPU:0, one launch (start us, length us, event | category | flops | bytes accessed | tf_op | source)
XLA Modules:
  0.0 58.6 jit_solution(4778451474426772510)
XLA Ops:
  0.0 57.6 %conditional.1 = (bf16[128,3584]{1,0:T(8,128)(2,1)S(1)}) conditional(s32[]{:T(128)} %clamp.3, (s32[128,8]{0,1:T(8,128)}, f32[128,8]{0,1:T(8,128)}, bf16[128,3584]{1,0:T(8,128)(2,1)}, f32[3584]{0:T(1024)}, bf16[1,3584,512]{2,1,0:T(8,128)(2,1)}, /*index=5*/bf16[1,3584,512]{2,1,0:T(8,128)(2,1)}, bf16[1,512,3584]{2,1,0:T(8,128)(2,1)}) %tuple.15, ...), branch_computations={%region_0.0_spmd, %region_1.0_spmd} | conditional | flops 7 | bytes 7569943 | solution.py:225
  0.0 1.9 %dispatch.2 = (bf16[128,128]{1,0:T(8,128)(2,1)S(1)}, bf16[24,3200]{1,0:T(8,128)(2,1)S(1)}, bf16[32,3200]{1,0:T(8,128)(2,1)S(1)}, bf16[8,3200]{1,0:T(8,128)(2,1)S(1)}, bf16[8,3200]{1,0:T(8,128)(2,1)S(1)}) custom-call(bf16[128,3584]{1,0:T(8,128)(2,1)} %get-tuple-element.36.tok_hbm, f32[3584]{0:T(1024)} %get-tuple-element.37.gain_hbm, s32[8,128]{1,0:T(8,128)} %bitcast.16, ...), custom_call_target="tpu_custom_call" | custom-call | tf_op jit(solution)/shard_map/cond/branch_0_fun/dispatch/pallas_call | solution.py:298
  1.9 2.4 %collective-permute-start = (bf16[32,3200]{1,0:T(8,128)(2,1)S(1)}, bf16[32,3200]{1,0:T(8,128)(2,1)S(1)}, u32[]{:S(2)}, u32[]{:S(2)}) collective-permute-start(bf16[32,3200]{1,0:T(8,128)(2,1)S(1)} %get-tuple-element.42), channel_id=1, source_target_pairs={{0,1},{1,0},{2,3},{3,2},{4,5},{5,4},{6,7},{7,6},{8,9},{9,8},{10,11... | collective-permute-start | bytes 614408 | tf_op jit(solution)/shard_map/cond/branch_0_fun/ppermute | solution.py:255
  4.3 1.1 %collective-permute-done.got_ref = bf16[32,3200]{1,0:T(8,128)(2,1)S(1)} collective-permute-done((bf16[32,3200]{1,0:T(8,128)(2,1)S(1)}, bf16[32,3200]{1,0:T(8,128)(2,1)S(1)}, u32[]{:S(2)}, u32[]{:S(2)}) %collective-permute-start) | collective-permute-done | bytes 204832 | tf_op jit(solution)/shard_map/cond/branch_0_fun/ppermute | solution.py:255
  5.4 5.9 %collective-permute-start.1 = (bf16[16,3200]{1,0:T(8,128)(2,1)S(1)}, bf16[16,3200]{1,0:T(8,128)(2,1)S(1)}, u32[]{:S(2)}, u32[]{:S(2)}) collective-permute-start(bf16[16,3200]{1,0:T(8,128)(2,1)S(1)} %get-tuple-element.43), channel_id=1, source_target_pairs={{0,8},{1,13},{2,10},{3,15},{4,12},{5,9},{6,14},{7,11},{8,0},{9,5},... | collective-permute-start | bytes 307208 | tf_op jit(solution)/shard_map/cond/branch_0_fun/ppermute | solution.py:261
  11.2 3.4 %collective-permute-start.2 = (bf16[16,3200]{1,0:T(8,128)(2,1)S(1)}, bf16[16,3200]{1,0:T(8,128)(2,1)S(1)}, u32[]{:S(2)}, u32[]{:S(2)}) collective-permute-start(bf16[16,3200]{1,0:T(8,128)(2,1)S(1)} %get-tuple-element.44), channel_id=1, source_target_pairs={{0,2},{1,5},{2,0},{3,7},{4,6},{5,1},{6,4},{7,3},{8,10},{9,13},{10,... | collective-permute-start | bytes 307208 | tf_op jit(solution)/shard_map/cond/branch_0_fun/ppermute | solution.py:261
  14.7 1.9 %collective-permute-start.3 = (bf16[16,3200]{1,0:T(8,128)(2,1)S(1)}, bf16[16,3200]{1,0:T(8,128)(2,1)S(1)}, u32[]{:S(2)}, u32[]{:S(2)}) collective-permute-start(bf16[16,3200]{1,0:T(8,128)(2,1)S(1)} %get-tuple-element.45), channel_id=1, source_target_pairs={{0,10},{1,15},{2,8},{3,13},{4,14},{5,11},{6,12},{7,9},{8,2},{9,7},... | collective-permute-start | bytes 307208 | tf_op jit(solution)/shard_map/cond/branch_0_fun/ppermute | solution.py:261
  16.6 4.7 %collective-permute-start.4 = (bf16[8,3200]{1,0:T(8,128)(2,1)S(1)}, bf16[8,3200]{1,0:T(8,128)(2,1)S(1)}, u32[]{:S(2)}, u32[]{:S(2)}) collective-permute-start(bf16[8,3200]{1,0:T(8,128)(2,1)S(1)} %get-tuple-element.46), channel_id=1, source_target_pairs={{0,6},{1,7},{2,4},{3,5},{4,2},{5,3},{6,0},{7,1},{8,14},{9,15},{10,... | collective-permute-start | bytes 153608 | tf_op jit(solution)/shard_map/cond/branch_0_fun/ppermute | solution.py:261
  21.3 4.3 %stage.2 = (bf16[3584,512]{1,0:T(8,128)(2,1)S(1)}, bf16[3584,512]{1,0:T(8,128)(2,1)S(1)}, bf16[512,3584]{1,0:T(8,128)(2,1)S(1)}) custom-call(bf16[3584,512]{1,0:T(8,128)(2,1)} %bitcast.10, bf16[3584,512]{1,0:T(8,128)(2,1)} %bitcast.12, bf16[512,3584]{1,0:T(8,128)(2,1)} %bitcast.14), custom_call_target="tpu_custom_call" | custom-call | flops 1 | bytes 1 | tf_op jit(solution)/shard_map/cond/branch_0_fun/stage/pallas_call | solution.py:265
  25.6 0.0 collective-permute-done.1.refs_0_
  25.6 0.0 collective-permute-done.2.refs_1_
  25.7 1.9 %collective-permute-start.5 = (bf16[56,3200]{1,0:T(8,128)(2,1)S(1)}, bf16[56,3200]{1,0:T(8,128)(2,1)S(1)}, u32[]{:S(2)}, u32[]{:S(2)}) collective-permute-start(bf16[56,3200]{1,0:T(8,128)(2,1)S(1)} %gather.2.refs_0_), channel_id=1, source_target_pairs={{0,1},{1,0},{2,3},{3,2},{4,5},{5,4},{6,7},{7,6},{8,9},{9,8},{10,11... | collective-permute-start | bytes 1075208 | tf_op jit(solution)/shard_map/cond/branch_0_fun/ppermute | solution.py:255
  27.6 1.6 %collective-permute-done.5.refs_2_ = bf16[56,3200]{1,0:T(8,128)(2,1)S(1)} collective-permute-done((bf16[56,3200]{1,0:T(8,128)(2,1)S(1)}, bf16[56,3200]{1,0:T(8,128)(2,1)S(1)}, u32[]{:S(2)}, u32[]{:S(2)}) %collective-permute-start.5) | collective-permute-done | bytes 358432 | tf_op jit(solution)/shard_map/cond/branch_0_fun/ppermute | solution.py:255
  29.2 1.8 %experts.2 = (bf16[32,3584]{1,0:T(8,128)(2,1)S(1)}, bf16[32,3584]{1,0:T(8,128)(2,1)S(1)}, bf16[32,3584]{1,0:T(8,128)(2,1)S(1)}, bf16[32,3584]{1,0:T(8,128)(2,1)S(1)}) custom-call(bf16[56,3200]{1,0:T(8,128)(2,1)S(1)} %gather.2.refs_0_, bf16[8,3200]{1,0:T(8,128)(2,1)S(1)} %get-tuple-element.57.refs_1_, bf16[56,3200]{1,0:T(8,128)(2,1)S(1)} %collective-permute-done.5.refs_2_, ...), custom_call_target="tpu_custom_call" | custom-call | flops 1 | bytes 1 | tf_op jit(solution)/shard_map/cond/branch_0_fun/experts/pallas_call | solution.py:236
  31.0 2.0 %collective-permute-start.6 = (bf16[32,3584]{1,0:T(8,128)(2,1)S(1)}, bf16[32,3584]{1,0:T(8,128)(2,1)S(1)}, u32[]{:S(2)}, u32[]{:S(2)}) collective-permute-start(bf16[32,3584]{1,0:T(8,128)(2,1)S(1)} %get-tuple-element.63), channel_id=1, source_target_pairs={{0,1},{1,0},{2,3},{3,2},{4,5},{5,4},{6,7},{7,6},{8,9},{9,8},{10,11... | collective-permute-start | bytes 688136 | tf_op jit(solution)/shard_map/cond/branch_0_fun/ppermute | solution.py:255
  33.1 2.3 %collective-permute-start.9 = (bf16[32,3584]{1,0:T(8,128)(2,1)S(1)}, bf16[32,3584]{1,0:T(8,128)(2,1)S(1)}, u32[]{:S(2)}, u32[]{:S(2)}) collective-permute-start(bf16[32,3584]{1,0:T(8,128)(2,1)S(1)} %get-tuple-element.67), channel_id=1, source_target_pairs={{0,1},{1,0},{2,3},{3,2},{4,5},{5,4},{6,7},{7,6},{8,9},{9,8},{10,11... | collective-permute-start | bytes 688136 | tf_op jit(solution)/shard_map/cond/branch_0_fun/ppermute | solution.py:255
  35.4 0.0 collective-permute-done.6.got_ref
  35.4 0.1 join.4
  35.5 4.5 %collective-permute-start.7 = (bf16[16,3200]{1,0:T(8,128)(2,1)S(1)}, bf16[16,3200]{1,0:T(8,128)(2,1)S(1)}, u32[]{:S(2)}, u32[]{:S(2)}) collective-permute-start(bf16[16,3200]{1,0:T(8,128)(2,1)S(1)} %get-tuple-element.64), channel_id=1, source_target_pairs={{0,8},{1,13},{2,10},{3,15},{4,12},{5,9},{6,14},{7,11},{8,0},{9,5},... | collective-permute-start | bytes 307208 | tf_op jit(solution)/shard_map/cond/branch_0_fun/ppermute | solution.py:261
  40.0 2.4 %collective-permute-start.8 = (bf16[16,3200]{1,0:T(8,128)(2,1)S(1)}, bf16[16,3200]{1,0:T(8,128)(2,1)S(1)}, u32[]{:S(2)}, u32[]{:S(2)}) collective-permute-start(bf16[16,3200]{1,0:T(8,128)(2,1)S(1)} %get-tuple-element.65), channel_id=1, source_target_pairs={{0,2},{1,5},{2,0},{3,7},{4,6},{5,1},{6,4},{7,3},{8,10},{9,13},{10,... | collective-permute-start | bytes 307208 | tf_op jit(solution)/shard_map/cond/branch_0_fun/ppermute | solution.py:261
  42.4 0.0 collective-permute-done.9.got_ref
  42.4 0.1 join.5
  42.5 3.2 %collective-permute-start.10 = (bf16[16,3200]{1,0:T(8,128)(2,1)S(1)}, bf16[16,3200]{1,0:T(8,128)(2,1)S(1)}, u32[]{:S(2)}, u32[]{:S(2)}) collective-permute-start(bf16[16,3200]{1,0:T(8,128)(2,1)S(1)} %get-tuple-element.68), channel_id=1, source_target_pairs={{0,10},{1,15},{2,8},{3,13},{4,14},{5,11},{6,12},{7,9},{8,2},{9,7},... | collective-permute-start | bytes 307208 | tf_op jit(solution)/shard_map/cond/branch_0_fun/ppermute | solution.py:261
  45.7 2.8 %collective-permute-start.11 = (bf16[8,3200]{1,0:T(8,128)(2,1)S(1)}, bf16[8,3200]{1,0:T(8,128)(2,1)S(1)}, u32[]{:S(2)}, u32[]{:S(2)}) collective-permute-start(bf16[8,3200]{1,0:T(8,128)(2,1)S(1)} %get-tuple-element.69), channel_id=1, source_target_pairs={{0,6},{1,7},{2,4},{3,5},{4,2},{5,3},{6,0},{7,1},{8,14},{9,15},{10,... | collective-permute-start | bytes 153608 | tf_op jit(solution)/shard_map/cond/branch_0_fun/ppermute | solution.py:261
  48.6 4.7 %collective-permute-done.11.refs_4_ = bf16[8,3200]{1,0:T(8,128)(2,1)S(1)} collective-permute-done((bf16[8,3200]{1,0:T(8,128)(2,1)S(1)}, bf16[8,3200]{1,0:T(8,128)(2,1)S(1)}, u32[]{:S(2)}, u32[]{:S(2)}) %collective-permute-start.11) | collective-permute-done | bytes 51232 | tf_op jit(solution)/shard_map/cond/branch_0_fun/ppermute | solution.py:261
  53.3 0.0 collective-permute-done.7.refs_0_
  53.3 0.0 collective-permute-done.8.refs_1_
  53.3 1.9 %collective-permute-start.12 = (bf16[24,3200]{1,0:T(8,128)(2,1)S(1)}, bf16[24,3200]{1,0:T(8,128)(2,1)S(1)}, u32[]{:S(2)}, u32[]{:S(2)}) collective-permute-start(bf16[24,3200]{1,0:T(8,128)(2,1)S(1)} %sift.2), channel_id=1, source_target_pairs={{0,1},{1,0},{2,3},{3,2},{4,5},{5,4},{6,7},{7,6},{8,9},{9,8},{10,11... | collective-permute-start | bytes 460808 | tf_op jit(solution)/shard_map/cond/branch_0_fun/ppermute | solution.py:255
  55.2 1.3 %collective-permute-done.12.refs_3_ = bf16[24,3200]{1,0:T(8,128)(2,1)S(1)} collective-permute-done((bf16[24,3200]{1,0:T(8,128)(2,1)S(1)}, bf16[24,3200]{1,0:T(8,128)(2,1)S(1)}, u32[]{:S(2)}, u32[]{:S(2)}) %collective-permute-start.12) | collective-permute-done | bytes 153632 | tf_op jit(solution)/shard_map/cond/branch_0_fun/ppermute | solution.py:255
  56.6 1.0 %combine.2 = bf16[128,3584]{1,0:T(8,128)(2,1)S(1)} custom-call(bf16[128,128]{1,0:T(8,128)(2,1)S(1)} %get-tuple-element.40.mix_ref, bf16[16,3200]{1,0:T(8,128)(2,1)S(1)} %collective-permute-done.7.refs_0_, bf16[16,3200]{1,0:T(8,128)(2,1)S(1)} %collective-permute-done.8.refs_1_, bf16[16,3200]{1,0:T(8,128)(2,1)S(1)} %collective-permute-done.10.refs_2_, ...), custom_call_target="tpu_custom_call" | custom-call | tf_op jit(solution)/shard_map/cond/branch_0_fun/combine/pallas_call | solution.py:284
  57.6 0.0 copy-start
  57.6 0.9 %copy-done = bf16[128,3584]{1,0:T(8,128)(2,1)} copy-done((bf16[128,3584]{1,0:T(8,128)(2,1)}, bf16[128,3584]{1,0:T(8,128)(2,1)S(1)}, u32[]{:S(2)}) %copy-start) | copy-done | bytes 917528
  (6 shorter events, 0.1 us)
Async XLA Ops:
  1.9 3.4 %collective-permute-start = (bf16[32,3200]{1,0:T(8,128)(2,1)S(1)}, bf16[32,3200]{1,0:T(8,128)(2,1)S(1)}, u32[]{:S(2)}, u32[]{:S(2)}) collective-permute-start(bf16[32,3200]{1,0:T(8,128)(2,1)S(1)} %get-tuple-element.42), channel_id=1, source_target_pairs={{0,1},{1,0},{2,3},{3,2},{4,5},{5,4},{6,7},{7,6},{8,9},{9,8},{10,11... | collective-permute-start | bytes 614408 | tf_op jit(solution)/shard_map/cond/branch_0_fun/ppermute | solution.py:255
  5.4 20.2 %collective-permute-start.1 = (bf16[16,3200]{1,0:T(8,128)(2,1)S(1)}, bf16[16,3200]{1,0:T(8,128)(2,1)S(1)}, u32[]{:S(2)}, u32[]{:S(2)}) collective-permute-start(bf16[16,3200]{1,0:T(8,128)(2,1)S(1)} %get-tuple-element.43), channel_id=1, source_target_pairs={{0,8},{1,13},{2,10},{3,15},{4,12},{5,9},{6,14},{7,11},{8,0},{9,5},... | collective-permute-start | bytes 307208 | tf_op jit(solution)/shard_map/cond/branch_0_fun/ppermute | solution.py:261
  11.2 14.4 %collective-permute-start.2 = (bf16[16,3200]{1,0:T(8,128)(2,1)S(1)}, bf16[16,3200]{1,0:T(8,128)(2,1)S(1)}, u32[]{:S(2)}, u32[]{:S(2)}) collective-permute-start(bf16[16,3200]{1,0:T(8,128)(2,1)S(1)} %get-tuple-element.44), channel_id=1, source_target_pairs={{0,2},{1,5},{2,0},{3,7},{4,6},{5,1},{6,4},{7,3},{8,10},{9,13},{10,... | collective-permute-start | bytes 307208 | tf_op jit(solution)/shard_map/cond/branch_0_fun/ppermute | solution.py:261
  14.7 10.9 %collective-permute-start.3 = (bf16[16,3200]{1,0:T(8,128)(2,1)S(1)}, bf16[16,3200]{1,0:T(8,128)(2,1)S(1)}, u32[]{:S(2)}, u32[]{:S(2)}) collective-permute-start(bf16[16,3200]{1,0:T(8,128)(2,1)S(1)} %get-tuple-element.45), channel_id=1, source_target_pairs={{0,10},{1,15},{2,8},{3,13},{4,14},{5,11},{6,12},{7,9},{8,2},{9,7},... | collective-permute-start | bytes 307208 | tf_op jit(solution)/shard_map/cond/branch_0_fun/ppermute | solution.py:261
  16.6 9.0 %collective-permute-start.4 = (bf16[8,3200]{1,0:T(8,128)(2,1)S(1)}, bf16[8,3200]{1,0:T(8,128)(2,1)S(1)}, u32[]{:S(2)}, u32[]{:S(2)}) collective-permute-start(bf16[8,3200]{1,0:T(8,128)(2,1)S(1)} %get-tuple-element.46), channel_id=1, source_target_pairs={{0,6},{1,7},{2,4},{3,5},{4,2},{5,3},{6,0},{7,1},{8,14},{9,15},{10,... | collective-permute-start | bytes 153608 | tf_op jit(solution)/shard_map/cond/branch_0_fun/ppermute | solution.py:261
  25.7 3.6 %collective-permute-start.5 = (bf16[56,3200]{1,0:T(8,128)(2,1)S(1)}, bf16[56,3200]{1,0:T(8,128)(2,1)S(1)}, u32[]{:S(2)}, u32[]{:S(2)}) collective-permute-start(bf16[56,3200]{1,0:T(8,128)(2,1)S(1)} %gather.2.refs_0_), channel_id=1, source_target_pairs={{0,1},{1,0},{2,3},{3,2},{4,5},{5,4},{6,7},{7,6},{8,9},{9,8},{10,11... | collective-permute-start | bytes 1075208 | tf_op jit(solution)/shard_map/cond/branch_0_fun/ppermute | solution.py:255
  31.0 4.3 %collective-permute-start.6 = (bf16[32,3584]{1,0:T(8,128)(2,1)S(1)}, bf16[32,3584]{1,0:T(8,128)(2,1)S(1)}, u32[]{:S(2)}, u32[]{:S(2)}) collective-permute-start(bf16[32,3584]{1,0:T(8,128)(2,1)S(1)} %get-tuple-element.63), channel_id=1, source_target_pairs={{0,1},{1,0},{2,3},{3,2},{4,5},{5,4},{6,7},{7,6},{8,9},{9,8},{10,11... | collective-permute-start | bytes 688136 | tf_op jit(solution)/shard_map/cond/branch_0_fun/ppermute | solution.py:255
  33.1 9.3 %collective-permute-start.9 = (bf16[32,3584]{1,0:T(8,128)(2,1)S(1)}, bf16[32,3584]{1,0:T(8,128)(2,1)S(1)}, u32[]{:S(2)}, u32[]{:S(2)}) collective-permute-start(bf16[32,3584]{1,0:T(8,128)(2,1)S(1)} %get-tuple-element.67), channel_id=1, source_target_pairs={{0,1},{1,0},{2,3},{3,2},{4,5},{5,4},{6,7},{7,6},{8,9},{9,8},{10,11... | collective-permute-start | bytes 688136 | tf_op jit(solution)/shard_map/cond/branch_0_fun/ppermute | solution.py:255
  35.5 17.8 %collective-permute-start.7 = (bf16[16,3200]{1,0:T(8,128)(2,1)S(1)}, bf16[16,3200]{1,0:T(8,128)(2,1)S(1)}, u32[]{:S(2)}, u32[]{:S(2)}) collective-permute-start(bf16[16,3200]{1,0:T(8,128)(2,1)S(1)} %get-tuple-element.64), channel_id=1, source_target_pairs={{0,8},{1,13},{2,10},{3,15},{4,12},{5,9},{6,14},{7,11},{8,0},{9,5},... | collective-permute-start | bytes 307208 | tf_op jit(solution)/shard_map/cond/branch_0_fun/ppermute | solution.py:261
  40.0 13.3 %collective-permute-start.8 = (bf16[16,3200]{1,0:T(8,128)(2,1)S(1)}, bf16[16,3200]{1,0:T(8,128)(2,1)S(1)}, u32[]{:S(2)}, u32[]{:S(2)}) collective-permute-start(bf16[16,3200]{1,0:T(8,128)(2,1)S(1)} %get-tuple-element.65), channel_id=1, source_target_pairs={{0,2},{1,5},{2,0},{3,7},{4,6},{5,1},{6,4},{7,3},{8,10},{9,13},{10,... | collective-permute-start | bytes 307208 | tf_op jit(solution)/shard_map/cond/branch_0_fun/ppermute | solution.py:261
  42.5 10.8 %collective-permute-start.10 = (bf16[16,3200]{1,0:T(8,128)(2,1)S(1)}, bf16[16,3200]{1,0:T(8,128)(2,1)S(1)}, u32[]{:S(2)}, u32[]{:S(2)}) collective-permute-start(bf16[16,3200]{1,0:T(8,128)(2,1)S(1)} %get-tuple-element.68), channel_id=1, source_target_pairs={{0,10},{1,15},{2,8},{3,13},{4,14},{5,11},{6,12},{7,9},{8,2},{9,7},... | collective-permute-start | bytes 307208 | tf_op jit(solution)/shard_map/cond/branch_0_fun/ppermute | solution.py:261
  45.7 7.5 %collective-permute-start.11 = (bf16[8,3200]{1,0:T(8,128)(2,1)S(1)}, bf16[8,3200]{1,0:T(8,128)(2,1)S(1)}, u32[]{:S(2)}, u32[]{:S(2)}) collective-permute-start(bf16[8,3200]{1,0:T(8,128)(2,1)S(1)} %get-tuple-element.69), channel_id=1, source_target_pairs={{0,6},{1,7},{2,4},{3,5},{4,2},{5,3},{6,0},{7,1},{8,14},{9,15},{10,... | collective-permute-start | bytes 153608 | tf_op jit(solution)/shard_map/cond/branch_0_fun/ppermute | solution.py:261
  53.3 3.3 %collective-permute-start.12 = (bf16[24,3200]{1,0:T(8,128)(2,1)S(1)}, bf16[24,3200]{1,0:T(8,128)(2,1)S(1)}, u32[]{:S(2)}, u32[]{:S(2)}) collective-permute-start(bf16[24,3200]{1,0:T(8,128)(2,1)S(1)} %sift.2), channel_id=1, source_target_pairs={{0,1},{1,0},{2,3},{3,2},{4,5},{5,4},{6,7},{7,6},{8,9},{9,8},{10,11... | collective-permute-start | bytes 460808 | tf_op jit(solution)/shard_map/cond/branch_0_fun/ppermute | solution.py:255
  57.6 0.9 %copy-start = (bf16[128,3584]{1,0:T(8,128)(2,1)}, bf16[128,3584]{1,0:T(8,128)(2,1)S(1)}, u32[]{:S(2)}) copy-start(bf16[128,3584]{1,0:T(8,128)(2,1)S(1)} %get-tuple-element.169) | copy-start | bytes 2752516

commit v18 on v15

--- a/solution.py
+++ b/solution.py
@@ -10,7 +10,6 @@
 SLOTS = 8
 CHUNKS = 4
 PIECES = 4
-OUT_PIECES = 4
 LANES = 128
 
 VMEM = pl.BlockSpec(memory_space=pltpu.VMEM)
@@ -55,10 +54,9 @@
     return jnp.concatenate([main, extra], axis=2).reshape(rows.shape[0], -1)
 
 
-def unpack(packed):
+def unpack_tail(packed):
     blocks = packed.reshape(-1, SLOTS, packed.shape[1])
     tail = (packed.shape[1] - LANES) // 6
-    main = blocks[:, :, : 6 * tail]
     last = jnp.concatenate(
         [blocks[:, k : k + 1, 6 * tail :] for k in range(tail // LANES)], axis=2
     )
@@ -66,7 +64,11 @@
     end = jnp.where(row == 6, last, 0.0)
     for j in range(6):
         end = jnp.where(row == j, blocks[:, 7:8, j * tail : (j + 1) * tail], end)
-    return jnp.concatenate([main, end], axis=2).reshape(packed.shape[0], -1)
+    return end.reshape(packed.shape[0], -1)
+
+
+def unpack(packed):
+    return jnp.concatenate([packed[:, : packed.shape[1] - LANES], unpack_tail(packed)], axis=1)
 
 
 def store(refs, rows):
@@ -139,8 +141,8 @@
         store(outs[2:], blocks[given:])
 
 
-def stage_kernel(*refs):
-    *refs, sems = refs
+def stage_kernel(mix_ref, *refs):
+    *refs, turned_ref, sems = refs
     sources, targets = refs[:3], refs[3:]
     copies = []
     for at, (source, target) in enumerate(zip(sources, targets)):
@@ -152,6 +154,7 @@
             )
     for copy in copies:
         copy.start()
+    turned_ref[...] = mix_ref[...].T
     for copy in copies:
         copy.wait()
 
@@ -169,8 +172,8 @@
     own_out[...] = got[len(outs) * SLOTS :].astype(jnp.bfloat16)
 
 
-def gather_kernel(*refs):
-    refs[-1][...] = together(refs[:-1]).astype(jnp.bfloat16)
+def gather_kernel(count, *refs):
+    store(refs[-count:], together(refs[:-count]))
 
 
 def sift_kernel(*refs):
@@ -196,21 +199,16 @@
 def combine_kernel(paired, mix_ref, *refs):
     *refs, out_hbm, out, sems = refs
     blocks = [r[...].astype(jnp.float32) for r in refs]
-    if paired:
-        blocks[:3] = [b[:SLOTS] for b in blocks[:3]]
-    rows = unpack(jnp.concatenate(blocks, axis=0)).astype(jnp.bfloat16)
-    both = jnp.concatenate([rows, rows], axis=0)
+    rows = jnp.concatenate([b[:SLOTS] for b in blocks[:paired]] + blocks[paired:], axis=0)
     mix = mix_ref[...]
-    part = out.shape[1] // OUT_PIECES
+    tail = out.shape[1] // 7
     copies = []
-    for i in range(OUT_PIECES):
-        here = pl.ds(i * part, part)
-        out[:, here] = lax.dot_general(
-            mix,
-            both[:, i * part : (i + 1) * part],
-            (((0,), (0,)), ((), ())),
-            preferred_element_type=jnp.float32,
-        ).astype(jnp.bfloat16)
+    for i in range(7):
+        here = pl.ds(i * tail, tail)
+        piece = rows[:, i * tail : (i + 1) * tail] if i < 6 else unpack_tail(rows)
+        piece = piece.astype(jnp.bfloat16)
+        both = jnp.concatenate([piece, piece], axis=0)
+        out[:, here] = jnp.dot(mix, both, preferred_element_type=jnp.float32).astype(jnp.bfloat16)
         copies.append(pltpu.make_async_copy(out.at[:, here], out_hbm.at[:, here], sems.at[i]))
         copies[-1].start()
     for copy in copies:
@@ -248,18 +246,19 @@
         pairs = [(n, n ^ (2 * distances[n % 2]) ^ cross) for n in range(owners)]
         return lax.ppermute(rows, "exp", pairs)
 
-    def stage():
+    def stage(mix):
         weights = w_gate[0], w_up[0], w_down[0]
+        outs = [jax.ShapeDtypeStruct(w.shape, w.dtype) for w in weights]
         return pl.pallas_call(
             stage_kernel,
-            out_shape=tuple(jax.ShapeDtypeStruct(w.shape, w.dtype) for w in weights),
-            in_specs=[HBM] * 3,
-            out_specs=(VMEM,) * 3,
+            out_shape=(*outs, jax.ShapeDtypeStruct(mix.shape[::-1], mix.dtype)),
+            in_specs=[VMEM] + [HBM] * 3,
+            out_specs=(VMEM,) * 4,
             scratch_shapes=[pltpu.SemaphoreType.DMA((3 * PIECES,))],
             compiler_params=pltpu.CompilerParams(vmem_limit_bytes=16 * 2**20),
             cost_estimate=SMALL,
             name="stage",
-        )(*in_hbm(*weights))
+        )(mix, *in_hbm(*weights))
 
     def experts(rows, weights):
         outs = full(*[flight // 2] * 4)
@@ -276,7 +275,7 @@
             out_specs=HBM,
             scratch_shapes=[
                 pltpu.VMEM((count, width), jnp.bfloat16),
-                pltpu.SemaphoreType.DMA((OUT_PIECES,)),
+                pltpu.SemaphoreType.DMA((7,)),
             ],
             compiler_params=pltpu.CompilerParams(vmem_limit_bytes=24 * 2**20),
             name="combine",
@@ -299,7 +298,7 @@
         name="dispatch",
     )(*in_hbm(tokens, norm_gain, expert_ids.T, gate_weights.T))
     if not few:
-        weights = stage()
+        *weights, mix = stage(mix)
         groups = [list(range(core, owners, 2)) for core in range(2)]
         exchange = functools.partial(
             lax.all_to_all,
@@ -314,7 +313,7 @@
         half = flight // 2
         (joined_one,) = join([half], mine_one, theirs_one)
         (joined_two,) = join([half], mine_two, theirs_two)
-        return combine(mix, [exchange(jnp.concatenate([joined_one, joined_two]))], False)
+        return combine(mix, [exchange(jnp.concatenate([joined_one, joined_two]))], 0)
 
     one, two, three = zip(*CARRIED)
     four = (SHARED, SHARED)
@@ -322,10 +321,11 @@
     *pairs, other_own = local(merge_kernel, packed(2, 2, 2, 1), "merge", kept, swap(given))
     shared = travel(shared, four)
     arrived = [travel(a, r) for a, r in zip(pairs, (one, two, three))] + [shared]
-    *arrived, gate, up, down = lax.optimization_barrier((*arrived, *stage()))
-    (rows,) = local(gather_kernel, packed(7), "gather", *arrived)
+    *arrived, gate, up, down, mix = lax.optimization_barrier((*arrived, *stage(mix)))
+    kernel = functools.partial(gather_kernel, 2)
+    rows = local(kernel, packed(4, 3), "gather", *arrived)
     mine_one, mine_two, theirs_one, theirs_two = experts(
-        (rows, own, swap(rows), other_own), (gate, up, down)
+        (*rows, own, *[swap(a) for a in rows], other_own), (gate, up, down)
     )
 
     first, second = join((2, 2), mine_one, theirs_one)
@@ -335,7 +335,7 @@
     ]
     *pairs, shared = lax.optimization_barrier(tuple(arrived))
     (others,) = local(sift_kernel, packed(3), "sift", *pairs)
-    return combine(mix, [*pairs, swap(others), shared, own], True)
+    return combine(mix, [*pairs, swap(others), shared, own], 3)
 
 
 def solution(mesh):

time: 38.6 us -> 38.5 us (level)
  waiting for transfers between devices: 14.1 us -> 13.5 us
  starting transfers between devices: 14.9 us -> 15.4 us
    ppermute x5 -> x6, starting transfers between devices: 1.24 us -> 1.73 us  [swap(): return lax.ppermute(rows, 'exp', [(n, n ^ 1) for n in range(owners)])]
    ppermute x5 -> x6, waiting for transfers between devices: 5.09 us -> 4.59 us  [swap(): return lax.ppermute(rows, 'exp', [(n, n ^ 1) for n in range(owners)])]
  transfers between devices with their start and end apart: 13 -> 14, of which waited for: 8 -> 8; matrix products, arithmetic and copies ran while one was open for 0% -> 0% of each run, Pallas kernels for 12% -> 12%
where the time goes in v18:
time: 38.5 us; the launch traced here: 38.4 us
  starting transfers between devices  15.4 us (40%)
  waiting for transfers between devices  13.5 us (35%)
  Pallas kernels  9.35 us (24%)
    ppermute x8, starting transfers between devices, travel(): return lax.ppermute(rows, 'exp', pairs)  13.7 us
    ppermute x8, waiting for transfers between devices, travel(): return lax.ppermute(rows, 'exp', pairs)  8.95 us
    ppermute x6, waiting for transfers between devices, swap(): return lax.ppermute(rows, 'exp', [(n, n ^ 1) for n in range(owners)])  4.59 us
    pallas_call x1, Pallas kernels, stage(): pl.pallas_call(stage_kernel, out_shape=(*outs, jax.ShapeDtypeStruct(mix.s...  4.25 us
    pallas_call x6, Pallas kernels, local(): pl.pallas_call(kernel, out_shape=outs, in_specs=[VMEM] * len(args), out_s...  2.03 us
    pallas_call x1, Pallas kernels, per_device(): pl.pallas_call(functools.partial(dispatch_kernel, flight), out_shape=(jax...  1.91 us
    ppermute x6, starting transfers between devices, swap(): return lax.ppermute(rows, 'exp', [(n, n ^ 1) for n in range(owners)])  1.73 us
    pallas_call x1, Pallas kernels, combine(): pl.pallas_call(functools.partial(combine_kernel, paired), out_shape=jax.S...  1.16 us
  transfers between devices with their start and end apart: 14, of which 8 were waited for; matrix products, arithmetic and copies ran while one was open for 0% of the time, Pallas kernels for 12%

profile of v18, /device:TPU:0, one launch (start us, length us, event | category | flops | bytes accessed | tf_op | source)
XLA Modules:
  0.0 38.4 jit_solution(1253471951563703390)
XLA Ops:
  0.0 1.9 %dispatch.1 = (bf16[128,128]{1,0:T(8,128)(2,1)S(1)}, bf16[24,3200]{1,0:T(8,128)(2,1)S(1)}, bf16[32,3200]{1,0:T(8,128)(2,1)S(1)}, bf16[8,3200]{1,0:T(8,128)(2,1)S(1)}, bf16[8,3200]{1,0:T(8,128)(2,1)S(1)}) custom-call(bf16[128,3584]{1,0:T(8,128)(2,1)} %tok_hbm.1, f32[3584]{0:T(1024)} %gain_hbm.1, s32[8,128]{1,0:T(8,128)} %bitcast.8, f32[8,128]{1,0:T(8,128)} %bitcast.9), custom_call_target="tpu_custom_call" | custom-call | tf_op jit(solution)/shard_map/dispatch/pallas_call | solution.py:285
  1.9 0.5 %collective-permute-start = (bf16[32,3200]{1,0:T(8,128)(2,1)S(1)}, bf16[32,3200]{1,0:T(8,128)(2,1)S(1)}, u32[]{:S(2)}, u32[]{:S(2)}) collective-permute-start(bf16[32,3200]{1,0:T(8,128)(2,1)S(1)} %get-tuple-element.42), channel_id=1, source_target_pairs={{0,1},{1,0},{2,3},{3,2},{4,5},{5,4},{6,7},{7,6},{8,9},{9,8},{10,11... | collective-permute-start | bytes 614408 | tf_op jit(solution)/shard_map/ppermute | solution.py:243
  2.4 1.1 %collective-permute-done.got_ref = bf16[32,3200]{1,0:T(8,128)(2,1)S(1)} collective-permute-done((bf16[32,3200]{1,0:T(8,128)(2,1)S(1)}, bf16[32,3200]{1,0:T(8,128)(2,1)S(1)}, u32[]{:S(2)}, u32[]{:S(2)}) %collective-permute-start) | collective-permute-done | bytes 204832 | tf_op jit(solution)/shard_map/ppermute | solution.py:243
  3.5 4.0 %collective-permute-start.1 = (bf16[16,3200]{1,0:T(8,128)(2,1)S(1)}, bf16[16,3200]{1,0:T(8,128)(2,1)S(1)}, u32[]{:S(2)}, u32[]{:S(2)}) collective-permute-start(bf16[16,3200]{1,0:T(8,128)(2,1)S(1)} %get-tuple-element.43), channel_id=1, source_target_pairs={{0,8},{1,13},{2,10},{3,15},{4,12},{5,9},{6,14},{7,11},{8,0},{9,5},... | collective-permute-start | bytes 307208 | tf_op jit(solution)/shard_map/ppermute | solution.py:247
  7.6 1.5 %collective-permute-start.2 = (bf16[16,3200]{1,0:T(8,128)(2,1)S(1)}, bf16[16,3200]{1,0:T(8,128)(2,1)S(1)}, u32[]{:S(2)}, u32[]{:S(2)}) collective-permute-start(bf16[16,3200]{1,0:T(8,128)(2,1)S(1)} %get-tuple-element.44), channel_id=1, source_target_pairs={{0,2},{1,5},{2,0},{3,7},{4,6},{5,1},{6,4},{7,3},{8,10},{9,13},{10,... | collective-permute-start | bytes 307208 | tf_op jit(solution)/shard_map/ppermute | solution.py:247
  9.1 0.0 collective-permute-start.3
  9.1 2.8 %collective-permute-start.4 = (bf16[8,3200]{1,0:T(8,128)(2,1)S(1)}, bf16[8,3200]{1,0:T(8,128)(2,1)S(1)}, u32[]{:S(2)}, u32[]{:S(2)}) collective-permute-start(bf16[8,3200]{1,0:T(8,128)(2,1)S(1)} %get-tuple-element.46), channel_id=1, source_target_pairs={{0,6},{1,7},{2,4},{3,5},{4,2},{5,3},{6,0},{7,1},{8,14},{9,15},{10,... | collective-permute-start | bytes 153608 | tf_op jit(solution)/shard_map/ppermute | solution.py:247
  11.9 4.2 %stage.1 = (bf16[3584,512]{1,0:T(8,128)(2,1)S(1)}, bf16[3584,512]{1,0:T(8,128)(2,1)S(1)}, bf16[512,3584]{1,0:T(8,128)(2,1)S(1)}, bf16[128,128]{1,0:T(8,128)(2,1)S(1)}) custom-call(bf16[128,128]{1,0:T(8,128)(2,1)S(1)} %get-tuple-element.47.mix_ref, bf16[3584,512]{1,0:T(8,128)(2,1)} %bitcast.5, bf16[3584,512]{1,0:T(8,128)(2,1)} %bitcast.6, ...), custom_call_target="tpu_custom_call" | custom-call | flops 1 | bytes 1 | tf_op jit(solution)/shard_map/stage/pallas_call | solution.py:252
  16.2 0.1 collective-permute-done.4.refs_3_
  16.2 0.0 collective-permute-done.1.refs_0_
  16.2 0.0 collective-permute-done.2.refs_1_
  16.2 2.3 %collective-permute-done.3.refs_2_ = bf16[16,3200]{1,0:T(8,128)(2,1)S(1)} collective-permute-done((bf16[16,3200]{1,0:T(8,128)(2,1)S(1)}, bf16[16,3200]{1,0:T(8,128)(2,1)S(1)}, u32[]{:S(2)}, u32[]{:S(2)}) %collective-permute-start.3) | collective-permute-done | bytes 102432 | tf_op jit(solution)/shard_map/ppermute | solution.py:247
  18.5 0.1 collective-permute-start.5
  18.6 0.5 %collective-permute-start.6 = (bf16[24,3200]{1,0:T(8,128)(2,1)S(1)}, bf16[24,3200]{1,0:T(8,128)(2,1)S(1)}, u32[]{:S(2)}, u32[]{:S(2)}) collective-permute-start(bf16[24,3200]{1,0:T(8,128)(2,1)S(1)} %get-tuple-element.58.refs_1_), channel_id=1, source_target_pairs={{0,1},{1,0},{2,3},{3,2},{4,5},{5,4},{6,7},{7,6},{8,9},{9,8},{10,11... | collective-permute-start | bytes 460808 | tf_op jit(solution)/shard_map/ppermute | solution.py:243
  19.1 1.2 %collective-permute-done.6.refs_4_ = bf16[24,3200]{1,0:T(8,128)(2,1)S(1)} collective-permute-done((bf16[24,3200]{1,0:T(8,128)(2,1)S(1)}, bf16[24,3200]{1,0:T(8,128)(2,1)S(1)}, u32[]{:S(2)}, u32[]{:S(2)}) %collective-permute-start.6) | collective-permute-done | bytes 153632 | tf_op jit(solution)/shard_map/ppermute | solution.py:243
  20.3 0.0 collective-permute-done.5.refs_3_
  20.3 1.8 %experts.1 = (bf16[32,3584]{1,0:T(8,128)(2,1)S(1)}, bf16[32,3584]{1,0:T(8,128)(2,1)S(1)}, bf16[32,3584]{1,0:T(8,128)(2,1)S(1)}, bf16[32,3584]{1,0:T(8,128)(2,1)S(1)}) custom-call(bf16[32,3200]{1,0:T(8,128)(2,1)S(1)} %get-tuple-element.57.refs_0_, bf16[24,3200]{1,0:T(8,128)(2,1)S(1)} %get-tuple-element.58.refs_1_, ...), custom_call_target="tpu_custom_call" | custom-call | flops 1 | bytes 1 | tf_op jit(solution)/shard_map/experts/pallas_call | solution.py:225
  22.1 0.3 collective-permute-start.7
  22.3 0.3 collective-permute-start.10
  22.6 1.0 %collective-permute-done.7.got_ref = bf16[32,3584]{1,0:T(8,128)(2,1)S(1)} collective-permute-done((bf16[32,3584]{1,0:T(8,128)(2,1)S(1)}, bf16[32,3584]{1,0:T(8,128)(2,1)S(1)}, u32[]{:S(2)}, u32[]{:S(2)}) %collective-permute-start.7) | collective-permute-done | bytes 229408 | tf_op jit(solution)/shard_map/ppermute | solution.py:243
  23.6 0.1 join.2
  23.7 0.7 %collective-permute-start.8 = (bf16[16,3200]{1,0:T(8,128)(2,1)S(1)}, bf16[16,3200]{1,0:T(8,128)(2,1)S(1)}, u32[]{:S(2)}, u32[]{:S(2)}) collective-permute-start(bf16[16,3200]{1,0:T(8,128)(2,1)S(1)} %get-tuple-element.66), channel_id=1, source_target_pairs={{0,8},{1,13},{2,10},{3,15},{4,12},{5,9},{6,14},{7,11},{8,0},{9,5},... | collective-permute-start | bytes 307208 | tf_op jit(solution)/shard_map/ppermute | solution.py:247
  24.4 0.5 %collective-permute-start.9 = (bf16[16,3200]{1,0:T(8,128)(2,1)S(1)}, bf16[16,3200]{1,0:T(8,128)(2,1)S(1)}, u32[]{:S(2)}, u32[]{:S(2)}) collective-permute-start(bf16[16,3200]{1,0:T(8,128)(2,1)S(1)} %get-tuple-element.67), channel_id=1, source_target_pairs={{0,2},{1,5},{2,0},{3,7},{4,6},{5,1},{6,4},{7,3},{8,10},{9,13},{10,... | collective-permute-start | bytes 307208 | tf_op jit(solution)/shard_map/ppermute | solution.py:247
  24.9 0.1 join.3
  25.0 3.3 %collective-permute-start.11 = (bf16[16,3200]{1,0:T(8,128)(2,1)S(1)}, bf16[16,3200]{1,0:T(8,128)(2,1)S(1)}, u32[]{:S(2)}, u32[]{:S(2)}) collective-permute-start(bf16[16,3200]{1,0:T(8,128)(2,1)S(1)} %get-tuple-element.70), channel_id=1, source_target_pairs={{0,10},{1,15},{2,8},{3,13},{4,14},{5,11},{6,12},{7,9},{8,2},{9,7},... | collective-permute-start | bytes 307208 | tf_op jit(solution)/shard_map/ppermute | solution.py:247
  28.3 0.8 %collective-permute-start.12 = (bf16[8,3200]{1,0:T(8,128)(2,1)S(1)}, bf16[8,3200]{1,0:T(8,128)(2,1)S(1)}, u32[]{:S(2)}, u32[]{:S(2)}) collective-permute-start(bf16[8,3200]{1,0:T(8,128)(2,1)S(1)} %get-tuple-element.71), channel_id=1, source_target_pairs={{0,6},{1,7},{2,4},{3,5},{4,2},{5,3},{6,0},{7,1},{8,14},{9,15},{10,... | collective-permute-start | bytes 153608 | tf_op jit(solution)/shard_map/ppermute | solution.py:247
  29.1 5.7 %collective-permute-done.12.refs_4_ = bf16[8,3200]{1,0:T(8,128)(2,1)S(1)} collective-permute-done((bf16[8,3200]{1,0:T(8,128)(2,1)S(1)}, bf16[8,3200]{1,0:T(8,128)(2,1)S(1)}, u32[]{:S(2)}, u32[]{:S(2)}) %collective-permute-start.12) | collective-permute-done | bytes 51232 | tf_op jit(solution)/shard_map/ppermute | solution.py:247
  34.8 0.0 collective-permute-done.8.refs_0_
  34.9 0.9 %collective-permute-done.11.refs_2_ = bf16[16,3200]{1,0:T(8,128)(2,1)S(1)} collective-permute-done((bf16[16,3200]{1,0:T(8,128)(2,1)S(1)}, bf16[16,3200]{1,0:T(8,128)(2,1)S(1)}, u32[]{:S(2)}, u32[]{:S(2)}) %collective-permute-start.11) | collective-permute-done | bytes 102432 | tf_op jit(solution)/shard_map/ppermute | solution.py:247
  35.7 0.1 collective-permute-start.13
  35.8 1.4 %collective-permute-done.13.refs_3_ = bf16[24,3200]{1,0:T(8,128)(2,1)S(1)} collective-permute-done((bf16[24,3200]{1,0:T(8,128)(2,1)S(1)}, bf16[24,3200]{1,0:T(8,128)(2,1)S(1)}, u32[]{:S(2)}, u32[]{:S(2)}) %collective-permute-start.13) | collective-permute-done | bytes 153632 | tf_op jit(solution)/shard_map/ppermute | solution.py:243
  37.2 1.2 %combine.1 = bf16[128,3584]{1,0:T(8,128)(2,1)} custom-call(bf16[128,128]{1,0:T(8,128)(2,1)S(1)} %get-tuple-element.52.mix_ref, bf16[16,3200]{1,0:T(8,128)(2,1)S(1)} %collective-permute-done.8.refs_0_, bf16[16,3200]{1,0:T(8,128)(2,1)S(1)} %collective-permute-done.9.refs_1_, bf16[16,3200]{1,0:T(8,128)(2,1)S(1)} %collective-permute-done.11.refs_2_, ...), custom_call_target="tpu_custom_call" | custom-call | tf_op jit(solution)/shard_map/combine/pallas_call | solution.py:271
  (5 shorter events, 0.1 us)
Async XLA Ops:
  1.9 1.6 %collective-permute-start = (bf16[32,3200]{1,0:T(8,128)(2,1)S(1)}, bf16[32,3200]{1,0:T(8,128)(2,1)S(1)}, u32[]{:S(2)}, u32[]{:S(2)}) collective-permute-start(bf16[32,3200]{1,0:T(8,128)(2,1)S(1)} %get-tuple-element.42), channel_id=1, source_target_pairs={{0,1},{1,0},{2,3},{3,2},{4,5},{5,4},{6,7},{7,6},{8,9},{9,8},{10,11... | collective-permute-start | bytes 614408 | tf_op jit(solution)/shard_map/ppermute | solution.py:243
  3.5 12.7 %collective-permute-start.1 = (bf16[16,3200]{1,0:T(8,128)(2,1)S(1)}, bf16[16,3200]{1,0:T(8,128)(2,1)S(1)}, u32[]{:S(2)}, u32[]{:S(2)}) collective-permute-start(bf16[16,3200]{1,0:T(8,128)(2,1)S(1)} %get-tuple-element.43), channel_id=1, source_target_pairs={{0,8},{1,13},{2,10},{3,15},{4,12},{5,9},{6,14},{7,11},{8,0},{9,5},... | collective-permute-start | bytes 307208 | tf_op jit(solution)/shard_map/ppermute | solution.py:247
  7.6 8.7 %collective-permute-start.2 = (bf16[16,3200]{1,0:T(8,128)(2,1)S(1)}, bf16[16,3200]{1,0:T(8,128)(2,1)S(1)}, u32[]{:S(2)}, u32[]{:S(2)}) collective-permute-start(bf16[16,3200]{1,0:T(8,128)(2,1)S(1)} %get-tuple-element.44), channel_id=1, source_target_pairs={{0,2},{1,5},{2,0},{3,7},{4,6},{5,1},{6,4},{7,3},{8,10},{9,13},{10,... | collective-permute-start | bytes 307208 | tf_op jit(solution)/shard_map/ppermute | solution.py:247
  9.1 9.4 %collective-permute-start.3 = (bf16[16,3200]{1,0:T(8,128)(2,1)S(1)}, bf16[16,3200]{1,0:T(8,128)(2,1)S(1)}, u32[]{:S(2)}, u32[]{:S(2)}) collective-permute-start(bf16[16,3200]{1,0:T(8,128)(2,1)S(1)} %get-tuple-element.45), channel_id=1, source_target_pairs={{0,10},{1,15},{2,8},{3,13},{4,14},{5,11},{6,12},{7,9},{8,2},{9,7},... | collective-permute-start | bytes 307208 | tf_op jit(solution)/shard_map/ppermute | solution.py:247
  9.1 7.1 %collective-permute-start.4 = (bf16[8,3200]{1,0:T(8,128)(2,1)S(1)}, bf16[8,3200]{1,0:T(8,128)(2,1)S(1)}, u32[]{:S(2)}, u32[]{:S(2)}) collective-permute-start(bf16[8,3200]{1,0:T(8,128)(2,1)S(1)} %get-tuple-element.46), channel_id=1, source_target_pairs={{0,6},{1,7},{2,4},{3,5},{4,2},{5,3},{6,0},{7,1},{8,14},{9,15},{10,... | collective-permute-start | bytes 153608 | tf_op jit(solution)/shard_map/ppermute | solution.py:247
  18.5 1.7 %collective-permute-start.5 = (bf16[32,3200]{1,0:T(8,128)(2,1)S(1)}, bf16[32,3200]{1,0:T(8,128)(2,1)S(1)}, u32[]{:S(2)}, u32[]{:S(2)}) collective-permute-start(bf16[32,3200]{1,0:T(8,128)(2,1)S(1)} %get-tuple-element.57.refs_0_), channel_id=1, source_target_pairs={{0,1},{1,0},{2,3},{3,2},{4,5},{5,4},{6,7},{7,6},{8,9},{9,8},{10,11... | collective-permute-start | bytes 614408 | tf_op jit(solution)/shard_map/ppermute | solution.py:243
  18.6 1.7 %collective-permute-start.6 = (bf16[24,3200]{1,0:T(8,128)(2,1)S(1)}, bf16[24,3200]{1,0:T(8,128)(2,1)S(1)}, u32[]{:S(2)}, u32[]{:S(2)}) collective-permute-start(bf16[24,3200]{1,0:T(8,128)(2,1)S(1)} %get-tuple-element.58.refs_1_), channel_id=1, source_target_pairs={{0,1},{1,0},{2,3},{3,2},{4,5},{5,4},{6,7},{7,6},{8,9},{9,8},{10,11... | collective-permute-start | bytes 460808 | tf_op jit(solution)/shard_map/ppermute | solution.py:243
  22.1 1.6 %collective-permute-start.7 = (bf16[32,3584]{1,0:T(8,128)(2,1)S(1)}, bf16[32,3584]{1,0:T(8,128)(2,1)S(1)}, u32[]{:S(2)}, u32[]{:S(2)}) collective-permute-start(bf16[32,3584]{1,0:T(8,128)(2,1)S(1)} %get-tuple-element.65), channel_id=1, source_target_pairs={{0,1},{1,0},{2,3},{3,2},{4,5},{5,4},{6,7},{7,6},{8,9},{9,8},{10,11... | collective-permute-start | bytes 688136 | tf_op jit(solution)/shard_map/ppermute | solution.py:243
  22.3 2.6 %collective-permute-start.10 = (bf16[32,3584]{1,0:T(8,128)(2,1)S(1)}, bf16[32,3584]{1,0:T(8,128)(2,1)S(1)}, u32[]{:S(2)}, u32[]{:S(2)}) collective-permute-start(bf16[32,3584]{1,0:T(8,128)(2,1)S(1)} %get-tuple-element.69), channel_id=1, source_target_pairs={{0,1},{1,0},{2,3},{3,2},{4,5},{5,4},{6,7},{7,6},{8,9},{9,8},{10,11... | collective-permute-start | bytes 688136 | tf_op jit(solution)/shard_map/ppermute | solution.py:243
  23.7 11.1 %collective-permute-start.8 = (bf16[16,3200]{1,0:T(8,128)(2,1)S(1)}, bf16[16,3200]{1,0:T(8,128)(2,1)S(1)}, u32[]{:S(2)}, u32[]{:S(2)}) collective-permute-start(bf16[16,3200]{1,0:T(8,128)(2,1)S(1)} %get-tuple-element.66), channel_id=1, source_target_pairs={{0,8},{1,13},{2,10},{3,15},{4,12},{5,9},{6,14},{7,11},{8,0},{9,5},... | collective-permute-start | bytes 307208 | tf_op jit(solution)/shard_map/ppermute | solution.py:247
  24.4 10.5 %collective-permute-start.9 = (bf16[16,3200]{1,0:T(8,128)(2,1)S(1)}, bf16[16,3200]{1,0:T(8,128)(2,1)S(1)}, u32[]{:S(2)}, u32[]{:S(2)}) collective-permute-start(bf16[16,3200]{1,0:T(8,128)(2,1)S(1)} %get-tuple-element.67), channel_id=1, source_target_pairs={{0,2},{1,5},{2,0},{3,7},{4,6},{5,1},{6,4},{7,3},{8,10},{9,13},{10,... | collective-permute-start | bytes 307208 | tf_op jit(solution)/shard_map/ppermute | solution.py:247
  25.0 10.7 %collective-permute-start.11 = (bf16[16,3200]{1,0:T(8,128)(2,1)S(1)}, bf16[16,3200]{1,0:T(8,128)(2,1)S(1)}, u32[]{:S(2)}, u32[]{:S(2)}) collective-permute-start(bf16[16,3200]{1,0:T(8,128)(2,1)S(1)} %get-tuple-element.70), channel_id=1, source_target_pairs={{0,10},{1,15},{2,8},{3,13},{4,14},{5,11},{6,12},{7,9},{8,2},{9,7},... | collective-permute-start | bytes 307208 | tf_op jit(solution)/shard_map/ppermute | solution.py:247
  28.3 6.5 %collective-permute-start.12 = (bf16[8,3200]{1,0:T(8,128)(2,1)S(1)}, bf16[8,3200]{1,0:T(8,128)(2,1)S(1)}, u32[]{:S(2)}, u32[]{:S(2)}) collective-permute-start(bf16[8,3200]{1,0:T(8,128)(2,1)S(1)} %get-tuple-element.71), channel_id=1, source_target_pairs={{0,6},{1,7},{2,4},{3,5},{4,2},{5,3},{6,0},{7,1},{8,14},{9,15},{10,... | collective-permute-start | bytes 153608 | tf_op jit(solution)/shard_map/ppermute | solution.py:247
  35.7 1.4 %collective-permute-start.13 = (bf16[24,3200]{1,0:T(8,128)(2,1)S(1)}, bf16[24,3200]{1,0:T(8,128)(2,1)S(1)}, u32[]{:S(2)}, u32[]{:S(2)}) collective-permute-start(bf16[24,3200]{1,0:T(8,128)(2,1)S(1)} %sift.1), channel_id=1, source_target_pairs={{0,1},{1,0},{2,3},{3,2},{4,5},{5,4},{6,7},{7,6},{8,9},{9,8},{10,11... | collective-permute-start | bytes 460808 | tf_op jit(solution)/shard_map/ppermute | solution.py:243

commit v19 on v18

--- a/solution.py
+++ b/solution.py
@@ -177,9 +177,9 @@
 
 
 def sift_kernel(*refs):
-    *refs, out_ref = refs
-    blocks = [r[...].astype(jnp.float32)[SLOTS:] for r in refs]
-    out_ref[...] = jnp.concatenate(blocks, axis=0).astype(jnp.bfloat16)
+    count = len(refs) // 2
+    for ref, out in zip(refs[:count], refs[count:]):
+        out[...] = ref[...].astype(jnp.float32)[SLOTS:].astype(jnp.bfloat16)
 
 
 def expert_kernel(*refs):
@@ -242,8 +242,8 @@
     def swap(rows):
         return lax.ppermute(rows, "exp", [(n, n ^ 1) for n in range(owners)])
 
-    def travel(rows, distances, cross=0):
-        pairs = [(n, n ^ (2 * distances[n % 2]) ^ cross) for n in range(owners)]
+    def travel(rows, distances, across=0):
+        pairs = [(n, n ^ (2 * distances[n % 2]) ^ across) for n in range(owners)]
         return lax.ppermute(rows, "exp", pairs)
 
     def stage(mix):
@@ -329,13 +329,12 @@
     )
 
     first, second = join((2, 2), mine_one, theirs_one)
-    third, shared, own = join((2, 1, 1), mine_two, theirs_two)
-    arrived = [
-        travel(a, r) for a, r in zip((first, second, third, shared), (one, two, three, four))
-    ]
-    *pairs, shared = lax.optimization_barrier(tuple(arrived))
-    (others,) = local(sift_kernel, packed(3), "sift", *pairs)
-    return combine(mix, [*pairs, swap(others), shared, own], 3)
+    third, third_across, shared, own = join((1, 1, 1, 1), mine_two, theirs_two)
+    first, second, shared = travel(first, one), travel(second, two), travel(shared, four)
+    third, third_across = travel(third, three), travel(third_across, three, 1)
+    others = local(sift_kernel, packed(1, 1), "sift", first, second)
+    others = [swap(a) for a in others]
+    return combine(mix, [first, second, third, *others, third_across, shared, own], 2)
 
 
 def solution(mesh):

time: 38.5 us -> 37.6 us (0.977)
  waiting for transfers between devices: 13.5 us -> 9.71 us
  starting transfers between devices: 15.4 us -> 18.3 us
    ppermute x8 -> x9, waiting for transfers between devices: 8.95 us -> 6.48 us  [travel(): return lax.ppermute(rows, 'exp', pairs)]
    ppermute x8 -> x9, starting transfers between devices: 13.7 us -> 16.1 us  [travel(): return lax.ppermute(rows, 'exp', pairs)]
    ppermute x6 -> x7, waiting for transfers between devices: 4.59 us -> 3.23 us  [swap(): return lax.ppermute(rows, 'exp', [(n, n ^ 1) for n in range(owners)])]
    ppermute x6 -> x7, starting transfers between devices: 1.73 us -> 2.23 us  [swap(): return lax.ppermute(rows, 'exp', [(n, n ^ 1) for n in range(owners)])]
  transfers between devices with their start and end apart: 14 -> 16, of which waited for: 8 -> 8; matrix products, arithmetic and copies ran while one was open for 0% -> 0% of each run, Pallas kernels for 12% -> 12%
where the time goes in v19:
time: 37.6 us; the launch traced here: 37.5 us
  starting transfers between devices  18.3 us (49%)
  waiting for transfers between devices  9.71 us (26%)
  Pallas kernels  9.36 us (25%)
    ppermute x9, starting transfers between devices, travel(): return lax.ppermute(rows, 'exp', pairs)  16.1 us
    ppermute x9, waiting for transfers between devices, travel(): return lax.ppermute(rows, 'exp', pairs)  6.48 us
    pallas_call x1, Pallas kernels, stage(): pl.pallas_call(stage_kernel, out_shape=(*outs, jax.ShapeDtypeStruct(mix.s...  4.25 us
    ppermute x7, waiting for transfers between devices, swap(): return lax.ppermute(rows, 'exp', [(n, n ^ 1) for n in range(owners)])  3.23 us
    ppermute x7, starting transfers between devices, swap(): return lax.ppermute(rows, 'exp', [(n, n ^ 1) for n in range(owners)])  2.23 us
    pallas_call x6, Pallas kernels, local(): pl.pallas_call(kernel, out_shape=outs, in_specs=[VMEM] * len(args), out_s...  2.03 us
    pallas_call x1, Pallas kernels, per_device(): pl.pallas_call(functools.partial(dispatch_kernel, flight), out_shape=(jax...  1.91 us
    pallas_call x1, Pallas kernels, combine(): pl.pallas_call(functools.partial(combine_kernel, paired), out_shape=jax.S...  1.17 us
  transfers between devices with their start and end apart: 16, of which 8 were waited for; matrix products, arithmetic and copies ran while one was open for 0% of the time, Pallas kernels for 12%

profile of v19, /device:TPU:0, one launch (start us, length us, event | category | flops | bytes accessed | tf_op | source)
XLA Modules:
  0.0 37.5 jit_solution(7285524175687713938)
XLA Ops:
  0.0 1.9 %dispatch.1 = (bf16[128,128]{1,0:T(8,128)(2,1)S(1)}, bf16[24,3200]{1,0:T(8,128)(2,1)S(1)}, bf16[32,3200]{1,0:T(8,128)(2,1)S(1)}, bf16[8,3200]{1,0:T(8,128)(2,1)S(1)}, bf16[8,3200]{1,0:T(8,128)(2,1)S(1)}) custom-call(bf16[128,3584]{1,0:T(8,128)(2,1)} %tok_hbm.1, f32[3584]{0:T(1024)} %gain_hbm.1, s32[8,128]{1,0:T(8,128)} %bitcast.8, f32[8,128]{1,0:T(8,128)} %bitcast.9), custom_call_target="tpu_custom_call" | custom-call | tf_op jit(solution)/shard_map/dispatch/pallas_call | solution.py:285
  1.9 0.5 %collective-permute-start = (bf16[32,3200]{1,0:T(8,128)(2,1)S(1)}, bf16[32,3200]{1,0:T(8,128)(2,1)S(1)}, u32[]{:S(2)}, u32[]{:S(2)}) collective-permute-start(bf16[32,3200]{1,0:T(8,128)(2,1)S(1)} %get-tuple-element.41), channel_id=1, source_target_pairs={{0,1},{1,0},{2,3},{3,2},{4,5},{5,4},{6,7},{7,6},{8,9},{9,8},{10,11... | collective-permute-start | bytes 614408 | tf_op jit(solution)/shard_map/ppermute | solution.py:243
  2.4 1.1 %collective-permute-done.got_ref = bf16[32,3200]{1,0:T(8,128)(2,1)S(1)} collective-permute-done((bf16[32,3200]{1,0:T(8,128)(2,1)S(1)}, bf16[32,3200]{1,0:T(8,128)(2,1)S(1)}, u32[]{:S(2)}, u32[]{:S(2)}) %collective-permute-start) | collective-permute-done | bytes 204832 | tf_op jit(solution)/shard_map/ppermute | solution.py:243
  3.5 4.0 %collective-permute-start.1 = (bf16[16,3200]{1,0:T(8,128)(2,1)S(1)}, bf16[16,3200]{1,0:T(8,128)(2,1)S(1)}, u32[]{:S(2)}, u32[]{:S(2)}) collective-permute-start(bf16[16,3200]{1,0:T(8,128)(2,1)S(1)} %get-tuple-element.42), channel_id=1, source_target_pairs={{0,8},{1,13},{2,10},{3,15},{4,12},{5,9},{6,14},{7,11},{8,0},{9,5},... | collective-permute-start | bytes 307208 | tf_op jit(solution)/shard_map/ppermute | solution.py:247
  7.6 1.5 %collective-permute-start.2 = (bf16[16,3200]{1,0:T(8,128)(2,1)S(1)}, bf16[16,3200]{1,0:T(8,128)(2,1)S(1)}, u32[]{:S(2)}, u32[]{:S(2)}) collective-permute-start(bf16[16,3200]{1,0:T(8,128)(2,1)S(1)} %get-tuple-element.43), channel_id=1, source_target_pairs={{0,2},{1,5},{2,0},{3,7},{4,6},{5,1},{6,4},{7,3},{8,10},{9,13},{10,... | collective-permute-start | bytes 307208 | tf_op jit(solution)/shard_map/ppermute | solution.py:247
  9.1 0.0 collective-permute-start.3
  9.1 2.8 %collective-permute-start.4 = (bf16[8,3200]{1,0:T(8,128)(2,1)S(1)}, bf16[8,3200]{1,0:T(8,128)(2,1)S(1)}, u32[]{:S(2)}, u32[]{:S(2)}) collective-permute-start(bf16[8,3200]{1,0:T(8,128)(2,1)S(1)} %get-tuple-element.45), channel_id=1, source_target_pairs={{0,6},{1,7},{2,4},{3,5},{4,2},{5,3},{6,0},{7,1},{8,14},{9,15},{10,... | collective-permute-start | bytes 153608 | tf_op jit(solution)/shard_map/ppermute | solution.py:247
  11.9 4.2 %stage.1 = (bf16[3584,512]{1,0:T(8,128)(2,1)S(1)}, bf16[3584,512]{1,0:T(8,128)(2,1)S(1)}, bf16[512,3584]{1,0:T(8,128)(2,1)S(1)}, bf16[128,128]{1,0:T(8,128)(2,1)S(1)}) custom-call(bf16[128,128]{1,0:T(8,128)(2,1)S(1)} %get-tuple-element.46.mix_ref, bf16[3584,512]{1,0:T(8,128)(2,1)} %bitcast.5, bf16[3584,512]{1,0:T(8,128)(2,1)} %bitcast.6, ...), custom_call_target="tpu_custom_call" | custom-call | flops 1 | bytes 1 | tf_op jit(solution)/shard_map/stage/pallas_call | solution.py:252
  16.2 0.1 collective-permute-done.4.refs_3_
  16.2 2.3 %collective-permute-done.3.refs_2_ = bf16[16,3200]{1,0:T(8,128)(2,1)S(1)} collective-permute-done((bf16[16,3200]{1,0:T(8,128)(2,1)S(1)}, bf16[16,3200]{1,0:T(8,128)(2,1)S(1)}, u32[]{:S(2)}, u32[]{:S(2)}) %collective-permute-start.3) | collective-permute-done | bytes 102432 | tf_op jit(solution)/shard_map/ppermute | solution.py:247
  18.5 0.1 collective-permute-start.5
  18.6 0.5 %collective-permute-start.6 = (bf16[24,3200]{1,0:T(8,128)(2,1)S(1)}, bf16[24,3200]{1,0:T(8,128)(2,1)S(1)}, u32[]{:S(2)}, u32[]{:S(2)}) collective-permute-start(bf16[24,3200]{1,0:T(8,128)(2,1)S(1)} %get-tuple-element.57.refs_1_), channel_id=1, source_target_pairs={{0,1},{1,0},{2,3},{3,2},{4,5},{5,4},{6,7},{7,6},{8,9},{9,8},{10,11... | collective-permute-start | bytes 460808 | tf_op jit(solution)/shard_map/ppermute | solution.py:243
  19.1 1.2 %collective-permute-done.6.refs_4_ = bf16[24,3200]{1,0:T(8,128)(2,1)S(1)} collective-permute-done((bf16[24,3200]{1,0:T(8,128)(2,1)S(1)}, bf16[24,3200]{1,0:T(8,128)(2,1)S(1)}, u32[]{:S(2)}, u32[]{:S(2)}) %collective-permute-start.6) | collective-permute-done | bytes 153632 | tf_op jit(solution)/shard_map/ppermute | solution.py:243
  20.3 0.0 collective-permute-done.5.refs_3_
  20.3 1.8 %experts.1 = (bf16[32,3584]{1,0:T(8,128)(2,1)S(1)}, bf16[32,3584]{1,0:T(8,128)(2,1)S(1)}, bf16[32,3584]{1,0:T(8,128)(2,1)S(1)}, bf16[32,3584]{1,0:T(8,128)(2,1)S(1)}) custom-call(bf16[32,3200]{1,0:T(8,128)(2,1)S(1)} %get-tuple-element.56.refs_0_, bf16[24,3200]{1,0:T(8,128)(2,1)S(1)} %get-tuple-element.57.refs_1_, ...), custom_call_target="tpu_custom_call" | custom-call | flops 1 | bytes 1 | tf_op jit(solution)/shard_map/experts/pallas_call | solution.py:225
  22.1 0.3 collective-permute-start.7
  22.3 0.3 collective-permute-start.10
  22.6 1.0 %collective-permute-done.7.got_ref = bf16[32,3584]{1,0:T(8,128)(2,1)S(1)} collective-permute-done((bf16[32,3584]{1,0:T(8,128)(2,1)S(1)}, bf16[32,3584]{1,0:T(8,128)(2,1)S(1)}, u32[]{:S(2)}, u32[]{:S(2)}) %collective-permute-start.7) | collective-permute-done | bytes 229408 | tf_op jit(solution)/shard_map/ppermute | solution.py:243
  23.6 0.1 join.2
  23.7 0.7 %collective-permute-start.8 = (bf16[16,3200]{1,0:T(8,128)(2,1)S(1)}, bf16[16,3200]{1,0:T(8,128)(2,1)S(1)}, u32[]{:S(2)}, u32[]{:S(2)}) collective-permute-start(bf16[16,3200]{1,0:T(8,128)(2,1)S(1)} %get-tuple-element.65), channel_id=1, source_target_pairs={{0,8},{1,13},{2,10},{3,15},{4,12},{5,9},{6,14},{7,11},{8,0},{9,5},... | collective-permute-start | bytes 307208 | tf_op jit(solution)/shard_map/ppermute | solution.py:247
  24.4 0.5 %collective-permute-start.9 = (bf16[16,3200]{1,0:T(8,128)(2,1)S(1)}, bf16[16,3200]{1,0:T(8,128)(2,1)S(1)}, u32[]{:S(2)}, u32[]{:S(2)}) collective-permute-start(bf16[16,3200]{1,0:T(8,128)(2,1)S(1)} %get-tuple-element.66), channel_id=1, source_target_pairs={{0,2},{1,5},{2,0},{3,7},{4,6},{5,1},{6,4},{7,3},{8,10},{9,13},{10,... | collective-permute-start | bytes 307208 | tf_op jit(solution)/shard_map/ppermute | solution.py:247
  24.9 0.0 collective-permute-done.10.got_ref
  24.9 0.1 join.3
  25.0 3.3 %collective-permute-start.11 = (bf16[8,3200]{1,0:T(8,128)(2,1)S(1)}, bf16[8,3200]{1,0:T(8,128)(2,1)S(1)}, u32[]{:S(2)}, u32[]{:S(2)}) collective-permute-start(bf16[8,3200]{1,0:T(8,128)(2,1)S(1)} %get-tuple-element.69), channel_id=1, source_target_pairs={{0,10},{1,15},{2,8},{3,13},{4,14},{5,11},{6,12},{7,9},{8,2},{9,7},... | collective-permute-start | bytes 153608 | tf_op jit(solution)/shard_map/ppermute | solution.py:247
  28.3 2.0 %collective-permute-start.14 = (bf16[8,3200]{1,0:T(8,128)(2,1)S(1)}, bf16[8,3200]{1,0:T(8,128)(2,1)S(1)}, u32[]{:S(2)}, u32[]{:S(2)}) collective-permute-start(bf16[8,3200]{1,0:T(8,128)(2,1)S(1)} %get-tuple-element.72), channel_id=1, source_target_pairs={{0,11},{1,14},{2,9},{3,12},{4,15},{5,10},{6,13},{7,8},{8,3},{9,6},... | collective-permute-start | bytes 153608 | tf_op jit(solution)/shard_map/ppermute | solution.py:247
  30.4 1.2 %collective-permute-start.15 = (bf16[8,3200]{1,0:T(8,128)(2,1)S(1)}, bf16[8,3200]{1,0:T(8,128)(2,1)S(1)}, u32[]{:S(2)}, u32[]{:S(2)}) collective-permute-start(bf16[8,3200]{1,0:T(8,128)(2,1)S(1)} %get-tuple-element.73), channel_id=1, source_target_pairs={{0,6},{1,7},{2,4},{3,5},{4,2},{5,3},{6,0},{7,1},{8,14},{9,15},{10,... | collective-permute-start | bytes 153608 | tf_op jit(solution)/shard_map/ppermute | solution.py:247
  31.6 1.3 %collective-permute-done.8.refs_0_ = bf16[16,3200]{1,0:T(8,128)(2,1)S(1)} collective-permute-done((bf16[16,3200]{1,0:T(8,128)(2,1)S(1)}, bf16[16,3200]{1,0:T(8,128)(2,1)S(1)}, u32[]{:S(2)}, u32[]{:S(2)}) %collective-permute-start.8) | collective-permute-done | bytes 102432 | tf_op jit(solution)/shard_map/ppermute | solution.py:247
  32.9 0.1 collective-permute-start.12
  33.0 0.5 %collective-permute-start.13 = (bf16[8,3200]{1,0:T(8,128)(2,1)S(1)}, bf16[8,3200]{1,0:T(8,128)(2,1)S(1)}, u32[]{:S(2)}, u32[]{:S(2)}) collective-permute-start(bf16[8,3200]{1,0:T(8,128)(2,1)S(1)} %get-tuple-element.71), channel_id=1, source_target_pairs={{0,1},{1,0},{2,3},{3,2},{4,5},{5,4},{6,7},{7,6},{8,9},{9,8},{10,11... | collective-permute-start | bytes 153608 | tf_op jit(solution)/shard_map/ppermute | solution.py:243
  33.5 1.2 %collective-permute-done.11.refs_2_ = bf16[8,3200]{1,0:T(8,128)(2,1)S(1)} collective-permute-done((bf16[8,3200]{1,0:T(8,128)(2,1)S(1)}, bf16[8,3200]{1,0:T(8,128)(2,1)S(1)}, u32[]{:S(2)}, u32[]{:S(2)}) %collective-permute-start.11) | collective-permute-done | bytes 51232 | tf_op jit(solution)/shard_map/ppermute | solution.py:247
  34.6 1.7 %collective-permute-done.15.refs_6_ = bf16[8,3200]{1,0:T(8,128)(2,1)S(1)} collective-permute-done((bf16[8,3200]{1,0:T(8,128)(2,1)S(1)}, bf16[8,3200]{1,0:T(8,128)(2,1)S(1)}, u32[]{:S(2)}, u32[]{:S(2)}) %collective-permute-start.15) | collective-permute-done | bytes 51232 | tf_op jit(solution)/shard_map/ppermute | solution.py:247
  36.3 1.2 %combine.1 = bf16[128,3584]{1,0:T(8,128)(2,1)} custom-call(bf16[128,128]{1,0:T(8,128)(2,1)S(1)} %get-tuple-element.51.mix_ref, bf16[16,3200]{1,0:T(8,128)(2,1)S(1)} %collective-permute-done.8.refs_0_, bf16[16,3200]{1,0:T(8,128)(2,1)S(1)} %collective-permute-done.9.refs_1_, bf16[8,3200]{1,0:T(8,128)(2,1)S(1)} %collective-permute-done.11.refs_2_, ...), custom_call_target="tpu_custom_call" | custom-call | tf_op jit(solution)/shard_map/combine/pallas_call | solution.py:271
  (9 shorter events, 0.1 us)
Async XLA Ops:
  1.9 1.6 %collective-permute-start = (bf16[32,3200]{1,0:T(8,128)(2,1)S(1)}, bf16[32,3200]{1,0:T(8,128)(2,1)S(1)}, u32[]{:S(2)}, u32[]{:S(2)}) collective-permute-start(bf16[32,3200]{1,0:T(8,128)(2,1)S(1)} %get-tuple-element.41), channel_id=1, source_target_pairs={{0,1},{1,0},{2,3},{3,2},{4,5},{5,4},{6,7},{7,6},{8,9},{9,8},{10,11... | collective-permute-start | bytes 614408 | tf_op jit(solution)/shard_map/ppermute | solution.py:243
  3.5 12.7 %collective-permute-start.1 = (bf16[16,3200]{1,0:T(8,128)(2,1)S(1)}, bf16[16,3200]{1,0:T(8,128)(2,1)S(1)}, u32[]{:S(2)}, u32[]{:S(2)}) collective-permute-start(bf16[16,3200]{1,0:T(8,128)(2,1)S(1)} %get-tuple-element.42), channel_id=1, source_target_pairs={{0,8},{1,13},{2,10},{3,15},{4,12},{5,9},{6,14},{7,11},{8,0},{9,5},... | collective-permute-start | bytes 307208 | tf_op jit(solution)/shard_map/ppermute | solution.py:247
  7.6 8.7 %collective-permute-start.2 = (bf16[16,3200]{1,0:T(8,128)(2,1)S(1)}, bf16[16,3200]{1,0:T(8,128)(2,1)S(1)}, u32[]{:S(2)}, u32[]{:S(2)}) collective-permute-start(bf16[16,3200]{1,0:T(8,128)(2,1)S(1)} %get-tuple-element.43), channel_id=1, source_target_pairs={{0,2},{1,5},{2,0},{3,7},{4,6},{5,1},{6,4},{7,3},{8,10},{9,13},{10,... | collective-permute-start | bytes 307208 | tf_op jit(solution)/shard_map/ppermute | solution.py:247
  9.1 9.4 %collective-permute-start.3 = (bf16[16,3200]{1,0:T(8,128)(2,1)S(1)}, bf16[16,3200]{1,0:T(8,128)(2,1)S(1)}, u32[]{:S(2)}, u32[]{:S(2)}) collective-permute-start(bf16[16,3200]{1,0:T(8,128)(2,1)S(1)} %get-tuple-element.44), channel_id=1, source_target_pairs={{0,10},{1,15},{2,8},{3,13},{4,14},{5,11},{6,12},{7,9},{8,2},{9,7},... | collective-permute-start | bytes 307208 | tf_op jit(solution)/shard_map/ppermute | solution.py:247
  9.1 7.1 %collective-permute-start.4 = (bf16[8,3200]{1,0:T(8,128)(2,1)S(1)}, bf16[8,3200]{1,0:T(8,128)(2,1)S(1)}, u32[]{:S(2)}, u32[]{:S(2)}) collective-permute-start(bf16[8,3200]{1,0:T(8,128)(2,1)S(1)} %get-tuple-element.45), channel_id=1, source_target_pairs={{0,6},{1,7},{2,4},{3,5},{4,2},{5,3},{6,0},{7,1},{8,14},{9,15},{10,... | collective-permute-start | bytes 153608 | tf_op jit(solution)/shard_map/ppermute | solution.py:247
  18.5 1.7 %collective-permute-start.5 = (bf16[32,3200]{1,0:T(8,128)(2,1)S(1)}, bf16[32,3200]{1,0:T(8,128)(2,1)S(1)}, u32[]{:S(2)}, u32[]{:S(2)}) collective-permute-start(bf16[32,3200]{1,0:T(8,128)(2,1)S(1)} %get-tuple-element.56.refs_0_), channel_id=1, source_target_pairs={{0,1},{1,0},{2,3},{3,2},{4,5},{5,4},{6,7},{7,6},{8,9},{9,8},{10,11... | collective-permute-start | bytes 614408 | tf_op jit(solution)/shard_map/ppermute | solution.py:243
  18.6 1.7 %collective-permute-start.6 = (bf16[24,3200]{1,0:T(8,128)(2,1)S(1)}, bf16[24,3200]{1,0:T(8,128)(2,1)S(1)}, u32[]{:S(2)}, u32[]{:S(2)}) collective-permute-start(bf16[24,3200]{1,0:T(8,128)(2,1)S(1)} %get-tuple-element.57.refs_1_), channel_id=1, source_target_pairs={{0,1},{1,0},{2,3},{3,2},{4,5},{5,4},{6,7},{7,6},{8,9},{9,8},{10,11... | collective-permute-start | bytes 460808 | tf_op jit(solution)/shard_map/ppermute | solution.py:243
  22.1 1.6 %collective-permute-start.7 = (bf16[32,3584]{1,0:T(8,128)(2,1)S(1)}, bf16[32,3584]{1,0:T(8,128)(2,1)S(1)}, u32[]{:S(2)}, u32[]{:S(2)}) collective-permute-start(bf16[32,3584]{1,0:T(8,128)(2,1)S(1)} %get-tuple-element.64), channel_id=1, source_target_pairs={{0,1},{1,0},{2,3},{3,2},{4,5},{5,4},{6,7},{7,6},{8,9},{9,8},{10,11... | collective-permute-start | bytes 688136 | tf_op jit(solution)/shard_map/ppermute | solution.py:243
  22.3 2.6 %collective-permute-start.10 = (bf16[32,3584]{1,0:T(8,128)(2,1)S(1)}, bf16[32,3584]{1,0:T(8,128)(2,1)S(1)}, u32[]{:S(2)}, u32[]{:S(2)}) collective-permute-start(bf16[32,3584]{1,0:T(8,128)(2,1)S(1)} %get-tuple-element.68), channel_id=1, source_target_pairs={{0,1},{1,0},{2,3},{3,2},{4,5},{5,4},{6,7},{7,6},{8,9},{9,8},{10,11... | collective-permute-start | bytes 688136 | tf_op jit(solution)/shard_map/ppermute | solution.py:243
  23.7 9.2 %collective-permute-start.8 = (bf16[16,3200]{1,0:T(8,128)(2,1)S(1)}, bf16[16,3200]{1,0:T(8,128)(2,1)S(1)}, u32[]{:S(2)}, u32[]{:S(2)}) collective-permute-start(bf16[16,3200]{1,0:T(8,128)(2,1)S(1)} %get-tuple-element.65), channel_id=1, source_target_pairs={{0,8},{1,13},{2,10},{3,15},{4,12},{5,9},{6,14},{7,11},{8,0},{9,5},... | collective-permute-start | bytes 307208 | tf_op jit(solution)/shard_map/ppermute | solution.py:247
  24.4 8.5 %collective-permute-start.9 = (bf16[16,3200]{1,0:T(8,128)(2,1)S(1)}, bf16[16,3200]{1,0:T(8,128)(2,1)S(1)}, u32[]{:S(2)}, u32[]{:S(2)}) collective-permute-start(bf16[16,3200]{1,0:T(8,128)(2,1)S(1)} %get-tuple-element.66), channel_id=1, source_target_pairs={{0,2},{1,5},{2,0},{3,7},{4,6},{5,1},{6,4},{7,3},{8,10},{9,13},{10,... | collective-permute-start | bytes 307208 | tf_op jit(solution)/shard_map/ppermute | solution.py:247
  25.0 9.6 %collective-permute-start.11 = (bf16[8,3200]{1,0:T(8,128)(2,1)S(1)}, bf16[8,3200]{1,0:T(8,128)(2,1)S(1)}, u32[]{:S(2)}, u32[]{:S(2)}) collective-permute-start(bf16[8,3200]{1,0:T(8,128)(2,1)S(1)} %get-tuple-element.69), channel_id=1, source_target_pairs={{0,10},{1,15},{2,8},{3,13},{4,14},{5,11},{6,12},{7,9},{8,2},{9,7},... | collective-permute-start | bytes 153608 | tf_op jit(solution)/shard_map/ppermute | solution.py:247
  28.3 6.3 %collective-permute-start.14 = (bf16[8,3200]{1,0:T(8,128)(2,1)S(1)}, bf16[8,3200]{1,0:T(8,128)(2,1)S(1)}, u32[]{:S(2)}, u32[]{:S(2)}) collective-permute-start(bf16[8,3200]{1,0:T(8,128)(2,1)S(1)} %get-tuple-element.72), channel_id=1, source_target_pairs={{0,11},{1,14},{2,9},{3,12},{4,15},{5,10},{6,13},{7,8},{8,3},{9,6},... | collective-permute-start | bytes 153608 | tf_op jit(solution)/shard_map/ppermute | solution.py:247
  30.4 5.9 %collective-permute-start.15 = (bf16[8,3200]{1,0:T(8,128)(2,1)S(1)}, bf16[8,3200]{1,0:T(8,128)(2,1)S(1)}, u32[]{:S(2)}, u32[]{:S(2)}) collective-permute-start(bf16[8,3200]{1,0:T(8,128)(2,1)S(1)} %get-tuple-element.73), channel_id=1, source_target_pairs={{0,6},{1,7},{2,4},{3,5},{4,2},{5,3},{6,0},{7,1},{8,14},{9,15},{10,... | collective-permute-start | bytes 153608 | tf_op jit(solution)/shard_map/ppermute | solution.py:247
  32.9 3.4 %collective-permute-start.12 = (bf16[8,3200]{1,0:T(8,128)(2,1)S(1)}, bf16[8,3200]{1,0:T(8,128)(2,1)S(1)}, u32[]{:S(2)}, u32[]{:S(2)}) collective-permute-start(bf16[8,3200]{1,0:T(8,128)(2,1)S(1)} %get-tuple-element.70), channel_id=1, source_target_pairs={{0,1},{1,0},{2,3},{3,2},{4,5},{5,4},{6,7},{7,6},{8,9},{9,8},{10,11... | collective-permute-start | bytes 153608 | tf_op jit(solution)/shard_map/ppermute | solution.py:243
  33.0 3.3 %collective-permute-start.13 = (bf16[8,3200]{1,0:T(8,128)(2,1)S(1)}, bf16[8,3200]{1,0:T(8,128)(2,1)S(1)}, u32[]{:S(2)}, u32[]{:S(2)}) collective-permute-start(bf16[8,3200]{1,0:T(8,128)(2,1)S(1)} %get-tuple-element.71), channel_id=1, source_target_pairs={{0,1},{1,0},{2,3},{3,2},{4,5},{5,4},{6,7},{7,6},{8,9},{9,8},{10,11... | collective-permute-start | bytes 153608 | tf_op jit(solution)/shard_map/ppermute | solution.py:243

commit v20 on v19

--- a/solution.py
+++ b/solution.py
@@ -131,14 +131,7 @@
     small[2].wait()
     rows = (wide * lax.rsqrt(mean_square + 1e-06) * gain[...]).astype(jnp.bfloat16)
     rows = rows.astype(jnp.float32)
-    blocks = pack(rows)
-    if len(outs) == 1:
-        store(outs, blocks)
-    else:
-        kept, given = 3 * SLOTS, 6 * SLOTS
-        store(outs[:1], blocks[:kept])
-        store(outs[1:2], jnp.concatenate([blocks[kept:given], blocks[given + SLOTS :]], axis=0))
-        store(outs[2:], blocks[given:])
+    store(outs, pack(rows))
 
 
 def stage_kernel(mix_ref, *refs):
@@ -161,15 +154,6 @@
 
 def together(refs):
     return jnp.concatenate([b[...].astype(jnp.float32) for b in refs], axis=0)
-
-
-def merge_kernel(kept_ref, got_ref, *outs):
-    *outs, own_out = outs
-    kept, got = kept_ref[...].astype(jnp.float32), got_ref[...].astype(jnp.float32)
-    for i, out in enumerate(outs):
-        here = slice(i * SLOTS, (i + 1) * SLOTS)
-        out[...] = jnp.concatenate([kept[here], got[here]], axis=0).astype(jnp.bfloat16)
-    own_out[...] = got[len(outs) * SLOTS :].astype(jnp.bfloat16)
 
 
 def gather_kernel(count, *refs):
@@ -281,7 +265,7 @@
             name="combine",
         )(mix, *arrays)
 
-    first = packed(3, 4, 1, 1) if few else packed(flight)
+    first = packed(*[1] * flight) if few else packed(flight)
     mix, *outgoing = pl.pallas_call(
         functools.partial(dispatch_kernel, flight),
         out_shape=(jax.ShapeDtypeStruct((2 * flight * SLOTS, count), jnp.bfloat16),) + first,
@@ -317,17 +301,25 @@
 
     one, two, three = zip(*CARRIED)
     four = (SHARED, SHARED)
-    kept, given, shared, own = outgoing
-    *pairs, other_own = local(merge_kernel, packed(2, 2, 2, 1), "merge", kept, swap(given))
-    shared = travel(shared, four)
-    arrived = [travel(a, r) for a, r in zip(pairs, (one, two, three))] + [shared]
+    first, second, third, first_across, second_across, third_across, shared, own = outgoing
+    arrived = [
+        travel(first, one),
+        travel(second, two),
+        travel(first_across, one[::-1], 1),
+        travel(second_across, two[::-1], 1),
+        travel(third, three),
+        travel(third_across, three[::-1], 1),
+        travel(shared, four),
+    ]
+    order = (1, 3, 0, 2, 4, 5, 6)
+    arrived = [arrived[i] for i in order]
     *arrived, gate, up, down, mix = lax.optimization_barrier((*arrived, *stage(mix)))
-    kernel = functools.partial(gather_kernel, 2)
-    rows = local(kernel, packed(4, 3), "gather", *arrived)
-    mine_one, mine_two, theirs_one, theirs_two = experts(
-        (*rows, own, *[swap(a) for a in rows], other_own), (gate, up, down)
+    first, second, first_across, second_across, third, third_across, shared = (
+        arrived[order.index(i)] for i in range(7)
     )
-
+    rows = (first, first_across, second, second_across, third, third_across, shared, own)
+    (rows,) = local(functools.partial(gather_kernel, 1), packed(flight), "gather", *rows)
+    mine_one, mine_two, theirs_one, theirs_two = experts((rows, swap(rows)), (gate, up, down))
     first, second = join((2, 2), mine_one, theirs_one)
     third, third_across, shared, own = join((1, 1, 1, 1), mine_two, theirs_two)
     first, second, shared = travel(first, one), travel(second, two), travel(shared, four)

time: 37.6 us -> 38.4 us (1.021)
  starting transfers between devices: 18.3 us -> 21.4 us
  waiting for transfers between devices: 9.71 us -> 7.37 us
    ppermute x9 -> x12, starting transfers between devices: 16.1 us -> 20.2 us  [travel(): return lax.ppermute(rows, 'exp', pairs)]
    ppermute x9 -> x12, waiting for transfers between devices: 6.48 us -> 4.65 us  [travel(): return lax.ppermute(rows, 'exp', pairs)]
    ppermute x7 -> x5, starting transfers between devices: 2.23 us -> 1.21 us  [swap(): return lax.ppermute(rows, 'exp', [(n, n ^ 1) for n in range(owners)])]
    ppermute x7 -> x5, waiting for transfers between devices: 3.23 us -> 2.72 us  [swap(): return lax.ppermute(rows, 'exp', [(n, n ^ 1) for n in range(owners)])]
    pallas_call x6 -> x5, Pallas kernels: 2.03 us -> 1.99 us  [local(): pl.pallas_call(kernel, out_shape=outs, in_specs=[VMEM] * len(args), out_s...]
  transfers between devices with their start and end apart: 16 -> 17, of which waited for: 8 -> 6; matrix products, arithmetic and copies ran while one was open for 0% -> 0% of each run, Pallas kernels for 12% -> 12%
where the time goes in v20:
time: 38.4 us; the launch traced here: 38.2 us
  starting transfers between devices  21.4 us (56%)
  Pallas kernels  9.31 us (24%)
  waiting for transfers between devices  7.37 us (19%)
    ppermute x12, starting transfers between devices, travel(): return lax.ppermute(rows, 'exp', pairs)  20.2 us
    ppermute x12, waiting for transfers between devices, travel(): return lax.ppermute(rows, 'exp', pairs)  4.65 us
    pallas_call x1, Pallas kernels, stage(): pl.pallas_call(stage_kernel, out_shape=(*outs, jax.ShapeDtypeStruct(mix.s...  4.25 us
    ppermute x5, waiting for transfers between devices, swap(): return lax.ppermute(rows, 'exp', [(n, n ^ 1) for n in range(owners)])  2.72 us
    pallas_call x5, Pallas kernels, local(): pl.pallas_call(kernel, out_shape=outs, in_specs=[VMEM] * len(args), out_s...  1.99 us
    pallas_call x1, Pallas kernels, per_device(): pl.pallas_call(functools.partial(dispatch_kernel, flight), out_shape=(jax...  1.91 us
    ppermute x5, starting transfers between devices, swap(): return lax.ppermute(rows, 'exp', [(n, n ^ 1) for n in range(owners)])  1.21 us
    pallas_call x1, Pallas kernels, combine(): pl.pallas_call(functools.partial(combine_kernel, paired), out_shape=jax.S...  1.17 us
  transfers between devices with their start and end apart: 17, of which 6 were waited for; matrix products, arithmetic and copies ran while one was open for 0% of the time, Pallas kernels for 12%

profile of v20, /device:TPU:0, one launch (start us, length us, event | category | flops | bytes accessed | tf_op | source)
XLA Modules:
  0.0 38.2 jit_solution(18250811787173940618)
XLA Ops:
  0.0 1.9 %dispatch.1 = (bf16[128,128]{1,0:T(8,128)(2,1)S(1)}, bf16[8,3200]{1,0:T(8,128)(2,1)S(1)}, bf16[8,3200]{1,0:T(8,128)(2,1)S(1)}, bf16[8,3200]{1,0:T(8,128)(2,1)S(1...) custom-call(bf16[128,3584]{1,0:T(8,128)(2,1)} %tok_hbm.1, ...), custom_call_target="tpu_custom_call" | custom-call | tf_op jit(solution)/shard_map/dispatch/pallas_call | solution.py:269
  1.9 3.0 %collective-permute-start = (bf16[8,3200]{1,0:T(8,128)(2,1)S(1)}, bf16[8,3200]{1,0:T(8,128)(2,1)S(1)}, u32[]{:S(2)}, u32[]{:S(2)}) collective-permute-start(bf16[8,3200]{1,0:T(8,128)(2,1)S(1)} %get-tuple-element.41), channel_id=1, source_target_pairs={{0,2},{1,5},{2,0},{3,7},{4,6},{5,1},{6,4},{7,3},{8,10},{9,13},{10,... | collective-permute-start | bytes 153608 | tf_op jit(solution)/shard_map/ppermute | solution.py:231
  5.0 2.6 %collective-permute-start.2 = (bf16[8,3200]{1,0:T(8,128)(2,1)S(1)}, bf16[8,3200]{1,0:T(8,128)(2,1)S(1)}, u32[]{:S(2)}, u32[]{:S(2)}) collective-permute-start(bf16[8,3200]{1,0:T(8,128)(2,1)S(1)} %get-tuple-element.43), channel_id=1, source_target_pairs={{0,8},{1,13},{2,10},{3,15},{4,12},{5,9},{6,14},{7,11},{8,0},{9,5},... | collective-permute-start | bytes 153608 | tf_op jit(solution)/shard_map/ppermute | solution.py:231
  7.5 1.3 %collective-permute-start.3 = (bf16[8,3200]{1,0:T(8,128)(2,1)S(1)}, bf16[8,3200]{1,0:T(8,128)(2,1)S(1)}, u32[]{:S(2)}, u32[]{:S(2)}) collective-permute-start(bf16[8,3200]{1,0:T(8,128)(2,1)S(1)} %get-tuple-element.44), channel_id=1, source_target_pairs={{0,13},{1,8},{2,15},{3,10},{4,9},{5,12},{6,11},{7,14},{8,5},{9,0},... | collective-permute-start | bytes 153608 | tf_op jit(solution)/shard_map/ppermute | solution.py:231
  8.8 1.7 %collective-permute-start.4 = (bf16[8,3200]{1,0:T(8,128)(2,1)S(1)}, bf16[8,3200]{1,0:T(8,128)(2,1)S(1)}, u32[]{:S(2)}, u32[]{:S(2)}) collective-permute-start(bf16[8,3200]{1,0:T(8,128)(2,1)S(1)} %get-tuple-element.45), channel_id=1, source_target_pairs={{0,10},{1,15},{2,8},{3,13},{4,14},{5,11},{6,12},{7,9},{8,2},{9,7},... | collective-permute-start | bytes 153608 | tf_op jit(solution)/shard_map/ppermute | solution.py:231
  10.5 2.5 %collective-permute-start.5 = (bf16[8,3200]{1,0:T(8,128)(2,1)S(1)}, bf16[8,3200]{1,0:T(8,128)(2,1)S(1)}, u32[]{:S(2)}, u32[]{:S(2)}) collective-permute-start(bf16[8,3200]{1,0:T(8,128)(2,1)S(1)} %get-tuple-element.46), channel_id=1, source_target_pairs={{0,15},{1,10},{2,13},{3,8},{4,11},{5,14},{6,9},{7,12},{8,7},{9,2},... | collective-permute-start | bytes 153608 | tf_op jit(solution)/shard_map/ppermute | solution.py:231
  12.9 0.9 %collective-permute-start.6 = (bf16[8,3200]{1,0:T(8,128)(2,1)S(1)}, bf16[8,3200]{1,0:T(8,128)(2,1)S(1)}, u32[]{:S(2)}, u32[]{:S(2)}) collective-permute-start(bf16[8,3200]{1,0:T(8,128)(2,1)S(1)} %get-tuple-element.47), channel_id=1, source_target_pairs={{0,6},{1,7},{2,4},{3,5},{4,2},{5,3},{6,0},{7,1},{8,14},{9,15},{10,... | collective-permute-start | bytes 153608 | tf_op jit(solution)/shard_map/ppermute | solution.py:231
  13.9 4.2 %stage.1 = (bf16[3584,512]{1,0:T(8,128)(2,1)S(1)}, bf16[3584,512]{1,0:T(8,128)(2,1)S(1)}, bf16[512,3584]{1,0:T(8,128)(2,1)S(1)}, bf16[128,128]{1,0:T(8,128)(2,1)S(1)}) custom-call(bf16[128,128]{1,0:T(8,128)(2,1)S(1)} %get-tuple-element.48.mix_ref, bf16[3584,512]{1,0:T(8,128)(2,1)} %bitcast.5, bf16[3584,512]{1,0:T(8,128)(2,1)} %bitcast.6, ...), custom_call_target="tpu_custom_call" | custom-call | flops 1 | bytes 1 | tf_op jit(solution)/shard_map/stage/pallas_call | solution.py:236
  18.1 0.0 collective-permute-done.3.refs_1_
  18.1 0.0 collective-permute-done.4.refs_4_
  18.2 0.7 %collective-permute-done.6.refs_6_ = bf16[8,3200]{1,0:T(8,128)(2,1)S(1)} collective-permute-done((bf16[8,3200]{1,0:T(8,128)(2,1)S(1)}, bf16[8,3200]{1,0:T(8,128)(2,1)S(1)}, u32[]{:S(2)}, u32[]{:S(2)}) %collective-permute-start.6) | collective-permute-done | bytes 51232 | tf_op jit(solution)/shard_map/ppermute | solution.py:231
  18.8 0.1 collective-permute-start.7
  18.9 1.7 %collective-permute-done.7.refs_1_ = bf16[64,3200]{1,0:T(8,128)(2,1)S(1)} collective-permute-done((bf16[64,3200]{1,0:T(8,128)(2,1)S(1)}, bf16[64,3200]{1,0:T(8,128)(2,1)S(1)}, u32[]{:S(2)}, u32[]{:S(2)}) %collective-permute-start.7) | collective-permute-done | bytes 409632 | tf_op jit(solution)/shard_map/ppermute | solution.py:227
  20.7 1.8 %experts.1 = (bf16[32,3584]{1,0:T(8,128)(2,1)S(1)}, bf16[32,3584]{1,0:T(8,128)(2,1)S(1)}, bf16[32,3584]{1,0:T(8,128)(2,1)S(1)}, bf16[32,3584]{1,0:T(8,128)(2,1)S(1)}) custom-call(bf16[64,3200]{1,0:T(8,128)(2,1)S(1)} %gather.1.refs_0_, bf16[64,3200]{1,0:T(8,128)(2,1)S(1)} %collective-permute-done.7.refs_1_, bf16[3584,512]{1,0:T(8,128)(2,1)S(1)} %get-tuple-element.62.refs_2_, ...), custom_call_target="tpu_custom_call" | custom-call | flops 1 | bytes 1 | tf_op jit(solution)/shard_map/experts/pallas_call | solution.py:209
  22.4 0.2 collective-permute-start.8
  22.6 0.4 collective-permute-start.11
  23.0 1.0 %collective-permute-done.8.got_ref = bf16[32,3584]{1,0:T(8,128)(2,1)S(1)} collective-permute-done((bf16[32,3584]{1,0:T(8,128)(2,1)S(1)}, bf16[32,3584]{1,0:T(8,128)(2,1)S(1)}, u32[]{:S(2)}, u32[]{:S(2)}) %collective-permute-start.8) | collective-permute-done | bytes 229408 | tf_op jit(solution)/shard_map/ppermute | solution.py:227
  24.0 0.1 join.2
  24.1 2.7 %collective-permute-start.9 = (bf16[16,3200]{1,0:T(8,128)(2,1)S(1)}, bf16[16,3200]{1,0:T(8,128)(2,1)S(1)}, u32[]{:S(2)}, u32[]{:S(2)}) collective-permute-start(bf16[16,3200]{1,0:T(8,128)(2,1)S(1)} %get-tuple-element.67), channel_id=1, source_target_pairs={{0,8},{1,13},{2,10},{3,15},{4,12},{5,9},{6,14},{7,11},{8,0},{9,5},... | collective-permute-start | bytes 307208 | tf_op jit(solution)/shard_map/ppermute | solution.py:231
  26.8 0.5 %collective-permute-start.10 = (bf16[16,3200]{1,0:T(8,128)(2,1)S(1)}, bf16[16,3200]{1,0:T(8,128)(2,1)S(1)}, u32[]{:S(2)}, u32[]{:S(2)}) collective-permute-start(bf16[16,3200]{1,0:T(8,128)(2,1)S(1)} %get-tuple-element.68), channel_id=1, source_target_pairs={{0,2},{1,5},{2,0},{3,7},{4,6},{5,1},{6,4},{7,3},{8,10},{9,13},{10,... | collective-permute-start | bytes 307208 | tf_op jit(solution)/shard_map/ppermute | solution.py:231
  27.3 0.1 join.3
  27.4 1.3 %collective-permute-start.12 = (bf16[8,3200]{1,0:T(8,128)(2,1)S(1)}, bf16[8,3200]{1,0:T(8,128)(2,1)S(1)}, u32[]{:S(2)}, u32[]{:S(2)}) collective-permute-start(bf16[8,3200]{1,0:T(8,128)(2,1)S(1)} %get-tuple-element.71), channel_id=1, source_target_pairs={{0,10},{1,15},{2,8},{3,13},{4,14},{5,11},{6,12},{7,9},{8,2},{9,7},... | collective-permute-start | bytes 153608 | tf_op jit(solution)/shard_map/ppermute | solution.py:231
  28.7 2.2 %collective-permute-start.15 = (bf16[8,3200]{1,0:T(8,128)(2,1)S(1)}, bf16[8,3200]{1,0:T(8,128)(2,1)S(1)}, u32[]{:S(2)}, u32[]{:S(2)}) collective-permute-start(bf16[8,3200]{1,0:T(8,128)(2,1)S(1)} %get-tuple-element.74), channel_id=1, source_target_pairs={{0,11},{1,14},{2,9},{3,12},{4,15},{5,10},{6,13},{7,8},{8,3},{9,6},... | collective-permute-start | bytes 153608 | tf_op jit(solution)/shard_map/ppermute | solution.py:231
  30.9 1.5 %collective-permute-start.16 = (bf16[8,3200]{1,0:T(8,128)(2,1)S(1)}, bf16[8,3200]{1,0:T(8,128)(2,1)S(1)}, u32[]{:S(2)}, u32[]{:S(2)}) collective-permute-start(bf16[8,3200]{1,0:T(8,128)(2,1)S(1)} %get-tuple-element.75), channel_id=1, source_target_pairs={{0,6},{1,7},{2,4},{3,5},{4,2},{5,3},{6,0},{7,1},{8,14},{9,15},{10,... | collective-permute-start | bytes 153608 | tf_op jit(solution)/shard_map/ppermute | solution.py:231
  32.4 1.1 %collective-permute-done.9.refs_0_ = bf16[16,3200]{1,0:T(8,128)(2,1)S(1)} collective-permute-done((bf16[16,3200]{1,0:T(8,128)(2,1)S(1)}, bf16[16,3200]{1,0:T(8,128)(2,1)S(1)}, u32[]{:S(2)}, u32[]{:S(2)}) %collective-permute-start.9) | collective-permute-done | bytes 102432 | tf_op jit(solution)/shard_map/ppermute | solution.py:231
  33.5 0.0 collective-permute-done.10.refs_1_
  33.5 0.1 collective-permute-start.13
  33.6 0.5 %collective-permute-start.14 = (bf16[8,3200]{1,0:T(8,128)(2,1)S(1)}, bf16[8,3200]{1,0:T(8,128)(2,1)S(1)}, u32[]{:S(2)}, u32[]{:S(2)}) collective-permute-start(bf16[8,3200]{1,0:T(8,128)(2,1)S(1)} %get-tuple-element.73), channel_id=1, source_target_pairs={{0,1},{1,0},{2,3},{3,2},{4,5},{5,4},{6,7},{7,6},{8,9},{9,8},{10,11... | collective-permute-start | bytes 153608 | tf_op jit(solution)/shard_map/ppermute | solution.py:227
  34.1 2.0 %collective-permute-done.12.refs_2_ = bf16[8,3200]{1,0:T(8,128)(2,1)S(1)} collective-permute-done((bf16[8,3200]{1,0:T(8,128)(2,1)S(1)}, bf16[8,3200]{1,0:T(8,128)(2,1)S(1)}, u32[]{:S(2)}, u32[]{:S(2)}) %collective-permute-start.12) | collective-permute-done | bytes 51232 | tf_op jit(solution)/shard_map/ppermute | solution.py:231
  36.1 0.0 collective-permute-done.15.refs_5_
  36.1 0.9 %collective-permute-done.16.refs_6_ = bf16[8,3200]{1,0:T(8,128)(2,1)S(1)} collective-permute-done((bf16[8,3200]{1,0:T(8,128)(2,1)S(1)}, bf16[8,3200]{1,0:T(8,128)(2,1)S(1)}, u32[]{:S(2)}, u32[]{:S(2)}) %collective-permute-start.16) | collective-permute-done | bytes 51232 | tf_op jit(solution)/shard_map/ppermute | solution.py:231
  37.0 1.2 %combine.1 = bf16[128,3584]{1,0:T(8,128)(2,1)} custom-call(bf16[128,128]{1,0:T(8,128)(2,1)S(1)} %get-tuple-element.53.mix_ref, bf16[16,3200]{1,0:T(8,128)(2,1)S(1)} %collective-permute-done.9.refs_0_, bf16[16,3200]{1,0:T(8,128)(2,1)S(1)} %collective-permute-done.10.refs_1_, bf16[8,3200]{1,0:T(8,128)(2,1)S(1)} %collective-permute-done.12.refs_2_, ...), custom_call_target="tpu_custom_call" | custom-call | tf_op jit(solution)/shard_map/combine/pallas_call | solution.py:255
  (10 shorter events, 0.1 us)
Async XLA Ops:
  1.9 8.5 %collective-permute-start = (bf16[8,3200]{1,0:T(8,128)(2,1)S(1)}, bf16[8,3200]{1,0:T(8,128)(2,1)S(1)}, u32[]{:S(2)}, u32[]{:S(2)}) collective-permute-start(bf16[8,3200]{1,0:T(8,128)(2,1)S(1)} %get-tuple-element.41), channel_id=1, source_target_pairs={{0,2},{1,5},{2,0},{3,7},{4,6},{5,1},{6,4},{7,3},{8,10},{9,13},{10,... | collective-permute-start | bytes 153608 | tf_op jit(solution)/shard_map/ppermute | solution.py:231
  5.0 8.0 %collective-permute-start.1 = (bf16[8,3200]{1,0:T(8,128)(2,1)S(1)}, bf16[8,3200]{1,0:T(8,128)(2,1)S(1)}, u32[]{:S(2)}, u32[]{:S(2)}) collective-permute-start(bf16[8,3200]{1,0:T(8,128)(2,1)S(1)} %get-tuple-element.42), channel_id=1, source_target_pairs={{0,5},{1,2},{2,7},{3,0},{4,1},{5,6},{6,3},{7,4},{8,13},{9,10},{10,... | collective-permute-start | bytes 153608 | tf_op jit(solution)/shard_map/ppermute | solution.py:231
  5.0 13.2 %collective-permute-start.2 = (bf16[8,3200]{1,0:T(8,128)(2,1)S(1)}, bf16[8,3200]{1,0:T(8,128)(2,1)S(1)}, u32[]{:S(2)}, u32[]{:S(2)}) collective-permute-start(bf16[8,3200]{1,0:T(8,128)(2,1)S(1)} %get-tuple-element.43), channel_id=1, source_target_pairs={{0,8},{1,13},{2,10},{3,15},{4,12},{5,9},{6,14},{7,11},{8,0},{9,5},... | collective-permute-start | bytes 153608 | tf_op jit(solution)/shard_map/ppermute | solution.py:231
  7.5 10.6 %collective-permute-start.3 = (bf16[8,3200]{1,0:T(8,128)(2,1)S(1)}, bf16[8,3200]{1,0:T(8,128)(2,1)S(1)}, u32[]{:S(2)}, u32[]{:S(2)}) collective-permute-start(bf16[8,3200]{1,0:T(8,128)(2,1)S(1)} %get-tuple-element.44), channel_id=1, source_target_pairs={{0,13},{1,8},{2,15},{3,10},{4,9},{5,12},{6,11},{7,14},{8,5},{9,0},... | collective-permute-start | bytes 153608 | tf_op jit(solution)/shard_map/ppermute | solution.py:231
  8.8 9.3 %collective-permute-start.4 = (bf16[8,3200]{1,0:T(8,128)(2,1)S(1)}, bf16[8,3200]{1,0:T(8,128)(2,1)S(1)}, u32[]{:S(2)}, u32[]{:S(2)}) collective-permute-start(bf16[8,3200]{1,0:T(8,128)(2,1)S(1)} %get-tuple-element.45), channel_id=1, source_target_pairs={{0,10},{1,15},{2,8},{3,13},{4,14},{5,11},{6,12},{7,9},{8,2},{9,7},... | collective-permute-start | bytes 153608 | tf_op jit(solution)/shard_map/ppermute | solution.py:231
  10.5 7.7 %collective-permute-start.5 = (bf16[8,3200]{1,0:T(8,128)(2,1)S(1)}, bf16[8,3200]{1,0:T(8,128)(2,1)S(1)}, u32[]{:S(2)}, u32[]{:S(2)}) collective-permute-start(bf16[8,3200]{1,0:T(8,128)(2,1)S(1)} %get-tuple-element.46), channel_id=1, source_target_pairs={{0,15},{1,10},{2,13},{3,8},{4,11},{5,14},{6,9},{7,12},{8,7},{9,2},... | collective-permute-start | bytes 153608 | tf_op jit(solution)/shard_map/ppermute | solution.py:231
  12.9 5.9 %collective-permute-start.6 = (bf16[8,3200]{1,0:T(8,128)(2,1)S(1)}, bf16[8,3200]{1,0:T(8,128)(2,1)S(1)}, u32[]{:S(2)}, u32[]{:S(2)}) collective-permute-start(bf16[8,3200]{1,0:T(8,128)(2,1)S(1)} %get-tuple-element.47), channel_id=1, source_target_pairs={{0,6},{1,7},{2,4},{3,5},{4,2},{5,3},{6,0},{7,1},{8,14},{9,15},{10,... | collective-permute-start | bytes 153608 | tf_op jit(solution)/shard_map/ppermute | solution.py:231
  18.8 1.8 %collective-permute-start.7 = (bf16[64,3200]{1,0:T(8,128)(2,1)S(1)}, bf16[64,3200]{1,0:T(8,128)(2,1)S(1)}, u32[]{:S(2)}, u32[]{:S(2)}) collective-permute-start(bf16[64,3200]{1,0:T(8,128)(2,1)S(1)} %gather.1.refs_0_), channel_id=1, source_target_pairs={{0,1},{1,0},{2,3},{3,2},{4,5},{5,4},{6,7},{7,6},{8,9},{9,8},{10,11... | collective-permute-start | bytes 1228808 | tf_op jit(solution)/shard_map/ppermute | solution.py:227
  22.4 1.6 %collective-permute-start.8 = (bf16[32,3584]{1,0:T(8,128)(2,1)S(1)}, bf16[32,3584]{1,0:T(8,128)(2,1)S(1)}, u32[]{:S(2)}, u32[]{:S(2)}) collective-permute-start(bf16[32,3584]{1,0:T(8,128)(2,1)S(1)} %get-tuple-element.66), channel_id=1, source_target_pairs={{0,1},{1,0},{2,3},{3,2},{4,5},{5,4},{6,7},{7,6},{8,9},{9,8},{10,11... | collective-permute-start | bytes 688136 | tf_op jit(solution)/shard_map/ppermute | solution.py:227
  22.6 4.7 %collective-permute-start.11 = (bf16[32,3584]{1,0:T(8,128)(2,1)S(1)}, bf16[32,3584]{1,0:T(8,128)(2,1)S(1)}, u32[]{:S(2)}, u32[]{:S(2)}) collective-permute-start(bf16[32,3584]{1,0:T(8,128)(2,1)S(1)} %get-tuple-element.70), channel_id=1, source_target_pairs={{0,1},{1,0},{2,3},{3,2},{4,5},{5,4},{6,7},{7,6},{8,9},{9,8},{10,11... | collective-permute-start | bytes 688136 | tf_op jit(solution)/shard_map/ppermute | solution.py:227
  24.1 9.4 %collective-permute-start.9 = (bf16[16,3200]{1,0:T(8,128)(2,1)S(1)}, bf16[16,3200]{1,0:T(8,128)(2,1)S(1)}, u32[]{:S(2)}, u32[]{:S(2)}) collective-permute-start(bf16[16,3200]{1,0:T(8,128)(2,1)S(1)} %get-tuple-element.67), channel_id=1, source_target_pairs={{0,8},{1,13},{2,10},{3,15},{4,12},{5,9},{6,14},{7,11},{8,0},{9,5},... | collective-permute-start | bytes 307208 | tf_op jit(solution)/shard_map/ppermute | solution.py:231
  26.8 6.7 %collective-permute-start.10 = (bf16[16,3200]{1,0:T(8,128)(2,1)S(1)}, bf16[16,3200]{1,0:T(8,128)(2,1)S(1)}, u32[]{:S(2)}, u32[]{:S(2)}) collective-permute-start(bf16[16,3200]{1,0:T(8,128)(2,1)S(1)} %get-tuple-element.68), channel_id=1, source_target_pairs={{0,2},{1,5},{2,0},{3,7},{4,6},{5,1},{6,4},{7,3},{8,10},{9,13},{10,... | collective-permute-start | bytes 307208 | tf_op jit(solution)/shard_map/ppermute | solution.py:231
  27.4 8.7 %collective-permute-start.12 = (bf16[8,3200]{1,0:T(8,128)(2,1)S(1)}, bf16[8,3200]{1,0:T(8,128)(2,1)S(1)}, u32[]{:S(2)}, u32[]{:S(2)}) collective-permute-start(bf16[8,3200]{1,0:T(8,128)(2,1)S(1)} %get-tuple-element.71), channel_id=1, source_target_pairs={{0,10},{1,15},{2,8},{3,13},{4,14},{5,11},{6,12},{7,9},{8,2},{9,7},... | collective-permute-start | bytes 153608 | tf_op jit(solution)/shard_map/ppermute | solution.py:231
  28.7 7.4 %collective-permute-start.15 = (bf16[8,3200]{1,0:T(8,128)(2,1)S(1)}, bf16[8,3200]{1,0:T(8,128)(2,1)S(1)}, u32[]{:S(2)}, u32[]{:S(2)}) collective-permute-start(bf16[8,3200]{1,0:T(8,128)(2,1)S(1)} %get-tuple-element.74), channel_id=1, source_target_pairs={{0,11},{1,14},{2,9},{3,12},{4,15},{5,10},{6,13},{7,8},{8,3},{9,6},... | collective-permute-start | bytes 153608 | tf_op jit(solution)/shard_map/ppermute | solution.py:231
  30.9 6.1 %collective-permute-start.16 = (bf16[8,3200]{1,0:T(8,128)(2,1)S(1)}, bf16[8,3200]{1,0:T(8,128)(2,1)S(1)}, u32[]{:S(2)}, u32[]{:S(2)}) collective-permute-start(bf16[8,3200]{1,0:T(8,128)(2,1)S(1)} %get-tuple-element.75), channel_id=1, source_target_pairs={{0,6},{1,7},{2,4},{3,5},{4,2},{5,3},{6,0},{7,1},{8,14},{9,15},{10,... | collective-permute-start | bytes 153608 | tf_op jit(solution)/shard_map/ppermute | solution.py:231
  33.5 3.5 %collective-permute-start.13 = (bf16[8,3200]{1,0:T(8,128)(2,1)S(1)}, bf16[8,3200]{1,0:T(8,128)(2,1)S(1)}, u32[]{:S(2)}, u32[]{:S(2)}) collective-permute-start(bf16[8,3200]{1,0:T(8,128)(2,1)S(1)} %get-tuple-element.72), channel_id=1, source_target_pairs={{0,1},{1,0},{2,3},{3,2},{4,5},{5,4},{6,7},{7,6},{8,9},{9,8},{10,11... | collective-permute-start | bytes 153608 | tf_op jit(solution)/shard_map/ppermute | solution.py:227
  33.6 3.4 %collective-permute-start.14 = (bf16[8,3200]{1,0:T(8,128)(2,1)S(1)}, bf16[8,3200]{1,0:T(8,128)(2,1)S(1)}, u32[]{:S(2)}, u32[]{:S(2)}) collective-permute-start(bf16[8,3200]{1,0:T(8,128)(2,1)S(1)} %get-tuple-element.73), channel_id=1, source_target_pairs={{0,1},{1,0},{2,3},{3,2},{4,5},{5,4},{6,7},{7,6},{8,9},{9,8},{10,11... | collective-permute-start | bytes 153608 | tf_op jit(solution)/shard_map/ppermute | solution.py:227

commit v21 on v19

--- a/solution.py
+++ b/solution.py
@@ -135,10 +135,9 @@
     if len(outs) == 1:
         store(outs, blocks)
     else:
-        kept, given = 3 * SLOTS, 6 * SLOTS
-        store(outs[:1], blocks[:kept])
-        store(outs[1:2], jnp.concatenate([blocks[kept:given], blocks[given + SLOTS :]], axis=0))
-        store(outs[2:], blocks[given:])
+        order = [0, 3, 1, 2, 4, 5, 7, 6, 7]
+        blocks = [blocks[i * SLOTS : (i + 1) * SLOTS] for i in order]
+        store(outs, jnp.concatenate(blocks, axis=0))
 
 
 def stage_kernel(mix_ref, *refs):
@@ -281,7 +280,7 @@
             name="combine",
         )(mix, *arrays)
 
-    first = packed(3, 4, 1, 1) if few else packed(flight)
+    first = packed(1, 1, 2, 3, 1, 1) if few else packed(flight)
     mix, *outgoing = pl.pallas_call(
         functools.partial(dispatch_kernel, flight),
         out_shape=(jax.ShapeDtypeStruct((2 * flight * SLOTS, count), jnp.bfloat16),) + first,
@@ -317,11 +316,14 @@
 
     one, two, three = zip(*CARRIED)
     four = (SHARED, SHARED)
-    kept, given, shared, own = outgoing
-    *pairs, other_own = local(merge_kernel, packed(2, 2, 2, 1), "merge", kept, swap(given))
-    shared = travel(shared, four)
-    arrived = [travel(a, r) for a, r in zip(pairs, (one, two, three))] + [shared]
-    *arrived, gate, up, down, mix = lax.optimization_barrier((*arrived, *stage(mix)))
+    first, first_across, kept, given, shared, own = outgoing
+    second, third, other_own = local(merge_kernel, packed(2, 2, 1), "merge", kept, swap(given))
+    first, first_across = travel(first, one), travel(first_across, one[::-1], 1)
+    shared, first, first_across, gate, up, down, mix = lax.optimization_barrier(
+        (shared, first, first_across, *stage(mix))
+    )
+    second, third, shared = travel(second, two), travel(third, three), travel(shared, four)
+    arrived = lax.optimization_barrier((first, first_across, second, third, shared))
     kernel = functools.partial(gather_kernel, 2)
     rows = local(kernel, packed(4, 3), "gather", *arrived)
     mine_one, mine_two, theirs_one, theirs_two = experts(

time: 37.6 us -> 39.3 us (1.045)
  starting transfers between devices: 18.3 us -> 21.3 us
  waiting for transfers between devices: 9.71 us -> 8.45 us
    ppermute x9 -> x10, starting transfers between devices: 16.1 us -> 19 us  [travel(): return lax.ppermute(rows, 'exp', pairs)]
    ppermute x9 -> x10, waiting for transfers between devices: 6.48 us -> 5.68 us  [travel(): return lax.ppermute(rows, 'exp', pairs)]
    ppermute x7, waiting for transfers between devices: 3.23 us -> 2.78 us  [swap(): return lax.ppermute(rows, 'exp', [(n, n ^ 1) for n in range(owners)])]
  transfers between devices with their start and end apart: 16 -> 17, of which waited for: 8 -> 7; matrix products, arithmetic and copies ran while one was open for 0% -> 0% of each run, Pallas kernels for 12% -> 11%
where the time goes in v21:
time: 39.3 us; the launch traced here: 39.2 us
  starting transfers between devices  21.3 us (54%)
  Pallas kernels  9.33 us (24%)
  waiting for transfers between devices  8.45 us (22%)
    ppermute x10, starting transfers between devices, travel(): return lax.ppermute(rows, 'exp', pairs)  19 us
    ppermute x10, waiting for transfers between devices, travel(): return lax.ppermute(rows, 'exp', pairs)  5.68 us
    pallas_call x1, Pallas kernels, stage(): pl.pallas_call(stage_kernel, out_shape=(*outs, jax.ShapeDtypeStruct(mix.s...  4.25 us
    ppermute x7, waiting for transfers between devices, swap(): return lax.ppermute(rows, 'exp', [(n, n ^ 1) for n in range(owners)])  2.78 us
    ppermute x7, starting transfers between devices, swap(): return lax.ppermute(rows, 'exp', [(n, n ^ 1) for n in range(owners)])  2.23 us
    pallas_call x6, Pallas kernels, local(): pl.pallas_call(kernel, out_shape=outs, in_specs=[VMEM] * len(args), out_s...  2.01 us
    pallas_call x1, Pallas kernels, per_device(): pl.pallas_call(functools.partial(dispatch_kernel, flight), out_shape=(jax...  1.91 us
    pallas_call x1, Pallas kernels, combine(): pl.pallas_call(functools.partial(combine_kernel, paired), out_shape=jax.S...  1.17 us
  transfers between devices with their start and end apart: 17, of which 7 were waited for; matrix products, arithmetic and copies ran while one was open for 0% of the time, Pallas kernels for 11%

profile of v21, /device:TPU:0, one launch (start us, length us, event | category | flops | bytes accessed | tf_op | source)
XLA Modules:
  0.0 39.2 jit_solution(8527863567555898565)
XLA Ops:
  0.0 1.9 %dispatch.1 = (bf16[128,128]{1,0:T(8,128)(2,1)S(1)}, bf16[8,3200]{1,0:T(8,128)(2,1)S(1)}, bf16[8,3200]{1,0:T(8,128)(2,1)S(1)}, bf16[16,3200]{1,0:T(8,128)(2,1)S(...) custom-call(bf16[128,3584]{1,0:T(8,128)(2,1)} %tok_hbm.1, ...), custom_call_target="tpu_custom_call" | custom-call | tf_op jit(solution)/shard_map/dispatch/pallas_call | solution.py:284
  1.9 0.5 %collective-permute-start.2 = (bf16[24,3200]{1,0:T(8,128)(2,1)S(1)}, bf16[24,3200]{1,0:T(8,128)(2,1)S(1)}, u32[]{:S(2)}, u32[]{:S(2)}) collective-permute-start(bf16[24,3200]{1,0:T(8,128)(2,1)S(1)} %get-tuple-element.57), channel_id=1, source_target_pairs={{0,1},{1,0},{2,3},{3,2},{4,5},{5,4},{6,7},{7,6},{8,9},{9,8},{10,11... | collective-permute-start | bytes 460808 | tf_op jit(solution)/shard_map/ppermute | solution.py:242
  2.4 3.7 %collective-permute-start = (bf16[8,3200]{1,0:T(8,128)(2,1)S(1)}, bf16[8,3200]{1,0:T(8,128)(2,1)S(1)}, u32[]{:S(2)}, u32[]{:S(2)}) collective-permute-start(bf16[8,3200]{1,0:T(8,128)(2,1)S(1)} %get-tuple-element.46), channel_id=1, source_target_pairs={{0,8},{1,13},{2,10},{3,15},{4,12},{5,9},{6,14},{7,11},{8,0},{9,5},... | collective-permute-start | bytes 153608 | tf_op jit(solution)/shard_map/ppermute | solution.py:246
  6.1 1.1 %collective-permute-start.1 = (bf16[8,3200]{1,0:T(8,128)(2,1)S(1)}, bf16[8,3200]{1,0:T(8,128)(2,1)S(1)}, u32[]{:S(2)}, u32[]{:S(2)}) collective-permute-start(bf16[8,3200]{1,0:T(8,128)(2,1)S(1)} %get-tuple-element.47), channel_id=1, source_target_pairs={{0,13},{1,8},{2,15},{3,10},{4,9},{5,12},{6,11},{7,14},{8,5},{9,0},... | collective-permute-start | bytes 153608 | tf_op jit(solution)/shard_map/ppermute | solution.py:246
  7.2 1.6 %collective-permute-start.3 = (bf16[16,3200]{1,0:T(8,128)(2,1)S(1)}, bf16[16,3200]{1,0:T(8,128)(2,1)S(1)}, u32[]{:S(2)}, u32[]{:S(2)}) collective-permute-start(bf16[16,3200]{1,0:T(8,128)(2,1)S(1)} %get-tuple-element.58), channel_id=1, source_target_pairs={{0,2},{1,5},{2,0},{3,7},{4,6},{5,1},{6,4},{7,3},{8,10},{9,13},{10,... | collective-permute-start | bytes 307208 | tf_op jit(solution)/shard_map/ppermute | solution.py:246
  8.8 0.6 %collective-permute-start.4 = (bf16[16,3200]{1,0:T(8,128)(2,1)S(1)}, bf16[16,3200]{1,0:T(8,128)(2,1)S(1)}, u32[]{:S(2)}, u32[]{:S(2)}) collective-permute-start(bf16[16,3200]{1,0:T(8,128)(2,1)S(1)} %get-tuple-element.59), channel_id=1, source_target_pairs={{0,10},{1,15},{2,8},{3,13},{4,14},{5,11},{6,12},{7,9},{8,2},{9,7},... | collective-permute-start | bytes 307208 | tf_op jit(solution)/shard_map/ppermute | solution.py:246
  9.4 4.2 %stage.1 = (bf16[3584,512]{1,0:T(8,128)(2,1)S(1)}, bf16[3584,512]{1,0:T(8,128)(2,1)S(1)}, bf16[512,3584]{1,0:T(8,128)(2,1)S(1)}, bf16[128,128]{1,0:T(8,128)(2,1)S(1)}) custom-call(bf16[128,128]{1,0:T(8,128)(2,1)S(1)} %get-tuple-element.48.mix_ref, bf16[3584,512]{1,0:T(8,128)(2,1)} %bitcast.5, bf16[3584,512]{1,0:T(8,128)(2,1)} %bitcast.6, ...), custom_call_target="tpu_custom_call" | custom-call | flops 1 | bytes 1 | tf_op jit(solution)/shard_map/stage/pallas_call | solution.py:251
  13.7 0.0 collective-permute-done.refs_0_
  13.7 4.4 %collective-permute-start.5 = (bf16[8,3200]{1,0:T(8,128)(2,1)S(1)}, bf16[8,3200]{1,0:T(8,128)(2,1)S(1)}, u32[]{:S(2)}, u32[]{:S(2)}) collective-permute-start(bf16[8,3200]{1,0:T(8,128)(2,1)S(1)} %get-tuple-element.60), channel_id=1, source_target_pairs={{0,6},{1,7},{2,4},{3,5},{4,2},{5,3},{6,0},{7,1},{8,14},{9,15},{10,... | collective-permute-start | bytes 153608 | tf_op jit(solution)/shard_map/ppermute | solution.py:246
  18.1 2.1 %collective-permute-done.5.refs_4_ = bf16[8,3200]{1,0:T(8,128)(2,1)S(1)} collective-permute-done((bf16[8,3200]{1,0:T(8,128)(2,1)S(1)}, bf16[8,3200]{1,0:T(8,128)(2,1)S(1)}, u32[]{:S(2)}, u32[]{:S(2)}) %collective-permute-start.5) | collective-permute-done | bytes 51232 | tf_op jit(solution)/shard_map/ppermute | solution.py:246
  20.2 0.0 collective-permute-done.3.refs_2_
  20.2 0.1 collective-permute-start.6
  20.3 0.5 %collective-permute-start.7 = (bf16[24,3200]{1,0:T(8,128)(2,1)S(1)}, bf16[24,3200]{1,0:T(8,128)(2,1)S(1)}, u32[]{:S(2)}, u32[]{:S(2)}) collective-permute-start(bf16[24,3200]{1,0:T(8,128)(2,1)S(1)} %get-tuple-element.67.refs_1_), channel_id=1, source_target_pairs={{0,1},{1,0},{2,3},{3,2},{4,5},{5,4},{6,7},{7,6},{8,9},{9,8},{10,11... | collective-permute-start | bytes 460808 | tf_op jit(solution)/shard_map/ppermute | solution.py:242
  20.8 1.2 %collective-permute-done.7.refs_4_ = bf16[24,3200]{1,0:T(8,128)(2,1)S(1)} collective-permute-done((bf16[24,3200]{1,0:T(8,128)(2,1)S(1)}, bf16[24,3200]{1,0:T(8,128)(2,1)S(1)}, u32[]{:S(2)}, u32[]{:S(2)}) %collective-permute-start.7) | collective-permute-done | bytes 153632 | tf_op jit(solution)/shard_map/ppermute | solution.py:242
  22.0 1.8 %experts.1 = (bf16[32,3584]{1,0:T(8,128)(2,1)S(1)}, bf16[32,3584]{1,0:T(8,128)(2,1)S(1)}, bf16[32,3584]{1,0:T(8,128)(2,1)S(1)}, bf16[32,3584]{1,0:T(8,128)(2,1)S(1)}) custom-call(bf16[32,3200]{1,0:T(8,128)(2,1)S(1)} %get-tuple-element.66.refs_0_, bf16[24,3200]{1,0:T(8,128)(2,1)S(1)} %get-tuple-element.67.refs_1_, ...), custom_call_target="tpu_custom_call" | custom-call | flops 1 | bytes 1 | tf_op jit(solution)/shard_map/experts/pallas_call | solution.py:224
  23.7 0.3 collective-permute-start.8
  24.0 0.3 collective-permute-start.11
  24.3 1.0 %collective-permute-done.8.got_ref = bf16[32,3584]{1,0:T(8,128)(2,1)S(1)} collective-permute-done((bf16[32,3584]{1,0:T(8,128)(2,1)S(1)}, bf16[32,3584]{1,0:T(8,128)(2,1)S(1)}, u32[]{:S(2)}, u32[]{:S(2)}) %collective-permute-start.8) | collective-permute-done | bytes 229408 | tf_op jit(solution)/shard_map/ppermute | solution.py:242
  25.3 0.1 join.2
  25.4 1.3 %collective-permute-start.9 = (bf16[16,3200]{1,0:T(8,128)(2,1)S(1)}, bf16[16,3200]{1,0:T(8,128)(2,1)S(1)}, u32[]{:S(2)}, u32[]{:S(2)}) collective-permute-start(bf16[16,3200]{1,0:T(8,128)(2,1)S(1)} %get-tuple-element.75), channel_id=1, source_target_pairs={{0,8},{1,13},{2,10},{3,15},{4,12},{5,9},{6,14},{7,11},{8,0},{9,5},... | collective-permute-start | bytes 307208 | tf_op jit(solution)/shard_map/ppermute | solution.py:246
  26.7 1.6 %collective-permute-start.10 = (bf16[16,3200]{1,0:T(8,128)(2,1)S(1)}, bf16[16,3200]{1,0:T(8,128)(2,1)S(1)}, u32[]{:S(2)}, u32[]{:S(2)}) collective-permute-start(bf16[16,3200]{1,0:T(8,128)(2,1)S(1)} %get-tuple-element.76), channel_id=1, source_target_pairs={{0,2},{1,5},{2,0},{3,7},{4,6},{5,1},{6,4},{7,3},{8,10},{9,13},{10,... | collective-permute-start | bytes 307208 | tf_op jit(solution)/shard_map/ppermute | solution.py:246
  28.3 0.1 join.3
  28.4 1.6 %collective-permute-start.12 = (bf16[8,3200]{1,0:T(8,128)(2,1)S(1)}, bf16[8,3200]{1,0:T(8,128)(2,1)S(1)}, u32[]{:S(2)}, u32[]{:S(2)}) collective-permute-start(bf16[8,3200]{1,0:T(8,128)(2,1)S(1)} %get-tuple-element.79), channel_id=1, source_target_pairs={{0,10},{1,15},{2,8},{3,13},{4,14},{5,11},{6,12},{7,9},{8,2},{9,7},... | collective-permute-start | bytes 153608 | tf_op jit(solution)/shard_map/ppermute | solution.py:246
  30.0 0.4 %collective-permute-start.15 = (bf16[8,3200]{1,0:T(8,128)(2,1)S(1)}, bf16[8,3200]{1,0:T(8,128)(2,1)S(1)}, u32[]{:S(2)}, u32[]{:S(2)}) collective-permute-start(bf16[8,3200]{1,0:T(8,128)(2,1)S(1)} %get-tuple-element.82), channel_id=1, source_target_pairs={{0,11},{1,14},{2,9},{3,12},{4,15},{5,10},{6,13},{7,8},{8,3},{9,6},... | collective-permute-start | bytes 153608 | tf_op jit(solution)/shard_map/ppermute | solution.py:246
  30.5 2.7 %collective-permute-start.16 = (bf16[8,3200]{1,0:T(8,128)(2,1)S(1)}, bf16[8,3200]{1,0:T(8,128)(2,1)S(1)}, u32[]{:S(2)}, u32[]{:S(2)}) collective-permute-start(bf16[8,3200]{1,0:T(8,128)(2,1)S(1)} %get-tuple-element.83), channel_id=1, source_target_pairs={{0,6},{1,7},{2,4},{3,5},{4,2},{5,3},{6,0},{7,1},{8,14},{9,15},{10,... | collective-permute-start | bytes 153608 | tf_op jit(solution)/shard_map/ppermute | solution.py:246
  33.2 3.3 %collective-permute-done.9.refs_0_ = bf16[16,3200]{1,0:T(8,128)(2,1)S(1)} collective-permute-done((bf16[16,3200]{1,0:T(8,128)(2,1)S(1)}, bf16[16,3200]{1,0:T(8,128)(2,1)S(1)}, u32[]{:S(2)}, u32[]{:S(2)}) %collective-permute-start.9) | collective-permute-done | bytes 102432 | tf_op jit(solution)/shard_map/ppermute | solution.py:246
  36.5 0.1 collective-permute-start.13
  36.6 0.5 %collective-permute-start.14 = (bf16[8,3200]{1,0:T(8,128)(2,1)S(1)}, bf16[8,3200]{1,0:T(8,128)(2,1)S(1)}, u32[]{:S(2)}, u32[]{:S(2)}) collective-permute-start(bf16[8,3200]{1,0:T(8,128)(2,1)S(1)} %get-tuple-element.81), channel_id=1, source_target_pairs={{0,1},{1,0},{2,3},{3,2},{4,5},{5,4},{6,7},{7,6},{8,9},{9,8},{10,11... | collective-permute-start | bytes 153608 | tf_op jit(solution)/shard_map/ppermute | solution.py:242
  37.1 0.2 collective-permute-done.12.refs_2_
  37.4 0.5 %collective-permute-done.13.refs_3_ = bf16[8,3200]{1,0:T(8,128)(2,1)S(1)} collective-permute-done((bf16[8,3200]{1,0:T(8,128)(2,1)S(1)}, bf16[8,3200]{1,0:T(8,128)(2,1)S(1)}, u32[]{:S(2)}, u32[]{:S(2)}) %collective-permute-start.13) | collective-permute-done | bytes 51232 | tf_op jit(solution)/shard_map/ppermute | solution.py:242
  37.8 0.2 collective-permute-done.14.refs_4_
  38.0 1.2 %combine.1 = bf16[128,3584]{1,0:T(8,128)(2,1)} custom-call(bf16[128,128]{1,0:T(8,128)(2,1)S(1)} %get-tuple-element.53.mix_ref, bf16[16,3200]{1,0:T(8,128)(2,1)S(1)} %collective-permute-done.9.refs_0_, bf16[16,3200]{1,0:T(8,128)(2,1)S(1)} %collective-permute-done.10.refs_1_, bf16[8,3200]{1,0:T(8,128)(2,1)S(1)} %collective-permute-done.12.refs_2_, ...), custom_call_target="tpu_custom_call" | custom-call | tf_op jit(solution)/shard_map/combine/pallas_call | solution.py:270
  (11 shorter events, 0.1 us)
Async XLA Ops:
  1.9 5.3 %collective-permute-start.2 = (bf16[24,3200]{1,0:T(8,128)(2,1)S(1)}, bf16[24,3200]{1,0:T(8,128)(2,1)S(1)}, u32[]{:S(2)}, u32[]{:S(2)}) collective-permute-start(bf16[24,3200]{1,0:T(8,128)(2,1)S(1)} %get-tuple-element.57), channel_id=1, source_target_pairs={{0,1},{1,0},{2,3},{3,2},{4,5},{5,4},{6,7},{7,6},{8,9},{9,8},{10,11... | collective-permute-start | bytes 460808 | tf_op jit(solution)/shard_map/ppermute | solution.py:242
  2.4 11.3 %collective-permute-start = (bf16[8,3200]{1,0:T(8,128)(2,1)S(1)}, bf16[8,3200]{1,0:T(8,128)(2,1)S(1)}, u32[]{:S(2)}, u32[]{:S(2)}) collective-permute-start(bf16[8,3200]{1,0:T(8,128)(2,1)S(1)} %get-tuple-element.46), channel_id=1, source_target_pairs={{0,8},{1,13},{2,10},{3,15},{4,12},{5,9},{6,14},{7,11},{8,0},{9,5},... | collective-permute-start | bytes 153608 | tf_op jit(solution)/shard_map/ppermute | solution.py:246
  6.1 7.6 %collective-permute-start.1 = (bf16[8,3200]{1,0:T(8,128)(2,1)S(1)}, bf16[8,3200]{1,0:T(8,128)(2,1)S(1)}, u32[]{:S(2)}, u32[]{:S(2)}) collective-permute-start(bf16[8,3200]{1,0:T(8,128)(2,1)S(1)} %get-tuple-element.47), channel_id=1, source_target_pairs={{0,13},{1,8},{2,15},{3,10},{4,9},{5,12},{6,11},{7,14},{8,5},{9,0},... | collective-permute-start | bytes 153608 | tf_op jit(solution)/shard_map/ppermute | solution.py:246
  7.2 13.0 %collective-permute-start.3 = (bf16[16,3200]{1,0:T(8,128)(2,1)S(1)}, bf16[16,3200]{1,0:T(8,128)(2,1)S(1)}, u32[]{:S(2)}, u32[]{:S(2)}) collective-permute-start(bf16[16,3200]{1,0:T(8,128)(2,1)S(1)} %get-tuple-element.58), channel_id=1, source_target_pairs={{0,2},{1,5},{2,0},{3,7},{4,6},{5,1},{6,4},{7,3},{8,10},{9,13},{10,... | collective-permute-start | bytes 307208 | tf_op jit(solution)/shard_map/ppermute | solution.py:246
  8.8 11.4 %collective-permute-start.4 = (bf16[16,3200]{1,0:T(8,128)(2,1)S(1)}, bf16[16,3200]{1,0:T(8,128)(2,1)S(1)}, u32[]{:S(2)}, u32[]{:S(2)}) collective-permute-start(bf16[16,3200]{1,0:T(8,128)(2,1)S(1)} %get-tuple-element.59), channel_id=1, source_target_pairs={{0,10},{1,15},{2,8},{3,13},{4,14},{5,11},{6,12},{7,9},{8,2},{9,7},... | collective-permute-start | bytes 307208 | tf_op jit(solution)/shard_map/ppermute | solution.py:246
  13.7 6.5 %collective-permute-start.5 = (bf16[8,3200]{1,0:T(8,128)(2,1)S(1)}, bf16[8,3200]{1,0:T(8,128)(2,1)S(1)}, u32[]{:S(2)}, u32[]{:S(2)}) collective-permute-start(bf16[8,3200]{1,0:T(8,128)(2,1)S(1)} %get-tuple-element.60), channel_id=1, source_target_pairs={{0,6},{1,7},{2,4},{3,5},{4,2},{5,3},{6,0},{7,1},{8,14},{9,15},{10,... | collective-permute-start | bytes 153608 | tf_op jit(solution)/shard_map/ppermute | solution.py:246
  20.2 1.7 %collective-permute-start.6 = (bf16[32,3200]{1,0:T(8,128)(2,1)S(1)}, bf16[32,3200]{1,0:T(8,128)(2,1)S(1)}, u32[]{:S(2)}, u32[]{:S(2)}) collective-permute-start(bf16[32,3200]{1,0:T(8,128)(2,1)S(1)} %get-tuple-element.66.refs_0_), channel_id=1, source_target_pairs={{0,1},{1,0},{2,3},{3,2},{4,5},{5,4},{6,7},{7,6},{8,9},{9,8},{10,11... | collective-permute-start | bytes 614408 | tf_op jit(solution)/shard_map/ppermute | solution.py:242
  20.3 1.7 %collective-permute-start.7 = (bf16[24,3200]{1,0:T(8,128)(2,1)S(1)}, bf16[24,3200]{1,0:T(8,128)(2,1)S(1)}, u32[]{:S(2)}, u32[]{:S(2)}) collective-permute-start(bf16[24,3200]{1,0:T(8,128)(2,1)S(1)} %get-tuple-element.67.refs_1_), channel_id=1, source_target_pairs={{0,1},{1,0},{2,3},{3,2},{4,5},{5,4},{6,7},{7,6},{8,9},{9,8},{10,11... | collective-permute-start | bytes 460808 | tf_op jit(solution)/shard_map/ppermute | solution.py:242
  23.7 1.6 %collective-permute-start.8 = (bf16[32,3584]{1,0:T(8,128)(2,1)S(1)}, bf16[32,3584]{1,0:T(8,128)(2,1)S(1)}, u32[]{:S(2)}, u32[]{:S(2)}) collective-permute-start(bf16[32,3584]{1,0:T(8,128)(2,1)S(1)} %get-tuple-element.74), channel_id=1, source_target_pairs={{0,1},{1,0},{2,3},{3,2},{4,5},{5,4},{6,7},{7,6},{8,9},{9,8},{10,11... | collective-permute-start | bytes 688136 | tf_op jit(solution)/shard_map/ppermute | solution.py:242
  24.0 4.2 %collective-permute-start.11 = (bf16[32,3584]{1,0:T(8,128)(2,1)S(1)}, bf16[32,3584]{1,0:T(8,128)(2,1)S(1)}, u32[]{:S(2)}, u32[]{:S(2)}) collective-permute-start(bf16[32,3584]{1,0:T(8,128)(2,1)S(1)} %get-tuple-element.78), channel_id=1, source_target_pairs={{0,1},{1,0},{2,3},{3,2},{4,5},{5,4},{6,7},{7,6},{8,9},{9,8},{10,11... | collective-permute-start | bytes 688136 | tf_op jit(solution)/shard_map/ppermute | solution.py:242
  25.4 11.1 %collective-permute-start.9 = (bf16[16,3200]{1,0:T(8,128)(2,1)S(1)}, bf16[16,3200]{1,0:T(8,128)(2,1)S(1)}, u32[]{:S(2)}, u32[]{:S(2)}) collective-permute-start(bf16[16,3200]{1,0:T(8,128)(2,1)S(1)} %get-tuple-element.75), channel_id=1, source_target_pairs={{0,8},{1,13},{2,10},{3,15},{4,12},{5,9},{6,14},{7,11},{8,0},{9,5},... | collective-permute-start | bytes 307208 | tf_op jit(solution)/shard_map/ppermute | solution.py:246
  26.7 9.8 %collective-permute-start.10 = (bf16[16,3200]{1,0:T(8,128)(2,1)S(1)}, bf16[16,3200]{1,0:T(8,128)(2,1)S(1)}, u32[]{:S(2)}, u32[]{:S(2)}) collective-permute-start(bf16[16,3200]{1,0:T(8,128)(2,1)S(1)} %get-tuple-element.76), channel_id=1, source_target_pairs={{0,2},{1,5},{2,0},{3,7},{4,6},{5,1},{6,4},{7,3},{8,10},{9,13},{10,... | collective-permute-start | bytes 307208 | tf_op jit(solution)/shard_map/ppermute | solution.py:246
  28.4 9.0 %collective-permute-start.12 = (bf16[8,3200]{1,0:T(8,128)(2,1)S(1)}, bf16[8,3200]{1,0:T(8,128)(2,1)S(1)}, u32[]{:S(2)}, u32[]{:S(2)}) collective-permute-start(bf16[8,3200]{1,0:T(8,128)(2,1)S(1)} %get-tuple-element.79), channel_id=1, source_target_pairs={{0,10},{1,15},{2,8},{3,13},{4,14},{5,11},{6,12},{7,9},{8,2},{9,7},... | collective-permute-start | bytes 153608 | tf_op jit(solution)/shard_map/ppermute | solution.py:246
  30.0 7.3 %collective-permute-start.15 = (bf16[8,3200]{1,0:T(8,128)(2,1)S(1)}, bf16[8,3200]{1,0:T(8,128)(2,1)S(1)}, u32[]{:S(2)}, u32[]{:S(2)}) collective-permute-start(bf16[8,3200]{1,0:T(8,128)(2,1)S(1)} %get-tuple-element.82), channel_id=1, source_target_pairs={{0,11},{1,14},{2,9},{3,12},{4,15},{5,10},{6,13},{7,8},{8,3},{9,6},... | collective-permute-start | bytes 153608 | tf_op jit(solution)/shard_map/ppermute | solution.py:246
  30.5 6.9 %collective-permute-start.16 = (bf16[8,3200]{1,0:T(8,128)(2,1)S(1)}, bf16[8,3200]{1,0:T(8,128)(2,1)S(1)}, u32[]{:S(2)}, u32[]{:S(2)}) collective-permute-start(bf16[8,3200]{1,0:T(8,128)(2,1)S(1)} %get-tuple-element.83), channel_id=1, source_target_pairs={{0,6},{1,7},{2,4},{3,5},{4,2},{5,3},{6,0},{7,1},{8,14},{9,15},{10,... | collective-permute-start | bytes 153608 | tf_op jit(solution)/shard_map/ppermute | solution.py:246
  36.5 1.3 %collective-permute-start.13 = (bf16[8,3200]{1,0:T(8,128)(2,1)S(1)}, bf16[8,3200]{1,0:T(8,128)(2,1)S(1)}, u32[]{:S(2)}, u32[]{:S(2)}) collective-permute-start(bf16[8,3200]{1,0:T(8,128)(2,1)S(1)} %get-tuple-element.80), channel_id=1, source_target_pairs={{0,1},{1,0},{2,3},{3,2},{4,5},{5,4},{6,7},{7,6},{8,9},{9,8},{10,11... | collective-permute-start | bytes 153608 | tf_op jit(solution)/shard_map/ppermute | solution.py:242
  36.6 1.4 %collective-permute-start.14 = (bf16[8,3200]{1,0:T(8,128)(2,1)S(1)}, bf16[8,3200]{1,0:T(8,128)(2,1)S(1)}, u32[]{:S(2)}, u32[]{:S(2)}) collective-permute-start(bf16[8,3200]{1,0:T(8,128)(2,1)S(1)} %get-tuple-element.81), channel_id=1, source_target_pairs={{0,1},{1,0},{2,3},{3,2},{4,5},{5,4},{6,7},{7,6},{8,9},{9,8},{10,11... | collective-permute-start | bytes 153608 | tf_op jit(solution)/shard_map/ppermute | solution.py:242

commit v22 on v21

--- a/solution.py
+++ b/solution.py
@@ -135,7 +135,7 @@
     if len(outs) == 1:
         store(outs, blocks)
     else:
-        order = [0, 3, 1, 2, 4, 5, 7, 6, 7]
+        order = [0, 1, 3, 4, 7, 2, 5, 6, 7]
         blocks = [blocks[i * SLOTS : (i + 1) * SLOTS] for i in order]
         store(outs, jnp.concatenate(blocks, axis=0))
 
@@ -280,7 +280,7 @@
             name="combine",
         )(mix, *arrays)
 
-    first = packed(1, 1, 2, 3, 1, 1) if few else packed(flight)
+    first = packed(2, 3, 1, 1, 1, 1) if few else packed(flight)
     mix, *outgoing = pl.pallas_call(
         functools.partial(dispatch_kernel, flight),
         out_shape=(jax.ShapeDtypeStruct((2 * flight * SLOTS, count), jnp.bfloat16),) + first,
@@ -316,14 +316,16 @@
 
     one, two, three = zip(*CARRIED)
     four = (SHARED, SHARED)
-    first, first_across, kept, given, shared, own = outgoing
-    second, third, other_own = local(merge_kernel, packed(2, 2, 1), "merge", kept, swap(given))
-    first, first_across = travel(first, one), travel(first_across, one[::-1], 1)
-    shared, first, first_across, gate, up, down, mix = lax.optimization_barrier(
-        (shared, first, first_across, *stage(mix))
-    )
-    second, third, shared = travel(second, two), travel(third, three), travel(shared, four)
-    arrived = lax.optimization_barrier((first, first_across, second, third, shared))
+    kept, given, third, third_across, shared, own = outgoing
+    first, second, other_own = local(merge_kernel, packed(2, 2, 1), "merge", kept, swap(given))
+    arrived = (
+        travel(first, one),
+        travel(second, two),
+        travel(third, three),
+        travel(third_across, three[::-1], 1),
+        travel(shared, four),
+    )
+    *arrived, gate, up, down, mix = lax.optimization_barrier((*arrived, *stage(mix)))
     kernel = functools.partial(gather_kernel, 2)
     rows = local(kernel, packed(4, 3), "gather", *arrived)
     mine_one, mine_two, theirs_one, theirs_two = experts(

time: 39.3 us -> 38.5 us (0.980)
  starting transfers between devices: 21.3 us -> 19.3 us
  waiting for transfers between devices: 8.45 us -> 9.65 us
    ppermute x10, starting transfers between devices: 19 us -> 17 us  [travel(): return lax.ppermute(rows, 'exp', pairs)]
    ppermute x10, waiting for transfers between devices: 5.68 us -> 6.49 us  [travel(): return lax.ppermute(rows, 'exp', pairs)]
  transfers between devices with their start and end apart: 17 -> 17, of which waited for: 7 -> 8; matrix products, arithmetic and copies ran while one was open for 0% -> 0% of each run, Pallas kernels for 11% -> 12%
where the time goes in v22:
time: 38.5 us; the launch traced here: 38.3 us
  starting transfers between devices  19.3 us (50%)
  waiting for transfers between devices  9.65 us (25%)
  Pallas kernels  9.34 us (24%)
    ppermute x10, starting transfers between devices, travel(): return lax.ppermute(rows, 'exp', pairs)  17 us
    ppermute x10, waiting for transfers between devices, travel(): return lax.ppermute(rows, 'exp', pairs)  6.49 us
    pallas_call x1, Pallas kernels, stage(): pl.pallas_call(stage_kernel, out_shape=(*outs, jax.ShapeDtypeStruct(mix.s...  4.25 us
    ppermute x7, waiting for transfers between devices, swap(): return lax.ppermute(rows, 'exp', [(n, n ^ 1) for n in range(owners)])  3.17 us
    ppermute x7, starting transfers between devices, swap(): return lax.ppermute(rows, 'exp', [(n, n ^ 1) for n in range(owners)])  2.24 us
    pallas_call x6, Pallas kernels, local(): pl.pallas_call(kernel, out_shape=outs, in_specs=[VMEM] * len(args), out_s...  2.01 us
    pallas_call x1, Pallas kernels, per_device(): pl.pallas_call(functools.partial(dispatch_kernel, flight), out_shape=(jax...  1.91 us
    pallas_call x1, Pallas kernels, combine(): pl.pallas_call(functools.partial(combine_kernel, paired), out_shape=jax.S...  1.17 us
  transfers between devices with their start and end apart: 17, of which 8 were waited for; matrix products, arithmetic and copies ran while one was open for 0% of the time, Pallas kernels for 12%

profile of v22, /device:TPU:0, one launch (start us, length us, event | category | flops | bytes accessed | tf_op | source)
XLA Modules:
  0.0 38.3 jit_solution(14200270494613122467)
XLA Ops:
  0.0 1.9 %dispatch.1 = (bf16[128,128]{1,0:T(8,128)(2,1)S(1)}, bf16[16,3200]{1,0:T(8,128)(2,1)S(1)}, bf16[24,3200]{1,0:T(8,128)(2,1)S(1)}, bf16[8,3200]{1,0:T(8,128)(2,1)S...) custom-call(bf16[128,3584]{1,0:T(8,128)(2,1)} %tok_hbm.1, ...), custom_call_target="tpu_custom_call" | custom-call | tf_op jit(solution)/shard_map/dispatch/pallas_call | solution.py:284
  1.9 0.5 %collective-permute-start = (bf16[24,3200]{1,0:T(8,128)(2,1)S(1)}, bf16[24,3200]{1,0:T(8,128)(2,1)S(1)}, u32[]{:S(2)}, u32[]{:S(2)}) collective-permute-start(bf16[24,3200]{1,0:T(8,128)(2,1)S(1)} %get-tuple-element.43), channel_id=1, source_target_pairs={{0,1},{1,0},{2,3},{3,2},{4,5},{5,4},{6,7},{7,6},{8,9},{9,8},{10,11... | collective-permute-start | bytes 460808 | tf_op jit(solution)/shard_map/ppermute | solution.py:242
  2.4 1.0 %collective-permute-done.got_ref = bf16[24,3200]{1,0:T(8,128)(2,1)S(1)} collective-permute-done((bf16[24,3200]{1,0:T(8,128)(2,1)S(1)}, bf16[24,3200]{1,0:T(8,128)(2,1)S(1)}, u32[]{:S(2)}, u32[]{:S(2)}) %collective-permute-start) | collective-permute-done | bytes 153632 | tf_op jit(solution)/shard_map/ppermute | solution.py:242
  3.5 4.0 %collective-permute-start.1 = (bf16[16,3200]{1,0:T(8,128)(2,1)S(1)}, bf16[16,3200]{1,0:T(8,128)(2,1)S(1)}, u32[]{:S(2)}, u32[]{:S(2)}) collective-permute-start(bf16[16,3200]{1,0:T(8,128)(2,1)S(1)} %get-tuple-element.44), channel_id=1, source_target_pairs={{0,8},{1,13},{2,10},{3,15},{4,12},{5,9},{6,14},{7,11},{8,0},{9,5},... | collective-permute-start | bytes 307208 | tf_op jit(solution)/shard_map/ppermute | solution.py:246
  7.5 1.5 %collective-permute-start.2 = (bf16[16,3200]{1,0:T(8,128)(2,1)S(1)}, bf16[16,3200]{1,0:T(8,128)(2,1)S(1)}, u32[]{:S(2)}, u32[]{:S(2)}) collective-permute-start(bf16[16,3200]{1,0:T(8,128)(2,1)S(1)} %get-tuple-element.45), channel_id=1, source_target_pairs={{0,2},{1,5},{2,0},{3,7},{4,6},{5,1},{6,4},{7,3},{8,10},{9,13},{10,... | collective-permute-start | bytes 307208 | tf_op jit(solution)/shard_map/ppermute | solution.py:246
  9.0 0.0 collective-permute-start.3
  9.0 3.4 %collective-permute-start.4 = (bf16[8,3200]{1,0:T(8,128)(2,1)S(1)}, bf16[8,3200]{1,0:T(8,128)(2,1)S(1)}, u32[]{:S(2)}, u32[]{:S(2)}) collective-permute-start(bf16[8,3200]{1,0:T(8,128)(2,1)S(1)} %get-tuple-element.47), channel_id=1, source_target_pairs={{0,15},{1,10},{2,13},{3,8},{4,11},{5,14},{6,9},{7,12},{8,7},{9,2},... | collective-permute-start | bytes 153608 | tf_op jit(solution)/shard_map/ppermute | solution.py:246
  12.4 0.9 %collective-permute-start.5 = (bf16[8,3200]{1,0:T(8,128)(2,1)S(1)}, bf16[8,3200]{1,0:T(8,128)(2,1)S(1)}, u32[]{:S(2)}, u32[]{:S(2)}) collective-permute-start(bf16[8,3200]{1,0:T(8,128)(2,1)S(1)} %get-tuple-element.48), channel_id=1, source_target_pairs={{0,6},{1,7},{2,4},{3,5},{4,2},{5,3},{6,0},{7,1},{8,14},{9,15},{10,... | collective-permute-start | bytes 153608 | tf_op jit(solution)/shard_map/ppermute | solution.py:246
  13.3 4.2 %stage.1 = (bf16[3584,512]{1,0:T(8,128)(2,1)S(1)}, bf16[3584,512]{1,0:T(8,128)(2,1)S(1)}, bf16[512,3584]{1,0:T(8,128)(2,1)S(1)}, bf16[128,128]{1,0:T(8,128)(2,1)S(1)}) custom-call(bf16[128,128]{1,0:T(8,128)(2,1)S(1)} %get-tuple-element.49.mix_ref, bf16[3584,512]{1,0:T(8,128)(2,1)} %bitcast.5, bf16[3584,512]{1,0:T(8,128)(2,1)} %bitcast.6, ...), custom_call_target="tpu_custom_call" | custom-call | flops 1 | bytes 1 | tf_op jit(solution)/shard_map/stage/pallas_call | solution.py:251
  17.6 0.4 collective-permute-done.3.refs_2_
  17.9 1.0 %collective-permute-done.5.refs_4_ = bf16[8,3200]{1,0:T(8,128)(2,1)S(1)} collective-permute-done((bf16[8,3200]{1,0:T(8,128)(2,1)S(1)}, bf16[8,3200]{1,0:T(8,128)(2,1)S(1)}, u32[]{:S(2)}, u32[]{:S(2)}) %collective-permute-start.5) | collective-permute-done | bytes 51232 | tf_op jit(solution)/shard_map/ppermute | solution.py:246
  19.0 0.1 collective-permute-start.6
  19.1 0.4 %collective-permute-start.7 = (bf16[24,3200]{1,0:T(8,128)(2,1)S(1)}, bf16[24,3200]{1,0:T(8,128)(2,1)S(1)}, u32[]{:S(2)}, u32[]{:S(2)}) collective-permute-start(bf16[24,3200]{1,0:T(8,128)(2,1)S(1)} %get-tuple-element.61.refs_1_), channel_id=1, source_target_pairs={{0,1},{1,0},{2,3},{3,2},{4,5},{5,4},{6,7},{7,6},{8,9},{9,8},{10,11... | collective-permute-start | bytes 460808 | tf_op jit(solution)/shard_map/ppermute | solution.py:242
  19.5 1.2 %collective-permute-done.7.refs_4_ = bf16[24,3200]{1,0:T(8,128)(2,1)S(1)} collective-permute-done((bf16[24,3200]{1,0:T(8,128)(2,1)S(1)}, bf16[24,3200]{1,0:T(8,128)(2,1)S(1)}, u32[]{:S(2)}, u32[]{:S(2)}) %collective-permute-start.7) | collective-permute-done | bytes 153632 | tf_op jit(solution)/shard_map/ppermute | solution.py:242
  20.7 0.0 collective-permute-done.6.refs_3_
  20.7 1.8 %experts.1 = (bf16[32,3584]{1,0:T(8,128)(2,1)S(1)}, bf16[32,3584]{1,0:T(8,128)(2,1)S(1)}, bf16[32,3584]{1,0:T(8,128)(2,1)S(1)}, bf16[32,3584]{1,0:T(8,128)(2,1)S(1)}) custom-call(bf16[32,3200]{1,0:T(8,128)(2,1)S(1)} %get-tuple-element.60.refs_0_, bf16[24,3200]{1,0:T(8,128)(2,1)S(1)} %get-tuple-element.61.refs_1_, ...), custom_call_target="tpu_custom_call" | custom-call | flops 1 | bytes 1 | tf_op jit(solution)/shard_map/experts/pallas_call | solution.py:224
  22.5 0.3 collective-permute-start.8
  22.8 0.3 collective-permute-start.11
  23.1 1.0 %collective-permute-done.8.got_ref = bf16[32,3584]{1,0:T(8,128)(2,1)S(1)} collective-permute-done((bf16[32,3584]{1,0:T(8,128)(2,1)S(1)}, bf16[32,3584]{1,0:T(8,128)(2,1)S(1)}, u32[]{:S(2)}, u32[]{:S(2)}) %collective-permute-start.8) | collective-permute-done | bytes 229408 | tf_op jit(solution)/shard_map/ppermute | solution.py:242
  24.0 0.1 join.2
  24.1 1.3 %collective-permute-start.9 = (bf16[16,3200]{1,0:T(8,128)(2,1)S(1)}, bf16[16,3200]{1,0:T(8,128)(2,1)S(1)}, u32[]{:S(2)}, u32[]{:S(2)}) collective-permute-start(bf16[16,3200]{1,0:T(8,128)(2,1)S(1)} %get-tuple-element.69), channel_id=1, source_target_pairs={{0,8},{1,13},{2,10},{3,15},{4,12},{5,9},{6,14},{7,11},{8,0},{9,5},... | collective-permute-start | bytes 307208 | tf_op jit(solution)/shard_map/ppermute | solution.py:246
  25.4 0.5 %collective-permute-start.10 = (bf16[16,3200]{1,0:T(8,128)(2,1)S(1)}, bf16[16,3200]{1,0:T(8,128)(2,1)S(1)}, u32[]{:S(2)}, u32[]{:S(2)}) collective-permute-start(bf16[16,3200]{1,0:T(8,128)(2,1)S(1)} %get-tuple-element.70), channel_id=1, source_target_pairs={{0,2},{1,5},{2,0},{3,7},{4,6},{5,1},{6,4},{7,3},{8,10},{9,13},{10,... | collective-permute-start | bytes 307208 | tf_op jit(solution)/shard_map/ppermute | solution.py:246
  25.9 0.1 join.3
  26.0 2.8 %collective-permute-start.12 = (bf16[8,3200]{1,0:T(8,128)(2,1)S(1)}, bf16[8,3200]{1,0:T(8,128)(2,1)S(1)}, u32[]{:S(2)}, u32[]{:S(2)}) collective-permute-start(bf16[8,3200]{1,0:T(8,128)(2,1)S(1)} %get-tuple-element.73), channel_id=1, source_target_pairs={{0,10},{1,15},{2,8},{3,13},{4,14},{5,11},{6,12},{7,9},{8,2},{9,7},... | collective-permute-start | bytes 153608 | tf_op jit(solution)/shard_map/ppermute | solution.py:246
  28.8 1.2 %collective-permute-start.15 = (bf16[8,3200]{1,0:T(8,128)(2,1)S(1)}, bf16[8,3200]{1,0:T(8,128)(2,1)S(1)}, u32[]{:S(2)}, u32[]{:S(2)}) collective-permute-start(bf16[8,3200]{1,0:T(8,128)(2,1)S(1)} %get-tuple-element.76), channel_id=1, source_target_pairs={{0,11},{1,14},{2,9},{3,12},{4,15},{5,10},{6,13},{7,8},{8,3},{9,6},... | collective-permute-start | bytes 153608 | tf_op jit(solution)/shard_map/ppermute | solution.py:246
  30.0 1.4 %collective-permute-start.16 = (bf16[8,3200]{1,0:T(8,128)(2,1)S(1)}, bf16[8,3200]{1,0:T(8,128)(2,1)S(1)}, u32[]{:S(2)}, u32[]{:S(2)}) collective-permute-start(bf16[8,3200]{1,0:T(8,128)(2,1)S(1)} %get-tuple-element.77), channel_id=1, source_target_pairs={{0,6},{1,7},{2,4},{3,5},{4,2},{5,3},{6,0},{7,1},{8,14},{9,15},{10,... | collective-permute-start | bytes 153608 | tf_op jit(solution)/shard_map/ppermute | solution.py:246
  31.4 3.6 %collective-permute-done.9.refs_0_ = bf16[16,3200]{1,0:T(8,128)(2,1)S(1)} collective-permute-done((bf16[16,3200]{1,0:T(8,128)(2,1)S(1)}, bf16[16,3200]{1,0:T(8,128)(2,1)S(1)}, u32[]{:S(2)}, u32[]{:S(2)}) %collective-permute-start.9) | collective-permute-done | bytes 102432 | tf_op jit(solution)/shard_map/ppermute | solution.py:246
  35.0 0.1 collective-permute-start.13
  35.1 0.5 %collective-permute-start.14 = (bf16[8,3200]{1,0:T(8,128)(2,1)S(1)}, bf16[8,3200]{1,0:T(8,128)(2,1)S(1)}, u32[]{:S(2)}, u32[]{:S(2)}) collective-permute-start(bf16[8,3200]{1,0:T(8,128)(2,1)S(1)} %get-tuple-element.75), channel_id=1, source_target_pairs={{0,1},{1,0},{2,3},{3,2},{4,5},{5,4},{6,7},{7,6},{8,9},{9,8},{10,11... | collective-permute-start | bytes 153608 | tf_op jit(solution)/shard_map/ppermute | solution.py:242
  35.6 0.4 collective-permute-done.12.refs_2_
  36.0 1.2 %collective-permute-done.16.refs_6_ = bf16[8,3200]{1,0:T(8,128)(2,1)S(1)} collective-permute-done((bf16[8,3200]{1,0:T(8,128)(2,1)S(1)}, bf16[8,3200]{1,0:T(8,128)(2,1)S(1)}, u32[]{:S(2)}, u32[]{:S(2)}) %collective-permute-start.16) | collective-permute-done | bytes 51232 | tf_op jit(solution)/shard_map/ppermute | solution.py:246
  37.1 1.2 %combine.1 = bf16[128,3584]{1,0:T(8,128)(2,1)} custom-call(bf16[128,128]{1,0:T(8,128)(2,1)S(1)} %get-tuple-element.54.mix_ref, bf16[16,3200]{1,0:T(8,128)(2,1)S(1)} %collective-permute-done.9.refs_0_, bf16[16,3200]{1,0:T(8,128)(2,1)S(1)} %collective-permute-done.10.refs_1_, bf16[8,3200]{1,0:T(8,128)(2,1)S(1)} %collective-permute-done.12.refs_2_, ...), custom_call_target="tpu_custom_call" | custom-call | tf_op jit(solution)/shard_map/combine/pallas_call | solution.py:270
  (11 shorter events, 0.1 us)
Async XLA Ops:
  1.9 1.5 %collective-permute-start = (bf16[24,3200]{1,0:T(8,128)(2,1)S(1)}, bf16[24,3200]{1,0:T(8,128)(2,1)S(1)}, u32[]{:S(2)}, u32[]{:S(2)}) collective-permute-start(bf16[24,3200]{1,0:T(8,128)(2,1)S(1)} %get-tuple-element.43), channel_id=1, source_target_pairs={{0,1},{1,0},{2,3},{3,2},{4,5},{5,4},{6,7},{7,6},{8,9},{9,8},{10,11... | collective-permute-start | bytes 460808 | tf_op jit(solution)/shard_map/ppermute | solution.py:242
  3.5 15.5 %collective-permute-start.1 = (bf16[16,3200]{1,0:T(8,128)(2,1)S(1)}, bf16[16,3200]{1,0:T(8,128)(2,1)S(1)}, u32[]{:S(2)}, u32[]{:S(2)}) collective-permute-start(bf16[16,3200]{1,0:T(8,128)(2,1)S(1)} %get-tuple-element.44), channel_id=1, source_target_pairs={{0,8},{1,13},{2,10},{3,15},{4,12},{5,9},{6,14},{7,11},{8,0},{9,5},... | collective-permute-start | bytes 307208 | tf_op jit(solution)/shard_map/ppermute | solution.py:246
  7.5 11.5 %collective-permute-start.2 = (bf16[16,3200]{1,0:T(8,128)(2,1)S(1)}, bf16[16,3200]{1,0:T(8,128)(2,1)S(1)}, u32[]{:S(2)}, u32[]{:S(2)}) collective-permute-start(bf16[16,3200]{1,0:T(8,128)(2,1)S(1)} %get-tuple-element.45), channel_id=1, source_target_pairs={{0,2},{1,5},{2,0},{3,7},{4,6},{5,1},{6,4},{7,3},{8,10},{9,13},{10,... | collective-permute-start | bytes 307208 | tf_op jit(solution)/shard_map/ppermute | solution.py:246
  9.0 8.9 %collective-permute-start.3 = (bf16[8,3200]{1,0:T(8,128)(2,1)S(1)}, bf16[8,3200]{1,0:T(8,128)(2,1)S(1)}, u32[]{:S(2)}, u32[]{:S(2)}) collective-permute-start(bf16[8,3200]{1,0:T(8,128)(2,1)S(1)} %get-tuple-element.46), channel_id=1, source_target_pairs={{0,10},{1,15},{2,8},{3,13},{4,14},{5,11},{6,12},{7,9},{8,2},{9,7},... | collective-permute-start | bytes 153608 | tf_op jit(solution)/shard_map/ppermute | solution.py:246
  9.0 8.9 %collective-permute-start.4 = (bf16[8,3200]{1,0:T(8,128)(2,1)S(1)}, bf16[8,3200]{1,0:T(8,128)(2,1)S(1)}, u32[]{:S(2)}, u32[]{:S(2)}) collective-permute-start(bf16[8,3200]{1,0:T(8,128)(2,1)S(1)} %get-tuple-element.47), channel_id=1, source_target_pairs={{0,15},{1,10},{2,13},{3,8},{4,11},{5,14},{6,9},{7,12},{8,7},{9,2},... | collective-permute-start | bytes 153608 | tf_op jit(solution)/shard_map/ppermute | solution.py:246
  12.4 6.5 %collective-permute-start.5 = (bf16[8,3200]{1,0:T(8,128)(2,1)S(1)}, bf16[8,3200]{1,0:T(8,128)(2,1)S(1)}, u32[]{:S(2)}, u32[]{:S(2)}) collective-permute-start(bf16[8,3200]{1,0:T(8,128)(2,1)S(1)} %get-tuple-element.48), channel_id=1, source_target_pairs={{0,6},{1,7},{2,4},{3,5},{4,2},{5,3},{6,0},{7,1},{8,14},{9,15},{10,... | collective-permute-start | bytes 153608 | tf_op jit(solution)/shard_map/ppermute | solution.py:246
  19.0 1.7 %collective-permute-start.6 = (bf16[32,3200]{1,0:T(8,128)(2,1)S(1)}, bf16[32,3200]{1,0:T(8,128)(2,1)S(1)}, u32[]{:S(2)}, u32[]{:S(2)}) collective-permute-start(bf16[32,3200]{1,0:T(8,128)(2,1)S(1)} %get-tuple-element.60.refs_0_), channel_id=1, source_target_pairs={{0,1},{1,0},{2,3},{3,2},{4,5},{5,4},{6,7},{7,6},{8,9},{9,8},{10,11... | collective-permute-start | bytes 614408 | tf_op jit(solution)/shard_map/ppermute | solution.py:242
  19.1 1.6 %collective-permute-start.7 = (bf16[24,3200]{1,0:T(8,128)(2,1)S(1)}, bf16[24,3200]{1,0:T(8,128)(2,1)S(1)}, u32[]{:S(2)}, u32[]{:S(2)}) collective-permute-start(bf16[24,3200]{1,0:T(8,128)(2,1)S(1)} %get-tuple-element.61.refs_1_), channel_id=1, source_target_pairs={{0,1},{1,0},{2,3},{3,2},{4,5},{5,4},{6,7},{7,6},{8,9},{9,8},{10,11... | collective-permute-start | bytes 460808 | tf_op jit(solution)/shard_map/ppermute | solution.py:242
  22.5 1.6 %collective-permute-start.8 = (bf16[32,3584]{1,0:T(8,128)(2,1)S(1)}, bf16[32,3584]{1,0:T(8,128)(2,1)S(1)}, u32[]{:S(2)}, u32[]{:S(2)}) collective-permute-start(bf16[32,3584]{1,0:T(8,128)(2,1)S(1)} %get-tuple-element.68), channel_id=1, source_target_pairs={{0,1},{1,0},{2,3},{3,2},{4,5},{5,4},{6,7},{7,6},{8,9},{9,8},{10,11... | collective-permute-start | bytes 688136 | tf_op jit(solution)/shard_map/ppermute | solution.py:242
  22.8 3.1 %collective-permute-start.11 = (bf16[32,3584]{1,0:T(8,128)(2,1)S(1)}, bf16[32,3584]{1,0:T(8,128)(2,1)S(1)}, u32[]{:S(2)}, u32[]{:S(2)}) collective-permute-start(bf16[32,3584]{1,0:T(8,128)(2,1)S(1)} %get-tuple-element.72), channel_id=1, source_target_pairs={{0,1},{1,0},{2,3},{3,2},{4,5},{5,4},{6,7},{7,6},{8,9},{9,8},{10,11... | collective-permute-start | bytes 688136 | tf_op jit(solution)/shard_map/ppermute | solution.py:242
  24.1 10.9 %collective-permute-start.9 = (bf16[16,3200]{1,0:T(8,128)(2,1)S(1)}, bf16[16,3200]{1,0:T(8,128)(2,1)S(1)}, u32[]{:S(2)}, u32[]{:S(2)}) collective-permute-start(bf16[16,3200]{1,0:T(8,128)(2,1)S(1)} %get-tuple-element.69), channel_id=1, source_target_pairs={{0,8},{1,13},{2,10},{3,15},{4,12},{5,9},{6,14},{7,11},{8,0},{9,5},... | collective-permute-start | bytes 307208 | tf_op jit(solution)/shard_map/ppermute | solution.py:246
  25.4 9.6 %collective-permute-start.10 = (bf16[16,3200]{1,0:T(8,128)(2,1)S(1)}, bf16[16,3200]{1,0:T(8,128)(2,1)S(1)}, u32[]{:S(2)}, u32[]{:S(2)}) collective-permute-start(bf16[16,3200]{1,0:T(8,128)(2,1)S(1)} %get-tuple-element.70), channel_id=1, source_target_pairs={{0,2},{1,5},{2,0},{3,7},{4,6},{5,1},{6,4},{7,3},{8,10},{9,13},{10,... | collective-permute-start | bytes 307208 | tf_op jit(solution)/shard_map/ppermute | solution.py:246
  26.0 9.9 %collective-permute-start.12 = (bf16[8,3200]{1,0:T(8,128)(2,1)S(1)}, bf16[8,3200]{1,0:T(8,128)(2,1)S(1)}, u32[]{:S(2)}, u32[]{:S(2)}) collective-permute-start(bf16[8,3200]{1,0:T(8,128)(2,1)S(1)} %get-tuple-element.73), channel_id=1, source_target_pairs={{0,10},{1,15},{2,8},{3,13},{4,14},{5,11},{6,12},{7,9},{8,2},{9,7},... | collective-permute-start | bytes 153608 | tf_op jit(solution)/shard_map/ppermute | solution.py:246
  28.8 7.2 %collective-permute-start.15 = (bf16[8,3200]{1,0:T(8,128)(2,1)S(1)}, bf16[8,3200]{1,0:T(8,128)(2,1)S(1)}, u32[]{:S(2)}, u32[]{:S(2)}) collective-permute-start(bf16[8,3200]{1,0:T(8,128)(2,1)S(1)} %get-tuple-element.76), channel_id=1, source_target_pairs={{0,11},{1,14},{2,9},{3,12},{4,15},{5,10},{6,13},{7,8},{8,3},{9,6},... | collective-permute-start | bytes 153608 | tf_op jit(solution)/shard_map/ppermute | solution.py:246
  30.0 7.1 %collective-permute-start.16 = (bf16[8,3200]{1,0:T(8,128)(2,1)S(1)}, bf16[8,3200]{1,0:T(8,128)(2,1)S(1)}, u32[]{:S(2)}, u32[]{:S(2)}) collective-permute-start(bf16[8,3200]{1,0:T(8,128)(2,1)S(1)} %get-tuple-element.77), channel_id=1, source_target_pairs={{0,6},{1,7},{2,4},{3,5},{4,2},{5,3},{6,0},{7,1},{8,14},{9,15},{10,... | collective-permute-start | bytes 153608 | tf_op jit(solution)/shard_map/ppermute | solution.py:246
  35.0 2.1 %collective-permute-start.13 = (bf16[8,3200]{1,0:T(8,128)(2,1)S(1)}, bf16[8,3200]{1,0:T(8,128)(2,1)S(1)}, u32[]{:S(2)}, u32[]{:S(2)}) collective-permute-start(bf16[8,3200]{1,0:T(8,128)(2,1)S(1)} %get-tuple-element.74), channel_id=1, source_target_pairs={{0,1},{1,0},{2,3},{3,2},{4,5},{5,4},{6,7},{7,6},{8,9},{9,8},{10,11... | collective-permute-start | bytes 153608 | tf_op jit(solution)/shard_map/ppermute | solution.py:242
  35.1 2.0 %collective-permute-start.14 = (bf16[8,3200]{1,0:T(8,128)(2,1)S(1)}, bf16[8,3200]{1,0:T(8,128)(2,1)S(1)}, u32[]{:S(2)}, u32[]{:S(2)}) collective-permute-start(bf16[8,3200]{1,0:T(8,128)(2,1)S(1)} %get-tuple-element.75), channel_id=1, source_target_pairs={{0,1},{1,0},{2,3},{3,2},{4,5},{5,4},{6,7},{7,6},{8,9},{9,8},{10,11... | collective-permute-start | bytes 153608 | tf_op jit(solution)/shard_map/ppermute | solution.py:242

commit v23 on v19

--- a/solution.py
+++ b/solution.py
@@ -332,6 +332,7 @@
     third, third_across, shared, own = join((1, 1, 1, 1), mine_two, theirs_two)
     first, second, shared = travel(first, one), travel(second, two), travel(shared, four)
     third, third_across = travel(third, three), travel(third_across, three, 1)
+    shared, third, third_across = lax.optimization_barrier((shared, third, third_across))
     others = local(sift_kernel, packed(1, 1), "sift", first, second)
     others = [swap(a) for a in others]
     return combine(mix, [first, second, third, *others, third_across, shared, own], 2)

time: 37.6 us -> 37.7 us (level)
  waiting for transfers between devices: 9.71 us -> 10.3 us
  starting transfers between devices: 18.3 us -> 17.8 us
    ppermute x9, starting transfers between devices: 16.1 us -> 15 us  [travel(): return lax.ppermute(rows, 'exp', pairs)]
    ppermute x9, waiting for transfers between devices: 6.48 us -> 7.06 us  [travel(): return lax.ppermute(rows, 'exp', pairs)]
    ppermute x7, starting transfers between devices: 2.23 us -> 2.8 us  [swap(): return lax.ppermute(rows, 'exp', [(n, n ^ 1) for n in range(owners)])]
  transfers between devices with their start and end apart: 16 -> 16, of which waited for: 8 -> 7; matrix products, arithmetic and copies ran while one was open for 0% -> 0% of each run, Pallas kernels for 12% -> 12%
where the time goes in v23:
time: 37.7 us; the launch traced here: 37.5 us
  starting transfers between devices  17.8 us (47%)
  waiting for transfers between devices  10.3 us (27%)
  Pallas kernels  9.36 us (25%)
    ppermute x9, starting transfers between devices, travel(): return lax.ppermute(rows, 'exp', pairs)  15 us
    ppermute x9, waiting for transfers between devices, travel(): return lax.ppermute(rows, 'exp', pairs)  7.06 us
    pallas_call x1, Pallas kernels, stage(): pl.pallas_call(stage_kernel, out_shape=(*outs, jax.ShapeDtypeStruct(mix.s...  4.25 us
    ppermute x7, waiting for transfers between devices, swap(): return lax.ppermute(rows, 'exp', [(n, n ^ 1) for n in range(owners)])  3.23 us
    ppermute x7, starting transfers between devices, swap(): return lax.ppermute(rows, 'exp', [(n, n ^ 1) for n in range(owners)])  2.8 us
    pallas_call x6, Pallas kernels, local(): pl.pallas_call(kernel, out_shape=outs, in_specs=[VMEM] * len(args), out_s...  2.03 us
    pallas_call x1, Pallas kernels, per_device(): pl.pallas_call(functools.partial(dispatch_kernel, flight), out_shape=(jax...  1.91 us
    pallas_call x1, Pallas kernels, combine(): pl.pallas_call(functools.partial(combine_kernel, paired), out_shape=jax.S...  1.18 us
  transfers between devices with their start and end apart: 16, of which 7 were waited for; matrix products, arithmetic and copies ran while one was open for 0% of the time, Pallas kernels for 12%

profile of v23, /device:TPU:0, one launch (start us, length us, event | category | flops | bytes accessed | tf_op | source)
XLA Modules:
  0.0 37.5 jit_solution(18173720925377363006)
XLA Ops:
  0.0 1.9 %dispatch.1 = (bf16[128,128]{1,0:T(8,128)(2,1)S(1)}, bf16[24,3200]{1,0:T(8,128)(2,1)S(1)}, bf16[32,3200]{1,0:T(8,128)(2,1)S(1)}, bf16[8,3200]{1,0:T(8,128)(2,1)S(1)}, bf16[8,3200]{1,0:T(8,128)(2,1)S(1)}) custom-call(bf16[128,3584]{1,0:T(8,128)(2,1)} %tok_hbm.1, f32[3584]{0:T(1024)} %gain_hbm.1, s32[8,128]{1,0:T(8,128)} %bitcast.8, f32[8,128]{1,0:T(8,128)} %bitcast.9), custom_call_target="tpu_custom_call" | custom-call | tf_op jit(solution)/shard_map/dispatch/pallas_call | solution.py:285
  1.9 0.5 %collective-permute-start = (bf16[32,3200]{1,0:T(8,128)(2,1)S(1)}, bf16[32,3200]{1,0:T(8,128)(2,1)S(1)}, u32[]{:S(2)}, u32[]{:S(2)}) collective-permute-start(bf16[32,3200]{1,0:T(8,128)(2,1)S(1)} %get-tuple-element.44), channel_id=1, source_target_pairs={{0,1},{1,0},{2,3},{3,2},{4,5},{5,4},{6,7},{7,6},{8,9},{9,8},{10,11... | collective-permute-start | bytes 614408 | tf_op jit(solution)/shard_map/ppermute | solution.py:243
  2.4 1.1 %collective-permute-done.got_ref = bf16[32,3200]{1,0:T(8,128)(2,1)S(1)} collective-permute-done((bf16[32,3200]{1,0:T(8,128)(2,1)S(1)}, bf16[32,3200]{1,0:T(8,128)(2,1)S(1)}, u32[]{:S(2)}, u32[]{:S(2)}) %collective-permute-start) | collective-permute-done | bytes 204832 | tf_op jit(solution)/shard_map/ppermute | solution.py:243
  3.5 4.0 %collective-permute-start.1 = (bf16[16,3200]{1,0:T(8,128)(2,1)S(1)}, bf16[16,3200]{1,0:T(8,128)(2,1)S(1)}, u32[]{:S(2)}, u32[]{:S(2)}) collective-permute-start(bf16[16,3200]{1,0:T(8,128)(2,1)S(1)} %get-tuple-element.45), channel_id=1, source_target_pairs={{0,8},{1,13},{2,10},{3,15},{4,12},{5,9},{6,14},{7,11},{8,0},{9,5},... | collective-permute-start | bytes 307208 | tf_op jit(solution)/shard_map/ppermute | solution.py:247
  7.6 1.5 %collective-permute-start.2 = (bf16[16,3200]{1,0:T(8,128)(2,1)S(1)}, bf16[16,3200]{1,0:T(8,128)(2,1)S(1)}, u32[]{:S(2)}, u32[]{:S(2)}) collective-permute-start(bf16[16,3200]{1,0:T(8,128)(2,1)S(1)} %get-tuple-element.46), channel_id=1, source_target_pairs={{0,2},{1,5},{2,0},{3,7},{4,6},{5,1},{6,4},{7,3},{8,10},{9,13},{10,... | collective-permute-start | bytes 307208 | tf_op jit(solution)/shard_map/ppermute | solution.py:247
  9.1 0.0 collective-permute-start.3
  9.1 2.8 %collective-permute-start.4 = (bf16[8,3200]{1,0:T(8,128)(2,1)S(1)}, bf16[8,3200]{1,0:T(8,128)(2,1)S(1)}, u32[]{:S(2)}, u32[]{:S(2)}) collective-permute-start(bf16[8,3200]{1,0:T(8,128)(2,1)S(1)} %get-tuple-element.48), channel_id=1, source_target_pairs={{0,6},{1,7},{2,4},{3,5},{4,2},{5,3},{6,0},{7,1},{8,14},{9,15},{10,... | collective-permute-start | bytes 153608 | tf_op jit(solution)/shard_map/ppermute | solution.py:247
  11.9 4.2 %stage.1 = (bf16[3584,512]{1,0:T(8,128)(2,1)S(1)}, bf16[3584,512]{1,0:T(8,128)(2,1)S(1)}, bf16[512,3584]{1,0:T(8,128)(2,1)S(1)}, bf16[128,128]{1,0:T(8,128)(2,1)S(1)}) custom-call(bf16[128,128]{1,0:T(8,128)(2,1)S(1)} %get-tuple-element.49.mix_ref, bf16[3584,512]{1,0:T(8,128)(2,1)} %bitcast.5, bf16[3584,512]{1,0:T(8,128)(2,1)} %bitcast.6, ...), custom_call_target="tpu_custom_call" | custom-call | flops 1 | bytes 1 | tf_op jit(solution)/shard_map/stage/pallas_call | solution.py:252
  16.2 0.1 collective-permute-done.4.refs_3_
  16.2 2.3 %collective-permute-done.3.refs_2_ = bf16[16,3200]{1,0:T(8,128)(2,1)S(1)} collective-permute-done((bf16[16,3200]{1,0:T(8,128)(2,1)S(1)}, bf16[16,3200]{1,0:T(8,128)(2,1)S(1)}, u32[]{:S(2)}, u32[]{:S(2)}) %collective-permute-start.3) | collective-permute-done | bytes 102432 | tf_op jit(solution)/shard_map/ppermute | solution.py:247
  18.5 0.1 collective-permute-start.5
  18.6 0.5 %collective-permute-start.6 = (bf16[24,3200]{1,0:T(8,128)(2,1)S(1)}, bf16[24,3200]{1,0:T(8,128)(2,1)S(1)}, u32[]{:S(2)}, u32[]{:S(2)}) collective-permute-start(bf16[24,3200]{1,0:T(8,128)(2,1)S(1)} %get-tuple-element.60.refs_1_), channel_id=1, source_target_pairs={{0,1},{1,0},{2,3},{3,2},{4,5},{5,4},{6,7},{7,6},{8,9},{9,8},{10,11... | collective-permute-start | bytes 460808 | tf_op jit(solution)/shard_map/ppermute | solution.py:243
  19.1 1.2 %collective-permute-done.6.refs_4_ = bf16[24,3200]{1,0:T(8,128)(2,1)S(1)} collective-permute-done((bf16[24,3200]{1,0:T(8,128)(2,1)S(1)}, bf16[24,3200]{1,0:T(8,128)(2,1)S(1)}, u32[]{:S(2)}, u32[]{:S(2)}) %collective-permute-start.6) | collective-permute-done | bytes 153632 | tf_op jit(solution)/shard_map/ppermute | solution.py:243
  20.3 1.8 %experts.1 = (bf16[32,3584]{1,0:T(8,128)(2,1)S(1)}, bf16[32,3584]{1,0:T(8,128)(2,1)S(1)}, bf16[32,3584]{1,0:T(8,128)(2,1)S(1)}, bf16[32,3584]{1,0:T(8,128)(2,1)S(1)}) custom-call(bf16[32,3200]{1,0:T(8,128)(2,1)S(1)} %get-tuple-element.59.refs_0_, bf16[24,3200]{1,0:T(8,128)(2,1)S(1)} %get-tuple-element.60.refs_1_, ...), custom_call_target="tpu_custom_call" | custom-call | flops 1 | bytes 1 | tf_op jit(solution)/shard_map/experts/pallas_call | solution.py:225
  22.1 0.3 collective-permute-start.7
  22.3 0.3 collective-permute-start.10
  22.6 1.0 %collective-permute-done.7.got_ref = bf16[32,3584]{1,0:T(8,128)(2,1)S(1)} collective-permute-done((bf16[32,3584]{1,0:T(8,128)(2,1)S(1)}, bf16[32,3584]{1,0:T(8,128)(2,1)S(1)}, u32[]{:S(2)}, u32[]{:S(2)}) %collective-permute-start.7) | collective-permute-done | bytes 229408 | tf_op jit(solution)/shard_map/ppermute | solution.py:243
  23.6 0.1 join.2
  23.7 0.7 %collective-permute-start.8 = (bf16[16,3200]{1,0:T(8,128)(2,1)S(1)}, bf16[16,3200]{1,0:T(8,128)(2,1)S(1)}, u32[]{:S(2)}, u32[]{:S(2)}) collective-permute-start(bf16[16,3200]{1,0:T(8,128)(2,1)S(1)} %get-tuple-element.68), channel_id=1, source_target_pairs={{0,8},{1,13},{2,10},{3,15},{4,12},{5,9},{6,14},{7,11},{8,0},{9,5},... | collective-permute-start | bytes 307208 | tf_op jit(solution)/shard_map/ppermute | solution.py:247
  24.4 0.5 %collective-permute-start.9 = (bf16[16,3200]{1,0:T(8,128)(2,1)S(1)}, bf16[16,3200]{1,0:T(8,128)(2,1)S(1)}, u32[]{:S(2)}, u32[]{:S(2)}) collective-permute-start(bf16[16,3200]{1,0:T(8,128)(2,1)S(1)} %get-tuple-element.69), channel_id=1, source_target_pairs={{0,2},{1,5},{2,0},{3,7},{4,6},{5,1},{6,4},{7,3},{8,10},{9,13},{10,... | collective-permute-start | bytes 307208 | tf_op jit(solution)/shard_map/ppermute | solution.py:247
  24.9 0.1 join.3
  25.0 4.0 %collective-permute-start.11 = (bf16[8,3200]{1,0:T(8,128)(2,1)S(1)}, bf16[8,3200]{1,0:T(8,128)(2,1)S(1)}, u32[]{:S(2)}, u32[]{:S(2)}) collective-permute-start(bf16[8,3200]{1,0:T(8,128)(2,1)S(1)} %get-tuple-element.72), channel_id=1, source_target_pairs={{0,6},{1,7},{2,4},{3,5},{4,2},{5,3},{6,0},{7,1},{8,14},{9,15},{10,... | collective-permute-start | bytes 153608 | tf_op jit(solution)/shard_map/ppermute | solution.py:247
  29.0 0.1 collective-permute-start.12
  29.1 1.3 %collective-permute-start.13 = (bf16[8,3200]{1,0:T(8,128)(2,1)S(1)}, bf16[8,3200]{1,0:T(8,128)(2,1)S(1)}, u32[]{:S(2)}, u32[]{:S(2)}) collective-permute-start(bf16[8,3200]{1,0:T(8,128)(2,1)S(1)} %get-tuple-element.74), channel_id=1, source_target_pairs={{0,11},{1,14},{2,9},{3,12},{4,15},{5,10},{6,13},{7,8},{8,3},{9,6},... | collective-permute-start | bytes 153608 | tf_op jit(solution)/shard_map/ppermute | solution.py:247
  30.4 1.2 %collective-permute-done.8.refs_0_ = bf16[16,3200]{1,0:T(8,128)(2,1)S(1)} collective-permute-done((bf16[16,3200]{1,0:T(8,128)(2,1)S(1)}, bf16[16,3200]{1,0:T(8,128)(2,1)S(1)}, u32[]{:S(2)}, u32[]{:S(2)}) %collective-permute-start.8) | collective-permute-done | bytes 102432 | tf_op jit(solution)/shard_map/ppermute | solution.py:247
  31.6 0.0 collective-permute-done.9.refs_1_
  31.6 1.1 %collective-permute-start.14 = (bf16[8,3200]{1,0:T(8,128)(2,1)S(1)}, bf16[8,3200]{1,0:T(8,128)(2,1)S(1)}, u32[]{:S(2)}, u32[]{:S(2)}) collective-permute-start(bf16[8,3200]{1,0:T(8,128)(2,1)S(1)} %get-tuple-element.76), channel_id=1, source_target_pairs={{0,1},{1,0},{2,3},{3,2},{4,5},{5,4},{6,7},{7,6},{8,9},{9,8},{10,11... | collective-permute-start | bytes 153608 | tf_op jit(solution)/shard_map/ppermute | solution.py:243
  32.7 0.1 collective-permute-start.15
  32.8 3.5 %collective-permute-done.12.refs_2_ = bf16[8,3200]{1,0:T(8,128)(2,1)S(1)} collective-permute-done((bf16[8,3200]{1,0:T(8,128)(2,1)S(1)}, bf16[8,3200]{1,0:T(8,128)(2,1)S(1)}, u32[]{:S(2)}, u32[]{:S(2)}) %collective-permute-start.12) | collective-permute-done | bytes 51232 | tf_op jit(solution)/shard_map/ppermute | solution.py:247
  36.3 0.0 collective-permute-done.13.refs_5_
  36.3 0.0 collective-permute-done.14.refs_3_
  36.3 1.2 %combine.1 = bf16[128,3584]{1,0:T(8,128)(2,1)} custom-call(bf16[128,128]{1,0:T(8,128)(2,1)S(1)} %get-tuple-element.54.mix_ref, bf16[16,3200]{1,0:T(8,128)(2,1)S(1)} %collective-permute-done.8.refs_0_, bf16[16,3200]{1,0:T(8,128)(2,1)S(1)} %collective-permute-done.9.refs_1_, bf16[8,3200]{1,0:T(8,128)(2,1)S(1)} %collective-permute-done.12.refs_2_, ...), custom_call_target="tpu_custom_call" | custom-call | tf_op jit(solution)/shard_map/combine/pallas_call | solution.py:271
  (9 shorter events, 0.1 us)
Async XLA Ops:
  1.9 1.6 %collective-permute-start = (bf16[32,3200]{1,0:T(8,128)(2,1)S(1)}, bf16[32,3200]{1,0:T(8,128)(2,1)S(1)}, u32[]{:S(2)}, u32[]{:S(2)}) collective-permute-start(bf16[32,3200]{1,0:T(8,128)(2,1)S(1)} %get-tuple-element.44), channel_id=1, source_target_pairs={{0,1},{1,0},{2,3},{3,2},{4,5},{5,4},{6,7},{7,6},{8,9},{9,8},{10,11... | collective-permute-start | bytes 614408 | tf_op jit(solution)/shard_map/ppermute | solution.py:243
  3.5 12.7 %collective-permute-start.1 = (bf16[16,3200]{1,0:T(8,128)(2,1)S(1)}, bf16[16,3200]{1,0:T(8,128)(2,1)S(1)}, u32[]{:S(2)}, u32[]{:S(2)}) collective-permute-start(bf16[16,3200]{1,0:T(8,128)(2,1)S(1)} %get-tuple-element.45), channel_id=1, source_target_pairs={{0,8},{1,13},{2,10},{3,15},{4,12},{5,9},{6,14},{7,11},{8,0},{9,5},... | collective-permute-start | bytes 307208 | tf_op jit(solution)/shard_map/ppermute | solution.py:247
  7.6 8.7 %collective-permute-start.2 = (bf16[16,3200]{1,0:T(8,128)(2,1)S(1)}, bf16[16,3200]{1,0:T(8,128)(2,1)S(1)}, u32[]{:S(2)}, u32[]{:S(2)}) collective-permute-start(bf16[16,3200]{1,0:T(8,128)(2,1)S(1)} %get-tuple-element.46), channel_id=1, source_target_pairs={{0,2},{1,5},{2,0},{3,7},{4,6},{5,1},{6,4},{7,3},{8,10},{9,13},{10,... | collective-permute-start | bytes 307208 | tf_op jit(solution)/shard_map/ppermute | solution.py:247
  9.1 9.4 %collective-permute-start.3 = (bf16[16,3200]{1,0:T(8,128)(2,1)S(1)}, bf16[16,3200]{1,0:T(8,128)(2,1)S(1)}, u32[]{:S(2)}, u32[]{:S(2)}) collective-permute-start(bf16[16,3200]{1,0:T(8,128)(2,1)S(1)} %get-tuple-element.47), channel_id=1, source_target_pairs={{0,10},{1,15},{2,8},{3,13},{4,14},{5,11},{6,12},{7,9},{8,2},{9,7},... | collective-permute-start | bytes 307208 | tf_op jit(solution)/shard_map/ppermute | solution.py:247
  9.1 7.1 %collective-permute-start.4 = (bf16[8,3200]{1,0:T(8,128)(2,1)S(1)}, bf16[8,3200]{1,0:T(8,128)(2,1)S(1)}, u32[]{:S(2)}, u32[]{:S(2)}) collective-permute-start(bf16[8,3200]{1,0:T(8,128)(2,1)S(1)} %get-tuple-element.48), channel_id=1, source_target_pairs={{0,6},{1,7},{2,4},{3,5},{4,2},{5,3},{6,0},{7,1},{8,14},{9,15},{10,... | collective-permute-start | bytes 153608 | tf_op jit(solution)/shard_map/ppermute | solution.py:247
  18.5 1.7 %collective-permute-start.5 = (bf16[32,3200]{1,0:T(8,128)(2,1)S(1)}, bf16[32,3200]{1,0:T(8,128)(2,1)S(1)}, u32[]{:S(2)}, u32[]{:S(2)}) collective-permute-start(bf16[32,3200]{1,0:T(8,128)(2,1)S(1)} %get-tuple-element.59.refs_0_), channel_id=1, source_target_pairs={{0,1},{1,0},{2,3},{3,2},{4,5},{5,4},{6,7},{7,6},{8,9},{9,8},{10,11... | collective-permute-start | bytes 614408 | tf_op jit(solution)/shard_map/ppermute | solution.py:243
  18.6 1.7 %collective-permute-start.6 = (bf16[24,3200]{1,0:T(8,128)(2,1)S(1)}, bf16[24,3200]{1,0:T(8,128)(2,1)S(1)}, u32[]{:S(2)}, u32[]{:S(2)}) collective-permute-start(bf16[24,3200]{1,0:T(8,128)(2,1)S(1)} %get-tuple-element.60.refs_1_), channel_id=1, source_target_pairs={{0,1},{1,0},{2,3},{3,2},{4,5},{5,4},{6,7},{7,6},{8,9},{9,8},{10,11... | collective-permute-start | bytes 460808 | tf_op jit(solution)/shard_map/ppermute | solution.py:243
  22.1 1.6 %collective-permute-start.7 = (bf16[32,3584]{1,0:T(8,128)(2,1)S(1)}, bf16[32,3584]{1,0:T(8,128)(2,1)S(1)}, u32[]{:S(2)}, u32[]{:S(2)}) collective-permute-start(bf16[32,3584]{1,0:T(8,128)(2,1)S(1)} %get-tuple-element.67), channel_id=1, source_target_pairs={{0,1},{1,0},{2,3},{3,2},{4,5},{5,4},{6,7},{7,6},{8,9},{9,8},{10,11... | collective-permute-start | bytes 688136 | tf_op jit(solution)/shard_map/ppermute | solution.py:243
  22.3 2.6 %collective-permute-start.10 = (bf16[32,3584]{1,0:T(8,128)(2,1)S(1)}, bf16[32,3584]{1,0:T(8,128)(2,1)S(1)}, u32[]{:S(2)}, u32[]{:S(2)}) collective-permute-start(bf16[32,3584]{1,0:T(8,128)(2,1)S(1)} %get-tuple-element.71), channel_id=1, source_target_pairs={{0,1},{1,0},{2,3},{3,2},{4,5},{5,4},{6,7},{7,6},{8,9},{9,8},{10,11... | collective-permute-start | bytes 688136 | tf_op jit(solution)/shard_map/ppermute | solution.py:243
  23.7 7.9 %collective-permute-start.8 = (bf16[16,3200]{1,0:T(8,128)(2,1)S(1)}, bf16[16,3200]{1,0:T(8,128)(2,1)S(1)}, u32[]{:S(2)}, u32[]{:S(2)}) collective-permute-start(bf16[16,3200]{1,0:T(8,128)(2,1)S(1)} %get-tuple-element.68), channel_id=1, source_target_pairs={{0,8},{1,13},{2,10},{3,15},{4,12},{5,9},{6,14},{7,11},{8,0},{9,5},... | collective-permute-start | bytes 307208 | tf_op jit(solution)/shard_map/ppermute | solution.py:247
  24.4 7.2 %collective-permute-start.9 = (bf16[16,3200]{1,0:T(8,128)(2,1)S(1)}, bf16[16,3200]{1,0:T(8,128)(2,1)S(1)}, u32[]{:S(2)}, u32[]{:S(2)}) collective-permute-start(bf16[16,3200]{1,0:T(8,128)(2,1)S(1)} %get-tuple-element.69), channel_id=1, source_target_pairs={{0,2},{1,5},{2,0},{3,7},{4,6},{5,1},{6,4},{7,3},{8,10},{9,13},{10,... | collective-permute-start | bytes 307208 | tf_op jit(solution)/shard_map/ppermute | solution.py:247
  25.0 7.8 %collective-permute-start.11 = (bf16[8,3200]{1,0:T(8,128)(2,1)S(1)}, bf16[8,3200]{1,0:T(8,128)(2,1)S(1)}, u32[]{:S(2)}, u32[]{:S(2)}) collective-permute-start(bf16[8,3200]{1,0:T(8,128)(2,1)S(1)} %get-tuple-element.72), channel_id=1, source_target_pairs={{0,6},{1,7},{2,4},{3,5},{4,2},{5,3},{6,0},{7,1},{8,14},{9,15},{10,... | collective-permute-start | bytes 153608 | tf_op jit(solution)/shard_map/ppermute | solution.py:247
  29.0 7.3 %collective-permute-start.12 = (bf16[8,3200]{1,0:T(8,128)(2,1)S(1)}, bf16[8,3200]{1,0:T(8,128)(2,1)S(1)}, u32[]{:S(2)}, u32[]{:S(2)}) collective-permute-start(bf16[8,3200]{1,0:T(8,128)(2,1)S(1)} %get-tuple-element.73), channel_id=1, source_target_pairs={{0,10},{1,15},{2,8},{3,13},{4,14},{5,11},{6,12},{7,9},{8,2},{9,7},... | collective-permute-start | bytes 153608 | tf_op jit(solution)/shard_map/ppermute | solution.py:247
  29.1 7.2 %collective-permute-start.13 = (bf16[8,3200]{1,0:T(8,128)(2,1)S(1)}, bf16[8,3200]{1,0:T(8,128)(2,1)S(1)}, u32[]{:S(2)}, u32[]{:S(2)}) collective-permute-start(bf16[8,3200]{1,0:T(8,128)(2,1)S(1)} %get-tuple-element.74), channel_id=1, source_target_pairs={{0,11},{1,14},{2,9},{3,12},{4,15},{5,10},{6,13},{7,8},{8,3},{9,6},... | collective-permute-start | bytes 153608 | tf_op jit(solution)/shard_map/ppermute | solution.py:247
  31.6 4.7 %collective-permute-start.14 = (bf16[8,3200]{1,0:T(8,128)(2,1)S(1)}, bf16[8,3200]{1,0:T(8,128)(2,1)S(1)}, u32[]{:S(2)}, u32[]{:S(2)}) collective-permute-start(bf16[8,3200]{1,0:T(8,128)(2,1)S(1)} %get-tuple-element.76), channel_id=1, source_target_pairs={{0,1},{1,0},{2,3},{3,2},{4,5},{5,4},{6,7},{7,6},{8,9},{9,8},{10,11... | collective-permute-start | bytes 153608 | tf_op jit(solution)/shard_map/ppermute | solution.py:243
  32.7 3.6 %collective-permute-start.15 = (bf16[8,3200]{1,0:T(8,128)(2,1)S(1)}, bf16[8,3200]{1,0:T(8,128)(2,1)S(1)}, u32[]{:S(2)}, u32[]{:S(2)}) collective-permute-start(bf16[8,3200]{1,0:T(8,128)(2,1)S(1)} %get-tuple-element.77), channel_id=1, source_target_pairs={{0,1},{1,0},{2,3},{3,2},{4,5},{5,4},{6,7},{7,6},{8,9},{9,8},{10,11... | collective-permute-start | bytes 153608 | tf_op jit(solution)/shard_map/ppermute | solution.py:243

commit v24 on v19

--- a/solution.py
+++ b/solution.py
@@ -178,7 +178,7 @@
 
 def sift_kernel(*refs):
     count = len(refs) // 2
-    for ref, out in zip(refs[:count], refs[count:]):
+    for ref, out in zip(refs[:count], refs[count + 1 :]):
         out[...] = ref[...].astype(jnp.float32)[SLOTS:].astype(jnp.bfloat16)
 
 
@@ -265,7 +265,7 @@
         return local(expert_kernel, outs, "experts", *rows, *weights, limit=24)
 
     def join(outs, mine, theirs):
-        return local(join_kernel, packed(*outs), "join", mine, swap(theirs))
+        return local(join_kernel, packed(*outs), "join", mine, theirs)
 
     def combine(mix, arrays, paired):
         return pl.pallas_call(
@@ -311,8 +311,8 @@
         own = exchange(outgoing[0])
         mine_one, mine_two, theirs_one, theirs_two = experts([own, swap(own)], weights)
         half = flight // 2
-        (joined_one,) = join([half], mine_one, theirs_one)
-        (joined_two,) = join([half], mine_two, theirs_two)
+        (joined_one,) = join([half], mine_one, swap(theirs_one))
+        (joined_two,) = join([half], mine_two, swap(theirs_two))
         return combine(mix, [exchange(jnp.concatenate([joined_one, joined_two]))], 0)
 
     one, two, three = zip(*CARRIED)
@@ -328,11 +328,14 @@
         (*rows, own, *[swap(a) for a in rows], other_own), (gate, up, down)
     )
 
+    theirs_one = swap(theirs_one)
+    theirs_two, theirs_one = lax.optimization_barrier((theirs_two, theirs_one))
     first, second = join((2, 2), mine_one, theirs_one)
-    third, third_across, shared, own = join((1, 1, 1, 1), mine_two, theirs_two)
+    third, third_across, shared, own = join((1, 1, 1, 1), mine_two, swap(theirs_two))
     first, second, shared = travel(first, one), travel(second, two), travel(shared, four)
+    before = third
     third, third_across = travel(third, three), travel(third_across, three, 1)
-    others = local(sift_kernel, packed(1, 1), "sift", first, second)
+    others = local(sift_kernel, packed(1, 1), "sift", first, second, before)
     others = [swap(a) for a in others]
     return combine(mix, [first, second, third, *others, third_across, shared, own], 2)
 

time: 37.6 us -> 37.8 us (level)
  starting transfers between devices: 18.3 us -> 19.5 us
  waiting for transfers between devices: 9.71 us -> 8.76 us
    ppermute x9, waiting for transfers between devices: 6.48 us -> 5.23 us  [travel(): return lax.ppermute(rows, 'exp', pairs)]
    ppermute x9, starting transfers between devices: 16.1 us -> 16.7 us  [travel(): return lax.ppermute(rows, 'exp', pairs)]
    ppermute x7, starting transfers between devices: 2.23 us -> 2.76 us  [swap(): return lax.ppermute(rows, 'exp', [(n, n ^ 1) for n in range(owners)])]
  transfers between devices with their start and end apart: 16 -> 16, of which waited for: 8 -> 7; matrix products, arithmetic and copies ran while one was open for 0% -> 0% of each run, Pallas kernels for 12% -> 12%
where the time goes in v24:
time: 37.8 us; the launch traced here: 37.7 us
  starting transfers between devices  19.5 us (52%)
  Pallas kernels  9.35 us (25%)
  waiting for transfers between devices  8.76 us (23%)
    ppermute x9, starting transfers between devices, travel(): return lax.ppermute(rows, 'exp', pairs)  16.7 us
    ppermute x9, waiting for transfers between devices, travel(): return lax.ppermute(rows, 'exp', pairs)  5.23 us
    pallas_call x1, Pallas kernels, stage(): pl.pallas_call(stage_kernel, out_shape=(*outs, jax.ShapeDtypeStruct(mix.s...  4.25 us
    ppermute x7, waiting for transfers between devices, swap(): return lax.ppermute(rows, 'exp', [(n, n ^ 1) for n in range(owners)])  3.53 us
    ppermute x7, starting transfers between devices, swap(): return lax.ppermute(rows, 'exp', [(n, n ^ 1) for n in range(owners)])  2.76 us
    pallas_call x6, Pallas kernels, local(): pl.pallas_call(kernel, out_shape=outs, in_specs=[VMEM] * len(args), out_s...  2.03 us
    pallas_call x1, Pallas kernels, per_device(): pl.pallas_call(functools.partial(dispatch_kernel, flight), out_shape=(jax...  1.91 us
    pallas_call x1, Pallas kernels, combine(): pl.pallas_call(functools.partial(combine_kernel, paired), out_shape=jax.S...  1.17 us
  transfers between devices with their start and end apart: 16, of which 7 were waited for; matrix products, arithmetic and copies ran while one was open for 0% of the time, Pallas kernels for 12%

profile of v24, /device:TPU:0, one launch (start us, length us, event | category | flops | bytes accessed | tf_op | source)
XLA Modules:
  0.0 37.7 jit_solution(6342224686748217711)
XLA Ops:
  0.0 1.9 %dispatch.1 = (bf16[128,128]{1,0:T(8,128)(2,1)S(1)}, bf16[24,3200]{1,0:T(8,128)(2,1)S(1)}, bf16[32,3200]{1,0:T(8,128)(2,1)S(1)}, bf16[8,3200]{1,0:T(8,128)(2,1)S(1)}, bf16[8,3200]{1,0:T(8,128)(2,1)S(1)}) custom-call(bf16[128,3584]{1,0:T(8,128)(2,1)} %tok_hbm.1, f32[3584]{0:T(1024)} %gain_hbm.1, s32[8,128]{1,0:T(8,128)} %bitcast.8, f32[8,128]{1,0:T(8,128)} %bitcast.9), custom_call_target="tpu_custom_call" | custom-call | tf_op jit(solution)/shard_map/dispatch/pallas_call | solution.py:285
  1.9 0.5 %collective-permute-start = (bf16[32,3200]{1,0:T(8,128)(2,1)S(1)}, bf16[32,3200]{1,0:T(8,128)(2,1)S(1)}, u32[]{:S(2)}, u32[]{:S(2)}) collective-permute-start(bf16[32,3200]{1,0:T(8,128)(2,1)S(1)} %get-tuple-element.43), channel_id=1, source_target_pairs={{0,1},{1,0},{2,3},{3,2},{4,5},{5,4},{6,7},{7,6},{8,9},{9,8},{10,11... | collective-permute-start | bytes 614408 | tf_op jit(solution)/shard_map/ppermute | solution.py:243
  2.4 1.1 %collective-permute-done.got_ref = bf16[32,3200]{1,0:T(8,128)(2,1)S(1)} collective-permute-done((bf16[32,3200]{1,0:T(8,128)(2,1)S(1)}, bf16[32,3200]{1,0:T(8,128)(2,1)S(1)}, u32[]{:S(2)}, u32[]{:S(2)}) %collective-permute-start) | collective-permute-done | bytes 204832 | tf_op jit(solution)/shard_map/ppermute | solution.py:243
  3.5 4.0 %collective-permute-start.1 = (bf16[16,3200]{1,0:T(8,128)(2,1)S(1)}, bf16[16,3200]{1,0:T(8,128)(2,1)S(1)}, u32[]{:S(2)}, u32[]{:S(2)}) collective-permute-start(bf16[16,3200]{1,0:T(8,128)(2,1)S(1)} %get-tuple-element.44), channel_id=1, source_target_pairs={{0,8},{1,13},{2,10},{3,15},{4,12},{5,9},{6,14},{7,11},{8,0},{9,5},... | collective-permute-start | bytes 307208 | tf_op jit(solution)/shard_map/ppermute | solution.py:247
  7.6 1.5 %collective-permute-start.2 = (bf16[16,3200]{1,0:T(8,128)(2,1)S(1)}, bf16[16,3200]{1,0:T(8,128)(2,1)S(1)}, u32[]{:S(2)}, u32[]{:S(2)}) collective-permute-start(bf16[16,3200]{1,0:T(8,128)(2,1)S(1)} %get-tuple-element.45), channel_id=1, source_target_pairs={{0,2},{1,5},{2,0},{3,7},{4,6},{5,1},{6,4},{7,3},{8,10},{9,13},{10,... | collective-permute-start | bytes 307208 | tf_op jit(solution)/shard_map/ppermute | solution.py:247
  9.1 0.0 collective-permute-start.3
  9.1 2.8 %collective-permute-start.4 = (bf16[8,3200]{1,0:T(8,128)(2,1)S(1)}, bf16[8,3200]{1,0:T(8,128)(2,1)S(1)}, u32[]{:S(2)}, u32[]{:S(2)}) collective-permute-start(bf16[8,3200]{1,0:T(8,128)(2,1)S(1)} %get-tuple-element.47), channel_id=1, source_target_pairs={{0,6},{1,7},{2,4},{3,5},{4,2},{5,3},{6,0},{7,1},{8,14},{9,15},{10,... | collective-permute-start | bytes 153608 | tf_op jit(solution)/shard_map/ppermute | solution.py:247
  11.9 4.2 %stage.1 = (bf16[3584,512]{1,0:T(8,128)(2,1)S(1)}, bf16[3584,512]{1,0:T(8,128)(2,1)S(1)}, bf16[512,3584]{1,0:T(8,128)(2,1)S(1)}, bf16[128,128]{1,0:T(8,128)(2,1)S(1)}) custom-call(bf16[128,128]{1,0:T(8,128)(2,1)S(1)} %get-tuple-element.48.mix_ref, bf16[3584,512]{1,0:T(8,128)(2,1)} %bitcast.5, bf16[3584,512]{1,0:T(8,128)(2,1)} %bitcast.6, ...), custom_call_target="tpu_custom_call" | custom-call | flops 1 | bytes 1 | tf_op jit(solution)/shard_map/stage/pallas_call | solution.py:252
  16.2 0.1 collective-permute-done.4.refs_3_
  16.2 0.0 collective-permute-done.1.refs_0_
  16.2 0.0 collective-permute-done.2.refs_1_
  16.2 2.3 %collective-permute-done.3.refs_2_ = bf16[16,3200]{1,0:T(8,128)(2,1)S(1)} collective-permute-done((bf16[16,3200]{1,0:T(8,128)(2,1)S(1)}, bf16[16,3200]{1,0:T(8,128)(2,1)S(1)}, u32[]{:S(2)}, u32[]{:S(2)}) %collective-permute-start.3) | collective-permute-done | bytes 102432 | tf_op jit(solution)/shard_map/ppermute | solution.py:247
  18.5 0.1 collective-permute-start.5
  18.6 0.5 %collective-permute-start.6 = (bf16[24,3200]{1,0:T(8,128)(2,1)S(1)}, bf16[24,3200]{1,0:T(8,128)(2,1)S(1)}, u32[]{:S(2)}, u32[]{:S(2)}) collective-permute-start(bf16[24,3200]{1,0:T(8,128)(2,1)S(1)} %get-tuple-element.59.refs_1_), channel_id=1, source_target_pairs={{0,1},{1,0},{2,3},{3,2},{4,5},{5,4},{6,7},{7,6},{8,9},{9,8},{10,11... | collective-permute-start | bytes 460808 | tf_op jit(solution)/shard_map/ppermute | solution.py:243
  19.1 1.2 %collective-permute-done.6.refs_4_ = bf16[24,3200]{1,0:T(8,128)(2,1)S(1)} collective-permute-done((bf16[24,3200]{1,0:T(8,128)(2,1)S(1)}, bf16[24,3200]{1,0:T(8,128)(2,1)S(1)}, u32[]{:S(2)}, u32[]{:S(2)}) %collective-permute-start.6) | collective-permute-done | bytes 153632 | tf_op jit(solution)/shard_map/ppermute | solution.py:243
  20.3 0.0 collective-permute-done.5.refs_3_
  20.3 1.8 %experts.1 = (bf16[32,3584]{1,0:T(8,128)(2,1)S(1)}, bf16[32,3584]{1,0:T(8,128)(2,1)S(1)}, bf16[32,3584]{1,0:T(8,128)(2,1)S(1)}, bf16[32,3584]{1,0:T(8,128)(2,1)S(1)}) custom-call(bf16[32,3200]{1,0:T(8,128)(2,1)S(1)} %get-tuple-element.58.refs_0_, bf16[24,3200]{1,0:T(8,128)(2,1)S(1)} %get-tuple-element.59.refs_1_, ...), custom_call_target="tpu_custom_call" | custom-call | flops 1 | bytes 1 | tf_op jit(solution)/shard_map/experts/pallas_call | solution.py:225
  22.1 0.3 collective-permute-start.7
  22.3 1.3 %collective-permute-done.7.got_ref = bf16[32,3584]{1,0:T(8,128)(2,1)S(1)} collective-permute-done((bf16[32,3584]{1,0:T(8,128)(2,1)S(1)}, bf16[32,3584]{1,0:T(8,128)(2,1)S(1)}, u32[]{:S(2)}, u32[]{:S(2)}) %collective-permute-start.7) | collective-permute-done | bytes 229408 | tf_op jit(solution)/shard_map/ppermute | solution.py:243
  23.6 0.2 collective-permute-start.10
  23.8 0.1 join.2
  23.9 0.8 %collective-permute-start.8 = (bf16[16,3200]{1,0:T(8,128)(2,1)S(1)}, bf16[16,3200]{1,0:T(8,128)(2,1)S(1)}, u32[]{:S(2)}, u32[]{:S(2)}) collective-permute-start(bf16[16,3200]{1,0:T(8,128)(2,1)S(1)} %get-tuple-element.69), channel_id=1, source_target_pairs={{0,8},{1,13},{2,10},{3,15},{4,12},{5,9},{6,14},{7,11},{8,0},{9,5},... | collective-permute-start | bytes 307208 | tf_op jit(solution)/shard_map/ppermute | solution.py:247
  24.7 0.5 %collective-permute-start.9 = (bf16[16,3200]{1,0:T(8,128)(2,1)S(1)}, bf16[16,3200]{1,0:T(8,128)(2,1)S(1)}, u32[]{:S(2)}, u32[]{:S(2)}) collective-permute-start(bf16[16,3200]{1,0:T(8,128)(2,1)S(1)} %get-tuple-element.70), channel_id=1, source_target_pairs={{0,2},{1,5},{2,0},{3,7},{4,6},{5,1},{6,4},{7,3},{8,10},{9,13},{10,... | collective-permute-start | bytes 307208 | tf_op jit(solution)/shard_map/ppermute | solution.py:247
  25.2 0.1 join.3
  25.3 2.5 %collective-permute-start.14 = (bf16[8,3200]{1,0:T(8,128)(2,1)S(1)}, bf16[8,3200]{1,0:T(8,128)(2,1)S(1)}, u32[]{:S(2)}, u32[]{:S(2)}) collective-permute-start(bf16[8,3200]{1,0:T(8,128)(2,1)S(1)} %get-tuple-element.76), channel_id=1, source_target_pairs={{0,11},{1,14},{2,9},{3,12},{4,15},{5,10},{6,13},{7,8},{8,3},{9,6},... | collective-permute-start | bytes 153608 | tf_op jit(solution)/shard_map/ppermute | solution.py:247
  27.8 1.8 %collective-permute-start.15 = (bf16[8,3200]{1,0:T(8,128)(2,1)S(1)}, bf16[8,3200]{1,0:T(8,128)(2,1)S(1)}, u32[]{:S(2)}, u32[]{:S(2)}) collective-permute-start(bf16[8,3200]{1,0:T(8,128)(2,1)S(1)} %get-tuple-element.77), channel_id=1, source_target_pairs={{0,6},{1,7},{2,4},{3,5},{4,2},{5,3},{6,0},{7,1},{8,14},{9,15},{10,... | collective-permute-start | bytes 153608 | tf_op jit(solution)/shard_map/ppermute | solution.py:247
  29.6 2.8 %collective-permute-start.11 = (bf16[8,3200]{1,0:T(8,128)(2,1)S(1)}, bf16[8,3200]{1,0:T(8,128)(2,1)S(1)}, u32[]{:S(2)}, u32[]{:S(2)}) collective-permute-start(bf16[8,3200]{1,0:T(8,128)(2,1)S(1)} %get-tuple-element.73.refs_2_), channel_id=1, source_target_pairs={{0,10},{1,15},{2,8},{3,13},{4,14},{5,11},{6,12},{7,9},{8,2},{9,7},... | collective-permute-start | bytes 153608 | tf_op jit(solution)/shard_map/ppermute | solution.py:247
  32.4 1.1 %collective-permute-start.12 = (bf16[8,3200]{1,0:T(8,128)(2,1)S(1)}, bf16[8,3200]{1,0:T(8,128)(2,1)S(1)}, u32[]{:S(2)}, u32[]{:S(2)}) collective-permute-start(bf16[8,3200]{1,0:T(8,128)(2,1)S(1)} %get-tuple-element.74), channel_id=1, source_target_pairs={{0,1},{1,0},{2,3},{3,2},{4,5},{5,4},{6,7},{7,6},{8,9},{9,8},{10,11... | collective-permute-start | bytes 153608 | tf_op jit(solution)/shard_map/ppermute | solution.py:243
  33.5 0.1 collective-permute-start.13
  33.6 0.7 %collective-permute-done.15.refs_6_ = bf16[8,3200]{1,0:T(8,128)(2,1)S(1)} collective-permute-done((bf16[8,3200]{1,0:T(8,128)(2,1)S(1)}, bf16[8,3200]{1,0:T(8,128)(2,1)S(1)}, u32[]{:S(2)}, u32[]{:S(2)}) %collective-permute-start.15) | collective-permute-done | bytes 51232 | tf_op jit(solution)/shard_map/ppermute | solution.py:247
  34.3 2.2 %collective-permute-done.11.refs_2_ = bf16[8,3200]{1,0:T(8,128)(2,1)S(1)} collective-permute-done((bf16[8,3200]{1,0:T(8,128)(2,1)S(1)}, bf16[8,3200]{1,0:T(8,128)(2,1)S(1)}, u32[]{:S(2)}, u32[]{:S(2)}) %collective-permute-start.11) | collective-permute-done | bytes 51232 | tf_op jit(solution)/shard_map/ppermute | solution.py:247
  36.5 1.2 %combine.1 = bf16[128,3584]{1,0:T(8,128)(2,1)} custom-call(bf16[128,128]{1,0:T(8,128)(2,1)S(1)} %get-tuple-element.53.mix_ref, bf16[16,3200]{1,0:T(8,128)(2,1)S(1)} %collective-permute-done.8.refs_0_, bf16[16,3200]{1,0:T(8,128)(2,1)S(1)} %collective-permute-done.9.refs_1_, bf16[8,3200]{1,0:T(8,128)(2,1)S(1)} %collective-permute-done.11.refs_2_, ...), custom_call_target="tpu_custom_call" | custom-call | tf_op jit(solution)/shard_map/combine/pallas_call | solution.py:271
  (9 shorter events, 0.1 us)
Async XLA Ops:
  1.9 1.6 %collective-permute-start = (bf16[32,3200]{1,0:T(8,128)(2,1)S(1)}, bf16[32,3200]{1,0:T(8,128)(2,1)S(1)}, u32[]{:S(2)}, u32[]{:S(2)}) collective-permute-start(bf16[32,3200]{1,0:T(8,128)(2,1)S(1)} %get-tuple-element.43), channel_id=1, source_target_pairs={{0,1},{1,0},{2,3},{3,2},{4,5},{5,4},{6,7},{7,6},{8,9},{9,8},{10,11... | collective-permute-start | bytes 614408 | tf_op jit(solution)/shard_map/ppermute | solution.py:243
  3.5 12.7 %collective-permute-start.1 = (bf16[16,3200]{1,0:T(8,128)(2,1)S(1)}, bf16[16,3200]{1,0:T(8,128)(2,1)S(1)}, u32[]{:S(2)}, u32[]{:S(2)}) collective-permute-start(bf16[16,3200]{1,0:T(8,128)(2,1)S(1)} %get-tuple-element.44), channel_id=1, source_target_pairs={{0,8},{1,13},{2,10},{3,15},{4,12},{5,9},{6,14},{7,11},{8,0},{9,5},... | collective-permute-start | bytes 307208 | tf_op jit(solution)/shard_map/ppermute | solution.py:247
  7.6 8.7 %collective-permute-start.2 = (bf16[16,3200]{1,0:T(8,128)(2,1)S(1)}, bf16[16,3200]{1,0:T(8,128)(2,1)S(1)}, u32[]{:S(2)}, u32[]{:S(2)}) collective-permute-start(bf16[16,3200]{1,0:T(8,128)(2,1)S(1)} %get-tuple-element.45), channel_id=1, source_target_pairs={{0,2},{1,5},{2,0},{3,7},{4,6},{5,1},{6,4},{7,3},{8,10},{9,13},{10,... | collective-permute-start | bytes 307208 | tf_op jit(solution)/shard_map/ppermute | solution.py:247
  9.1 9.4 %collective-permute-start.3 = (bf16[16,3200]{1,0:T(8,128)(2,1)S(1)}, bf16[16,3200]{1,0:T(8,128)(2,1)S(1)}, u32[]{:S(2)}, u32[]{:S(2)}) collective-permute-start(bf16[16,3200]{1,0:T(8,128)(2,1)S(1)} %get-tuple-element.46), channel_id=1, source_target_pairs={{0,10},{1,15},{2,8},{3,13},{4,14},{5,11},{6,12},{7,9},{8,2},{9,7},... | collective-permute-start | bytes 307208 | tf_op jit(solution)/shard_map/ppermute | solution.py:247
  9.1 7.1 %collective-permute-start.4 = (bf16[8,3200]{1,0:T(8,128)(2,1)S(1)}, bf16[8,3200]{1,0:T(8,128)(2,1)S(1)}, u32[]{:S(2)}, u32[]{:S(2)}) collective-permute-start(bf16[8,3200]{1,0:T(8,128)(2,1)S(1)} %get-tuple-element.47), channel_id=1, source_target_pairs={{0,6},{1,7},{2,4},{3,5},{4,2},{5,3},{6,0},{7,1},{8,14},{9,15},{10,... | collective-permute-start | bytes 153608 | tf_op jit(solution)/shard_map/ppermute | solution.py:247
  18.5 1.7 %collective-permute-start.5 = (bf16[32,3200]{1,0:T(8,128)(2,1)S(1)}, bf16[32,3200]{1,0:T(8,128)(2,1)S(1)}, u32[]{:S(2)}, u32[]{:S(2)}) collective-permute-start(bf16[32,3200]{1,0:T(8,128)(2,1)S(1)} %get-tuple-element.58.refs_0_), channel_id=1, source_target_pairs={{0,1},{1,0},{2,3},{3,2},{4,5},{5,4},{6,7},{7,6},{8,9},{9,8},{10,11... | collective-permute-start | bytes 614408 | tf_op jit(solution)/shard_map/ppermute | solution.py:243
  18.6 1.7 %collective-permute-start.6 = (bf16[24,3200]{1,0:T(8,128)(2,1)S(1)}, bf16[24,3200]{1,0:T(8,128)(2,1)S(1)}, u32[]{:S(2)}, u32[]{:S(2)}) collective-permute-start(bf16[24,3200]{1,0:T(8,128)(2,1)S(1)} %get-tuple-element.59.refs_1_), channel_id=1, source_target_pairs={{0,1},{1,0},{2,3},{3,2},{4,5},{5,4},{6,7},{7,6},{8,9},{9,8},{10,11... | collective-permute-start | bytes 460808 | tf_op jit(solution)/shard_map/ppermute | solution.py:243
  22.1 1.6 %collective-permute-start.7 = (bf16[32,3584]{1,0:T(8,128)(2,1)S(1)}, bf16[32,3584]{1,0:T(8,128)(2,1)S(1)}, u32[]{:S(2)}, u32[]{:S(2)}) collective-permute-start(bf16[32,3584]{1,0:T(8,128)(2,1)S(1)} %get-tuple-element.67), channel_id=1, source_target_pairs={{0,1},{1,0},{2,3},{3,2},{4,5},{5,4},{6,7},{7,6},{8,9},{9,8},{10,11... | collective-permute-start | bytes 688136 | tf_op jit(solution)/shard_map/ppermute | solution.py:243
  23.6 1.6 %collective-permute-start.10 = (bf16[32,3584]{1,0:T(8,128)(2,1)S(1)}, bf16[32,3584]{1,0:T(8,128)(2,1)S(1)}, u32[]{:S(2)}, u32[]{:S(2)}) collective-permute-start(bf16[32,3584]{1,0:T(8,128)(2,1)S(1)} %get-tuple-element.72), channel_id=1, source_target_pairs={{0,1},{1,0},{2,3},{3,2},{4,5},{5,4},{6,7},{7,6},{8,9},{9,8},{10,11... | collective-permute-start | bytes 688136 | tf_op jit(solution)/shard_map/ppermute | solution.py:243
  23.9 8.5 %collective-permute-start.8 = (bf16[16,3200]{1,0:T(8,128)(2,1)S(1)}, bf16[16,3200]{1,0:T(8,128)(2,1)S(1)}, u32[]{:S(2)}, u32[]{:S(2)}) collective-permute-start(bf16[16,3200]{1,0:T(8,128)(2,1)S(1)} %get-tuple-element.69), channel_id=1, source_target_pairs={{0,8},{1,13},{2,10},{3,15},{4,12},{5,9},{6,14},{7,11},{8,0},{9,5},... | collective-permute-start | bytes 307208 | tf_op jit(solution)/shard_map/ppermute | solution.py:247
  24.7 7.7 %collective-permute-start.9 = (bf16[16,3200]{1,0:T(8,128)(2,1)S(1)}, bf16[16,3200]{1,0:T(8,128)(2,1)S(1)}, u32[]{:S(2)}, u32[]{:S(2)}) collective-permute-start(bf16[16,3200]{1,0:T(8,128)(2,1)S(1)} %get-tuple-element.70), channel_id=1, source_target_pairs={{0,2},{1,5},{2,0},{3,7},{4,6},{5,1},{6,4},{7,3},{8,10},{9,13},{10,... | collective-permute-start | bytes 307208 | tf_op jit(solution)/shard_map/ppermute | solution.py:247
  25.3 8.3 %collective-permute-start.14 = (bf16[8,3200]{1,0:T(8,128)(2,1)S(1)}, bf16[8,3200]{1,0:T(8,128)(2,1)S(1)}, u32[]{:S(2)}, u32[]{:S(2)}) collective-permute-start(bf16[8,3200]{1,0:T(8,128)(2,1)S(1)} %get-tuple-element.76), channel_id=1, source_target_pairs={{0,11},{1,14},{2,9},{3,12},{4,15},{5,10},{6,13},{7,8},{8,3},{9,6},... | collective-permute-start | bytes 153608 | tf_op jit(solution)/shard_map/ppermute | solution.py:247
  27.8 6.5 %collective-permute-start.15 = (bf16[8,3200]{1,0:T(8,128)(2,1)S(1)}, bf16[8,3200]{1,0:T(8,128)(2,1)S(1)}, u32[]{:S(2)}, u32[]{:S(2)}) collective-permute-start(bf16[8,3200]{1,0:T(8,128)(2,1)S(1)} %get-tuple-element.77), channel_id=1, source_target_pairs={{0,6},{1,7},{2,4},{3,5},{4,2},{5,3},{6,0},{7,1},{8,14},{9,15},{10,... | collective-permute-start | bytes 153608 | tf_op jit(solution)/shard_map/ppermute | solution.py:247
  29.6 6.9 %collective-permute-start.11 = (bf16[8,3200]{1,0:T(8,128)(2,1)S(1)}, bf16[8,3200]{1,0:T(8,128)(2,1)S(1)}, u32[]{:S(2)}, u32[]{:S(2)}) collective-permute-start(bf16[8,3200]{1,0:T(8,128)(2,1)S(1)} %get-tuple-element.73.refs_2_), channel_id=1, source_target_pairs={{0,10},{1,15},{2,8},{3,13},{4,14},{5,11},{6,12},{7,9},{8,2},{9,7},... | collective-permute-start | bytes 153608 | tf_op jit(solution)/shard_map/ppermute | solution.py:247
  32.4 4.1 %collective-permute-start.12 = (bf16[8,3200]{1,0:T(8,128)(2,1)S(1)}, bf16[8,3200]{1,0:T(8,128)(2,1)S(1)}, u32[]{:S(2)}, u32[]{:S(2)}) collective-permute-start(bf16[8,3200]{1,0:T(8,128)(2,1)S(1)} %get-tuple-element.74), channel_id=1, source_target_pairs={{0,1},{1,0},{2,3},{3,2},{4,5},{5,4},{6,7},{7,6},{8,9},{9,8},{10,11... | collective-permute-start | bytes 153608 | tf_op jit(solution)/shard_map/ppermute | solution.py:243
  33.5 3.0 %collective-permute-start.13 = (bf16[8,3200]{1,0:T(8,128)(2,1)S(1)}, bf16[8,3200]{1,0:T(8,128)(2,1)S(1)}, u32[]{:S(2)}, u32[]{:S(2)}) collective-permute-start(bf16[8,3200]{1,0:T(8,128)(2,1)S(1)} %get-tuple-element.75), channel_id=1, source_target_pairs={{0,1},{1,0},{2,3},{3,2},{4,5},{5,4},{6,7},{7,6},{8,9},{9,8},{10,11... | collective-permute-start | bytes 153608 | tf_op jit(solution)/shard_map/ppermute | solution.py:243

commit v25 on v19

--- a/solution.py
+++ b/solution.py
@@ -322,8 +322,8 @@
     shared = travel(shared, four)
     arrived = [travel(a, r) for a, r in zip(pairs, (one, two, three))] + [shared]
     *arrived, gate, up, down, mix = lax.optimization_barrier((*arrived, *stage(mix)))
-    kernel = functools.partial(gather_kernel, 2)
-    rows = local(kernel, packed(4, 3), "gather", *arrived)
+    kernel = functools.partial(gather_kernel, 1)
+    rows = local(kernel, packed(7), "gather", *arrived)
     mine_one, mine_two, theirs_one, theirs_two = experts(
         (*rows, own, *[swap(a) for a in rows], other_own), (gate, up, down)
     )

time: 37.6 us -> 37.6 us (level)
  starting transfers between devices: 18.3 us -> 17.7 us
  waiting for transfers between devices: 9.71 us -> 10.2 us
    ppermute x7 -> x6, starting transfers between devices: 2.23 us -> 1.73 us  [swap(): return lax.ppermute(rows, 'exp', [(n, n ^ 1) for n in range(owners)])]
    ppermute x7 -> x6, waiting for transfers between devices: 3.23 us -> 3.73 us  [swap(): return lax.ppermute(rows, 'exp', [(n, n ^ 1) for n in range(owners)])]
  transfers between devices with their start and end apart: 16 -> 15, of which waited for: 8 -> 8; matrix products, arithmetic and copies ran while one was open for 0% -> 0% of each run, Pallas kernels for 12% -> 12%
where the time goes in v25:
time: 37.6 us; the launch traced here: 37.4 us
  starting transfers between devices  17.7 us (47%)
  waiting for transfers between devices  10.2 us (27%)
  Pallas kernels  9.34 us (25%)
    ppermute x9, starting transfers between devices, travel(): return lax.ppermute(rows, 'exp', pairs)  16 us
    ppermute x9, waiting for transfers between devices, travel(): return lax.ppermute(rows, 'exp', pairs)  6.52 us
    pallas_call x1, Pallas kernels, stage(): pl.pallas_call(stage_kernel, out_shape=(*outs, jax.ShapeDtypeStruct(mix.s...  4.25 us
    ppermute x6, waiting for transfers between devices, swap(): return lax.ppermute(rows, 'exp', [(n, n ^ 1) for n in range(owners)])  3.73 us
    pallas_call x6, Pallas kernels, local(): pl.pallas_call(kernel, out_shape=outs, in_specs=[VMEM] * len(args), out_s...  2.02 us
    pallas_call x1, Pallas kernels, per_device(): pl.pallas_call(functools.partial(dispatch_kernel, flight), out_shape=(jax...  1.91 us
    ppermute x6, starting transfers between devices, swap(): return lax.ppermute(rows, 'exp', [(n, n ^ 1) for n in range(owners)])  1.73 us
    pallas_call x1, Pallas kernels, combine(): pl.pallas_call(functools.partial(combine_kernel, paired), out_shape=jax.S...  1.17 us
  transfers between devices with their start and end apart: 15, of which 8 were waited for; matrix products, arithmetic and copies ran while one was open for 0% of the time, Pallas kernels for 12%

profile of v25, /device:TPU:0, one launch (start us, length us, event | category | flops | bytes accessed | tf_op | source)
XLA Modules:
  0.0 37.4 jit_solution(16252059334543456240)
XLA Ops:
  0.0 1.9 %dispatch.1 = (bf16[128,128]{1,0:T(8,128)(2,1)S(1)}, bf16[24,3200]{1,0:T(8,128)(2,1)S(1)}, bf16[32,3200]{1,0:T(8,128)(2,1)S(1)}, bf16[8,3200]{1,0:T(8,128)(2,1)S(1)}, bf16[8,3200]{1,0:T(8,128)(2,1)S(1)}) custom-call(bf16[128,3584]{1,0:T(8,128)(2,1)} %tok_hbm.1, f32[3584]{0:T(1024)} %gain_hbm.1, s32[8,128]{1,0:T(8,128)} %bitcast.8, f32[8,128]{1,0:T(8,128)} %bitcast.9), custom_call_target="tpu_custom_call" | custom-call | tf_op jit(solution)/shard_map/dispatch/pallas_call | solution.py:285
  1.9 0.5 %collective-permute-start = (bf16[32,3200]{1,0:T(8,128)(2,1)S(1)}, bf16[32,3200]{1,0:T(8,128)(2,1)S(1)}, u32[]{:S(2)}, u32[]{:S(2)}) collective-permute-start(bf16[32,3200]{1,0:T(8,128)(2,1)S(1)} %get-tuple-element.39), channel_id=1, source_target_pairs={{0,1},{1,0},{2,3},{3,2},{4,5},{5,4},{6,7},{7,6},{8,9},{9,8},{10,11... | collective-permute-start | bytes 614408 | tf_op jit(solution)/shard_map/ppermute | solution.py:243
  2.4 1.1 %collective-permute-done.got_ref = bf16[32,3200]{1,0:T(8,128)(2,1)S(1)} collective-permute-done((bf16[32,3200]{1,0:T(8,128)(2,1)S(1)}, bf16[32,3200]{1,0:T(8,128)(2,1)S(1)}, u32[]{:S(2)}, u32[]{:S(2)}) %collective-permute-start) | collective-permute-done | bytes 204832 | tf_op jit(solution)/shard_map/ppermute | solution.py:243
  3.5 4.0 %collective-permute-start.1 = (bf16[16,3200]{1,0:T(8,128)(2,1)S(1)}, bf16[16,3200]{1,0:T(8,128)(2,1)S(1)}, u32[]{:S(2)}, u32[]{:S(2)}) collective-permute-start(bf16[16,3200]{1,0:T(8,128)(2,1)S(1)} %get-tuple-element.40), channel_id=1, source_target_pairs={{0,8},{1,13},{2,10},{3,15},{4,12},{5,9},{6,14},{7,11},{8,0},{9,5},... | collective-permute-start | bytes 307208 | tf_op jit(solution)/shard_map/ppermute | solution.py:247
  7.6 1.5 %collective-permute-start.2 = (bf16[16,3200]{1,0:T(8,128)(2,1)S(1)}, bf16[16,3200]{1,0:T(8,128)(2,1)S(1)}, u32[]{:S(2)}, u32[]{:S(2)}) collective-permute-start(bf16[16,3200]{1,0:T(8,128)(2,1)S(1)} %get-tuple-element.41), channel_id=1, source_target_pairs={{0,2},{1,5},{2,0},{3,7},{4,6},{5,1},{6,4},{7,3},{8,10},{9,13},{10,... | collective-permute-start | bytes 307208 | tf_op jit(solution)/shard_map/ppermute | solution.py:247
  9.1 0.0 collective-permute-start.3
  9.1 2.8 %collective-permute-start.4 = (bf16[8,3200]{1,0:T(8,128)(2,1)S(1)}, bf16[8,3200]{1,0:T(8,128)(2,1)S(1)}, u32[]{:S(2)}, u32[]{:S(2)}) collective-permute-start(bf16[8,3200]{1,0:T(8,128)(2,1)S(1)} %get-tuple-element.43), channel_id=1, source_target_pairs={{0,6},{1,7},{2,4},{3,5},{4,2},{5,3},{6,0},{7,1},{8,14},{9,15},{10,... | collective-permute-start | bytes 153608 | tf_op jit(solution)/shard_map/ppermute | solution.py:247
  11.9 4.2 %stage.1 = (bf16[3584,512]{1,0:T(8,128)(2,1)S(1)}, bf16[3584,512]{1,0:T(8,128)(2,1)S(1)}, bf16[512,3584]{1,0:T(8,128)(2,1)S(1)}, bf16[128,128]{1,0:T(8,128)(2,1)S(1)}) custom-call(bf16[128,128]{1,0:T(8,128)(2,1)S(1)} %get-tuple-element.44.mix_ref, bf16[3584,512]{1,0:T(8,128)(2,1)} %bitcast.5, bf16[3584,512]{1,0:T(8,128)(2,1)} %bitcast.6, ...), custom_call_target="tpu_custom_call" | custom-call | flops 1 | bytes 1 | tf_op jit(solution)/shard_map/stage/pallas_call | solution.py:252
  16.2 0.1 collective-permute-done.4.refs_3_
  16.2 0.0 collective-permute-done.1.refs_0_
  16.2 0.0 collective-permute-done.2.refs_1_
  16.2 2.3 %collective-permute-done.3.refs_2_ = bf16[16,3200]{1,0:T(8,128)(2,1)S(1)} collective-permute-done((bf16[16,3200]{1,0:T(8,128)(2,1)S(1)}, bf16[16,3200]{1,0:T(8,128)(2,1)S(1)}, u32[]{:S(2)}, u32[]{:S(2)}) %collective-permute-start.3) | collective-permute-done | bytes 102432 | tf_op jit(solution)/shard_map/ppermute | solution.py:247
  18.5 0.1 collective-permute-start.5
  18.6 1.7 %collective-permute-done.5.refs_2_ = bf16[56,3200]{1,0:T(8,128)(2,1)S(1)} collective-permute-done((bf16[56,3200]{1,0:T(8,128)(2,1)S(1)}, bf16[56,3200]{1,0:T(8,128)(2,1)S(1)}, u32[]{:S(2)}, u32[]{:S(2)}) %collective-permute-start.5) | collective-permute-done | bytes 358432 | tf_op jit(solution)/shard_map/ppermute | solution.py:243
  20.3 1.8 %experts.1 = (bf16[32,3584]{1,0:T(8,128)(2,1)S(1)}, bf16[32,3584]{1,0:T(8,128)(2,1)S(1)}, bf16[32,3584]{1,0:T(8,128)(2,1)S(1)}, bf16[32,3584]{1,0:T(8,128)(2,1)S(1)}) custom-call(bf16[56,3200]{1,0:T(8,128)(2,1)S(1)} %gather.1.refs_0_, bf16[8,3200]{1,0:T(8,128)(2,1)S(1)} %get-tuple-element.54.refs_1_, bf16[56,3200]{1,0:T(8,128)(2,1)S(1)} %collective-permute-done.5.refs_2_, ...), custom_call_target="tpu_custom_call" | custom-call | flops 1 | bytes 1 | tf_op jit(solution)/shard_map/experts/pallas_call | solution.py:225
  22.0 0.2 collective-permute-start.6
  22.2 0.4 collective-permute-start.9
  22.6 1.0 %collective-permute-done.6.got_ref = bf16[32,3584]{1,0:T(8,128)(2,1)S(1)} collective-permute-done((bf16[32,3584]{1,0:T(8,128)(2,1)S(1)}, bf16[32,3584]{1,0:T(8,128)(2,1)S(1)}, u32[]{:S(2)}, u32[]{:S(2)}) %collective-permute-start.6) | collective-permute-done | bytes 229408 | tf_op jit(solution)/shard_map/ppermute | solution.py:243
  23.6 0.1 join.2
  23.7 0.6 %collective-permute-start.7 = (bf16[16,3200]{1,0:T(8,128)(2,1)S(1)}, bf16[16,3200]{1,0:T(8,128)(2,1)S(1)}, u32[]{:S(2)}, u32[]{:S(2)}) collective-permute-start(bf16[16,3200]{1,0:T(8,128)(2,1)S(1)} %get-tuple-element.61), channel_id=1, source_target_pairs={{0,8},{1,13},{2,10},{3,15},{4,12},{5,9},{6,14},{7,11},{8,0},{9,5},... | collective-permute-start | bytes 307208 | tf_op jit(solution)/shard_map/ppermute | solution.py:247
  24.3 0.5 %collective-permute-start.8 = (bf16[16,3200]{1,0:T(8,128)(2,1)S(1)}, bf16[16,3200]{1,0:T(8,128)(2,1)S(1)}, u32[]{:S(2)}, u32[]{:S(2)}) collective-permute-start(bf16[16,3200]{1,0:T(8,128)(2,1)S(1)} %get-tuple-element.62), channel_id=1, source_target_pairs={{0,2},{1,5},{2,0},{3,7},{4,6},{5,1},{6,4},{7,3},{8,10},{9,13},{10,... | collective-permute-start | bytes 307208 | tf_op jit(solution)/shard_map/ppermute | solution.py:247
  24.8 0.1 join.3
  24.9 3.4 %collective-permute-start.10 = (bf16[8,3200]{1,0:T(8,128)(2,1)S(1)}, bf16[8,3200]{1,0:T(8,128)(2,1)S(1)}, u32[]{:S(2)}, u32[]{:S(2)}) collective-permute-start(bf16[8,3200]{1,0:T(8,128)(2,1)S(1)} %get-tuple-element.65), channel_id=1, source_target_pairs={{0,10},{1,15},{2,8},{3,13},{4,14},{5,11},{6,12},{7,9},{8,2},{9,7},... | collective-permute-start | bytes 153608 | tf_op jit(solution)/shard_map/ppermute | solution.py:247
  28.3 2.0 %collective-permute-start.13 = (bf16[8,3200]{1,0:T(8,128)(2,1)S(1)}, bf16[8,3200]{1,0:T(8,128)(2,1)S(1)}, u32[]{:S(2)}, u32[]{:S(2)}) collective-permute-start(bf16[8,3200]{1,0:T(8,128)(2,1)S(1)} %get-tuple-element.68), channel_id=1, source_target_pairs={{0,11},{1,14},{2,9},{3,12},{4,15},{5,10},{6,13},{7,8},{8,3},{9,6},... | collective-permute-start | bytes 153608 | tf_op jit(solution)/shard_map/ppermute | solution.py:247
  30.3 1.2 %collective-permute-start.14 = (bf16[8,3200]{1,0:T(8,128)(2,1)S(1)}, bf16[8,3200]{1,0:T(8,128)(2,1)S(1)}, u32[]{:S(2)}, u32[]{:S(2)}) collective-permute-start(bf16[8,3200]{1,0:T(8,128)(2,1)S(1)} %get-tuple-element.69), channel_id=1, source_target_pairs={{0,6},{1,7},{2,4},{3,5},{4,2},{5,3},{6,0},{7,1},{8,14},{9,15},{10,... | collective-permute-start | bytes 153608 | tf_op jit(solution)/shard_map/ppermute | solution.py:247
  31.5 1.5 %collective-permute-done.7.refs_0_ = bf16[16,3200]{1,0:T(8,128)(2,1)S(1)} collective-permute-done((bf16[16,3200]{1,0:T(8,128)(2,1)S(1)}, bf16[16,3200]{1,0:T(8,128)(2,1)S(1)}, u32[]{:S(2)}, u32[]{:S(2)}) %collective-permute-start.7) | collective-permute-done | bytes 102432 | tf_op jit(solution)/shard_map/ppermute | solution.py:247
  33.0 0.1 collective-permute-start.11
  33.1 0.5 %collective-permute-start.12 = (bf16[8,3200]{1,0:T(8,128)(2,1)S(1)}, bf16[8,3200]{1,0:T(8,128)(2,1)S(1)}, u32[]{:S(2)}, u32[]{:S(2)}) collective-permute-start(bf16[8,3200]{1,0:T(8,128)(2,1)S(1)} %get-tuple-element.67), channel_id=1, source_target_pairs={{0,1},{1,0},{2,3},{3,2},{4,5},{5,4},{6,7},{7,6},{8,9},{9,8},{10,11... | collective-permute-start | bytes 153608 | tf_op jit(solution)/shard_map/ppermute | solution.py:243
  33.6 1.1 %collective-permute-done.10.refs_2_ = bf16[8,3200]{1,0:T(8,128)(2,1)S(1)} collective-permute-done((bf16[8,3200]{1,0:T(8,128)(2,1)S(1)}, bf16[8,3200]{1,0:T(8,128)(2,1)S(1)}, u32[]{:S(2)}, u32[]{:S(2)}) %collective-permute-start.10) | collective-permute-done | bytes 51232 | tf_op jit(solution)/shard_map/ppermute | solution.py:247
  34.7 0.0 collective-permute-done.13.refs_5_
  34.7 1.6 %collective-permute-done.14.refs_6_ = bf16[8,3200]{1,0:T(8,128)(2,1)S(1)} collective-permute-done((bf16[8,3200]{1,0:T(8,128)(2,1)S(1)}, bf16[8,3200]{1,0:T(8,128)(2,1)S(1)}, u32[]{:S(2)}, u32[]{:S(2)}) %collective-permute-start.14) | collective-permute-done | bytes 51232 | tf_op jit(solution)/shard_map/ppermute | solution.py:247
  36.2 1.2 %combine.1 = bf16[128,3584]{1,0:T(8,128)(2,1)} custom-call(bf16[128,128]{1,0:T(8,128)(2,1)S(1)} %get-tuple-element.49.mix_ref, bf16[16,3200]{1,0:T(8,128)(2,1)S(1)} %collective-permute-done.7.refs_0_, bf16[16,3200]{1,0:T(8,128)(2,1)S(1)} %collective-permute-done.8.refs_1_, bf16[8,3200]{1,0:T(8,128)(2,1)S(1)} %collective-permute-done.10.refs_2_, ...), custom_call_target="tpu_custom_call" | custom-call | tf_op jit(solution)/shard_map/combine/pallas_call | solution.py:271
  (7 shorter events, 0.1 us)
Async XLA Ops:
  1.9 1.6 %collective-permute-start = (bf16[32,3200]{1,0:T(8,128)(2,1)S(1)}, bf16[32,3200]{1,0:T(8,128)(2,1)S(1)}, u32[]{:S(2)}, u32[]{:S(2)}) collective-permute-start(bf16[32,3200]{1,0:T(8,128)(2,1)S(1)} %get-tuple-element.39), channel_id=1, source_target_pairs={{0,1},{1,0},{2,3},{3,2},{4,5},{5,4},{6,7},{7,6},{8,9},{9,8},{10,11... | collective-permute-start | bytes 614408 | tf_op jit(solution)/shard_map/ppermute | solution.py:243
  3.5 12.7 %collective-permute-start.1 = (bf16[16,3200]{1,0:T(8,128)(2,1)S(1)}, bf16[16,3200]{1,0:T(8,128)(2,1)S(1)}, u32[]{:S(2)}, u32[]{:S(2)}) collective-permute-start(bf16[16,3200]{1,0:T(8,128)(2,1)S(1)} %get-tuple-element.40), channel_id=1, source_target_pairs={{0,8},{1,13},{2,10},{3,15},{4,12},{5,9},{6,14},{7,11},{8,0},{9,5},... | collective-permute-start | bytes 307208 | tf_op jit(solution)/shard_map/ppermute | solution.py:247
  7.6 8.7 %collective-permute-start.2 = (bf16[16,3200]{1,0:T(8,128)(2,1)S(1)}, bf16[16,3200]{1,0:T(8,128)(2,1)S(1)}, u32[]{:S(2)}, u32[]{:S(2)}) collective-permute-start(bf16[16,3200]{1,0:T(8,128)(2,1)S(1)} %get-tuple-element.41), channel_id=1, source_target_pairs={{0,2},{1,5},{2,0},{3,7},{4,6},{5,1},{6,4},{7,3},{8,10},{9,13},{10,... | collective-permute-start | bytes 307208 | tf_op jit(solution)/shard_map/ppermute | solution.py:247
  9.1 9.4 %collective-permute-start.3 = (bf16[16,3200]{1,0:T(8,128)(2,1)S(1)}, bf16[16,3200]{1,0:T(8,128)(2,1)S(1)}, u32[]{:S(2)}, u32[]{:S(2)}) collective-permute-start(bf16[16,3200]{1,0:T(8,128)(2,1)S(1)} %get-tuple-element.42), channel_id=1, source_target_pairs={{0,10},{1,15},{2,8},{3,13},{4,14},{5,11},{6,12},{7,9},{8,2},{9,7},... | collective-permute-start | bytes 307208 | tf_op jit(solution)/shard_map/ppermute | solution.py:247
  9.1 7.1 %collective-permute-start.4 = (bf16[8,3200]{1,0:T(8,128)(2,1)S(1)}, bf16[8,3200]{1,0:T(8,128)(2,1)S(1)}, u32[]{:S(2)}, u32[]{:S(2)}) collective-permute-start(bf16[8,3200]{1,0:T(8,128)(2,1)S(1)} %get-tuple-element.43), channel_id=1, source_target_pairs={{0,6},{1,7},{2,4},{3,5},{4,2},{5,3},{6,0},{7,1},{8,14},{9,15},{10,... | collective-permute-start | bytes 153608 | tf_op jit(solution)/shard_map/ppermute | solution.py:247
  18.5 1.7 %collective-permute-start.5 = (bf16[56,3200]{1,0:T(8,128)(2,1)S(1)}, bf16[56,3200]{1,0:T(8,128)(2,1)S(1)}, u32[]{:S(2)}, u32[]{:S(2)}) collective-permute-start(bf16[56,3200]{1,0:T(8,128)(2,1)S(1)} %gather.1.refs_0_), channel_id=1, source_target_pairs={{0,1},{1,0},{2,3},{3,2},{4,5},{5,4},{6,7},{7,6},{8,9},{9,8},{10,11... | collective-permute-start | bytes 1075208 | tf_op jit(solution)/shard_map/ppermute | solution.py:243
  22.0 1.6 %collective-permute-start.6 = (bf16[32,3584]{1,0:T(8,128)(2,1)S(1)}, bf16[32,3584]{1,0:T(8,128)(2,1)S(1)}, u32[]{:S(2)}, u32[]{:S(2)}) collective-permute-start(bf16[32,3584]{1,0:T(8,128)(2,1)S(1)} %get-tuple-element.60), channel_id=1, source_target_pairs={{0,1},{1,0},{2,3},{3,2},{4,5},{5,4},{6,7},{7,6},{8,9},{9,8},{10,11... | collective-permute-start | bytes 688136 | tf_op jit(solution)/shard_map/ppermute | solution.py:243
  22.2 2.6 %collective-permute-start.9 = (bf16[32,3584]{1,0:T(8,128)(2,1)S(1)}, bf16[32,3584]{1,0:T(8,128)(2,1)S(1)}, u32[]{:S(2)}, u32[]{:S(2)}) collective-permute-start(bf16[32,3584]{1,0:T(8,128)(2,1)S(1)} %get-tuple-element.64), channel_id=1, source_target_pairs={{0,1},{1,0},{2,3},{3,2},{4,5},{5,4},{6,7},{7,6},{8,9},{9,8},{10,11... | collective-permute-start | bytes 688136 | tf_op jit(solution)/shard_map/ppermute | solution.py:243
  23.7 9.3 %collective-permute-start.7 = (bf16[16,3200]{1,0:T(8,128)(2,1)S(1)}, bf16[16,3200]{1,0:T(8,128)(2,1)S(1)}, u32[]{:S(2)}, u32[]{:S(2)}) collective-permute-start(bf16[16,3200]{1,0:T(8,128)(2,1)S(1)} %get-tuple-element.61), channel_id=1, source_target_pairs={{0,8},{1,13},{2,10},{3,15},{4,12},{5,9},{6,14},{7,11},{8,0},{9,5},... | collective-permute-start | bytes 307208 | tf_op jit(solution)/shard_map/ppermute | solution.py:247
  24.3 8.7 %collective-permute-start.8 = (bf16[16,3200]{1,0:T(8,128)(2,1)S(1)}, bf16[16,3200]{1,0:T(8,128)(2,1)S(1)}, u32[]{:S(2)}, u32[]{:S(2)}) collective-permute-start(bf16[16,3200]{1,0:T(8,128)(2,1)S(1)} %get-tuple-element.62), channel_id=1, source_target_pairs={{0,2},{1,5},{2,0},{3,7},{4,6},{5,1},{6,4},{7,3},{8,10},{9,13},{10,... | collective-permute-start | bytes 307208 | tf_op jit(solution)/shard_map/ppermute | solution.py:247
  24.9 9.8 %collective-permute-start.10 = (bf16[8,3200]{1,0:T(8,128)(2,1)S(1)}, bf16[8,3200]{1,0:T(8,128)(2,1)S(1)}, u32[]{:S(2)}, u32[]{:S(2)}) collective-permute-start(bf16[8,3200]{1,0:T(8,128)(2,1)S(1)} %get-tuple-element.65), channel_id=1, source_target_pairs={{0,10},{1,15},{2,8},{3,13},{4,14},{5,11},{6,12},{7,9},{8,2},{9,7},... | collective-permute-start | bytes 153608 | tf_op jit(solution)/shard_map/ppermute | solution.py:247
  28.3 6.4 %collective-permute-start.13 = (bf16[8,3200]{1,0:T(8,128)(2,1)S(1)}, bf16[8,3200]{1,0:T(8,128)(2,1)S(1)}, u32[]{:S(2)}, u32[]{:S(2)}) collective-permute-start(bf16[8,3200]{1,0:T(8,128)(2,1)S(1)} %get-tuple-element.68), channel_id=1, source_target_pairs={{0,11},{1,14},{2,9},{3,12},{4,15},{5,10},{6,13},{7,8},{8,3},{9,6},... | collective-permute-start | bytes 153608 | tf_op jit(solution)/shard_map/ppermute | solution.py:247
  30.3 6.0 %collective-permute-start.14 = (bf16[8,3200]{1,0:T(8,128)(2,1)S(1)}, bf16[8,3200]{1,0:T(8,128)(2,1)S(1)}, u32[]{:S(2)}, u32[]{:S(2)}) collective-permute-start(bf16[8,3200]{1,0:T(8,128)(2,1)S(1)} %get-tuple-element.69), channel_id=1, source_target_pairs={{0,6},{1,7},{2,4},{3,5},{4,2},{5,3},{6,0},{7,1},{8,14},{9,15},{10,... | collective-permute-start | bytes 153608 | tf_op jit(solution)/shard_map/ppermute | solution.py:247
  33.0 3.3 %collective-permute-start.11 = (bf16[8,3200]{1,0:T(8,128)(2,1)S(1)}, bf16[8,3200]{1,0:T(8,128)(2,1)S(1)}, u32[]{:S(2)}, u32[]{:S(2)}) collective-permute-start(bf16[8,3200]{1,0:T(8,128)(2,1)S(1)} %get-tuple-element.66), channel_id=1, source_target_pairs={{0,1},{1,0},{2,3},{3,2},{4,5},{5,4},{6,7},{7,6},{8,9},{9,8},{10,11... | collective-permute-start | bytes 153608 | tf_op jit(solution)/shard_map/ppermute | solution.py:243
  33.1 3.2 %collective-permute-start.12 = (bf16[8,3200]{1,0:T(8,128)(2,1)S(1)}, bf16[8,3200]{1,0:T(8,128)(2,1)S(1)}, u32[]{:S(2)}, u32[]{:S(2)}) collective-permute-start(bf16[8,3200]{1,0:T(8,128)(2,1)S(1)} %get-tuple-element.67), channel_id=1, source_target_pairs={{0,1},{1,0},{2,3},{3,2},{4,5},{5,4},{6,7},{7,6},{8,9},{9,8},{10,11... | collective-permute-start | bytes 153608 | tf_op jit(solution)/shard_map/ppermute | solution.py:243
